TPU v7x, 32 devices: a whole 2x2x4 slice. The times are simulated.
32 devices in a mesh: replica: 8 (over y, x, core), tensor: 4 (over z).
Axes of the slice: x: 2, y: 2, z: 4, core: 2. Of those that a mesh axis runs over, the one named last changes fastest.
Arguments:
- x_in: bfloat16 [4096, 4096], P('replica', 'tensor'), may hold values from -6 to 6
- gate_z: bfloat16 [4096, 4096], P('replica', 'tensor'), may hold values from -6 to 6
- b_proj: bfloat16 [4096, 1024], P('replica', 'tensor'), may hold values from -2 to 2
- c_proj: bfloat16 [4096, 1024], P('replica', 'tensor'), may hold values from -2 to 2
- dt_raw: float32 [4096, 64], P('replica', 'tensor'), may hold values from -5 to 5
- a_log: float32 [64], P('tensor'), may hold values from 0 to 2.77
- dt_bias: float32 [64], P('tensor'), may hold values from -6 to -2
- skip_d: float32 [64], P('tensor'), may hold values from 0.5 to 1.5
- norm_gain: float32 [4096], P('tensor'), may hold values from 0.5 to 1.5
- out_weight: bfloat16 [8, 2048, 4096], P('replica', None, 'tensor'), may hold values from -0.125 to 0.125
- global_weight: float32 [2048, 4096], P('replica', 'tensor'), may hold values from -0.09375 to 0.09375
- momentum: float32 [2048, 4096], P('replica', 'tensor'), may hold values from -0.04 to 0.04
- target: bfloat16 [4096, 2048], P(('replica', 'tensor')), may hold values from -6 to 6
Outputs:
- grad_x: bfloat16 [4096, 4096], P('replica', 'tensor')
- new_weight: bfloat16 [2048, 4096], P(None, 'tensor')
- new_global: float32 [2048, 4096], P('replica', 'tensor')
- new_momentum: float32 [2048, 4096], P('replica', 'tensor')
All inputs are finite; a program needn't handle non-finite values.
Results may differ from a plain program's by a relative error of at most 0.0085.
Values may be sent and summed in bfloat16 or wider, within the bound.
No kernel may reach another device: no remote copies, remote signals or barrier semaphores. Data moves between devices by JAX's collectives and lax.ppermute only.
A program may use at most 128 MiB of HBM per device.

v0:
```python
import jax
import jax.numpy as jnp
from jax import lax
from jax.sharding import PartitionSpec as P

HEAD_DIM = 64
STATE = 128
SPAN = 256


inner_rate = 0.001
outer_rate = 0.7
outer_beta = 0.9
clip_rms = 0.005


def gated_ssd(inputs_f, gate_z, b_proj, c_proj, dt_raw, a_log, dt_bias, skip_d, norm_gain):
    tokens = inputs_f.shape[0]
    head_count = a_log.shape[0]
    group_count = b_proj.shape[1] // STATE
    per_group = head_count // group_count
    block_count = tokens // SPAN
    values = inputs_f.reshape(block_count, SPAN, group_count, per_group, HEAD_DIM)
    step_size = jax.nn.softplus(dt_raw + dt_bias).reshape(block_count, SPAN, group_count, per_group)
    log_decay = (-jnp.exp(a_log)).reshape(group_count, per_group) * step_size
    cum_decay = jnp.cumsum(log_decay, axis=1)
    key_proj = b_proj.astype(jnp.float32).reshape(block_count, SPAN, group_count, STATE)
    query_proj = c_proj.astype(jnp.float32).reshape(block_count, SPAN, group_count, STATE)
    scores = jnp.einsum("clgn,csgn->cgls", query_proj, key_proj)
    cumulative = cum_decay.transpose(0, 2, 3, 1)
    gap_decay = cumulative[..., :, None] - cumulative[..., None, :]
    causal_mask = jnp.tril(jnp.ones((SPAN, SPAN), dtype=bool))
    decay_table = jnp.where(causal_mask, jnp.exp(jnp.where(causal_mask, gap_decay, 0.0)), 0.0)
    weights = scores[:, :, None] * decay_table * step_size.transpose(0, 2, 3, 1)[..., None, :]
    inside = jnp.einsum("cgrls,csgrp->clgrp", weights, values)
    tail_weight = jnp.exp(cum_decay[:, -1:] - cum_decay) * step_size
    states = jnp.einsum("csgn,csgr,csgrp->cgrpn", key_proj, tail_weight, values)
    span_fade = jnp.exp(cum_decay[:, -1])

    def carry_state(carried, inputs_pair):
        fade_now, state_now = inputs_pair
        return (fade_now[..., None, None] * carried + state_now, carried)

    _, entering = lax.scan(
        carry_state, jnp.zeros(states.shape[1:], jnp.float32), (span_fade, states)
    )
    outside = jnp.einsum("clgn,cgrpn->clgrp", query_proj, entering) * jnp.exp(cum_decay)[..., None]
    ssd_out = inside + outside + skip_d.reshape(group_count, per_group)[..., None] * values
    width = per_group * HEAD_DIM
    gated_vals = ssd_out.reshape(tokens, group_count, width) * jax.nn.silu(
        gate_z.astype(jnp.float32)
    ).reshape(tokens, group_count, width)
    inv_norm = lax.rsqrt(jnp.mean(gated_vals * gated_vals, axis=-1, keepdims=True) + 1e-05)
    return (gated_vals * inv_norm).reshape(tokens, head_count * HEAD_DIM) * norm_gain


def shards(
    x_in,
    gate_z,
    b_proj,
    c_proj,
    dt_raw,
    a_log,
    dt_bias,
    skip_d,
    norm_gain,
    out_weight,
    global_weight,
    momentum,
    target,
):
    local_weight = out_weight[0]

    def forward(inputs_f):
        return gated_ssd(
            inputs_f, gate_z, b_proj, c_proj, dt_raw, a_log, dt_bias, skip_d, norm_gain
        )

    normed_f, pull_back = jax.vjp(forward, x_in.astype(jnp.float32))
    normed = normed_f.astype(jnp.bfloat16)
    layer_part = lax.psum_scatter(
        lax.dot_general(
            normed, local_weight, (((1,), (1,)), ((), ())), preferred_element_type=jnp.float32
        ),
        "tensor",
        scatter_dimension=0,
        tiled=True,
    )
    cotangent_part = (layer_part - target.astype(jnp.float32)).astype(jnp.bfloat16)
    cotangent = lax.all_gather(cotangent_part, "tensor", axis=0, tiled=True)
    d_normed = jnp.dot(cotangent, local_weight, preferred_element_type=jnp.float32)
    grad_input = pull_back(d_normed)[0]
    weight_grad = lax.dot_general(
        cotangent, normed, (((0,), (0,)), ((), ())), preferred_element_type=jnp.float32
    )
    own_rows = local_weight.astype(jnp.float32)
    whole_term = own_rows - inner_rate * weight_grad
    summed = lax.psum_scatter(whole_term, "replica", scatter_dimension=0, tiled=True)
    replicas = lax.axis_size("replica")
    delta = global_weight - summed / replicas
    square_sum = lax.psum(jnp.sum(delta * delta), ("replica", "tensor"))
    entry_count = delta.shape[0] * delta.shape[1] * replicas * lax.axis_size("tensor")
    factor = jnp.minimum(1.0, clip_rms / jnp.sqrt(square_sum / entry_count + 1e-06))
    clipped = factor * delta
    new_momentum = outer_beta * momentum + clipped
    new_global = global_weight - outer_rate * (clipped + outer_beta * new_momentum)
    new_weight = lax.all_gather(new_global.astype(jnp.bfloat16), "replica", axis=0, tiled=True)
    return (grad_input.astype(jnp.bfloat16), new_weight, new_global, new_momentum)


def solution(mesh):
    placed = (
        P("replica", "tensor"),
        P("replica", "tensor"),
        P("replica", "tensor"),
        P("replica", "tensor"),
        P("replica", "tensor"),
        P("tensor"),
        P("tensor"),
        P("tensor"),
        P("tensor"),
        P("replica", None, "tensor"),
        P("replica", "tensor"),
        P("replica", "tensor"),
        P(("replica", "tensor"), None),
    )
    return jax.shard_map(
        shards,
        mesh=mesh,
        in_specs=placed,
        out_specs=(
            P("replica", "tensor"),
            P(None, "tensor"),
            P("replica", "tensor"),
            P("replica", "tensor"),
        ),
        check_vma=False,
    )
```

profile of v0, /device:TPU:0, one launch (start us, length us, event | category | flops | bytes accessed | tf_op | source)
XLA Modules:
  0.0 372.4 jit_solution(13002523262921048617)
XLA Ops:
  19.1 2.3 reshape.106
  21.4 4.0 %reshape.119 = bf16[2,256,2,8,64]{4,3,2,1,0:T(8,128)(2,1)} reshape(bf16[512,1024]{1,0:T(8,128)(2,1)} %param.17) | data formatting | bytes 2097152 | tf_op jit(solution)/shard_map/jvp()/reshape | solution.py:23
  25.5 3.6 copy.97
  36.6 4.3 %multiply_reduce_fusion.1 = (f32[2,256,2]{1,2,0:T(2,128)S(1)}, f32[2,256,2,8,64]{1,4,3,2,0:T(8,128)S(1)}) fusion(f32[2,256,2,8,64]{1,0,4,3,2:T(2,128)S(1)} %copy-done.4, bf16[2,256,2,8,64]{1,4,3,2,0:T(8,128)(2,1)S(1)} %copy-done.6, f32[2,8]{1,0:T(2,128)S(1)} %mul.205, f32[2,256,2,8]{1,3,2,0:T(8,128)S(1)} %get-tuple-element.219, ...), kind=kOutput, calls=%fused_computation.51 | convolution fusion | flops 283114496 | bytes 8556608 | tf_op jit(solution)/shard_map/jvp(cgrls,csgrp->clgrp)/dot_general | solution.py:35
  43.6 3.8 %copy.127 = f32[2,256,2,8,64]{4,3,2,1,0:T(8,128)} copy(f32[2,256,2,8,64]{1,4,3,2,0:T(8,128)S(1)} %get-tuple-element.224) | data formatting | bytes 4194304 | tf_op jit(solution)/shard_map/jvp()/reshape | solution.py:50
  47.3 4.9 %reshape.116 = f32[512,1024]{1,0:T(8,128)} reshape(f32[2,256,2,8,64]{4,3,2,1,0:T(8,128)} %copy.127) | data formatting | bytes 4194304 | tf_op jit(solution)/shard_map/jvp()/reshape | solution.py:50
  52.3 3.2 multiply_convert_fusion
  56.4 4.4 %fusion.5 = f32[512,2048]{1,0:T(8,128)} fusion(bf16[512,1024]{1,0:T(8,128)(2,1)S(1)} %multiply_convert_fusion, bf16[1,2048,1024]{2,1,0:T(8,128)(2,1)S(1)} %copy-done.22), kind=kOutput, calls=%fused_computation.14 | convolution fusion | flops 2147483648 | bytes 9437184 | tf_op jit(solution)/shard_map/dot_general | solution.py:82
  60.9 79.5 %reduce-scatter.3.cloned.1.call-done = f32[128,2048]{1,0:T(8,128)} async-done(((f32[512,2048]{1,0:T(8,128)}), f32[128,2048]{1,0:T(8,128)}) %reduce-scatter.3.cloned.1.call-update) | async-done | bytes 1048592 | tf_op jit(solution)/shard_map/reduce_scatter | solution.py:81
  142.8 46.6 %all-gather.3.cloned.1.call-done = bf16[512,2048]{1,0:T(8,128)(2,1)} async-done(((bf16[128,2048]{1,0:T(8,128)(2,1)}), bf16[512,2048]{1,0:T(8,128)(2,1)}) %all-gather.3.cloned.1.call-update) | async-done | bytes 2097168 | tf_op jit(solution)/shard_map/all_gather | solution.py:90
  189.3 8.5 %multiply_subtract_fusion = f32[2048,1024]{1,0:T(8,128)} fusion(bf16[512,2048]{1,0:T(8,128)(2,1)} %all-gather.3.cloned.1.call-done, bf16[512,1024]{1,0:T(8,128)(2,1)S(1)} %copy-done.16, bf16[1,2048,1024]{2,1,0:T(8,128)(2,1)} %param.26), kind=kOutput, calls=%fused_computation.8 | convolution fusion | flops 2153775104 | bytes 15728640 | tf_op jit(solution)/shard_map/dot_general | solution.py:93
  197.9 70.1 %reduce-scatter.5.cloned.1.call-done = f32[256,1024]{1,0:T(8,128)} async-done(((f32[2048,1024]{1,0:T(8,128)}), f32[256,1024]{1,0:T(8,128)}) %reduce-scatter.5.cloned.1.call-update) | async-done | bytes 1048592 | tf_op jit(solution)/shard_map/reduce_scatter | solution.py:98
  270.1 39.5 %psum.7 = f32[]{:T(128)} all-reduce(f32[]{:T(128)} %multiply_reduce_fusion.2), channel_id=1, replica_groups=mesh['replica'=8,'tensor'=4] {'replica','tensor'}, use_global_device_ids=true, to_apply=%region_11.12 | all-reduce | flops 1 | bytes 8 | tf_op jit(solution)/shard_map/psum | solution.py:101
  310.3 3.5 fusion.50
  313.9 3.0 copy.102
  316.8 3.9 %reshape.108 = f32[512,2,512]{0,2,1:T(8,128)} reshape(f32[2,256,2,8,64]{1,0,4,3,2:T(2,128)} %copy.102) | data formatting | bytes 4194304 | tf_op jit(solution)/shard_map/jvp()/reshape | solution.py:50
  320.8 6.9 %fusion.32 = f32[512,1024]{1,0:T(8,128)} fusion(bf16[512,2048]{1,0:T(8,128)(2,1)} %all-gather.3.cloned.1.call-done, bf16[1,2048,1024]{2,1,0:T(8,128)(2,1)} %param.26, f32[1024]{0:T(1024)S(1)} %copy-done.21), kind=kOutput, calls=%fused_computation.53 | convolution fusion | flops 2148007936 | bytes 8392704 | tf_op jit(solution)/shard_map/dot_general | solution.py:91
  327.6 4.5 %reshape.117 = f32[2,256,2,8,64]{4,3,2,1,0:T(8,128)} reshape(f32[512,1024]{1,0:T(8,128)} %fusion.32) | data formatting | bytes 4194304 | tf_op jit(solution)/shard_map/transpose(jvp())/reshape | solution.py:54
  332.1 2.9 copy.131
  335.1 4.9 %copy.108 = f32[2,256,2,8,64]{1,4,3,2,0:T(8,128)} copy(f32[2,256,2,8,64]{4,3,2,1,0:T(8,128)} %reshape.117) | data formatting | bytes 4194304 | tf_op jit(solution)/shard_map/transpose(jvp())/reshape | solution.py:54
  339.9 3.6 multiply_reduce_fusion
  347.0 4.0 %fusion.1 = f32[2,2,8,64,256]{4,3,2,1,0:T(8,128)} fusion(f32[2,2,8,256]{3,2,1,0:T(8,128)S(1)} %copy-done.20, f32[2,2,8,256]{3,2,1,0:T(8,128)S(1)} %copy-done.18, f32[2,2,256,256]{3,2,1,0:T(8,128)S(1)} %copy-done.14, pred[256,256]{1,0:T(8,128)(4,1)S(1)} %iota_compare_fusion, f32[2,256,2,8,64]{1,4,3,2,0:T(8,128)S(1)} %fusion.24), kind=kOutput, calls=%fused_computation.10 | convolution fusion | flops 278921216 | bytes 5373952 | tf_op jit(solution)/shard_map/transpose(jvp(cgrls,csgrp->clgrp))/dot_general | solution.py:35
  351.2 2.7 while.33
  361.2 4.6 %copy.195 = bf16[2048,1024]{1,0:T(8,128)(2,1)} copy(bf16[2048,1024]{1,0:T(8,128)(2,1)} %all-gather.5.cloned.1.call-done) | data formatting | bytes 8388608
  (116 shorter events, 42.8 us)
Async XLA Ops:
  7.2 8.1 %copy-start.7 = (bf16[512,1024]{1,0:T(8,128)(2,1)S(1)}, bf16[512,1024]{1,0:T(8,128)(2,1)}, u32[]{:S(2)}) copy-start(bf16[512,1024]{1,0:T(8,128)(2,1)} %param.18) | copy-start | bytes 3145732
  7.2 133.3 %reduce-scatter.3.cloned.1.call-start = ((), (), s32[]{:S(2)}) async-start(), calls=%async_computation.2 | async-start | bytes 5242880 | tf_op jit(solution)/shard_map/reduce_scatter | solution.py:81
  15.3 13.8 %copy-start.10 = (bf16[2,256,2,128]{3,2,1,0:T(2,128)(2,1)}, bf16[2,256,2,128]{3,2,1,0:T(2,128)(2,1)S(1)}, u32[]{:S(2)}) copy-start(bf16[2,256,2,128]{3,2,1,0:T(2,128)(2,1)S(1)} %reshape.99) | copy-start | bytes 786436
  19.1 6.4 %copy-start.2 = (f32[512,1024]{0,1:T(8,128)}, f32[512,1024]{0,1:T(8,128)S(1)}, u32[]{:S(2)}) copy-start(f32[512,1024]{0,1:T(8,128)S(1)} %copy.104) | copy-start | bytes 6291460
  25.5 3.6 copy-start.23
  33.0 1.9 copy-start.11
  33.0 3.5 copy-start.6
  34.8 1.7 copy-start.4
  34.8 1.7 copy-start.17
  47.3 4.9 %copy-start.8 = (bf16[512,1024]{1,0:T(8,128)(2,1)S(1)}, bf16[512,1024]{1,0:T(8,128)(2,1)}, u32[]{:S(2)}) copy-start(bf16[512,1024]{1,0:T(8,128)(2,1)} %param.18) | copy-start | bytes 3145732
  52.3 4.2 %copy-start.22 = (bf16[1,2048,1024]{2,1,0:T(8,128)(2,1)S(1)}, bf16[1,2048,1024]{2,1,0:T(8,128)(2,1)}, u32[]{:S(2)}) copy-start(bf16[1,2048,1024]{2,1,0:T(8,128)(2,1)} %param.26) | copy-start | bytes 12582916
  60.8 128.5 %copy-start.16 = (bf16[512,1024]{1,0:T(8,128)(2,1)S(1)}, bf16[512,1024]{1,0:T(8,128)(2,1)}, u32[]{:S(2)}) copy-start(bf16[512,1024]{1,0:T(8,128)(2,1)} %copy-done.15) | copy-start | bytes 3145732
  60.9 128.5 %all-gather.3.cloned.1.call-start = ((), (), s32[]{:S(2)}) async-start(), calls=%async_computation.3 | async-start | bytes 2621440 | tf_op jit(solution)/shard_map/all_gather | solution.py:90
  142.7 125.2 %reduce-scatter.5.cloned.1.call-start = ((), (), s32[]{:S(2)}) async-start(), calls=%async_computation.4 | async-start | bytes 9437184 | tf_op jit(solution)/shard_map/reduce_scatter | solution.py:98
  197.8 70.2 %copy-start.9 = (f32[256,1024]{1,0:T(8,128)S(1)}, f32[256,1024]{1,0:T(8,128)}, u32[]{:S(2)}) copy-start(f32[256,1024]{1,0:T(8,128)} %param.27) | copy-start | bytes 3145732
  197.8 163.4 %all-gather.5.cloned.1.call-start = ((), (), s32[]{:S(2)}) async-start(), calls=%async_computation.5 | async-start | bytes 4718592 | tf_op jit(solution)/shard_map/all_gather | solution.py:107
  316.8 3.9 %copy-start.21 = (f32[1024]{0:T(1024)S(1)}, f32[1024]{0:T(1024)}, u32[]{:S(2)}) copy-start(f32[1024]{0:T(1024)} %param.25) | copy-start | bytes 12292
  339.9 3.6 copy-start.3
  339.9 4.2 %copy-start.5 = (f32[2,256,2,8,64]{1,0,4,3,2:T(2,128)S(1)}, f32[2,256,2,8,64]{1,0,4,3,2:T(2,128)}, u32[]{:S(2)}) copy-start(f32[2,256,2,8,64]{1,0,4,3,2:T(2,128)} %reshape.106) | copy-start | bytes 6291460
  345.0 6.0 %copy-start = (f32[2,256,2,8,64]{1,4,3,2,0:T(8,128)}, f32[2,256,2,8,64]{1,4,3,2,0:T(8,128)S(1)}, u32[]{:S(2)}) copy-start(f32[2,256,2,8,64]{1,4,3,2,0:T(8,128)S(1)} %fusion.24) | copy-start | bytes 6291460
  345.0 2.0 copy-start.14
  345.1 2.0 copy-start.18
  345.1 2.0 copy-start.20
  351.2 3.5 copy-start.1
  (4 other events, 4.5 us)
Sparse Core Ops, SparseCore 0:
  61.0 79.4 reduce-scatter.2
  142.9 46.4 all-gather.2
  197.9 69.9 reduce-scatter.4
  314.0 37.5 all-gather.4
where the time goes:
time: 373 us; the launch traced here: 372 us
  waiting for transfers between devices  196 us (53%)
  local copies, waits for them, and re-layouts  58.8 us (16%)
  blocking collectives  39.5 us (11%)
  matrix products  36.3 us (10%)
  other arithmetic  26.4 us (7%)
  between operations  14.8 us (4%)
    reduce_scatter x1, waiting for transfers between devices, shards(): lax.psum_scatter(lax.dot_general(normed, local_weight, (((1,), (1,)), (()...  79.5 us
    reduce_scatter x1, waiting for transfers between devices, shards(): lax.psum_scatter(whole_term, 'replica', scatter_dimension=0, tiled=True)  70.1 us
    all_gather x1, waiting for transfers between devices, shards(): cotangent = lax.all_gather(cotangent_part, 'tensor', axis=0, tiled=True)  46.6 us
    psum x1, blocking collectives, shards(): square_sum = lax.psum(jnp.sum(delta * delta), ('replica', 'tensor'))  39.5 us
    unnamed x52, local copies, waits for them, and re-layouts  13.9 us
    reshape x3, local copies, waits for them, and re-layouts, gated_ssd(): ssd_out.reshape(tokens, group_count, width)  12.6 us
    reshape x3, local copies, waits for them, and re-layouts, gated_ssd(): (gated_vals * inv_norm).reshape(tokens, head_count * HEAD_DIM) * norm_gain  12.3 us
    dot_general x1, matrix products, shards(): lax.dot_general(cotangent, normed, (((0,), (0,)), ((), ())), preferred_el...  8.46 us
  transfers between devices with their start and end apart: 4, of which 3 were waited for; matrix products, arithmetic and copies ran while one was open for 12% of the time, Pallas kernels for 0%

commit v1 on v0

v1 whole, which is shorter than its diff:
```python
import functools

import jax
import jax.numpy as jnp
from jax import lax
from jax.experimental import pallas as pl
from jax.experimental.pallas import tpu as pltpu
from jax.sharding import PartitionSpec as P

HEAD_DIM = 64
STATE = 128
SPAN = 256
HALF = SPAN // 2

inner_rate = 0.001
outer_rate = 0.7
outer_beta = 0.9
clip_rms = 0.005
LOG2E = 1.4426950408889634

F32 = jnp.float32
BF16 = jnp.bfloat16
NN = (((1,), (0,)), ((), ()))
NT = (((1,), (1,)), ((), ()))
TN = (((0,), (0,)), ((), ()))


def exact_dot(a, b, dims):
    return lax.dot_general(a, b, dims, precision=lax.Precision.HIGHEST, preferred_element_type=F32)


def fast_dot(a, b, dims):
    return lax.dot_general(a, b, dims, preferred_element_type=F32)


def silu(z):
    return z * (1.0 / (1.0 + jnp.exp(-z)))


def softplus(v):
    return jnp.maximum(v, 0.0) + jnp.log1p(jnp.exp(-jnp.abs(v)))


def head_tables(dt_ref, a_ref, bias_ref, per_group):
    first = pl.program_id(0) * per_group
    tokens, heads = dt_ref.shape
    pick = lax.broadcasted_iota(jnp.int32, (per_group, heads), 1) == (
        lax.broadcasted_iota(jnp.int32, (per_group, heads), 0) + first
    )
    dt = exact_dot(pick.astype(F32), dt_ref[...], NT)
    row = lax.broadcasted_iota(jnp.int32, (per_group, tokens), 0)
    bias = jnp.zeros((per_group, tokens), F32)
    a_log = jnp.zeros((per_group, tokens), F32)
    for h in range(per_group):
        bias = jnp.where(row == h, bias_ref[first + h], bias)
        a_log = jnp.where(row == h, a_ref[first + h], a_log)
    step = softplus(dt + bias)
    return step, -jnp.exp(a_log) * step * LOG2E


def span_tables(step, rate, lo, per_group, width):
    s_at = lax.broadcasted_iota(jnp.int32, (SPAN, SPAN), 0)
    t_at = lax.broadcasted_iota(jnp.int32, (SPAN, SPAN), 1)
    upper = (s_at <= t_at).astype(F32)
    step_k = step[:, lo : lo + SPAN]
    cum = exact_dot(rate[:, lo : lo + SPAN], upper, NN)
    cum_col = exact_dot((s_at == t_at).astype(F32), cum, NT)
    spread = (
        lax.broadcasted_iota(jnp.int32, (per_group, width), 1) // HEAD_DIM
        == lax.broadcasted_iota(jnp.int32, (per_group, width), 0)
    ).astype(F32)
    step_x = exact_dot(step_k, spread, TN)
    fade_x = exact_dot(jnp.exp2(cum), spread, TN)
    tail_x = exact_dot(jnp.exp2(cum[:, SPAN - 1 :] - cum) * step_k, spread, TN)
    return cum, cum_col, step_x, fade_x, tail_x


def forward_kernel(dt_ref, x_ref, z_ref, b_ref, c_ref, gain_ref, a_ref, bias_ref, skip_ref, normed_ref, inv_ref):
    tokens, width = x_ref.shape
    per_group = width // HEAD_DIM
    first = pl.program_id(0) * per_group
    step, rate = head_tables(dt_ref, a_ref, bias_ref, per_group)
    causal = lax.broadcasted_iota(jnp.int32, (HALF, HALF), 0) >= lax.broadcasted_iota(jnp.int32, (HALF, HALF), 1)
    spans = tokens // SPAN
    entering = None
    for k in range(spans):
        rows = slice(k * SPAN, (k + 1) * SPAN)
        cum, cum_col, step_x, fade_x, tail_x = span_tables(step, rate, k * SPAN, per_group, width)
        x = x_ref[rows, :].astype(F32)
        b, c = b_ref[rows, :], c_ref[rows, :]
        scores = fast_dot(c, b, NT)
        stepped = (x * step_x).astype(BF16)
        pieces = []
        for h in range(per_group):
            channels = slice(h * HEAD_DIM, (h + 1) * HEAD_DIM)
            col, line = cum_col[:, h : h + 1], cum[h : h + 1, :]
            top = jnp.exp2(jnp.where(causal, col[:HALF] - line[:, :HALF], -1e30)) * scores[:HALF, :HALF]
            left = jnp.exp2(col[HALF:] - line[:, :HALF]) * scores[HALF:, :HALF]
            low = jnp.exp2(jnp.where(causal, col[HALF:] - line[:, HALF:], -1e30)) * scores[HALF:, HALF:]
            bottom = jnp.concatenate([left, low], axis=1)
            value = stepped[:, channels]
            inside = jnp.concatenate(
                [fast_dot(top.astype(BF16), value[:HALF], NN), fast_dot(bottom.astype(BF16), value, NN)], axis=0
            )
            pieces.append(inside + skip_ref[first + h] * x[:, channels])
        ssd = jnp.concatenate(pieces, axis=1)
        if entering is not None:
            ssd = ssd + fast_dot(c, entering.astype(BF16), NN) * fade_x
        if k + 1 < spans:
            state = fast_dot(b, (x * tail_x).astype(BF16), TN)
            entering = state if entering is None else entering * fade_x[SPAN - 1 :, :] + state
        gated = ssd * silu(z_ref[rows, :].astype(F32))
        inv = lax.rsqrt(jnp.mean(gated * gated, axis=1, keepdims=True) + 1e-05)
        normed_ref[rows, :] = (gated * inv * gain_ref[...]).astype(BF16)
        inv_ref[0, rows, :] = inv


def backward_kernel(
    dt_ref, dn_ref, normed_ref, inv_ref, z_ref, b_ref, c_ref, gain_ref, a_ref, bias_ref, skip_ref, dx_ref
):
    tokens, width = dn_ref.shape
    per_group = width // HEAD_DIM
    first = pl.program_id(0) * per_group
    step, rate = head_tables(dt_ref, a_ref, bias_ref, per_group)
    causal = lax.broadcasted_iota(jnp.int32, (HALF, HALF), 1) >= lax.broadcasted_iota(jnp.int32, (HALF, HALF), 0)
    spans = tokens // SPAN
    d_state = None
    for k in reversed(range(spans)):
        rows = slice(k * SPAN, (k + 1) * SPAN)
        cum, cum_col, step_x, fade_x, tail_x = span_tables(step, rate, k * SPAN, per_group, width)
        dn = dn_ref[rows, :].astype(F32)
        gain = gain_ref[...]
        normed = normed_ref[rows, :].astype(F32)
        shared = jnp.mean(normed * dn, axis=1, keepdims=True)
        d_gated = inv_ref[0, rows, :] * (gain * dn - (normed / gain) * shared)
        d_ssd = d_gated * silu(z_ref[rows, :].astype(F32))
        d_low = d_ssd.astype(BF16)
        b, c = b_ref[rows, :], c_ref[rows, :]
        scores = fast_dot(b, c, NT)
        pieces = []
        skips = []
        for h in range(per_group):
            channels = slice(h * HEAD_DIM, (h + 1) * HEAD_DIM)
            col, line = cum_col[:, h : h + 1], cum[h : h + 1, :]
            high = jnp.exp2(jnp.where(causal, line[:, :HALF] - col[:HALF], -1e30)) * scores[:HALF, :HALF]
            right = jnp.exp2(line[:, HALF:] - col[:HALF]) * scores[:HALF, HALF:]
            low = jnp.exp2(jnp.where(causal, line[:, HALF:] - col[HALF:], -1e30)) * scores[HALF:, HALF:]
            top = jnp.concatenate([high, right], axis=1)
            value = d_low[:, channels]
            pieces.append(
                jnp.concatenate(
                    [fast_dot(top.astype(BF16), value, NN), fast_dot(low.astype(BF16), value[HALF:], NN)], axis=0
                )
            )
            skips.append(skip_ref[first + h] * d_ssd[:, channels])
        dx = jnp.concatenate(pieces, axis=1) * step_x + jnp.concatenate(skips, axis=1)
        if d_state is not None:
            dx = dx + fast_dot(b, d_state.astype(BF16), NN) * tail_x
        dx_ref[rows, :] = dx.astype(BF16)
        if k > 0:
            own = fast_dot(c, (d_ssd * fade_x).astype(BF16), TN)
            d_state = own if d_state is None else own + d_state * fade_x[SPAN - 1 :, :]


def group_call(kernel, dt_raw, wide, narrow, gain, scalars, outs, out_specs, cost):
    tokens, heads = dt_raw.shape
    groups = narrow[0].shape[1] // STATE
    width = heads * HEAD_DIM // groups
    wide_spec = pl.BlockSpec((tokens, width), lambda g: (0, g))
    state_spec = pl.BlockSpec((tokens, STATE), lambda g: (0, g))
    inv_spec = pl.BlockSpec((1, tokens, 1), lambda g: (g, 0, 0))
    whole = pl.BlockSpec((tokens, heads), lambda g: (0, 0))
    specs = [whole]
    specs += [inv_spec if v.ndim == 3 else wide_spec for v in wide]
    specs += [state_spec] * len(narrow)
    specs += [pl.BlockSpec((1, width), lambda g: (0, g))]
    specs += [pl.BlockSpec(memory_space=pltpu.SMEM)] * len(scalars)
    return pl.pallas_call(
        kernel,
        grid=(groups,),
        in_specs=specs,
        out_specs=[{"wide": wide_spec, "inv": inv_spec}[s] for s in out_specs],
        out_shape=outs,
        cost_estimate=cost,
        compiler_params=pltpu.CompilerParams(vmem_limit_bytes=48 * 1024 * 1024),
    )(dt_raw, *wide, *narrow, gain.reshape(1, -1), *scalars)


def shards(
    x_in,
    gate_z,
    b_proj,
    c_proj,
    dt_raw,
    a_log,
    dt_bias,
    skip_d,
    norm_gain,
    out_weight,
    global_weight,
    momentum,
    target,
):
    weight = out_weight[0]
    tokens, inner = x_in.shape
    groups = b_proj.shape[1] // STATE
    cost = pl.CostEstimate(flops=3 * tokens * inner * SPAN * 2, bytes_accessed=8 * tokens * inner, transcendentals=tokens * SPAN * 16)
    scalars = (a_log, dt_bias, skip_d)
    normed, inv = group_call(
        forward_kernel,
        dt_raw,
        [x_in, gate_z],
        [b_proj, c_proj],
        norm_gain,
        scalars,
        [jax.ShapeDtypeStruct((tokens, inner), BF16), jax.ShapeDtypeStruct((groups, tokens, 1), F32)],
        ["wide", "inv"],
        cost,
    )
    kept = global_weight - outer_rate * outer_beta * outer_beta * momentum
    kept_all = lax.all_gather(kept.astype(BF16), "replica", axis=0, tiled=True)

    layer_part = lax.psum_scatter(
        lax.dot_general(normed, weight, NT, preferred_element_type=F32).astype(BF16),
        "tensor",
        scatter_dimension=0,
        tiled=True,
    )
    cotangent_part = (layer_part.astype(F32) - target.astype(F32)).astype(BF16)
    cotangent = lax.all_gather(cotangent_part, "tensor", axis=0, tiled=True)
    weight_grad = lax.dot_general(cotangent, normed, TN, preferred_element_type=F32)
    local_new = (weight.astype(F32) - inner_rate * weight_grad).astype(BF16)
    summed = lax.psum_scatter(local_new, "replica", scatter_dimension=0, tiled=True)
    replicas = lax.axis_size("replica")
    delta = global_weight - summed.astype(F32) / replicas
    delta_all = lax.all_gather(delta.astype(BF16), "replica", axis=0, tiled=True)

    d_normed = lax.dot_general(cotangent, weight, NN, preferred_element_type=F32)
    (grad_input,) = group_call(
        backward_kernel,
        dt_raw,
        [d_normed, normed, inv, gate_z],
        [b_proj, c_proj],
        norm_gain,
        scalars,
        [jax.ShapeDtypeStruct((tokens, inner), BF16)],
        ["wide"],
        cost,
    )

    wide_delta = delta_all.astype(F32)
    own_sum = jnp.sum(wide_delta * wide_delta)
    sums = lax.all_gather(jnp.full((8, 128), own_sum, F32), "tensor", axis=0, tiled=False)
    square_sum = jnp.sum(sums[:, 0, 0])
    entry_count = delta_all.shape[0] * delta_all.shape[1] * lax.axis_size("tensor")
    factor = jnp.minimum(1.0, clip_rms / jnp.sqrt(square_sum / entry_count + 1e-06))
    clipped = factor * delta
    new_momentum = outer_beta * momentum + clipped
    new_global = global_weight - outer_rate * (clipped + outer_beta * new_momentum)
    new_weight = (kept_all.astype(F32) - (outer_rate * (1.0 + outer_beta)) * factor * wide_delta).astype(BF16)
    return (grad_input, new_weight, new_global, new_momentum)


def solution(mesh):
    placed = (
        P("replica", "tensor"),
        P("replica", "tensor"),
        P("replica", "tensor"),
        P("replica", "tensor"),
        P("replica", "tensor"),
        P("tensor"),
        P("tensor"),
        P("tensor"),
        P("tensor"),
        P("replica", None, "tensor"),
        P("replica", "tensor"),
        P("replica", "tensor"),
        P(("replica", "tensor"), None),
    )
    return jax.shard_map(
        shards,
        mesh=mesh,
        in_specs=placed,
        out_specs=(
            P("replica", "tensor"),
            P(None, "tensor"),
            P("replica", "tensor"),
            P("replica", "tensor"),
        ),
        check_vma=False,
    )
```

time: 373 us -> 293 us (0.79)
  local copies, waits for them, and re-layouts: 58.8 us -> 9.92 us
  blocking collectives: 39.5 us -> 11.8 us
  Pallas kernels: 0 us -> 19.2 us
  matrix products: 36.3 us -> 18.5 us
  other arithmetic: 26.4 us -> 20.3 us
    all_gather x1 -> x2, waiting for transfers between devices: 0.01 us -> 54.9 us  [the longest x1 36.3 us: shards(): lax.all_gather(delta.astype(BF16), 'replica', axis=0, tiled=True)]
    reduce_scatter x2, waiting for transfers between devices: 150 us -> 96.8 us  [the longest x1 50.1 us: shards(): lax.psum_scatter(local_new, 'replica', scatter_dimension=0, tiled=True)]
    psum x1 -> x0, blocking collectives: 39.5 us -> none  [shards(): square_sum = lax.psum(jnp.sum(delta * delta), ('replica', 'tensor'))]
    reshape x14 -> x0, local copies, waits for them, and re-layouts: 36.9 us -> none  [the longest x3 12.6 us: gated_ssd(): ssd_out.reshape(tokens, group_count, width)]
    pallas_call x0 -> x2, Pallas kernels: none -> 19.2 us  [group_call(): pl.pallas_call(kernel, grid=(groups,), in_specs=specs, out_specs=[{'wide'...]
    dot_general x10 -> x3, matrix products: 36.3 us -> 18.5 us  [the longest x1 7.36 us: shards(): lax.dot_general(cotangent, normed, TN, preferred_element_type=F32)]
    unnamed x0 -> x1, blocking collectives: none -> 11.8 us
    unnamed x52 -> x42, local copies, waits for them, and re-layouts: 13.9 us -> 9.92 us
  transfers between devices with their start and end apart: 4 -> 5, of which waited for: 3 -> 5; matrix products, arithmetic and copies ran while one was open for 12% -> 2% of each run, Pallas kernels for 0% -> 3%
where the time goes in v1:
time: 293 us; the launch traced here: 292 us
  waiting for transfers between devices  197 us (67%)
  other arithmetic  20.3 us (7%)
  Pallas kernels  19.2 us (7%)
  matrix products  18.5 us (6%)
  between operations  14.7 us (5%)
  blocking collectives  11.8 us (4%)
  local copies, waits for them, and re-layouts  9.92 us (3%)
    reduce_scatter x1, waiting for transfers between devices, shards(): lax.psum_scatter(local_new, 'replica', scatter_dimension=0, tiled=True)  50.1 us
    reduce_scatter x1, waiting for transfers between devices, shards(): lax.psum_scatter(lax.dot_general(normed, weight, NT, preferred_element_ty...  46.7 us
    all_gather x1, waiting for transfers between devices, shards(): cotangent = lax.all_gather(cotangent_part, 'tensor', axis=0, tiled=True)  45.5 us
    all_gather x1, waiting for transfers between devices, shards(): lax.all_gather(delta.astype(BF16), 'replica', axis=0, tiled=True)  36.3 us
    pallas_call x2, Pallas kernels, group_call(): pl.pallas_call(kernel, grid=(groups,), in_specs=specs, out_specs=[{'wide'...  19.2 us
    all_gather x1, waiting for transfers between devices, shards(): kept_all = lax.all_gather(kept.astype(BF16), 'replica', axis=0, tiled=True)  18.6 us
    unnamed x1, blocking collectives  11.8 us
    unnamed x42, local copies, waits for them, and re-layouts  9.92 us
  transfers between devices with their start and end apart: 5, of which 5 were waited for; matrix products, arithmetic and copies ran while one was open for 2% of the time, Pallas kernels for 3%

profile of v1, /device:TPU:0, one launch (start us, length us, event | category | flops | bytes accessed | tf_op | source)
XLA Modules:
  0.0 291.9 jit_solution(10709369964618993637)
XLA Ops:
  7.2 0.9 copy.18.dt_ref
  8.1 1.2 copy-done
  9.3 0.9 copy-done.2
  10.3 0.9 copy-done.4
  11.2 0.7 copy-done.6
  11.9 0.7 copy-done.8
  13.9 1.2 copy-done.14
  15.1 9.1 %shard_map.156 = (bf16[512,1024]{1,0:T(8,128)(2,1)S(1)}, f32[2,512,1]{2,1,0:T(8,128)S(1)}) custom-call(f32[512,16]{1,0:T(8,128)S(1)} %copy.18.dt_ref, bf16[512,1024]{1,0:T(8,128)(2,1)S(1)} %copy-done.14, bf16[512,1024]{1,0:T(8,128)(2,1)S(1)} %copy-done, bf16[512,256]{1,0:T(8,128)(2,1)S(1)} %copy-done.2, bf16[512,256]{1,0:T(8,128)(2,1)S(1)} %copy-done.4, ...), custom_call_target="tpu_custom_call" | custom-call | flops 805306368 | bytes 4194304 | tf_op jit(solution)/shard_map/pallas_call | solution.py:178
  24.3 5.9 %fusion.7 = bf16[512,2048]{1,0:T(8,128)(2,1)} fusion(bf16[512,1024]{1,0:T(8,128)(2,1)S(1)} %get-tuple-element.6.normed_ref, bf16[1,2048,1024]{2,1,0:T(8,128)(2,1)} %param.22), kind=kOutput, calls=%fused_computation.10 | convolution fusion | flops 2148532224 | bytes 7340032 | tf_op jit(solution)/shard_map/dot_general | solution.py:224
  30.3 46.7 %reduce-scatter.3.cloned.1.call-done = bf16[128,2048]{1,0:T(8,128)(2,1)} async-done(((bf16[512,2048]{1,0:T(8,128)(2,1)}), bf16[128,2048]{1,0:T(8,128)(2,1)}) %reduce-scatter.3.cloned.1.call-update) | async-done | bytes 524304 | tf_op jit(solution)/shard_map/reduce_scatter | solution.py:223
  76.9 2.0 subtract_convert_fusion.2
  79.0 45.5 %all-gather.4.cloned.1.call-done = bf16[512,2048]{1,0:T(8,128)(2,1)} async-done(((bf16[128,2048]{1,0:T(8,128)(2,1)}), bf16[512,2048]{1,0:T(8,128)(2,1)}) %all-gather.4.cloned.1.call-update) | async-done | bytes 2097168 | tf_op jit(solution)/shard_map/all_gather | solution.py:230
  124.4 7.4 %subtract_convert_fusion = bf16[2048,1024]{1,0:T(8,128)(2,1)} fusion(bf16[512,2048]{1,0:T(8,128)(2,1)} %all-gather.4.cloned.1.call-done, bf16[512,1024]{1,0:T(8,128)(2,1)S(1)} %get-tuple-element.6.normed_ref, bf16[1,2048,1024]{2,1,0:T(8,128)(2,1)} %param.22), kind=kOutput, calls=%fused_computation.5 | convolution fusion | flops 2155872256 | bytes 11534336 | tf_op jit(solution)/shard_map/dot_general | solution.py:231
  131.9 50.1 %reduce-scatter.5.cloned.1.call-done = bf16[256,1024]{1,0:T(8,128)(2,1)} async-done(((bf16[2048,1024]{1,0:T(8,128)(2,1)}), bf16[256,1024]{1,0:T(8,128)(2,1)}) %reduce-scatter.5.cloned.1.call-update) | async-done | bytes 524304 | tf_op jit(solution)/shard_map/reduce_scatter | solution.py:233
  182.0 2.1 fusion.10
  184.8 36.3 %all-gather.8.cloned.1.call-done = bf16[2048,1024]{1,0:T(8,128)(2,1)} async-done(((bf16[256,1024]{1,0:T(8,128)(2,1)}), bf16[2048,1024]{1,0:T(8,128)(2,1)}) %all-gather.8.cloned.1.call-update) | async-done | bytes 4194320 | tf_op jit(solution)/shard_map/all_gather | solution.py:236
  221.1 4.9 %fusion = f32[]{:T(128)} fusion(bf16[2048,1024]{1,0:T(8,128)(2,1)} %all-gather.8.cloned.1.call-done), kind=kLoop, calls=%fused_computation.2 | loop fusion | flops 6291455 | bytes 4194308 | tf_op jit(solution)/shard_map/reduce_sum | solution.py:252
  226.0 1.4 dynamic-update-slice
  227.4 11.8 %all-reduce = f32[4]{0:T(128)S(1)} all-reduce(f32[4]{0:T(128)S(1)} %dynamic-update-slice), channel_id=2, replica_groups=mesh['replica'=8,'tensor'=4] {'tensor'}, use_global_device_ids=true, to_apply=%add | all-reduce | flops 4 | bytes 32
  240.6 3.1 %multiply_subtract_fusion = (f32[256,1024]{1,0:T(8,128)}, f32[256,1024]{1,0:T(8,128)}, bf16[256,1024]{1,0:T(8,128)(2,1)}) fusion(f32[256,1024]{1,0:T(8,128)S(1)} %copy-done.15, bf16[256,1024]{1,0:T(8,128)(2,1)S(1)} %copy-done.16, f32[]{:T(128)S(6)} %min_shard_map.3, f32[256,1024]{1,0:T(8,128)} %param.24), kind=kLoop, calls=%fused_computation.11 | loop fusion | flops 3407872 | bytes 5242884 | tf_op jit(solution)/shard_map/sub | solution.py:259
  243.8 5.3 %fusion.3.dn_ref = f32[512,1024]{1,0:T(8,128)S(1)} fusion(bf16[512,2048]{1,0:T(8,128)(2,1)} %all-gather.4.cloned.1.call-done, bf16[1,2048,1024]{2,1,0:T(8,128)(2,1)} %param.22), kind=kOutput, calls=%fused_computation.6 | convolution fusion | flops 2147483648 | bytes 8388608 | tf_op jit(solution)/shard_map/dot_general | solution.py:238
  249.1 10.1 %shard_map.157 = bf16[512,1024]{1,0:T(8,128)(2,1)} custom-call(f32[512,16]{1,0:T(8,128)S(1)} %copy.18.dt_ref, f32[512,1024]{1,0:T(8,128)S(1)} %fusion.3.dn_ref, bf16[512,1024]{1,0:T(8,128)(2,1)S(1)} %get-tuple-element.6.normed_ref, f32[2,512,1]{2,1,0:T(8,128)S(1)} %get-tuple-element.7.inv_ref, bf16[512,1024]{1,0:T(8,128)(2,1)S(1)} %copy-done.1, ...), custom_call_target="tpu_custom_call" | custom-call | flops 805306368 | bytes 4194304 | tf_op jit(solution)/shard_map/pallas_call | solution.py:178
  259.2 18.6 %all-gather.6.cloned.1.call-done = bf16[2048,1024]{1,0:T(8,128)(2,1)} async-done(((bf16[256,1024]{1,0:T(8,128)(2,1)}), bf16[2048,1024]{1,0:T(8,128)(2,1)}) %all-gather.6.cloned.1.call-update) | async-done | bytes 4194320 | tf_op jit(solution)/shard_map/all_gather | solution.py:221
  277.8 7.6 %fusion.2 = bf16[2048,1024]{1,0:T(8,128)(2,1)} fusion(bf16[2048,1024]{1,0:T(8,128)(2,1)} %all-gather.8.cloned.1.call-done, bf16[2048,1024]{1,0:T(8,128)(2,1)} %all-gather.6.cloned.1.call-done, f32[]{:T(128)S(6)} %mul_shard_map.3), kind=kLoop, calls=%fused_computation.4 | loop fusion | flops 10485760 | bytes 12582916 | tf_op jit(solution)/shard_map/convert_element_type | solution.py:260
  (45 shorter events, 2.9 us)
Async XLA Ops:
  7.2 69.8 %reduce-scatter.3.cloned.1.call-start = ((), (), s32[]{:S(2)}) async-start(), calls=%async_computation.2 | async-start | bytes 2621440 | tf_op jit(solution)/shard_map/reduce_scatter | solution.py:223
  8.1 1.2 copy-start
  9.3 0.9 copy-start.2
  10.3 0.9 copy-start.4
  11.2 0.7 copy-start.6
  11.9 0.7 copy-start.8
  12.6 0.7 copy-start.10
  13.2 0.7 copy-start.12
  13.9 1.2 copy-start.14
  24.2 52.7 %copy-start.17 = (bf16[128,2048]{1,0:T(8,128)(2,1)S(1)}, bf16[128,2048]{1,0:T(8,128)(2,1)}, u32[]{:S(2)}) copy-start(bf16[128,2048]{1,0:T(8,128)(2,1)} %param.25) | copy-start | bytes 1572868
  30.2 94.2 %all-gather.4.cloned.1.call-start = ((), (), s32[]{:S(2)}) async-start(), calls=%async_computation.3 | async-start | bytes 2621440 | tf_op jit(solution)/shard_map/all_gather | solution.py:230
  78.9 103.1 %reduce-scatter.5.cloned.1.call-start = ((), (), s32[]{:S(2)}) async-start(), calls=%async_computation.5 | async-start | bytes 4718592 | tf_op jit(solution)/shard_map/reduce_scatter | solution.py:233
  131.8 50.2 %copy-start.15 = (f32[256,1024]{1,0:T(8,128)S(1)}, f32[256,1024]{1,0:T(8,128)}, u32[]{:S(2)}) copy-start(f32[256,1024]{1,0:T(8,128)} %param.23) | copy-start | bytes 3145732
  131.8 52.4 %copy-start.18 = (u32[32]{0:T(128)S(1)}, u32[32]{0:T(128)}, u32[]{:S(2)}) copy-start(u32[32]{0:T(128)} %constant.27) | copy-start | bytes 388
  131.8 89.2 %all-gather.8.cloned.1.call-start = ((), (), s32[]{:S(2)}) async-start(), calls=%async_computation.6 | async-start | bytes 4718592 | tf_op jit(solution)/shard_map/all_gather | solution.py:236
  182.0 58.5 %copy-start.16 = (bf16[256,1024]{1,0:T(8,128)(2,1)S(1)}, bf16[256,1024]{1,0:T(8,128)(2,1)}, u32[]{:S(2)}) copy-start(bf16[256,1024]{1,0:T(8,128)(2,1)} %reduce-scatter.5.cloned.1.call-done) | copy-start | bytes 1572868
  184.1 93.7 %all-gather.6.cloned.1.call-start = ((), (), s32[]{:S(2)}) async-start(), calls=%async_computation.4 | async-start | bytes 4718592 | tf_op jit(solution)/shard_map/all_gather | solution.py:221
  243.7 5.3 %copy-start.1 = (bf16[512,1024]{1,0:T(8,128)(2,1)S(1)}, bf16[512,1024]{1,0:T(8,128)(2,1)}, u32[]{:S(2)}) copy-start(bf16[512,1024]{1,0:T(8,128)(2,1)} %z_ref.3) | copy-start | bytes 3145732
  243.7 5.3 %copy-start.3 = (bf16[512,256]{1,0:T(8,128)(2,1)S(1)}, bf16[512,256]{1,0:T(8,128)(2,1)}, u32[]{:S(2)}) copy-start(bf16[512,256]{1,0:T(8,128)(2,1)} %b_ref.3) | copy-start | bytes 786436
  243.7 5.3 %copy-start.5 = (bf16[512,256]{1,0:T(8,128)(2,1)S(1)}, bf16[512,256]{1,0:T(8,128)(2,1)}, u32[]{:S(2)}) copy-start(bf16[512,256]{1,0:T(8,128)(2,1)} %c_ref.3) | copy-start | bytes 786436
  243.7 5.3 %copy-start.7 = (f32[1024]{0:T(1024)S(1)}, f32[1024]{0:T(1024)}, u32[]{:S(2)}) copy-start(f32[1024]{0:T(1024)} %param.21) | copy-start | bytes 12292
  243.7 5.3 %copy-start.9 = (f32[16]{0:T(128)S(1)}, f32[16]{0:T(128)}, u32[]{:S(2)}) copy-start(f32[16]{0:T(128)} %a_ref.3) | copy-start | bytes 196
  243.8 5.3 %copy-start.11 = (f32[16]{0:T(128)S(1)}, f32[16]{0:T(128)}, u32[]{:S(2)}) copy-start(f32[16]{0:T(128)} %bias_ref.3) | copy-start | bytes 196
  243.8 5.3 %copy-start.13 = (f32[16]{0:T(128)S(1)}, f32[16]{0:T(128)}, u32[]{:S(2)}) copy-start(f32[16]{0:T(128)} %skip_ref.3) | copy-start | bytes 196
Sparse Core Ops, SparseCore 0:
  30.3 46.5 reduce-scatter.2
  79.2 45.2 all-gather.3
  132.0 50.0 reduce-scatter.4
  184.3 36.6 all-gather.7
  243.8 33.9 all-gather.5

commit v2 on v1

--- a/solution.py
+++ b/solution.py
@@ -17,6 +17,7 @@
 outer_beta = 0.9
 clip_rms = 0.005
 LOG2E = 1.4426950408889634
+DEPTH = 2
 
 F32 = jnp.float32
 BF16 = jnp.bfloat16
@@ -75,7 +76,11 @@
     return cum, cum_col, step_x, fade_x, tail_x
 
 
-def forward_kernel(dt_ref, x_ref, z_ref, b_ref, c_ref, gain_ref, a_ref, bias_ref, skip_ref, normed_ref, inv_ref):
+def forward_kernel(
+    place_ref, dt_ref, x_ref, z_ref, b_ref, c_ref, gain_ref, a_ref, bias_ref, skip_ref, weight_ref, target_ref,
+    normed_ref, inv_ref, *part_refs_and_total
+):
+    *part_refs, total_ref = part_refs_and_total
     tokens, width = x_ref.shape
     per_group = width // HEAD_DIM
     first = pl.program_id(0) * per_group
@@ -114,13 +119,60 @@
         normed_ref[rows, :] = (gated * inv * gain_ref[...]).astype(BF16)
         inv_ref[0, rows, :] = inv
 
+    replicas, owned, _ = weight_ref.shape
+    chunks = len(part_refs)
+    piece = owned // chunks
+    for n in range(chunks):
+        weight = weight_ref[:, n * piece : (n + 1) * piece, :].reshape(replicas * piece, width)
+        part = fast_dot(normed_ref[...], weight, NT)
+
+        @pl.when(pl.program_id(0) == 0)
+        def _():
+            total_ref[n] = part
+
+        @pl.when(pl.program_id(0) > 0)
+        def _():
+            total_ref[n] = total_ref[n] + part
+
+        @pl.when(pl.program_id(0) == pl.num_programs(0) - 1)
+        def _():
+            held = target_ref.shape[0]
+            own = pl.ds(pl.multiple_of(place_ref[0] * held, held), held)
+            goal = jnp.concatenate(
+                [target_ref[:, r * owned + n * piece : r * owned + (n + 1) * piece] for r in range(replicas)], axis=1
+            )
+            total_ref[n, own, :] = total_ref[n, own, :] - goal.astype(F32)
+            part_refs[n][...] = total_ref[n].astype(BF16)
+
+
+def gradient_kernel(place_ref, mid_ref, sent_ref, normed_ref, weight_ref, cot_ref, keep_ref, send_ref):
+    middle = place_ref[1] == 1
+    cot = jnp.where(middle, mid_ref[...], sent_ref[...])
+    cot_ref[...] = cot
+    replicas, piece, width = weight_ref.shape
+    grad = fast_dot(cot, normed_ref[...], TN)
+    new = weight_ref[...].reshape(replicas * piece, width).astype(F32) - inner_rate * grad
+    new = new.astype(BF16).reshape(replicas // 2, 2, piece, width)
+    odd = place_ref[2] == 1
+    keep_ref[...] = jnp.where(odd, new[:, 1], new[:, 0])
+    send_ref[...] = jnp.where(odd, new[:, 0], new[:, 1])
+
 
 def backward_kernel(
-    dt_ref, dn_ref, normed_ref, inv_ref, z_ref, b_ref, c_ref, gain_ref, a_ref, bias_ref, skip_ref, dx_ref
+    dt_ref, normed_ref, inv_ref, z_ref, b_ref, c_ref, gain_ref, a_ref, bias_ref, skip_ref, weight_ref, *refs
 ):
-    tokens, width = dn_ref.shape
+    *cot_refs, dx_ref, dn_ref = refs
+    tokens, width = normed_ref.shape
     per_group = width // HEAD_DIM
     first = pl.program_id(0) * per_group
+    replicas, owned, _ = weight_ref.shape
+    piece = owned // len(cot_refs)
+    d_normed = None
+    for n, cot_ref in enumerate(cot_refs):
+        weight = weight_ref[:, n * piece : (n + 1) * piece, :].reshape(replicas * piece, width)
+        term = fast_dot(cot_ref[...], weight, NN)
+        d_normed = term if d_normed is None else d_normed + term
+    dn_ref[...] = d_normed
     step, rate = head_tables(dt_ref, a_ref, bias_ref, per_group)
     causal = lax.broadcasted_iota(jnp.int32, (HALF, HALF), 1) >= lax.broadcasted_iota(jnp.int32, (HALF, HALF), 0)
     spans = tokens // SPAN
@@ -128,7 +180,7 @@
     for k in reversed(range(spans)):
         rows = slice(k * SPAN, (k + 1) * SPAN)
         cum, cum_col, step_x, fade_x, tail_x = span_tables(step, rate, k * SPAN, per_group, width)
-        dn = dn_ref[rows, :].astype(F32)
+        dn = dn_ref[rows, :]
         gain = gain_ref[...]
         normed = normed_ref[rows, :].astype(F32)
         shared = jnp.mean(normed * dn, axis=1, keepdims=True)
@@ -162,28 +214,18 @@
             d_state = own if d_state is None else own + d_state * fade_x[SPAN - 1 :, :]
 
 
-def group_call(kernel, dt_raw, wide, narrow, gain, scalars, outs, out_specs, cost):
-    tokens, heads = dt_raw.shape
-    groups = narrow[0].shape[1] // STATE
-    width = heads * HEAD_DIM // groups
-    wide_spec = pl.BlockSpec((tokens, width), lambda g: (0, g))
-    state_spec = pl.BlockSpec((tokens, STATE), lambda g: (0, g))
-    inv_spec = pl.BlockSpec((1, tokens, 1), lambda g: (g, 0, 0))
-    whole = pl.BlockSpec((tokens, heads), lambda g: (0, 0))
-    specs = [whole]
-    specs += [inv_spec if v.ndim == 3 else wide_spec for v in wide]
-    specs += [state_spec] * len(narrow)
-    specs += [pl.BlockSpec((1, width), lambda g: (0, g))]
-    specs += [pl.BlockSpec(memory_space=pltpu.SMEM)] * len(scalars)
-    return pl.pallas_call(
-        kernel,
-        grid=(groups,),
-        in_specs=specs,
-        out_specs=[{"wide": wide_spec, "inv": inv_spec}[s] for s in out_specs],
-        out_shape=outs,
-        cost_estimate=cost,
-        compiler_params=pltpu.CompilerParams(vmem_limit_bytes=48 * 1024 * 1024),
-    )(dt_raw, *wide, *narrow, gain.reshape(1, -1), *scalars)
+def inward(axis_size):
+    half = axis_size // 2
+    hops = [[(s, s + 1), (axis_size - 1 - s, axis_size - 2 - s)] for s in range(half - 1)]
+    return hops, [(half - 1, half), (half, half - 1)]
+
+
+def add16(a, b):
+    return (a.astype(F32) + b.astype(F32)).astype(BF16)
+
+
+def after(value, *others):
+    return lax.optimization_barrier((value, *others))[0]
 
 
 def shards(
@@ -201,64 +243,160 @@
     momentum,
     target,
 ):
-    weight = out_weight[0]
     tokens, inner = x_in.shape
+    features = out_weight.shape[1]
+    replicas = lax.axis_size("replica")
+    heads_over = lax.axis_size("tensor")
     groups = b_proj.shape[1] // STATE
-    cost = pl.CostEstimate(flops=3 * tokens * inner * SPAN * 2, bytes_accessed=8 * tokens * inner, transcendentals=tokens * SPAN * 16)
-    scalars = (a_log, dt_bias, skip_d)
-    normed, inv = group_call(
-        forward_kernel,
-        dt_raw,
-        [x_in, gate_z],
-        [b_proj, c_proj],
-        norm_gain,
-        scalars,
-        [jax.ShapeDtypeStruct((tokens, inner), BF16), jax.ShapeDtypeStruct((groups, tokens, 1), F32)],
-        ["wide", "inv"],
-        cost,
+    heads = dt_raw.shape[1]
+    width = inner // groups
+    owned = features // replicas
+    chunks = max(1, min(4, owned // 16))
+    piece = owned // chunks
+    span_rows = replicas * piece
+    place = lax.axis_index("tensor")
+    me = lax.axis_index("replica")
+    in_middle = (place == heads_over // 2 - 1) | (place == heads_over // 2)
+    places = jnp.stack([place, in_middle.astype(jnp.int32), lax.rem(me, 2)]).astype(jnp.int32)
+    weight = out_weight[0].reshape(replicas, owned, inner)
+    gain = norm_gain.reshape(1, inner)
+
+    smem = pl.BlockSpec(memory_space=pltpu.SMEM)
+    by_group = pl.BlockSpec((tokens, width), lambda g: (0, g))
+    by_state = pl.BlockSpec((tokens, STATE), lambda g: (0, g))
+    inv_spec = pl.BlockSpec((1, tokens, 1), lambda g: (g, 0, 0))
+    all_heads = pl.BlockSpec((tokens, heads), lambda g: (0, 0))
+    gain_spec = pl.BlockSpec((1, width), lambda g: (0, g))
+    weight_spec = pl.BlockSpec((replicas, owned, width), lambda g: (0, 0, g))
+    chunk_spec = pl.BlockSpec((tokens, span_rows), lambda g: (0, 0))
+    params = pltpu.CompilerParams(vmem_limit_bytes=56 * 1024 * 1024)
+    cost = pl.CostEstimate(
+        flops=2 * tokens * inner * (features + 3 * SPAN),
+        bytes_accessed=2 * inner * (features + 4 * tokens),
+        transcendentals=tokens * SPAN * heads,
     )
+
     kept = global_weight - outer_rate * outer_beta * outer_beta * momentum
     kept_all = lax.all_gather(kept.astype(BF16), "replica", axis=0, tiled=True)
 
-    layer_part = lax.psum_scatter(
-        lax.dot_general(normed, weight, NT, preferred_element_type=F32).astype(BF16),
-        "tensor",
-        scatter_dimension=0,
-        tiled=True,
-    )
-    cotangent_part = (layer_part.astype(F32) - target.astype(F32)).astype(BF16)
-    cotangent = lax.all_gather(cotangent_part, "tensor", axis=0, tiled=True)
-    weight_grad = lax.dot_general(cotangent, normed, TN, preferred_element_type=F32)
-    local_new = (weight.astype(F32) - inner_rate * weight_grad).astype(BF16)
-    summed = lax.psum_scatter(local_new, "replica", scatter_dimension=0, tiled=True)
-    replicas = lax.axis_size("replica")
-    delta = global_weight - summed.astype(F32) / replicas
-    delta_all = lax.all_gather(delta.astype(BF16), "replica", axis=0, tiled=True)
-
-    d_normed = lax.dot_general(cotangent, weight, NN, preferred_element_type=F32)
-    (grad_input,) = group_call(
+    normed, inv, *parts = pl.pallas_call(
+        forward_kernel,
+        grid=(groups,),
+        in_specs=[smem, all_heads, by_group, by_group, by_state, by_state, gain_spec, smem, smem, smem, weight_spec,
+                  pl.BlockSpec(target.shape, lambda g: (0, 0))],
+        out_specs=[by_group, inv_spec] + [chunk_spec] * chunks,
+        out_shape=[jax.ShapeDtypeStruct((tokens, inner), BF16), jax.ShapeDtypeStruct((groups, tokens, 1), F32)]
+        + [jax.ShapeDtypeStruct((tokens, span_rows), BF16)] * chunks,
+        scratch_shapes=[pltpu.VMEM((chunks, tokens, span_rows), F32)],
+        cost_estimate=cost,
+        compiler_params=params,
+    )(places, dt_raw, x_in, gate_z, b_proj, c_proj, gain, a_log, dt_bias, skip_d, weight, target)
+
+    in_hops, across = inward(heads_over)
+    first_landed = []
+    cots, deltas, gathered = [], [], []
+    for n in range(chunks):
+        held = parts[n]
+        if n >= DEPTH:
+            held = after(held, first_landed[n - DEPTH])
+        for at, pairs in enumerate(in_hops):
+            landed = lax.ppermute(held, "tensor", pairs)
+            if at == 0:
+                first_landed.append(landed)
+            held = add16(held, landed)
+        mid = add16(held, lax.ppermute(held, "tensor", across))
+        out = mid
+        for pairs in reversed(in_hops):
+            back = lax.ppermute(out, "tensor", [(b, a) for a, b in pairs])
+            out = jnp.where(in_middle, mid, back) if pairs is not in_hops[0] else back
+
+        col_tile = min(inner, 512)
+        cot, keep, send = pl.pallas_call(
+            gradient_kernel,
+            grid=(inner // col_tile,),
+            in_specs=[smem, chunk_spec, chunk_spec, pl.BlockSpec((tokens, col_tile), lambda i: (0, i)),
+                      pl.BlockSpec((replicas, piece, col_tile), lambda i, n=n: (0, n, i))],
+            out_specs=[chunk_spec] + [pl.BlockSpec((replicas // 2, piece, col_tile), lambda i: (0, 0, i))] * 2,
+            out_shape=[jax.ShapeDtypeStruct((tokens, span_rows), BF16)]
+            + [jax.ShapeDtypeStruct((replicas // 2, piece, inner), BF16)] * 2,
+            cost_estimate=pl.CostEstimate(
+                flops=2 * tokens * span_rows * inner, bytes_accessed=2 * (tokens + 2 * span_rows) * inner, transcendentals=0
+            ),
+            compiler_params=params,
+        )(places, mid, out, normed, weight)
+        cots.append(cot)
+
+        landed = [lax.ppermute(send, "replica", [(r, r ^ 1) for r in range(replicas)])]
+        mine = [keep]
+        bit = 1
+        left = replicas // 2
+        while left > 1:
+            bits = 2 if left >= 4 else 1
+            ways = 1 << bits
+            my = lax.rem(lax.div(me, 1 << bit), ways)
+            terms = [t.reshape(left // ways, ways, piece, inner) for t in mine + landed]
+
+            def total(mask):
+                at = lax.bitwise_xor(my, jnp.int32(mask))
+                cut = [lax.dynamic_index_in_dim(t, at, 1, keepdims=False).astype(F32) for t in terms]
+                return functools.reduce(jnp.add, cut).astype(BF16)
+
+            landed = [
+                lax.ppermute(total(mask), "replica", [(r, r ^ (mask << bit)) for r in range(replicas)])
+                for mask in range(1, ways)
+            ]
+            mine = [total(0)]
+            bit += bits
+            left //= ways
+        summed = functools.reduce(jnp.add, [t.reshape(piece, inner).astype(F32) for t in mine + landed])
+        delta = global_weight[n * piece : (n + 1) * piece] - summed / replicas
+        deltas.append(delta)
+        gathered.append(lax.all_gather(delta.astype(BF16), "replica", axis=0, tiled=True))
+
+    (grad_input,) = pl.pallas_call(
         backward_kernel,
-        dt_raw,
-        [d_normed, normed, inv, gate_z],
-        [b_proj, c_proj],
-        norm_gain,
-        scalars,
-        [jax.ShapeDtypeStruct((tokens, inner), BF16)],
-        ["wide"],
-        cost,
-    )
-
-    wide_delta = delta_all.astype(F32)
-    own_sum = jnp.sum(wide_delta * wide_delta)
-    sums = lax.all_gather(jnp.full((8, 128), own_sum, F32), "tensor", axis=0, tiled=False)
-    square_sum = jnp.sum(sums[:, 0, 0])
-    entry_count = delta_all.shape[0] * delta_all.shape[1] * lax.axis_size("tensor")
-    factor = jnp.minimum(1.0, clip_rms / jnp.sqrt(square_sum / entry_count + 1e-06))
-    clipped = factor * delta
+        grid=(groups,),
+        in_specs=[all_heads, by_group, inv_spec, by_group, by_state, by_state, gain_spec, smem, smem, smem, weight_spec]
+        + [chunk_spec] * chunks,
+        out_specs=[by_group],
+        out_shape=[jax.ShapeDtypeStruct((tokens, inner), BF16)],
+        scratch_shapes=[pltpu.VMEM((tokens, width), F32)],
+        cost_estimate=cost,
+        compiler_params=params,
+    )(dt_raw, normed, inv, gate_z, b_proj, c_proj, gain, a_log, dt_bias, skip_d, weight, *cots)
+
+    square_sum = functools.reduce(jnp.add, [jnp.sum(d * d) for d in deltas])
+    spread = jnp.full((8, 128), square_sum, F32)
+    for pairs in [[(r, r ^ (1 << bit)) for r in range(replicas)] for bit in range(replicas.bit_length() - 1)]:
+        spread = spread + lax.ppermute(spread, "replica", pairs)
+    for bit in range(heads_over.bit_length() - 1):
+        spread = spread + lax.ppermute(spread, "tensor", [(t, t ^ (1 << bit)) for t in range(heads_over)])
+    entry_count = features * inner * heads_over
+    factor = jnp.minimum(1.0, clip_rms / jnp.sqrt(spread[0, 0] / entry_count + 1e-06))
+    clipped = factor * jnp.concatenate(deltas, axis=0)
     new_momentum = outer_beta * momentum + clipped
     new_global = global_weight - outer_rate * (clipped + outer_beta * new_momentum)
-    new_weight = (kept_all.astype(F32) - (outer_rate * (1.0 + outer_beta)) * factor * wide_delta).astype(BF16)
+    scale = (outer_rate * (1.0 + outer_beta)) * factor
+    new_weight = pl.pallas_call(
+        weight_kernel,
+        grid=(replicas,),
+        in_specs=[smem, pl.BlockSpec((owned, inner), lambda r: (r, 0))]
+        + [pl.BlockSpec((piece, inner), lambda r: (r, 0))] * chunks,
+        out_specs=pl.BlockSpec((owned, inner), lambda r: (r, 0)),
+        out_shape=jax.ShapeDtypeStruct((features, inner), BF16),
+        cost_estimate=pl.CostEstimate(flops=2 * features * inner, bytes_accessed=6 * features * inner, transcendentals=0),
+        compiler_params=params,
+    )(scale.reshape(1), kept_all, *gathered)
     return (grad_input, new_weight, new_global, new_momentum)
+
+
+def weight_kernel(scale_ref, kept_ref, *refs):
+    *delta_refs, new_ref = refs
+    piece = delta_refs[0].shape[0]
+    for n, delta_ref in enumerate(delta_refs):
+        rows = slice(n * piece, (n + 1) * piece)
+        new = kept_ref[rows, :].astype(F32) - scale_ref[0] * delta_ref[...].astype(F32)
+        new_ref[rows, :] = new.astype(BF16)
 
 
 def solution(mesh):

time: 293 us -> 274 us (0.935)
  waiting for transfers between devices: 197 us -> 137 us
  starting transfers between devices: 0.21 us -> 45.6 us
  Pallas kernels: 19.2 us -> 53.2 us
  matrix products: 18.5 us -> 0 us
  blocking collectives: 11.8 us -> 0 us
  other arithmetic: 20.3 us -> 14.9 us
  local copies, waits for them, and re-layouts: 9.92 us -> 4.6 us
    reduce_scatter x2 -> x0, waiting for transfers between devices: 96.8 us -> none  [the longest x1 50.1 us: shards(): lax.psum_scatter(local_new, 'replica', scatter_dimension=0, tiled=True)]
    ppermute x0 -> x33, waiting for transfers between devices: none -> 64.4 us  [the longest x4 18.4 us: shards(): back = lax.ppermute(out, 'tensor', [(b, a) for a, b in pairs])]
    all_gather x1 -> x0, waiting for transfers between devices: 45.5 us -> none  [shards(): cotangent = lax.all_gather(cotangent_part, 'tensor', axis=0, tiled=True)]
    ppermute x0 -> x33, starting transfers between devices: none -> 45.4 us  [the longest x4 17.8 us: shards(): landed = lax.ppermute(held, 'tensor', pairs)]
    pallas_call x2 -> x7, Pallas kernels: 19.2 us -> 53.2 us  [the longest x1 17.1 us: shards(): pl.pallas_call(forward_kernel, grid=(groups,), in_specs=[smem, all_heads,...]
    all_gather x1, waiting for transfers between devices: 18.6 us -> 38.5 us  [shards(): kept_all = lax.all_gather(kept.astype(BF16), 'replica', axis=0, tiled=True)]
    dot_general x3 -> x0, matrix products: 18.5 us -> none  [the longest x1 7.36 us: shards(): lax.dot_general(cotangent, normed, TN, preferred_element_type=F32)]
    unnamed x1 -> x0, blocking collectives: 11.8 us -> none
  transfers between devices with their start and end apart: 5 -> 38, of which waited for: 5 -> 23; matrix products, arithmetic and copies ran while one was open for 2% -> 5% of each run, Pallas kernels for 3% -> 10%
where the time goes in v2:
time: 274 us; the launch traced here: 273 us
  waiting for transfers between devices  137 us (50%)
  Pallas kernels  53.2 us (19%)
  starting transfers between devices  45.6 us (17%)
  between operations  17.5 us (6%)
  other arithmetic  14.9 us (5%)
  local copies, waits for them, and re-layouts  4.6 us (2%)
    all_gather x1, waiting for transfers between devices, shards(): kept_all = lax.all_gather(kept.astype(BF16), 'replica', axis=0, tiled=True)  38.5 us
    all_gather x4, waiting for transfers between devices, shards(): lax.all_gather(delta.astype(BF16), 'replica', axis=0, tiled=True)  33.3 us
    ppermute x4, waiting for transfers between devices, shards(): back = lax.ppermute(out, 'tensor', [(b, a) for a, b in pairs])  18.4 us
    ppermute x4, starting transfers between devices, shards(): landed = lax.ppermute(held, 'tensor', pairs)  17.8 us
    pallas_call x1, Pallas kernels, shards(): pl.pallas_call(forward_kernel, grid=(groups,), in_specs=[smem, all_heads,...  17.1 us
    ppermute x4, waiting for transfers between devices, shards(): landed = lax.ppermute(held, 'tensor', pairs)  16.9 us
    ppermute x12, waiting for transfers between devices, shards(): lax.ppermute(total(mask), 'replica', [(r, r ^ mask << bit) for r in range...  15.5 us
    ppermute x12, starting transfers between devices, shards(): lax.ppermute(total(mask), 'replica', [(r, r ^ mask << bit) for r in range...  15.2 us
  transfers between devices with their start and end apart: 38, of which 23 were waited for; matrix products, arithmetic and copies ran while one was open for 5% of the time, Pallas kernels for 10%

profile of v2, /device:TPU:0, one launch (start us, length us, event | category | flops | bytes accessed | tf_op | source)
XLA Modules:
  0.0 273.3 jit_solution(13806469161909344191)
XLA Ops:
  9.4 17.1 %shard_map.156 = (bf16[512,1024]{1,0:T(8,128)(2,1)}, f32[2,512,1]{2,1,0:T(8,128)}, bf16[512,512]{1,0:T(8,128)(2,1)}, bf16[512,512]{1,0:T(8,128)(2,1)}, bf16[512,...) custom-call(s32[3]{0:T(128)} %pad_add_fusion.place_ref, f32[512,16]{1,0:T(8,128)} %copy.18.dt_ref, bf16[512,1024]{1,0:T(8,128)(2,1)} %x_ref.1, ...), custom_call_target="tpu_custom_call" | custom-call | flops 2952790016 | bytes 8388608 | tf_op jit(solution)/shard_map/pallas_call | solution.py:282
  26.5 5.1 %collective-permute-start = (bf16[512,512]{1,0:T(8,128)(2,1)}, bf16[512,512]{1,0:T(8,128)(2,1)S(1)}, u32[]{:S(2)}, u32[]{:S(2)}) collective-permute-start(bf16[512,512]{1,0:T(8,128)(2,1)} %get-tuple-element.26), channel_id=1, source_target_pairs={{0,1},{3,2},{4,5},{7,6},{8,9},{11,10},{12,13},{15,14},{16,17},{19,... | collective-permute-start | bytes 1572872 | tf_op jit(solution)/shard_map/ppermute | solution.py:303
  32.9 11.3 %collective-permute-done = bf16[512,512]{1,0:T(8,128)(2,1)S(1)} collective-permute-done((bf16[512,512]{1,0:T(8,128)(2,1)}, bf16[512,512]{1,0:T(8,128)(2,1)S(1)}, u32[]{:S(2)}, u32[]{:S(2)}) %collective-permute-start) | collective-permute-done | bytes 524320 | tf_op jit(solution)/shard_map/ppermute | solution.py:303
  46.1 7.1 %collective-permute-start.6 = (bf16[512,512]{1,0:T(8,128)(2,1)}, bf16[512,512]{1,0:T(8,128)(2,1)S(1)}, u32[]{:S(2)}, u32[]{:S(2)}) collective-permute-start(bf16[512,512]{1,0:T(8,128)(2,1)} %get-tuple-element.31), channel_id=1, source_target_pairs={{0,1},{3,2},{4,5},{7,6},{8,9},{11,10},{12,13},{15,14},{16,17},{19,... | collective-permute-start | bytes 1572872 | tf_op jit(solution)/shard_map/ppermute | solution.py:303
  53.2 2.2 collective-permute-done.3
  55.4 4.3 %collective-permute-start.9 = (bf16[512,512]{1,0:T(8,128)(2,1)}, bf16[512,512]{1,0:T(8,128)(2,1)S(1)}, u32[]{:S(2)}, u32[]{:S(2)}) collective-permute-start(bf16[512,512]{1,0:T(8,128)(2,1)} %get-tuple-element.34), channel_id=1, source_target_pairs={{0,1},{3,2},{4,5},{7,6},{8,9},{11,10},{12,13},{15,14},{16,17},{19,... | collective-permute-start | bytes 1572872 | tf_op jit(solution)/shard_map/ppermute | solution.py:303
  63.2 3.4 %collective-permute-done.6 = bf16[512,512]{1,0:T(8,128)(2,1)S(1)} collective-permute-done((bf16[512,512]{1,0:T(8,128)(2,1)}, bf16[512,512]{1,0:T(8,128)(2,1)S(1)}, u32[]{:S(2)}, u32[]{:S(2)}) %collective-permute-start.6) | collective-permute-done | bytes 524320 | tf_op jit(solution)/shard_map/ppermute | solution.py:303
  67.5 5.7 %collective-permute-done.2.sent_ref = bf16[512,512]{1,0:T(8,128)(2,1)S(1)} collective-permute-done((bf16[512,512]{1,0:T(8,128)(2,1)S(1)}, bf16[512,512]{1,0:T(8,128)(2,1)S(1)}, u32[]{:S(2)}, u32[]{:S(2)}) %collective-permute-start.2) | collective-permute-done | bytes 524320 | tf_op jit(solution)/shard_map/ppermute | solution.py:310
  73.9 3.4 %shard_map.157 = (bf16[512,512]{1,0:T(8,128)(2,1)}, bf16[4,64,1024]{2,1,0:T(8,128)(2,1)}, bf16[4,64,1024]{2,1,0:T(8,128)(2,1)}) custom-call(s32[3]{0:T(128)} %pad_add_fusion.place_ref, bf16[512,512]{1,0:T(8,128)(2,1)} %copy-done.4, bf16[512,512]{1,0:T(8,128)(2,1)} %copy-done.12, bf16[512,1024]{1,0:T(8,128)(2,1)} %get-tuple-element.24.normed_ref, ...), custom_call_target="tpu_custom_call" | custom-call | flops 536870912 | bytes 3145728 | tf_op jit(solution)/shard_map/pallas_call | solution.py:314
  85.5 2.7 collective-permute-done.13
  98.1 3.4 %shard_map.158 = (bf16[512,512]{1,0:T(8,128)(2,1)}, bf16[4,64,1024]{2,1,0:T(8,128)(2,1)}, bf16[4,64,1024]{2,1,0:T(8,128)(2,1)}) custom-call(s32[3]{0:T(128)} %pad_add_fusion.place_ref, bf16[512,512]{1,0:T(8,128)(2,1)} %copy-done.1, bf16[512,512]{1,0:T(8,128)(2,1)} %copy-done.10, bf16[512,1024]{1,0:T(8,128)(2,1)} %get-tuple-element.24.normed_ref, ...), custom_call_target="tpu_custom_call" | custom-call | flops 536870912 | bytes 3145728 | tf_op jit(solution)/shard_map/pallas_call | solution.py:314
  101.6 7.5 %collective-permute-done.8.sent_ref = bf16[512,512]{1,0:T(8,128)(2,1)} collective-permute-done((bf16[512,512]{1,0:T(8,128)(2,1)S(1)}, bf16[512,512]{1,0:T(8,128)(2,1)}, u32[]{:S(2)}, u32[]{:S(2)}) %collective-permute-start.8) | collective-permute-done | bytes 524320 | tf_op jit(solution)/shard_map/ppermute | solution.py:310
  109.1 3.4 %shard_map.159 = (bf16[512,512]{1,0:T(8,128)(2,1)}, bf16[4,64,1024]{2,1,0:T(8,128)(2,1)}, bf16[4,64,1024]{2,1,0:T(8,128)(2,1)}) custom-call(s32[3]{0:T(128)} %pad_add_fusion.place_ref, bf16[512,512]{1,0:T(8,128)(2,1)} %copy-done.2, bf16[512,512]{1,0:T(8,128)(2,1)} %collective-permute-done.8.sent_ref, bf16[512,1024]{1,0:T(8,128)(2,1)} %get-tuple-element.24.normed_ref, ...), custom_call_target="tpu_custom_call" | custom-call | flops 536870912 | bytes 3145728 | tf_op jit(solution)/shard_map/pallas_call | solution.py:314
  112.6 5.3 %collective-permute-done.11.sent_ref = bf16[512,512]{1,0:T(8,128)(2,1)S(1)} collective-permute-done((bf16[512,512]{1,0:T(8,128)(2,1)S(1)}, bf16[512,512]{1,0:T(8,128)(2,1)S(1)}, u32[]{:S(2)}, u32[]{:S(2)}) %collective-permute-start.11) | collective-permute-done | bytes 524320 | tf_op jit(solution)/shard_map/ppermute | solution.py:310
  118.7 3.4 %shard_map.160 = (bf16[512,512]{1,0:T(8,128)(2,1)}, bf16[4,64,1024]{2,1,0:T(8,128)(2,1)}, bf16[4,64,1024]{2,1,0:T(8,128)(2,1)}) custom-call(s32[3]{0:T(128)} %pad_add_fusion.place_ref, bf16[512,512]{1,0:T(8,128)(2,1)} %copy-done.3, bf16[512,512]{1,0:T(8,128)(2,1)} %copy-done.11, bf16[512,1024]{1,0:T(8,128)(2,1)} %get-tuple-element.24.normed_ref, ...), custom_call_target="tpu_custom_call" | custom-call | flops 536870912 | bytes 3145728 | tf_op jit(solution)/shard_map/pallas_call | solution.py:314
  140.2 3.4 %collective-permute-done.27 = bf16[1,64,1024]{2,1,0:T(8,128)(2,1)S(1)} collective-permute-done((bf16[1,64,1024]{2,1,0:T(8,128)(2,1)S(1)}, bf16[1,64,1024]{2,1,0:T(8,128)(2,1)S(1)}, u32[]{:S(2)}, u32[]{:S(2)}) %collective-permute-start.27) | collective-permute-done | bytes 131104 | tf_op jit(solution)/shard_map/ppermute | solution.py:345
  158.1 3.1 %collective-permute-done.30 = f32[8,128]{1,0:T(8,128)S(1)} collective-permute-done((f32[8,128]{1,0:T(8,128)S(1)}, f32[8,128]{1,0:T(8,128)S(1)}, u32[]{:S(2)}, u32[]{:S(2)}) %collective-permute-start.30) | collective-permute-done | bytes 4128 | tf_op jit(solution)/shard_map/ppermute | solution.py:371
  161.2 3.6 %collective-permute-done.31 = f32[8,128]{1,0:T(8,128)S(1)} collective-permute-done((f32[8,128]{1,0:T(8,128)S(1)}, f32[8,128]{1,0:T(8,128)S(1)}, u32[]{:S(2)}, u32[]{:S(2)}) %collective-permute-start.31) | collective-permute-done | bytes 4128 | tf_op jit(solution)/shard_map/ppermute | solution.py:373
  165.8 3.5 %collective-permute-done.32 = f32[8,128]{1,0:T(8,128)S(1)} collective-permute-done((f32[8,128]{1,0:T(8,128)S(1)}, f32[8,128]{1,0:T(8,128)S(1)}, u32[]{:S(2)}, u32[]{:S(2)}) %collective-permute-start.32) | collective-permute-done | bytes 4128 | tf_op jit(solution)/shard_map/ppermute | solution.py:373
  172.5 14.6 %shard_map.161 = bf16[512,1024]{1,0:T(8,128)(2,1)} custom-call(f32[512,16]{1,0:T(8,128)} %copy.18.dt_ref, bf16[512,1024]{1,0:T(8,128)(2,1)} %get-tuple-element.24.normed_ref, f32[2,512,1]{2,1,0:T(8,128)} %get-tuple-element.25.inv_ref, bf16[512,1024]{1,0:T(8,128)(2,1)} %z_ref.3, bf16[512,256]{1,0:T(8,128)(2,1)} %b_ref.3, bf16[512,256]{1,0:T(8,128)(2,1)} %c_ref.3, ...), custom_call_target="tpu_custom_call" | custom-call | flops 2952790016 | bytes 8388608 | tf_op jit(solution)/shard_map/pallas_call | solution.py:356
  187.1 8.0 %all-gather.10.cloned.1.call-done.refs_1_ = bf16[512,1024]{1,0:T(8,128)(2,1)} async-done(((bf16[64,1024]{1,0:T(8,128)(2,1)}), bf16[512,1024]{1,0:T(8,128)(2,1)}) %all-gather.10.cloned.1.call-update) | async-done | bytes 1048592 | tf_op jit(solution)/shard_map/all_gather | solution.py:354
  195.1 25.3 %all-gather.12.cloned.1.call-done.refs_2_ = bf16[512,1024]{1,0:T(8,128)(2,1)} async-done(((bf16[64,1024]{1,0:T(8,128)(2,1)}), bf16[512,1024]{1,0:T(8,128)(2,1)}) %all-gather.12.cloned.1.call-update) | async-done | bytes 1048592 | tf_op jit(solution)/shard_map/all_gather | solution.py:354
  220.3 38.5 %all-gather.6.cloned.1.call-done.kept_ref = bf16[2048,1024]{1,0:T(8,128)(2,1)} async-done(((bf16[256,1024]{1,0:T(8,128)(2,1)}), bf16[2048,1024]{1,0:T(8,128)(2,1)}) %all-gather.6.cloned.1.call-update) | async-done | bytes 4194320 | tf_op jit(solution)/shard_map/all_gather | solution.py:280
  258.8 7.9 %shard_map.162 = bf16[2048,1024]{1,0:T(8,128)(2,1)} custom-call(f32[1]{0:T(128)} %bitcast.10.scale_ref, bf16[2048,1024]{1,0:T(8,128)(2,1)} %all-gather.6.cloned.1.call-done.kept_ref, bf16[512,1024]{1,0:T(8,128)(2,1)} %all-gather.8.cloned.1.call-done.refs_0_, bf16[512,1024]{1,0:T(8,128)(2,1)} %all-gather.10.cloned.1.call-done.refs_1_, ...), custom_call_target="tpu_custom_call" | custom-call | flops 4194304 | bytes 12582912 | tf_op jit(solution)/shard_map/pallas_call | solution.py:380
  (117 shorter events, 62.7 us)
Async XLA Ops:
  7.2 179.9 %all-gather.8.cloned.1.call-start = ((), (), s32[]{:S(2)}) async-start(), calls=%async_computation.1 | async-start | bytes 1179648 | tf_op jit(solution)/shard_map/all_gather | solution.py:354
  26.5 17.7 %collective-permute-start = (bf16[512,512]{1,0:T(8,128)(2,1)}, bf16[512,512]{1,0:T(8,128)(2,1)S(1)}, u32[]{:S(2)}, u32[]{:S(2)}) collective-permute-start(bf16[512,512]{1,0:T(8,128)(2,1)} %get-tuple-element.26), channel_id=1, source_target_pairs={{0,1},{3,2},{4,5},{7,6},{8,9},{11,10},{12,13},{15,14},{16,17},{19,... | collective-permute-start | bytes 1572872 | tf_op jit(solution)/shard_map/ppermute | solution.py:303
  31.6 23.8 %collective-permute-start.3 = (bf16[512,512]{1,0:T(8,128)(2,1)}, bf16[512,512]{1,0:T(8,128)(2,1)S(1)}, u32[]{:S(2)}, u32[]{:S(2)}) collective-permute-start(bf16[512,512]{1,0:T(8,128)(2,1)} %get-tuple-element.28), channel_id=1, source_target_pairs={{0,1},{3,2},{4,5},{7,6},{8,9},{11,10},{12,13},{15,14},{16,17},{19,... | collective-permute-start | bytes 1572872 | tf_op jit(solution)/shard_map/ppermute | solution.py:303
  45.4 14.4 %collective-permute-start.1 = (bf16[512,512]{1,0:T(8,128)(2,1)S(1)}, bf16[512,512]{1,0:T(8,128)(2,1)S(1)}, u32[]{:S(2)}, u32[]{:S(2)}) collective-permute-start(bf16[512,512]{1,0:T(8,128)(2,1)S(1)} %add_convert_fusion.7), channel_id=1, source_target_pairs={{1,2},{2,1},{5,6},{6,5},{9,10},{10,9},{13,14},{14,13},{17,18},{18,... | collective-permute-start | bytes 1572872 | tf_op jit(solution)/shard_map/ppermute | solution.py:307
  46.1 20.6 %collective-permute-start.6 = (bf16[512,512]{1,0:T(8,128)(2,1)}, bf16[512,512]{1,0:T(8,128)(2,1)S(1)}, u32[]{:S(2)}, u32[]{:S(2)}) collective-permute-start(bf16[512,512]{1,0:T(8,128)(2,1)} %get-tuple-element.31), channel_id=1, source_target_pairs={{0,1},{3,2},{4,5},{7,6},{8,9},{11,10},{12,13},{15,14},{16,17},{19,... | collective-permute-start | bytes 1572872 | tf_op jit(solution)/shard_map/ppermute | solution.py:303
  55.4 22.0 %collective-permute-start.9 = (bf16[512,512]{1,0:T(8,128)(2,1)}, bf16[512,512]{1,0:T(8,128)(2,1)S(1)}, u32[]{:S(2)}, u32[]{:S(2)}) collective-permute-start(bf16[512,512]{1,0:T(8,128)(2,1)} %get-tuple-element.34), channel_id=1, source_target_pairs={{0,1},{3,2},{4,5},{7,6},{8,9},{11,10},{12,13},{15,14},{16,17},{19,... | collective-permute-start | bytes 1572872 | tf_op jit(solution)/shard_map/ppermute | solution.py:303
  59.9 13.3 %collective-permute-start.2 = (bf16[512,512]{1,0:T(8,128)(2,1)S(1)}, bf16[512,512]{1,0:T(8,128)(2,1)S(1)}, u32[]{:S(2)}, u32[]{:S(2)}) collective-permute-start(bf16[512,512]{1,0:T(8,128)(2,1)S(1)} %add_convert_fusion.6.mid_ref), channel_id=1, source_target_pairs={{1,0},{2,3},{5,4},{6,7},{9,8},{10,11},{13,12},{14,15},{17,16},{18,... | collective-permute-start | bytes 1572872 | tf_op jit(solution)/shard_map/ppermute | solution.py:310
  62.4 16.8 %collective-permute-start.4 = (bf16[512,512]{1,0:T(8,128)(2,1)S(1)}, bf16[512,512]{1,0:T(8,128)(2,1)S(1)}, u32[]{:S(2)}, u32[]{:S(2)}) collective-permute-start(bf16[512,512]{1,0:T(8,128)(2,1)S(1)} %add_convert_fusion.5), channel_id=1, source_target_pairs={{1,2},{2,1},{5,6},{6,5},{9,10},{10,9},{13,14},{14,13},{17,18},{18,... | collective-permute-start | bytes 1572872 | tf_op jit(solution)/shard_map/ppermute | solution.py:307
  66.8 18.1 %collective-permute-start.7 = (bf16[512,512]{1,0:T(8,128)(2,1)S(1)}, bf16[512,512]{1,0:T(8,128)(2,1)S(1)}, u32[]{:S(2)}, u32[]{:S(2)}) collective-permute-start(bf16[512,512]{1,0:T(8,128)(2,1)S(1)} %add_convert_fusion.3), channel_id=1, source_target_pairs={{1,2},{2,1},{5,6},{6,5},{9,10},{10,9},{13,14},{14,13},{17,18},{18,... | collective-permute-start | bytes 1572872 | tf_op jit(solution)/shard_map/ppermute | solution.py:307
  77.6 17.0 %collective-permute-start.10 = (bf16[512,512]{1,0:T(8,128)(2,1)S(1)}, bf16[512,512]{1,0:T(8,128)(2,1)}, u32[]{:S(2)}, u32[]{:S(2)}) collective-permute-start(bf16[512,512]{1,0:T(8,128)(2,1)S(1)} %add_convert_fusion.1), channel_id=1, source_target_pairs={{1,2},{2,1},{5,6},{6,5},{9,10},{10,9},{13,14},{14,13},{17,18},{18,... | collective-permute-start | bytes 1572872 | tf_op jit(solution)/shard_map/ppermute | solution.py:307
  79.3 18.0 %collective-permute-start.5 = (bf16[512,512]{1,0:T(8,128)(2,1)S(1)}, bf16[512,512]{1,0:T(8,128)(2,1)S(1)}, u32[]{:S(2)}, u32[]{:S(2)}) collective-permute-start(bf16[512,512]{1,0:T(8,128)(2,1)S(1)} %add_convert_fusion.4.mid_ref), channel_id=1, source_target_pairs={{1,0},{2,3},{5,4},{6,7},{9,8},{10,11},{13,12},{14,15},{17,16},{18,... | collective-permute-start | bytes 1572872 | tf_op jit(solution)/shard_map/ppermute | solution.py:310
  88.2 20.9 %collective-permute-start.8 = (bf16[512,512]{1,0:T(8,128)(2,1)S(1)}, bf16[512,512]{1,0:T(8,128)(2,1)}, u32[]{:S(2)}, u32[]{:S(2)}) collective-permute-start(bf16[512,512]{1,0:T(8,128)(2,1)S(1)} %add_convert_fusion.2.mid_ref), channel_id=1, source_target_pairs={{1,0},{2,3},{5,4},{6,7},{9,8},{10,11},{13,12},{14,15},{17,16},{18,... | collective-permute-start | bytes 1572872 | tf_op jit(solution)/shard_map/ppermute | solution.py:310
  94.6 92.5 %all-gather.14.cloned.1.call-start = ((), (), s32[]{:S(2)}) async-start(), calls=%async_computation.4 | async-start | bytes 1179648 | tf_op jit(solution)/shard_map/all_gather | solution.py:354
  95.8 22.1 %collective-permute-start.11 = (bf16[512,512]{1,0:T(8,128)(2,1)S(1)}, bf16[512,512]{1,0:T(8,128)(2,1)S(1)}, u32[]{:S(2)}, u32[]{:S(2)}) collective-permute-start(bf16[512,512]{1,0:T(8,128)(2,1)S(1)} %add_convert_fusion.mid_ref), channel_id=1, source_target_pairs={{1,0},{2,3},{5,4},{6,7},{9,8},{10,11},{13,12},{14,15},{17,16},{18,... | collective-permute-start | bytes 1572872 | tf_op jit(solution)/shard_map/ppermute | solution.py:310
  101.5 20.7 %collective-permute-start.16 = (bf16[4,64,1024]{2,1,0:T(8,128)(2,1)}, bf16[4,64,1024]{2,1,0:T(8,128)(2,1)S(1)}, u32[]{:S(2)}, u32[]{:S(2)}) collective-permute-start(bf16[4,64,1024]{2,1,0:T(8,128)(2,1)} %get-tuple-element.39), channel_id=1, source_target_pairs={{0,4},{4,0},{8,12},{12,8},{16,20},{20,16},{24,28},{28,24},{1,5},{5... | collective-permute-start | bytes 1572872 | tf_op jit(solution)/shard_map/ppermute | solution.py:329
  112.5 13.5 %collective-permute-start.20 = (bf16[4,64,1024]{2,1,0:T(8,128)(2,1)}, bf16[4,64,1024]{2,1,0:T(8,128)(2,1)S(1)}, u32[]{:S(2)}, u32[]{:S(2)}) collective-permute-start(bf16[4,64,1024]{2,1,0:T(8,128)(2,1)} %get-tuple-element.41), channel_id=1, source_target_pairs={{0,4},{4,0},{8,12},{12,8},{16,20},{20,16},{24,28},{28,24},{1,5},{5... | collective-permute-start | bytes 1572872 | tf_op jit(solution)/shard_map/ppermute | solution.py:329
  125.4 9.1 %collective-permute-start.18 = (bf16[1,64,1024]{2,1,0:T(8,128)(2,1)S(1)}, bf16[1,64,1024]{2,1,0:T(8,128)(2,1)S(1)}, u32[]{:S(2)}, u32[]{:S(2)}) collective-permute-start(bf16[1,64,1024]{2,1,0:T(8,128)(2,1)S(1)} %get-tuple-element.67), channel_id=1, source_target_pairs={{0,16},{4,20},{8,24},{12,28},{16,0},{20,4},{24,8},{28,12},{1,17},{... | collective-permute-start | bytes 393224 | tf_op jit(solution)/shard_map/ppermute | solution.py:345
  126.1 9.9 %collective-permute-start.21 = (bf16[1,64,1024]{2,1,0:T(8,128)(2,1)S(1)}, bf16[1,64,1024]{2,1,0:T(8,128)(2,1)S(1)}, u32[]{:S(2)}, u32[]{:S(2)}) collective-permute-start(bf16[1,64,1024]{2,1,0:T(8,128)(2,1)S(1)} %get-tuple-element.62), channel_id=1, source_target_pairs={{0,8},{4,12},{8,0},{12,4},{16,24},{20,28},{24,16},{28,20},{1,9},{5... | collective-permute-start | bytes 393224 | tf_op jit(solution)/shard_map/ppermute | solution.py:345
  127.6 10.6 %collective-permute-start.23 = (bf16[1,64,1024]{2,1,0:T(8,128)(2,1)S(1)}, bf16[1,64,1024]{2,1,0:T(8,128)(2,1)S(1)}, u32[]{:S(2)}, u32[]{:S(2)}) collective-permute-start(bf16[1,64,1024]{2,1,0:T(8,128)(2,1)S(1)} %get-tuple-element.63), channel_id=1, source_target_pairs={{0,24},{4,28},{8,16},{12,20},{16,8},{20,12},{24,0},{28,4},{1,25},{... | collective-permute-start | bytes 393224 | tf_op jit(solution)/shard_map/ppermute | solution.py:345
  130.3 9.9 %collective-permute-start.22 = (bf16[1,64,1024]{2,1,0:T(8,128)(2,1)S(1)}, bf16[1,64,1024]{2,1,0:T(8,128)(2,1)S(1)}, u32[]{:S(2)}, u32[]{:S(2)}) collective-permute-start(bf16[1,64,1024]{2,1,0:T(8,128)(2,1)S(1)} %get-tuple-element.64), channel_id=1, source_target_pairs={{0,16},{4,20},{8,24},{12,28},{16,0},{20,4},{24,8},{28,12},{1,17},{... | collective-permute-start | bytes 393224 | tf_op jit(solution)/shard_map/ppermute | solution.py:345
  134.6 9.0 %collective-permute-start.27 = (bf16[1,64,1024]{2,1,0:T(8,128)(2,1)S(1)}, bf16[1,64,1024]{2,1,0:T(8,128)(2,1)S(1)}, u32[]{:S(2)}, u32[]{:S(2)}) collective-permute-start(bf16[1,64,1024]{2,1,0:T(8,128)(2,1)S(1)} %get-tuple-element.60), channel_id=1, source_target_pairs={{0,24},{4,28},{8,16},{12,20},{16,8},{20,12},{24,0},{28,4},{1,25},{... | collective-permute-start | bytes 393224 | tf_op jit(solution)/shard_map/ppermute | solution.py:345
  146.8 48.3 %all-gather.10.cloned.1.call-start = ((), (), s32[]{:S(2)}) async-start(), calls=%async_computation.2 | async-start | bytes 1179648 | tf_op jit(solution)/shard_map/all_gather | solution.py:354
  147.5 72.8 %all-gather.12.cloned.1.call-start = ((), (), s32[]{:S(2)}) async-start(), calls=%async_computation.3 | async-start | bytes 1179648 | tf_op jit(solution)/shard_map/all_gather | solution.py:354
  148.1 110.7 %all-gather.6.cloned.1.call-start = ((), (), s32[]{:S(2)}) async-start(), calls=%async_computation | async-start | bytes 4718592 | tf_op jit(solution)/shard_map/all_gather | solution.py:280
  (27 other events, 289.3 us)
Sparse Core Ops, SparseCore 0:
  94.7 27.4 all-gather.7
  146.9 22.6 all-gather.13
  171.5 23.4 all-gather.9
  196.8 23.4 all-gather.11
  222.1 36.6 all-gather.5

commit v3 on v2

v3 whole, which is shorter than its diff:
```python
import functools

import jax
import jax.numpy as jnp
from jax import lax
from jax.experimental import pallas as pl
from jax.experimental.pallas import tpu as pltpu
from jax.sharding import PartitionSpec as P

HEAD_DIM = 64
STATE = 128
SPAN = 256
HALF = SPAN // 2
LANES = 128

inner_rate = 0.001
outer_rate = 0.7
outer_beta = 0.9
clip_rms = 0.005
LOG2E = 1.4426950408889634
DEPTH = 2

F32 = jnp.float32
BF16 = jnp.bfloat16
NN = (((1,), (0,)), ((), ()))
NT = (((1,), (1,)), ((), ()))
TN = (((0,), (0,)), ((), ()))


def dot(a, b, dims):
    return lax.dot_general(a, b, dims, preferred_element_type=F32)


def silu(z):
    return z * (1.0 / (1.0 + jnp.exp(-z)))


def softplus(v):
    return jnp.maximum(v, 0.0) + jnp.log1p(jnp.exp(-jnp.abs(v)))


def iota(shape, axis):
    return lax.broadcasted_iota(jnp.int32, shape, axis)


def thirds(v):
    high = v.astype(BF16).astype(F32)
    middle = (v - high).astype(BF16).astype(F32)
    return jnp.concatenate([high, middle, v - high - middle], axis=0).astype(BF16)


def by_head(refs, first, per_group, tokens):
    row = iota((per_group, tokens), 0)
    rows = []
    for ref in refs:
        value = jnp.zeros((per_group, tokens), F32)
        for h in range(per_group):
            value = jnp.where(row == h, ref[first + h], value)
        rows.append(value)
    return rows


def head_tables(dt_ref, a_ref, bias_ref, per_group):
    first = pl.program_id(0) * per_group
    bias, a_log = by_head([bias_ref, a_ref], first, per_group, dt_ref.shape[1])
    step = softplus(dt_ref[...] + bias)
    return step, -jnp.exp(a_log) * step * LOG2E


def span_tables(step, rate, lo, per_group, width):
    upper = (iota((SPAN, SPAN), 0) <= iota((SPAN, SPAN), 1)).astype(BF16)
    step_k = step[:, lo : lo + SPAN]
    sums = dot(thirds(rate[:, lo : lo + SPAN]), upper, NN)
    cum = sums[:per_group] + sums[per_group : 2 * per_group] + sums[2 * per_group :]
    spread = (iota((3 * per_group, width), 1) // HEAD_DIM == iota((3 * per_group, width), 0) % per_group).astype(BF16)
    turn = (iota((3 * per_group, per_group), 1) == iota((3 * per_group, per_group), 0) % per_group).astype(BF16)
    cum_col = dot(thirds(cum), turn, TN)
    step_x = dot(thirds(step_k), spread, TN)
    fade_x = dot(thirds(jnp.exp2(cum)), spread, TN)
    tail_x = dot(thirds(jnp.exp2(cum[:, SPAN - 1 :] - cum) * step_k), spread, TN)
    return cum, cum_col, step_x, fade_x, tail_x


def skip_row(skip_ref, first, per_group, width):
    head = iota((1, width), 1) // HEAD_DIM
    row = jnp.zeros((1, width), F32)
    for h in range(per_group):
        row = jnp.where(head == h, skip_ref[first + h], row)
    return row


def decay(gap, mask=None):
    return jnp.exp2(gap if mask is None else jnp.where(mask, gap, -1e30))


def even_odd(v):
    first = iota(v.shape, 1) % (2 * HEAD_DIM) < HEAD_DIM
    return jnp.where(first, v, 0.0).astype(BF16), jnp.where(first, 0.0, v).astype(BF16)


def forward_kernel(dt_ref, x_ref, z_ref, b_ref, c_ref, gain_ref, a_ref, bias_ref, skip_ref, normed_ref, inv_ref):
    tokens, width = x_ref.shape
    per_group = width // HEAD_DIM
    step, rate = head_tables(dt_ref, a_ref, bias_ref, per_group)
    skip = skip_row(skip_ref, pl.program_id(0) * per_group, per_group, width)
    causal = iota((HALF, HALF), 0) >= iota((HALF, HALF), 1)
    spans = tokens // SPAN
    entering = None
    for k in range(spans):
        rows = slice(k * SPAN, (k + 1) * SPAN)
        cum, cum_col, step_x, fade_x, tail_x = span_tables(step, rate, k * SPAN, per_group, width)
        x = x_ref[rows, :].astype(F32)
        b, c = b_ref[rows, :], c_ref[rows, :]
        scores = dot(c, b, NT)
        values = even_odd(x * step_x)
        pieces = []
        for pair in range(per_group // 2):
            lanes = slice(2 * pair * HEAD_DIM, 2 * (pair + 1) * HEAD_DIM)
            tops, bottoms = [], []
            for h in (2 * pair, 2 * pair + 1):
                col, line = cum_col[:, h : h + 1], cum[h : h + 1, :]
                top = decay(col[:HALF] - line[:, :HALF], causal) * scores[:HALF, :HALF]
                left = decay(col[HALF:] - line[:, :HALF]) * scores[HALF:, :HALF]
                low = decay(col[HALF:] - line[:, HALF:], causal) * scores[HALF:, HALF:]
                tops.append(top.astype(BF16))
                bottoms += [left.astype(BF16), low.astype(BF16)]
            upper_values = jnp.concatenate([v[:HALF, lanes] for v in values], axis=0)
            all_values = jnp.concatenate([v[:, lanes] for v in values], axis=0)
            pieces.append(
                jnp.concatenate(
                    [
                        dot(jnp.concatenate(tops, axis=1), upper_values, NN),
                        dot(jnp.concatenate(bottoms, axis=1), all_values, NN),
                    ],
                    axis=0,
                )
            )
        ssd = jnp.concatenate(pieces, axis=1) + skip * x
        if entering is not None:
            ssd = ssd + dot(c, entering.astype(BF16), NN) * fade_x
        if k + 1 < spans:
            state = dot(b, (x * tail_x).astype(BF16), TN)
            entering = state if entering is None else entering * fade_x[SPAN - 1 :, :] + state
        gated = ssd * silu(z_ref[rows, :].astype(F32))
        inv = lax.rsqrt(jnp.mean(gated * gated, axis=1, keepdims=True) + 1e-05)
        normed_ref[rows, :] = (gated * inv * gain_ref[...]).astype(BF16)
        inv_ref[0, rows, :] = inv


def project_kernel(chunk, place_ref, weight_ref, normed_ref, target_ref, part_ref):
    owners, piece, inner = weight_ref.shape
    held, lanes = target_ref.shape
    owned = lanes // owners
    part = dot(weight_ref[...].reshape(owners * piece, inner), normed_ref[...], NT)
    goal = jnp.concatenate(
        [target_ref[:, o * owned + chunk * piece : o * owned + (chunk + 1) * piece] for o in range(owners)], axis=1
    )
    eye = (iota((held, held), 0) == iota((held, held), 1)).astype(BF16)
    turned = dot(goal, eye, TN)
    tiled = jnp.concatenate([turned] * (part.shape[1] // held), axis=1)
    part = part - jnp.where(iota(part.shape, 1) // held == place_ref[0], tiled, 0.0)
    part_ref[...] = part.astype(BF16)


def gradient_kernel(count, split, place_ref, *refs):
    cot_refs, (normed_ref, weight_ref), outs = refs[: 2 * count], refs[2 * count : 2 * count + 2], refs[2 * count + 2 :]
    middle = place_ref[1] == 1
    owners, rows, inner = weight_ref.shape
    piece = rows // count
    for n in range(count):
        cot = jnp.where(middle, cot_refs[2 * n][...], cot_refs[2 * n + 1][...])
        weight = weight_ref[:, n * piece : (n + 1) * piece, :].reshape(owners * piece, inner).astype(F32)
        new = (weight - inner_rate * dot(cot, normed_ref[...], NN)).astype(BF16).reshape(owners, piece, inner)
        at = slice(n * piece, (n + 1) * piece)
        if split:
            odd = place_ref[2] == 1
            outs[0][0, at, :] = jnp.where(odd, new[1], new[0])
            outs[1][0, at, :] = jnp.where(odd, new[0], new[1])
        else:
            outs[0][:, at, :] = new


def backward_kernel(
    place_ref, dt_ref, normed_ref, inv_ref, z_ref, b_ref, c_ref, gain_ref, a_ref, bias_ref, skip_ref, weight_ref, *refs
):
    *cot_refs, dx_ref, dn_ref = refs
    tokens, width = normed_ref.shape
    per_group = width // HEAD_DIM
    replicas, owned, _ = weight_ref.shape
    chunks = len(cot_refs) // 2
    piece = owned // chunks
    middle = place_ref[1] == 1
    for n in range(chunks):
        weight = weight_ref[:, n * piece : (n + 1) * piece, :].reshape(replicas * piece, width)
        term = dot(jnp.where(middle, cot_refs[2 * n][...], cot_refs[2 * n + 1][...]), weight, TN)
        dn_ref[...] = term if n == 0 else dn_ref[...] + term
    step, rate = head_tables(dt_ref, a_ref, bias_ref, per_group)
    skip = skip_row(skip_ref, pl.program_id(0) * per_group, per_group, width)
    causal = iota((HALF, HALF), 1) >= iota((HALF, HALF), 0)
    spans = tokens // SPAN
    d_state = None
    for k in reversed(range(spans)):
        rows = slice(k * SPAN, (k + 1) * SPAN)
        cum, cum_col, step_x, fade_x, tail_x = span_tables(step, rate, k * SPAN, per_group, width)
        dn = dn_ref[rows, :]
        gain = gain_ref[...]
        normed = normed_ref[rows, :].astype(F32)
        shared = jnp.mean(normed * dn, axis=1, keepdims=True)
        d_gated = inv_ref[0, rows, :] * (gain * dn - (normed / gain) * shared)
        d_ssd = d_gated * silu(z_ref[rows, :].astype(F32))
        values = even_odd(d_ssd)
        b, c = b_ref[rows, :], c_ref[rows, :]
        scores = dot(b, c, NT)
        pieces = []
        for pair in range(per_group // 2):
            lanes = slice(2 * pair * HEAD_DIM, 2 * (pair + 1) * HEAD_DIM)
            tops, bottoms = [], []
            for h in (2 * pair, 2 * pair + 1):
                col, line = cum_col[:, h : h + 1], cum[h : h + 1, :]
                high = decay(line[:, :HALF] - col[:HALF], causal) * scores[:HALF, :HALF]
                right = decay(line[:, HALF:] - col[:HALF]) * scores[:HALF, HALF:]
                low = decay(line[:, HALF:] - col[HALF:], causal) * scores[HALF:, HALF:]
                tops += [high.astype(BF16), right.astype(BF16)]
                bottoms.append(low.astype(BF16))
            lower_values = jnp.concatenate([v[HALF:, lanes] for v in values], axis=0)
            all_values = jnp.concatenate([v[:, lanes] for v in values], axis=0)
            pieces.append(
                jnp.concatenate(
                    [
                        dot(jnp.concatenate(tops, axis=1), all_values, NN),
                        dot(jnp.concatenate(bottoms, axis=1), lower_values, NN),
                    ],
                    axis=0,
                )
            )
        dx = jnp.concatenate(pieces, axis=1) * step_x + skip * d_ssd
        if d_state is not None:
            dx = dx + dot(b, d_state.astype(BF16), NN) * tail_x
        dx_ref[rows, :] = dx.astype(BF16)
        if k > 0:
            own = dot(c, (d_ssd * fade_x).astype(BF16), TN)
            d_state = own if d_state is None else own + d_state * fade_x[SPAN - 1 :, :]


def weight_kernel(place_ref, scale_ref, kept_ref, whole_ref, *refs):
    *pair_refs, new_ref = refs
    mine = lax.rem(pl.program_id(0), 2) == place_ref[2]
    pieces = [whole_ref[...]]
    for own_ref, other_ref in zip(pair_refs[::2], pair_refs[1::2]):
        pieces.append(jnp.where(mine, own_ref[0], other_ref[0]))
    lo = 0
    for piece in pieces:
        rows = slice(lo, lo + piece.shape[0])
        lo += piece.shape[0]
        new_ref[rows, :] = (kept_ref[rows, :].astype(F32) - scale_ref[0] * piece.astype(F32)).astype(BF16)


def inward(axis_size):
    half = axis_size // 2
    hops = [[(s, s + 1), (axis_size - 1 - s, axis_size - 2 - s)] for s in range(half - 1)]
    return hops, [(half - 1, half), (half, half - 1)]


def add16(a, b):
    return (a.astype(F32) + b.astype(F32)).astype(BF16)


def after(value, *others):
    return lax.optimization_barrier((value, *others))[0]


def stages(replicas):
    bit, left, found = 1, replicas // 2, []
    while left > 1:
        bits = 2 if left >= 4 else 1
        found.append((bit, bits))
        bit, left = bit + bits, left >> bits
    return found


def reduce_rows(keep, send, replicas, me):
    _, piece, inner = keep.shape
    mine, landed = keep, [lax.ppermute(send, "replica", [(r, r ^ 1) for r in range(replicas)])]
    left = replicas // 2
    for bit, bits in stages(replicas):
        ways = 1 << bits
        my = lax.rem(lax.div(me, 1 << bit), ways)
        terms = [t.reshape(left // ways, ways, piece, inner) for t in [mine] + landed]

        def total(mask):
            at = lax.bitwise_xor(my, jnp.int32(mask))
            cut = [lax.dynamic_index_in_dim(t, at, 1, keepdims=False).astype(F32) for t in terms]
            return functools.reduce(jnp.add, cut).astype(BF16)

        landed = [
            lax.ppermute(total(mask), "replica", [(r, r ^ (mask << bit)) for r in range(replicas)])
            for mask in range(1, ways)
        ]
        mine = total(0)
        left //= ways
    return functools.reduce(jnp.add, [t.reshape(piece, inner).astype(F32) for t in [mine] + landed])


def gather_rows(rows, replicas):
    held = rows[None]
    for bit, bits in stages(replicas):
        parts = [held] + [
            lax.ppermute(held, "replica", [(r, r ^ (mask << bit)) for r in range(replicas)]) for mask in range(1, 1 << bits)
        ]
        held = jnp.concatenate(parts, axis=0)
    return held, lax.ppermute(held, "replica", [(r, r ^ 1) for r in range(replicas)])


def shards(
    x_in,
    gate_z,
    b_proj,
    c_proj,
    dt_raw,
    a_log,
    dt_bias,
    skip_d,
    norm_gain,
    out_weight,
    global_weight,
    momentum,
    target,
):
    tokens, inner = x_in.shape
    features = out_weight.shape[1]
    replicas = lax.axis_size("replica")
    heads_over = lax.axis_size("tensor")
    groups = b_proj.shape[1] // STATE
    heads = dt_raw.shape[1]
    width = inner // groups
    owned = features // replicas
    chunks = max(2, min(4, owned // 16))
    batches = [list(range(max(1, chunks - 2)))] + [[n] for n in range(max(1, chunks - 2), chunks)]
    piece = owned // chunks
    span_rows = replicas * piece
    place = lax.axis_index("tensor")
    me = lax.axis_index("replica")
    in_middle = (place == heads_over // 2 - 1) | (place == heads_over // 2)
    places = jnp.stack([place, in_middle.astype(jnp.int32), lax.rem(me, 2), lax.div(me, 2)]).astype(jnp.int32)
    weight = out_weight[0].reshape(replicas, owned, inner)
    gain = norm_gain.reshape(1, inner)
    dt_rows = dt_raw.T

    smem = pl.BlockSpec(memory_space=pltpu.SMEM)
    by_group = pl.BlockSpec((tokens, width), lambda g: (0, g))
    by_state = pl.BlockSpec((tokens, STATE), lambda g: (0, g))
    inv_spec = pl.BlockSpec((1, tokens, 1), lambda g: (g, 0, 0))
    dt_spec = pl.BlockSpec((heads // groups, tokens), lambda g: (g, 0))
    gain_spec = pl.BlockSpec((1, width), lambda g: (0, g))
    weight_spec = pl.BlockSpec((replicas, owned, width), lambda g: (0, 0, g))
    normed_spec = pl.BlockSpec((tokens, inner), lambda i: (0, 0))
    by_chip = pl.BlockSpec((2 * piece, tokens), lambda i: (i, 0))
    params = pltpu.CompilerParams(vmem_limit_bytes=56 * 1024 * 1024)
    cost = pl.CostEstimate(
        flops=2 * tokens * inner * 4 * SPAN, bytes_accessed=8 * inner * tokens, transcendentals=tokens * SPAN * heads
    )

    kept = global_weight - outer_rate * outer_beta * outer_beta * momentum
    kept_all = lax.all_gather(kept.astype(BF16), "replica", axis=0, tiled=True)

    normed, inv = pl.pallas_call(
        forward_kernel,
        grid=(groups,),
        in_specs=[dt_spec, by_group, by_group, by_state, by_state, gain_spec, smem, smem, smem],
        out_specs=[by_group, inv_spec],
        out_shape=[jax.ShapeDtypeStruct((tokens, inner), BF16), jax.ShapeDtypeStruct((groups, tokens, 1), F32)],
        cost_estimate=cost,
        compiler_params=params,
    )(dt_rows, x_in, gate_z, b_proj, c_proj, gain, a_log, dt_bias, skip_d)

    owners = min(replicas, max(2, LANES // owned))

    def project(n):
        return pl.pallas_call(
            functools.partial(project_kernel, n),
            grid=(replicas // owners,),
            in_specs=[
                smem,
                pl.BlockSpec((owners, piece, inner), lambda i: (i, n, 0)),
                normed_spec,
                pl.BlockSpec((target.shape[0], owners * owned), lambda i: (0, i)),
            ],
            out_specs=pl.BlockSpec((owners * piece, tokens), lambda i: (i, 0)),
            out_shape=jax.ShapeDtypeStruct((span_rows, tokens), BF16),
            cost_estimate=pl.CostEstimate(
                flops=2 * tokens * span_rows * inner, bytes_accessed=2 * (tokens + span_rows) * inner, transcendentals=0
            ),
            compiler_params=params,
        )(places, weight, normed, target)

    in_hops, across = inward(heads_over)
    first_landed = []
    cots = []

    def sum_over_heads(n):
        held = project(n)
        if n >= DEPTH:
            held = after(held, first_landed[n - DEPTH])
        for at, pairs in enumerate(in_hops):
            landed = lax.ppermute(held, "tensor", pairs)
            if at == 0:
                first_landed.append(landed)
            held = add16(held, landed)
        mid = add16(held, lax.ppermute(held, "tensor", across))
        out = mid
        for pairs in reversed(in_hops):
            back = lax.ppermute(out, "tensor", [(b, a) for a, b in pairs])
            out = back if pairs is in_hops[0] else jnp.where(in_middle, mid, back)
        return [mid, out]

    def updated(batch, split):
        rows = len(batch) * piece
        shape = (replicas // 2 if split else replicas, rows, inner)
        out_spec = pl.BlockSpec((1 if split else 2, rows, inner), lambda i: (i, 0, 0))
        count = 2 if split else 1
        return pl.pallas_call(
            functools.partial(gradient_kernel, len(batch), split),
            grid=(replicas // 2,),
            in_specs=[smem]
            + [by_chip] * (2 * len(batch))
            + [normed_spec, pl.BlockSpec((2, rows, inner), lambda i: (i, batch[0] // len(batch), 0))],
            out_specs=[out_spec] * count,
            out_shape=[jax.ShapeDtypeStruct(shape, BF16)] * count,
            cost_estimate=pl.CostEstimate(
                flops=2 * tokens * replicas * rows * inner,
                bytes_accessed=2 * (tokens + 2 * replicas * rows) * inner,
                transcendentals=0,
            ),
            compiler_params=params,
        )(places, *[c for n in batch for c in cots[n]], normed, weight)

    deltas, gathered = [], []
    for batch in batches:
        for n in batch:
            cots.append(sum_over_heads(n))
        here = global_weight[batch[0] * piece : (batch[-1] + 1) * piece]
        if batch is batches[0]:
            (new,) = updated(batch, False)
            new = after(new, kept_all)
            summed = lax.psum_scatter(new.reshape(-1, inner), "replica", scatter_dimension=0, tiled=True).astype(F32)
            deltas.append(here - summed / replicas)
            gathered.append(lax.all_gather(deltas[-1].astype(BF16), "replica", axis=0, tiled=True))
        else:
            summed = reduce_rows(*updated(batch, True), replicas, me)
            deltas.append(here - summed / replicas)
            gathered += gather_rows(deltas[-1].astype(BF16), replicas)

    (grad_input,) = pl.pallas_call(
        backward_kernel,
        grid=(groups,),
        in_specs=[smem, dt_spec, by_group, inv_spec, by_group, by_state, by_state, gain_spec, smem, smem, smem, weight_spec]
        + [pl.BlockSpec((span_rows, tokens), lambda g: (0, 0))] * (2 * chunks),
        out_specs=[by_group],
        out_shape=[jax.ShapeDtypeStruct((tokens, inner), BF16)],
        scratch_shapes=[pltpu.VMEM((tokens, width), F32)],
        cost_estimate=cost,
        compiler_params=params,
    )(places, dt_rows, normed, inv, gate_z, b_proj, c_proj, gain, a_log, dt_bias, skip_d, weight, *[c for p in cots for c in p])

    square_sum = functools.reduce(jnp.add, [jnp.sum(d * d) for d in deltas])
    spread = jnp.full((8, LANES), square_sum, F32)
    for axis, size in (("replica", replicas), ("tensor", heads_over)):
        for bit in range(size.bit_length() - 1):
            spread = spread + lax.ppermute(spread, axis, [(r, r ^ (1 << bit)) for r in range(size)])
    entry_count = features * inner * heads_over
    factor = jnp.minimum(1.0, clip_rms / jnp.sqrt(spread[0, 0] / entry_count + 1e-06))
    clipped = factor * jnp.concatenate(deltas, axis=0)
    new_momentum = outer_beta * momentum + clipped
    new_global = global_weight - outer_rate * (clipped + outer_beta * new_momentum)
    scale = (outer_rate * (1.0 + outer_beta)) * factor
    chip_spec = pl.BlockSpec((1, piece, inner), lambda r, place: (lax.bitwise_xor(lax.div(r, 2), place[3]), 0, 0))
    new_weight = pl.pallas_call(
        weight_kernel,
        grid_spec=pltpu.PrefetchScalarGridSpec(
            num_scalar_prefetch=1,
            grid=(replicas,),
            in_specs=[
                smem,
                pl.BlockSpec((owned, inner), lambda r, place: (r, 0)),
                pl.BlockSpec((len(batches[0]) * piece, inner), lambda r, place: (r, 0)),
            ]
            + [chip_spec] * (len(gathered) - 1),
            out_specs=pl.BlockSpec((owned, inner), lambda r, place: (r, 0)),
        ),
        out_shape=jax.ShapeDtypeStruct((features, inner), BF16),
        cost_estimate=pl.CostEstimate(flops=2 * features * inner, bytes_accessed=6 * features * inner, transcendentals=0),
        compiler_params=params,
    )(places, scale.reshape(1), kept_all, *gathered)
    return (grad_input, new_weight, new_global, new_momentum)


def solution(mesh):
    placed = (
        P("replica", "tensor"),
        P("replica", "tensor"),
        P("replica", "tensor"),
        P("replica", "tensor"),
        P("replica", "tensor"),
        P("tensor"),
        P("tensor"),
        P("tensor"),
        P("tensor"),
        P("replica", None, "tensor"),
        P("replica", "tensor"),
        P("replica", "tensor"),
        P(("replica", "tensor"), None),
    )
    return jax.shard_map(
        shards,
        mesh=mesh,
        in_specs=placed,
        out_specs=(
            P("replica", "tensor"),
            P(None, "tensor"),
            P("replica", "tensor"),
            P("replica", "tensor"),
        ),
        check_vma=False,
    )
```

time: 274 us -> 240 us (0.88)
  waiting for transfers between devices: 137 us -> 104 us
  starting transfers between devices: 45.6 us -> 35.5 us
  Pallas kernels: 53.2 us -> 60.9 us
  other arithmetic: 14.9 us -> 18.3 us
    all_gather x1, waiting for transfers between devices: 38.5 us -> 0.01 us  [shards(): kept_all = lax.all_gather(kept.astype(BF16), 'replica', axis=0, tiled=True)]
    all_gather x4 -> x1, waiting for transfers between devices: 33.3 us -> 0.01 us  [shards(): lax.all_gather(deltas[-1].astype(BF16), 'replica', axis=0, tiled=True)]
    ppermute x33, waiting for transfers between devices: 64.4 us -> 93.7 us  [the longest x4 42.9 us: sum_over_heads(): back = lax.ppermute(out, 'tensor', [(b, a) for a, b in pairs])]
    reduce_scatter x0 -> x1, waiting for transfers between devices: none -> 10.7 us  [shards(): lax.psum_scatter(new.reshape(-1, inner), 'replica', scatter_dimension=0,...]
    ppermute x33, starting transfers between devices: 45.4 us -> 35.4 us  [the longest x4 9.41 us: sum_over_heads(): landed = lax.ppermute(held, 'tensor', pairs)]
    pallas_call x7 -> x10, Pallas kernels: 53.2 us -> 60.9 us  [the longest x4 19.2 us: project(): pl.pallas_call(functools.partial(project_kernel, n), grid=(replicas // ow...]
  transfers between devices with their start and end apart: 38 -> 36, of which waited for: 23 -> 18; matrix products, arithmetic and copies ran while one was open for 5% -> 7% of each run, Pallas kernels for 10% -> 22%
where the time goes in v3:
time: 240 us; the launch traced here: 239 us
  waiting for transfers between devices  104 us (43%)
  Pallas kernels  60.9 us (25%)
  starting transfers between devices  35.5 us (15%)
  other arithmetic  18.3 us (8%)
  between operations  16.6 us (7%)
  local copies, waits for them, and re-layouts  3.04 us (1%)
    ppermute x4, waiting for transfers between devices, sum_over_heads(): back = lax.ppermute(out, 'tensor', [(b, a) for a, b in pairs])  42.9 us
    ppermute x4, waiting for transfers between devices, sum_over_heads(): landed = lax.ppermute(held, 'tensor', pairs)  29.7 us
    pallas_call x4, Pallas kernels, project(): pl.pallas_call(functools.partial(project_kernel, n), grid=(replicas // ow...  19.2 us
    pallas_call x3, Pallas kernels, updated(): pl.pallas_call(functools.partial(gradient_kernel, len(batch), split), gri...  14.9 us
    pallas_call x1, Pallas kernels, shards(): pl.pallas_call(backward_kernel, grid=(groups,), in_specs=[smem, dt_spec,...  11.1 us
    reduce_scatter x1, waiting for transfers between devices, shards(): lax.psum_scatter(new.reshape(-1, inner), 'replica', scatter_dimension=0,...  10.7 us
    ppermute x4, starting transfers between devices, sum_over_heads(): landed = lax.ppermute(held, 'tensor', pairs)  9.41 us
    pallas_call x1, Pallas kernels, shards(): pl.pallas_call(weight_kernel, grid_spec=pltpu.PrefetchScalarGridSpec(num_...  8.79 us
  transfers between devices with their start and end apart: 36, of which 18 were waited for; matrix products, arithmetic and copies ran while one was open for 7% of the time, Pallas kernels for 22%

profile of v3, /device:TPU:0, one launch (start us, length us, event | category | flops | bytes accessed | tf_op | source)
XLA Modules:
  0.0 238.7 jit_solution(14734494803973451348)
XLA Ops:
  9.8 6.8 %shard_map.156 = (bf16[512,1024]{1,0:T(8,128)(2,1)}, f32[2,512,1]{2,1,0:T(8,128)}) custom-call(f32[16,512]{1,0:T(8,128)} %bitcast.29, bf16[512,1024]{1,0:T(8,128)(2,1)} %x_ref.1, bf16[512,1024]{1,0:T(8,128)(2,1)} %z_ref.3, bf16[512,256]{1,0:T(8,128)(2,1)} %b_ref.3, bf16[512,256]{1,0:T(8,128)(2,1)} %c_ref.3, f32[1,1024]{1,0:T(1,128)} %bitcast.31, f32[16]{0:T(128)} %a_ref.3, ...), custom_call_target="tpu_custom_call" | custom-call | flops 1073741824 | bytes 4194304 | tf_op jit(solution)/shard_map/pallas_call | solution.py:366
  17.2 4.8 %shard_map.157 = bf16[512,512]{1,0:T(8,128)(2,1)} custom-call(s32[4]{0:T(128)} %pad_add_fusion.place_ref, bf16[8,256,1024]{2,1,0:T(8,128)(2,1)} %bitcast.20, bf16[512,1024]{1,0:T(8,128)(2,1)} %get-tuple-element.13.normed_ref.refs_4_.refs_2_, bf16[128,2048]{1,0:T(8,128)(2,1)} %target_ref.7), custom_call_target="tpu_custom_call" | custom-call | flops 536870912 | bytes 2097152 | tf_op jit(solution)/shard_map/pallas_call | solution.py:379
  22.0 5.2 %collective-permute-start = (bf16[512,512]{1,0:T(8,128)(2,1)}, bf16[512,512]{1,0:T(8,128)(2,1)S(1)}, u32[]{:S(2)}, u32[]{:S(2)}) collective-permute-start(bf16[512,512]{1,0:T(8,128)(2,1)} %shard_map.157), channel_id=1, source_target_pairs={{0,1},{3,2},{4,5},{7,6},{8,9},{11,10},{12,13},{15,14},{16,17},{19,... | collective-permute-start | bytes 1572872 | tf_op jit(solution)/shard_map/ppermute | solution.py:405
  27.2 4.8 %shard_map.158 = bf16[512,512]{1,0:T(8,128)(2,1)} custom-call(s32[4]{0:T(128)} %pad_add_fusion.place_ref, bf16[8,256,1024]{2,1,0:T(8,128)(2,1)} %bitcast.21, bf16[512,1024]{1,0:T(8,128)(2,1)} %get-tuple-element.13.normed_ref.refs_4_.refs_2_, bf16[128,2048]{1,0:T(8,128)(2,1)} %target_ref.7), custom_call_target="tpu_custom_call" | custom-call | flops 536870912 | bytes 2097152 | tf_op jit(solution)/shard_map/pallas_call | solution.py:379
  33.3 6.5 %collective-permute-done = bf16[512,512]{1,0:T(8,128)(2,1)S(1)} collective-permute-done((bf16[512,512]{1,0:T(8,128)(2,1)}, bf16[512,512]{1,0:T(8,128)(2,1)S(1)}, u32[]{:S(2)}, u32[]{:S(2)}) %collective-permute-start) | collective-permute-done | bytes 524320 | tf_op jit(solution)/shard_map/ppermute | solution.py:405
  40.6 9.3 %collective-permute-done.3 = bf16[512,512]{1,0:T(8,128)(2,1)S(1)} collective-permute-done((bf16[512,512]{1,0:T(8,128)(2,1)}, bf16[512,512]{1,0:T(8,128)(2,1)S(1)}, u32[]{:S(2)}, u32[]{:S(2)}) %collective-permute-start.3) | collective-permute-done | bytes 524320 | tf_op jit(solution)/shard_map/ppermute | solution.py:405
  54.7 14.9 %collective-permute-done.2.refs_1_ = bf16[512,512]{1,0:T(8,128)(2,1)S(1)} collective-permute-done((bf16[512,512]{1,0:T(8,128)(2,1)S(1)}, bf16[512,512]{1,0:T(8,128)(2,1)S(1)}, u32[]{:S(2)}, u32[]{:S(2)}) %collective-permute-start.2) | collective-permute-done | bytes 524320 | tf_op jit(solution)/shard_map/ppermute | solution.py:412
  69.6 10.7 %collective-permute-done.5.refs_3_ = bf16[512,512]{1,0:T(8,128)(2,1)S(1)} collective-permute-done((bf16[512,512]{1,0:T(8,128)(2,1)S(1)}, bf16[512,512]{1,0:T(8,128)(2,1)S(1)}, u32[]{:S(2)}, u32[]{:S(2)}) %collective-permute-start.5) | collective-permute-done | bytes 524320 | tf_op jit(solution)/shard_map/ppermute | solution.py:412
  81.2 5.6 %shard_map.162 = bf16[8,128,1024]{2,1,0:T(8,128)(2,1)} custom-call(s32[4]{0:T(128)} %pad_add_fusion.place_ref, bf16[512,512]{1,0:T(8,128)(2,1)} %copy-done.1, bf16[512,512]{1,0:T(8,128)(2,1)} %copy-done.6, bf16[512,512]{1,0:T(8,128)(2,1)} %copy-done.2, bf16[512,512]{1,0:T(8,128)(2,1)} %copy-done.7, ...), custom_call_target="tpu_custom_call" | custom-call | flops 1073741824 | bytes 5242880 | tf_op jit(solution)/shard_map/pallas_call | solution.py:421
  86.9 4.8 %shard_map.160 = bf16[512,512]{1,0:T(8,128)(2,1)} custom-call(s32[4]{0:T(128)} %pad_add_fusion.place_ref, bf16[8,256,1024]{2,1,0:T(8,128)(2,1)} %bitcast.23, bf16[512,1024]{1,0:T(8,128)(2,1)} %get-tuple-element.13.normed_ref.refs_4_.refs_2_, bf16[128,2048]{1,0:T(8,128)(2,1)} %target_ref.7), custom_call_target="tpu_custom_call" | custom-call | flops 536870912 | bytes 2097152 | tf_op jit(solution)/shard_map/pallas_call | solution.py:379
  93.3 4.9 %shard_map.159 = bf16[512,512]{1,0:T(8,128)(2,1)} custom-call(s32[4]{0:T(128)} %pad_add_fusion.place_ref, bf16[8,256,1024]{2,1,0:T(8,128)(2,1)} %bitcast.24, bf16[512,1024]{1,0:T(8,128)(2,1)} %get-tuple-element.13.normed_ref.refs_4_.refs_2_, bf16[128,2048]{1,0:T(8,128)(2,1)} %target_ref.7), custom_call_target="tpu_custom_call" | custom-call | flops 536870912 | bytes 2097152 | tf_op jit(solution)/shard_map/pallas_call | solution.py:379
  99.6 6.4 %collective-permute-done.9 = bf16[512,512]{1,0:T(8,128)(2,1)S(1)} collective-permute-done((bf16[512,512]{1,0:T(8,128)(2,1)}, bf16[512,512]{1,0:T(8,128)(2,1)S(1)}, u32[]{:S(2)}, u32[]{:S(2)}) %collective-permute-start.9) | collective-permute-done | bytes 524320 | tf_op jit(solution)/shard_map/ppermute | solution.py:405
  106.8 7.5 %collective-permute-done.6 = bf16[512,512]{1,0:T(8,128)(2,1)S(1)} collective-permute-done((bf16[512,512]{1,0:T(8,128)(2,1)}, bf16[512,512]{1,0:T(8,128)(2,1)S(1)}, u32[]{:S(2)}, u32[]{:S(2)}) %collective-permute-start.6) | collective-permute-done | bytes 524320 | tf_op jit(solution)/shard_map/ppermute | solution.py:405
  117.0 10.7 %reduce-scatter.2.cloned.1.call-done = bf16[128,1024]{1,0:T(8,128)(2,1)} async-done(((bf16[1024,1024]{1,0:T(8,128)(2,1)}), bf16[128,1024]{1,0:T(8,128)(2,1)}) %reduce-scatter.2.cloned.1.call-update) | async-done | bytes 262160 | tf_op jit(solution)/shard_map/reduce_scatter | solution.py:445
  133.6 12.7 %collective-permute-done.11.refs_7_.refs_1_ = bf16[512,512]{1,0:T(8,128)(2,1)S(1)} collective-permute-done((bf16[512,512]{1,0:T(8,128)(2,1)S(1)}, bf16[512,512]{1,0:T(8,128)(2,1)S(1)}, u32[]{:S(2)}, u32[]{:S(2)}) %collective-permute-start.11) | collective-permute-done | bytes 524320 | tf_op jit(solution)/shard_map/ppermute | solution.py:412
  147.1 4.7 %shard_map.164 = (bf16[4,64,1024]{2,1,0:T(8,128)(2,1)}, bf16[4,64,1024]{2,1,0:T(8,128)(2,1)}) custom-call(s32[4]{0:T(128)} %pad_add_fusion.place_ref, bf16[512,512]{1,0:T(8,128)(2,1)} %copy-done.3, bf16[512,512]{1,0:T(8,128)(2,1)} %copy-done.8, bf16[512,1024]{1,0:T(8,128)(2,1)} %get-tuple-element.13.normed_ref.refs_4_.refs_2_, bf16[8,256,1024]{2,1,0:T(8,128)(2,1)} %bitcast.25), custom_call_target="tpu_custom_call" | custom-call | flops 536870912 | bytes 3145728 | tf_op jit(solution)/shard_map/pallas_call | solution.py:421
  151.9 4.5 %collective-permute-done.8.refs_5_.refs_1_ = bf16[512,512]{1,0:T(8,128)(2,1)S(1)} collective-permute-done((bf16[512,512]{1,0:T(8,128)(2,1)S(1)}, bf16[512,512]{1,0:T(8,128)(2,1)S(1)}, u32[]{:S(2)}, u32[]{:S(2)}) %collective-permute-start.8) | collective-permute-done | bytes 524320 | tf_op jit(solution)/shard_map/ppermute | solution.py:412
  157.2 4.6 %shard_map.163 = (bf16[4,64,1024]{2,1,0:T(8,128)(2,1)}, bf16[4,64,1024]{2,1,0:T(8,128)(2,1)}) custom-call(s32[4]{0:T(128)} %pad_add_fusion.place_ref, bf16[512,512]{1,0:T(8,128)(2,1)} %copy-done.4, bf16[512,512]{1,0:T(8,128)(2,1)} %copy-done.9, bf16[512,1024]{1,0:T(8,128)(2,1)} %get-tuple-element.13.normed_ref.refs_4_.refs_2_, bf16[8,256,1024]{2,1,0:T(8,128)(2,1)} %bitcast.26), custom_call_target="tpu_custom_call" | custom-call | flops 536870912 | bytes 3145728 | tf_op jit(solution)/shard_map/pallas_call | solution.py:421
  175.1 3.0 %collective-permute-done.15 = bf16[1,64,1024]{2,1,0:T(8,128)(2,1)} collective-permute-done((bf16[1,64,1024]{2,1,0:T(8,128)(2,1)}, bf16[1,64,1024]{2,1,0:T(8,128)(2,1)}, u32[]{:S(2)}, u32[]{:S(2)}) %collective-permute-start.15) | collective-permute-done | bytes 131104 | tf_op jit(solution)/shard_map/ppermute | solution.py:296
  191.9 3.3 %collective-permute-done.26 = bf16[1,64,1024]{2,1,0:T(8,128)(2,1)S(1)} collective-permute-done((bf16[1,64,1024]{2,1,0:T(8,128)(2,1)S(1)}, bf16[1,64,1024]{2,1,0:T(8,128)(2,1)S(1)}, u32[]{:S(2)}, u32[]{:S(2)}) %collective-permute-start.26) | collective-permute-done | bytes 131104 | tf_op jit(solution)/shard_map/ppermute | solution.py:308
  200.8 3.0 %collective-permute-done.22 = f32[8,128]{1,0:T(8,128)S(1)} collective-permute-done((f32[8,128]{1,0:T(8,128)S(1)}, f32[8,128]{1,0:T(8,128)S(1)}, u32[]{:S(2)}, u32[]{:S(2)}) %collective-permute-start.22) | collective-permute-done | bytes 4128 | tf_op jit(solution)/shard_map/ppermute | solution.py:469
  203.8 3.6 %collective-permute-done.23 = f32[8,128]{1,0:T(8,128)S(1)} collective-permute-done((f32[8,128]{1,0:T(8,128)S(1)}, f32[8,128]{1,0:T(8,128)S(1)}, u32[]{:S(2)}, u32[]{:S(2)}) %collective-permute-start.23) | collective-permute-done | bytes 4128 | tf_op jit(solution)/shard_map/ppermute | solution.py:469
  209.3 11.1 %shard_map.161 = bf16[512,1024]{1,0:T(8,128)(2,1)} custom-call(s32[4]{0:T(128)} %pad_add_fusion.place_ref, f32[16,512]{1,0:T(8,128)} %bitcast.30, bf16[512,1024]{1,0:T(8,128)(2,1)} %get-tuple-element.13.normed_ref.refs_4_.refs_2_, f32[2,512,1]{2,1,0:T(8,128)} %get-tuple-element.14.inv_ref, bf16[512,1024]{1,0:T(8,128)(2,1)} %z_ref.3, bf16[512,256]{1,0:T(8,128)(2,1)} %b_ref.3, ...), custom_call_target="tpu_custom_call" | custom-call | flops 1073741824 | bytes 4194304 | tf_op jit(solution)/shard_map/pallas_call | solution.py:453
  223.4 8.8 %shard_map.165 = bf16[2048,1024]{1,0:T(8,128)(2,1)} custom-call(s32[4]{0:T(128)} %pad_add_fusion.place_ref, f32[1]{0:T(128)} %bitcast.11.scale_ref, bf16[2048,1024]{1,0:T(8,128)(2,1)} %all-gather.3.cloned.1.call-done.kept_ref, bf16[1024,1024]{1,0:T(8,128)(2,1)} %all-gather.5.cloned.1.call-done.whole_ref, bf16[4,64,1024]{2,1,0:T(8,128)(2,1)} %pad_maximum_fusion.refs_0_, ...), custom_call_target="tpu_custom_call" | custom-call | flops 4194304 | bytes 12582912 | tf_op jit(solution)/shard_map/pallas_call | solution.py:477
  (119 shorter events, 59.9 us)
Async XLA Ops:
  7.2 79.7 %all-gather.3.cloned.1.call-start = ((), (), s32[]{:S(2)}) async-start(), calls=%async_computation.1 | async-start | bytes 4718592 | tf_op jit(solution)/shard_map/all_gather | solution.py:364
  9.8 117.9 %reduce-scatter.2.cloned.1.call-start = ((), (), s32[]{:S(2)}) async-start(), calls=%async_computation.2 | async-start | bytes 2359296 | tf_op jit(solution)/shard_map/reduce_scatter | solution.py:445
  22.0 17.8 %collective-permute-start = (bf16[512,512]{1,0:T(8,128)(2,1)}, bf16[512,512]{1,0:T(8,128)(2,1)S(1)}, u32[]{:S(2)}, u32[]{:S(2)}) collective-permute-start(bf16[512,512]{1,0:T(8,128)(2,1)} %shard_map.157), channel_id=1, source_target_pairs={{0,1},{3,2},{4,5},{7,6},{8,9},{11,10},{12,13},{15,14},{16,17},{19,... | collective-permute-start | bytes 1572872 | tf_op jit(solution)/shard_map/ppermute | solution.py:405
  31.9 17.9 %collective-permute-start.3 = (bf16[512,512]{1,0:T(8,128)(2,1)}, bf16[512,512]{1,0:T(8,128)(2,1)S(1)}, u32[]{:S(2)}, u32[]{:S(2)}) collective-permute-start(bf16[512,512]{1,0:T(8,128)(2,1)} %shard_map.158), channel_id=1, source_target_pairs={{0,1},{3,2},{4,5},{7,6},{8,9},{11,10},{12,13},{15,14},{16,17},{19,... | collective-permute-start | bytes 1572872 | tf_op jit(solution)/shard_map/ppermute | solution.py:405
  39.9 11.9 %collective-permute-start.1 = (bf16[512,512]{1,0:T(8,128)(2,1)S(1)}, bf16[512,512]{1,0:T(8,128)(2,1)S(1)}, u32[]{:S(2)}, u32[]{:S(2)}) collective-permute-start(bf16[512,512]{1,0:T(8,128)(2,1)S(1)} %add_convert_fusion.7), channel_id=1, source_target_pairs={{1,2},{2,1},{5,6},{6,5},{9,10},{10,9},{13,14},{14,13},{17,18},{18,... | collective-permute-start | bytes 1572872 | tf_op jit(solution)/shard_map/ppermute | solution.py:409
  51.9 17.7 %collective-permute-start.2 = (bf16[512,512]{1,0:T(8,128)(2,1)S(1)}, bf16[512,512]{1,0:T(8,128)(2,1)S(1)}, u32[]{:S(2)}, u32[]{:S(2)}) collective-permute-start(bf16[512,512]{1,0:T(8,128)(2,1)S(1)} %add_convert_fusion.6.refs_0_), channel_id=1, source_target_pairs={{1,0},{2,3},{5,4},{6,7},{9,8},{10,11},{13,12},{14,15},{17,16},{18,... | collective-permute-start | bytes 1572872 | tf_op jit(solution)/shard_map/ppermute | solution.py:412
  53.4 27.0 %collective-permute-start.5 = (bf16[512,512]{1,0:T(8,128)(2,1)S(1)}, bf16[512,512]{1,0:T(8,128)(2,1)S(1)}, u32[]{:S(2)}, u32[]{:S(2)}) collective-permute-start(bf16[512,512]{1,0:T(8,128)(2,1)S(1)} %add_convert_fusion.4.refs_2_), channel_id=1, source_target_pairs={{1,0},{2,3},{5,4},{6,7},{9,8},{10,11},{13,12},{14,15},{17,16},{18,... | collective-permute-start | bytes 1572872 | tf_op jit(solution)/shard_map/ppermute | solution.py:412
  86.9 136.5 %all-gather.5.cloned.1.call-start = ((), (), s32[]{:S(2)}) async-start(), calls=%async_computation.3 | async-start | bytes 2359296 | tf_op jit(solution)/shard_map/all_gather | solution.py:447
  91.7 14.3 %collective-permute-start.9 = (bf16[512,512]{1,0:T(8,128)(2,1)}, bf16[512,512]{1,0:T(8,128)(2,1)S(1)}, u32[]{:S(2)}, u32[]{:S(2)}) collective-permute-start(bf16[512,512]{1,0:T(8,128)(2,1)} %shard_map.160), channel_id=1, source_target_pairs={{0,1},{3,2},{4,5},{7,6},{8,9},{11,10},{12,13},{15,14},{16,17},{19,... | collective-permute-start | bytes 1572872 | tf_op jit(solution)/shard_map/ppermute | solution.py:405
  98.2 16.1 %collective-permute-start.6 = (bf16[512,512]{1,0:T(8,128)(2,1)}, bf16[512,512]{1,0:T(8,128)(2,1)S(1)}, u32[]{:S(2)}, u32[]{:S(2)}) collective-permute-start(bf16[512,512]{1,0:T(8,128)(2,1)} %shard_map.159), channel_id=1, source_target_pairs={{0,1},{3,2},{4,5},{7,6},{8,9},{11,10},{12,13},{15,14},{16,17},{19,... | collective-permute-start | bytes 1572872 | tf_op jit(solution)/shard_map/ppermute | solution.py:405
  106.1 23.3 %collective-permute-start.10 = (bf16[512,512]{1,0:T(8,128)(2,1)S(1)}, bf16[512,512]{1,0:T(8,128)(2,1)S(1)}, u32[]{:S(2)}, u32[]{:S(2)}) collective-permute-start(bf16[512,512]{1,0:T(8,128)(2,1)S(1)} %add_convert_fusion.1), channel_id=1, source_target_pairs={{1,2},{2,1},{5,6},{6,5},{9,10},{10,9},{13,14},{14,13},{17,18},{18,... | collective-permute-start | bytes 1572872 | tf_op jit(solution)/shard_map/ppermute | solution.py:409
  115.5 15.4 %collective-permute-start.7 = (bf16[512,512]{1,0:T(8,128)(2,1)S(1)}, bf16[512,512]{1,0:T(8,128)(2,1)}, u32[]{:S(2)}, u32[]{:S(2)}) collective-permute-start(bf16[512,512]{1,0:T(8,128)(2,1)S(1)} %add_convert_fusion.3), channel_id=1, source_target_pairs={{1,2},{2,1},{5,6},{6,5},{9,10},{10,9},{13,14},{14,13},{17,18},{18,... | collective-permute-start | bytes 1572872 | tf_op jit(solution)/shard_map/ppermute | solution.py:409
  129.6 16.7 %collective-permute-start.11 = (bf16[512,512]{1,0:T(8,128)(2,1)S(1)}, bf16[512,512]{1,0:T(8,128)(2,1)S(1)}, u32[]{:S(2)}, u32[]{:S(2)}) collective-permute-start(bf16[512,512]{1,0:T(8,128)(2,1)S(1)} %add_convert_fusion.refs_6_.refs_0_), channel_id=1, source_target_pairs={{1,0},{2,3},{5,4},{6,7},{9,8},{10,11},{13,12},{14,15},{17,16},{18,... | collective-permute-start | bytes 1572872 | tf_op jit(solution)/shard_map/ppermute | solution.py:412
  132.1 24.3 %collective-permute-start.8 = (bf16[512,512]{1,0:T(8,128)(2,1)S(1)}, bf16[512,512]{1,0:T(8,128)(2,1)S(1)}, u32[]{:S(2)}, u32[]{:S(2)}) collective-permute-start(bf16[512,512]{1,0:T(8,128)(2,1)S(1)} %add_convert_fusion.2.refs_4_.refs_0_), channel_id=1, source_target_pairs={{1,0},{2,3},{5,4},{6,7},{9,8},{10,11},{13,12},{14,15},{17,16},{18,... | collective-permute-start | bytes 1572872 | tf_op jit(solution)/shard_map/ppermute | solution.py:412
  151.8 10.0 %collective-permute-start.16 = (bf16[4,64,1024]{2,1,0:T(8,128)(2,1)}, bf16[4,64,1024]{2,1,0:T(8,128)(2,1)S(1)}, u32[]{:S(2)}, u32[]{:S(2)}) collective-permute-start(bf16[4,64,1024]{2,1,0:T(8,128)(2,1)} %get-tuple-element.21), channel_id=1, source_target_pairs={{0,4},{4,0},{8,12},{12,8},{16,20},{20,16},{24,28},{28,24},{1,5},{5... | collective-permute-start | bytes 1572872 | tf_op jit(solution)/shard_map/ppermute | solution.py:283
  164.2 8.6 %collective-permute-start.19 = (bf16[1,64,1024]{2,1,0:T(8,128)(2,1)}, bf16[1,64,1024]{2,1,0:T(8,128)(2,1)S(1)}, u32[]{:S(2)}, u32[]{:S(2)}) collective-permute-start(bf16[1,64,1024]{2,1,0:T(8,128)(2,1)} %get-tuple-element.33), channel_id=1, source_target_pairs={{0,24},{4,28},{8,16},{12,20},{16,8},{20,12},{24,0},{28,4},{1,25},{... | collective-permute-start | bytes 393224 | tf_op jit(solution)/shard_map/ppermute | solution.py:296
  165.6 9.5 %collective-permute-start.18 = (bf16[1,64,1024]{2,1,0:T(8,128)(2,1)}, bf16[1,64,1024]{2,1,0:T(8,128)(2,1)S(1)}, u32[]{:S(2)}, u32[]{:S(2)}) collective-permute-start(bf16[1,64,1024]{2,1,0:T(8,128)(2,1)} %get-tuple-element.34), channel_id=1, source_target_pairs={{0,16},{4,20},{8,24},{12,28},{16,0},{20,4},{24,8},{28,12},{1,17},{... | collective-permute-start | bytes 393224 | tf_op jit(solution)/shard_map/ppermute | solution.py:296
  181.1 16.0 %collective-permute-start.31 = (bf16[1,64,1024]{2,1,0:T(8,128)(2,1)S(1)}, bf16[1,64,1024]{2,1,0:T(8,128)(2,1)S(1)}, u32[]{:S(2)}, u32[]{:S(2)}) collective-permute-start(bf16[1,64,1024]{2,1,0:T(8,128)(2,1)S(1)} %get-tuple-element.24), channel_id=1, source_target_pairs={{0,24},{4,28},{8,16},{12,20},{16,8},{20,12},{24,0},{28,4},{1,25},{... | collective-permute-start | bytes 393224 | tf_op jit(solution)/shard_map/ppermute | solution.py:308
  182.7 14.5 %collective-permute-start.30 = (bf16[1,64,1024]{2,1,0:T(8,128)(2,1)S(1)}, bf16[1,64,1024]{2,1,0:T(8,128)(2,1)S(1)}, u32[]{:S(2)}, u32[]{:S(2)}) collective-permute-start(bf16[1,64,1024]{2,1,0:T(8,128)(2,1)S(1)} %get-tuple-element.24), channel_id=1, source_target_pairs={{0,16},{4,20},{8,24},{12,28},{16,0},{20,4},{24,8},{28,12},{1,17},{... | collective-permute-start | bytes 393224 | tf_op jit(solution)/shard_map/ppermute | solution.py:308
  184.7 10.4 %collective-permute-start.26 = (bf16[1,64,1024]{2,1,0:T(8,128)(2,1)S(1)}, bf16[1,64,1024]{2,1,0:T(8,128)(2,1)S(1)}, u32[]{:S(2)}, u32[]{:S(2)}) collective-permute-start(bf16[1,64,1024]{2,1,0:T(8,128)(2,1)S(1)} %get-tuple-element.30), channel_id=1, source_target_pairs={{0,16},{4,20},{8,24},{12,28},{16,0},{20,4},{24,8},{28,12},{1,17},{... | collective-permute-start | bytes 393224 | tf_op jit(solution)/shard_map/ppermute | solution.py:308
  186.2 9.0 %collective-permute-start.25 = (bf16[1,64,1024]{2,1,0:T(8,128)(2,1)S(1)}, bf16[1,64,1024]{2,1,0:T(8,128)(2,1)S(1)}, u32[]{:S(2)}, u32[]{:S(2)}) collective-permute-start(bf16[1,64,1024]{2,1,0:T(8,128)(2,1)S(1)} %get-tuple-element.30), channel_id=1, source_target_pairs={{0,8},{4,12},{8,0},{12,4},{16,24},{20,28},{24,16},{28,20},{1,9},{5... | collective-permute-start | bytes 393224 | tf_op jit(solution)/shard_map/ppermute | solution.py:308
  196.0 27.3 %collective-permute-start.28 = (bf16[4,64,1024]{2,1,0:T(8,128)(2,1)}, bf16[4,64,1024]{2,1,0:T(8,128)(2,1)}, u32[]{:S(2)}, u32[]{:S(2)}) collective-permute-start(bf16[4,64,1024]{2,1,0:T(8,128)(2,1)} %pad_maximum_fusion.refs_0_), channel_id=1, source_target_pairs={{0,4},{4,0},{8,12},{12,8},{16,20},{20,16},{24,28},{28,24},{1,5},{5... | collective-permute-start | bytes 1572872 | tf_op jit(solution)/shard_map/ppermute | solution.py:311
  198.0 25.4 %collective-permute-start.32 = (bf16[4,64,1024]{2,1,0:T(8,128)(2,1)}, bf16[4,64,1024]{2,1,0:T(8,128)(2,1)}, u32[]{:S(2)}, u32[]{:S(2)}) collective-permute-start(bf16[4,64,1024]{2,1,0:T(8,128)(2,1)} %pad_maximum_fusion.1.refs_2_), channel_id=1, source_target_pairs={{0,4},{4,0},{8,12},{12,8},{16,20},{20,16},{24,28},{28,24},{1,5},{5... | collective-permute-start | bytes 1572872 | tf_op jit(solution)/shard_map/ppermute | solution.py:311
  207.4 13.0 %collective-permute-start.24 = (f32[8,128]{1,0:T(8,128)S(1)}, f32[8,128]{1,0:T(8,128)S(1)}, u32[]{:S(2)}, u32[]{:S(2)}) collective-permute-start(f32[8,128]{1,0:T(8,128)S(1)} %add.183), channel_id=1, source_target_pairs={{0,2},{1,3},{2,0},{3,1},{4,6},{5,7},{6,4},{7,5},{8,10},{9,11},{10,... | collective-permute-start | bytes 12296 | tf_op jit(solution)/shard_map/ppermute | solution.py:469
  (28 other events, 285.4 us)
Sparse Core Ops, SparseCore 0:
  9.9 39.4 all-gather.2
  87.0 40.6 reduce-scatter.1
  129.7 27.8 all-gather.4

commit v4 on v3

--- a/solution.py
+++ b/solution.py
@@ -147,37 +147,44 @@
         inv_ref[0, rows, :] = inv
 
 
-def project_kernel(chunk, place_ref, weight_ref, normed_ref, target_ref, part_ref):
-    owners, piece, inner = weight_ref.shape
-    held, lanes = target_ref.shape
-    owned = lanes // owners
-    part = dot(weight_ref[...].reshape(owners * piece, inner), normed_ref[...], NT)
-    goal = jnp.concatenate(
-        [target_ref[:, o * owned + chunk * piece : o * owned + (chunk + 1) * piece] for o in range(owners)], axis=1
-    )
+def project_kernel(chunks, place_ref, weight_ref, normed_ref, target_ref, *part_refs):
+    replicas, owned, inner = weight_ref.shape
+    held, features = target_ref.shape
+    piece = part_refs[0].shape[0] // replicas
+    tokens = normed_ref.shape[0]
     eye = (iota((held, held), 0) == iota((held, held), 1)).astype(BF16)
-    turned = dot(goal, eye, TN)
-    tiled = jnp.concatenate([turned] * (part.shape[1] // held), axis=1)
-    part = part - jnp.where(iota(part.shape, 1) // held == place_ref[0], tiled, 0.0)
-    part_ref[...] = part.astype(BF16)
-
-
-def gradient_kernel(count, split, place_ref, *refs):
-    cot_refs, (normed_ref, weight_ref), outs = refs[: 2 * count], refs[2 * count : 2 * count + 2], refs[2 * count + 2 :]
+    turned = dot(target_ref[...], eye, TN).reshape(replicas, owned, held)
+    here = iota((replicas * piece, tokens), 1) // held == place_ref[0]
+    for n, part_ref in zip(chunks, part_refs):
+        at = slice(n * piece, (n + 1) * piece)
+        part = dot(weight_ref[:, at, :].reshape(replicas * piece, inner), normed_ref[...], NT)
+        goal = jnp.concatenate([turned[:, at, :].reshape(replicas * piece, held)] * (tokens // held), axis=1)
+        part_ref[...] = (part - jnp.where(here, goal, 0.0)).astype(BF16)
+
+
+def add_kernel(a_ref, b_ref, sum_ref):
+    sum_ref[...] = (a_ref[...].astype(F32) + b_ref[...].astype(F32)).astype(BF16)
+
+
+def gradient_kernel(batch, place_ref, *refs):
+    count = len(batch)
+    cot_refs, (normed_ref, weight_ref, keep_ref, send_ref) = refs[: 2 * count], refs[2 * count :]
     middle = place_ref[1] == 1
-    owners, rows, inner = weight_ref.shape
-    piece = rows // count
-    for n in range(count):
+    odd = place_ref[2] == 1
+    replicas, _, inner = weight_ref.shape
+    piece = keep_ref.shape[1] // count
+    tile = min(inner, 512)
+    for n, chunk in enumerate(batch):
         cot = jnp.where(middle, cot_refs[2 * n][...], cot_refs[2 * n + 1][...])
-        weight = weight_ref[:, n * piece : (n + 1) * piece, :].reshape(owners * piece, inner).astype(F32)
-        new = (weight - inner_rate * dot(cot, normed_ref[...], NN)).astype(BF16).reshape(owners, piece, inner)
+        rows = slice(chunk * piece, (chunk + 1) * piece)
         at = slice(n * piece, (n + 1) * piece)
-        if split:
-            odd = place_ref[2] == 1
-            outs[0][0, at, :] = jnp.where(odd, new[1], new[0])
-            outs[1][0, at, :] = jnp.where(odd, new[0], new[1])
-        else:
-            outs[0][:, at, :] = new
+        for lo in range(0, inner, tile):
+            cols = slice(lo, lo + tile)
+            weight = weight_ref[:, rows, cols].reshape(replicas * piece, tile).astype(F32)
+            new = weight - inner_rate * dot(cot, normed_ref[:, cols], NN)
+            new = new.astype(BF16).reshape(replicas // 2, 2, piece, tile)
+            keep_ref[:, at, cols] = jnp.where(odd, new[:, 1], new[:, 0])
+            send_ref[:, at, cols] = jnp.where(odd, new[:, 0], new[:, 1])
 
 
 def backward_kernel(
@@ -261,10 +268,6 @@
     return hops, [(half - 1, half), (half, half - 1)]
 
 
-def add16(a, b):
-    return (a.astype(F32) + b.astype(F32)).astype(BF16)
-
-
 def after(value, *others):
     return lax.optimization_barrier((value, *others))[0]
 
@@ -347,15 +350,15 @@
     dt_rows = dt_raw.T
 
     smem = pl.BlockSpec(memory_space=pltpu.SMEM)
+    vmem = pl.BlockSpec(memory_space=pltpu.VMEM)
     by_group = pl.BlockSpec((tokens, width), lambda g: (0, g))
     by_state = pl.BlockSpec((tokens, STATE), lambda g: (0, g))
     inv_spec = pl.BlockSpec((1, tokens, 1), lambda g: (g, 0, 0))
     dt_spec = pl.BlockSpec((heads // groups, tokens), lambda g: (g, 0))
     gain_spec = pl.BlockSpec((1, width), lambda g: (0, g))
     weight_spec = pl.BlockSpec((replicas, owned, width), lambda g: (0, 0, g))
-    normed_spec = pl.BlockSpec((tokens, inner), lambda i: (0, 0))
-    by_chip = pl.BlockSpec((2 * piece, tokens), lambda i: (i, 0))
-    params = pltpu.CompilerParams(vmem_limit_bytes=56 * 1024 * 1024)
+    params = pltpu.CompilerParams(vmem_limit_bytes=28 * 1024 * 1024)
+    small = pltpu.CompilerParams(vmem_limit_bytes=16 * 1024 * 1024)
     cost = pl.CostEstimate(
         flops=2 * tokens * inner * 4 * SPAN, bytes_accessed=8 * inner * tokens, transcendentals=tokens * SPAN * heads
     )
@@ -373,94 +376,103 @@
         compiler_params=params,
     )(dt_rows, x_in, gate_z, b_proj, c_proj, gain, a_log, dt_bias, skip_d)
 
-    owners = min(replicas, max(2, LANES // owned))
-
-    def project(n):
+    def project(picked):
         return pl.pallas_call(
-            functools.partial(project_kernel, n),
-            grid=(replicas // owners,),
-            in_specs=[
-                smem,
-                pl.BlockSpec((owners, piece, inner), lambda i: (i, n, 0)),
-                normed_spec,
-                pl.BlockSpec((target.shape[0], owners * owned), lambda i: (0, i)),
-            ],
-            out_specs=pl.BlockSpec((owners * piece, tokens), lambda i: (i, 0)),
-            out_shape=jax.ShapeDtypeStruct((span_rows, tokens), BF16),
+            functools.partial(project_kernel, picked),
+            in_specs=[smem, vmem, vmem, vmem],
+            out_specs=[vmem] * len(picked),
+            out_shape=[jax.ShapeDtypeStruct((span_rows, tokens), BF16)] * len(picked),
             cost_estimate=pl.CostEstimate(
-                flops=2 * tokens * span_rows * inner, bytes_accessed=2 * (tokens + span_rows) * inner, transcendentals=0
+                flops=2 * tokens * span_rows * inner * len(picked), bytes_accessed=2 * tokens * inner, transcendentals=0
             ),
-            compiler_params=params,
+            compiler_params=small,
         )(places, weight, normed, target)
 
+    def add(a, b):
+        return pl.pallas_call(
+            add_kernel,
+            in_specs=[vmem, vmem],
+            out_specs=vmem,
+            out_shape=jax.ShapeDtypeStruct(a.shape, BF16),
+            cost_estimate=pl.CostEstimate(flops=a.size, bytes_accessed=2 * a.size, transcendentals=0),
+            compiler_params=small,
+        )(a, b)
+
+    def updated(batch):
+        shape = jax.ShapeDtypeStruct((replicas // 2, len(batch) * piece, inner), BF16)
+        return pl.pallas_call(
+            functools.partial(gradient_kernel, batch),
+            in_specs=[smem] + [vmem] * (2 * len(batch) + 2),
+            out_specs=[vmem] * 2,
+            out_shape=[shape] * 2,
+            cost_estimate=pl.CostEstimate(
+                flops=2 * tokens * len(batch) * span_rows * inner, bytes_accessed=2 * tokens * inner, transcendentals=0
+            ),
+            compiler_params=small,
+        )(places, *[c for n in batch for c in cots[n]], normed, weight)
+
     in_hops, across = inward(heads_over)
-    first_landed = []
-    cots = []
-
-    def sum_over_heads(n):
-        held = project(n)
-        if n >= DEPTH:
-            held = after(held, first_landed[n - DEPTH])
+    parts = list(project([0]))
+    parts += project(list(range(1, chunks)))
+    landed_first, sums, cots = {}, {}, {}
+    last = parts[-1]
+
+    def hop_in(n):
+        held = parts[n] if n < DEPTH or not in_hops else after(parts[n], landed_first[n - DEPTH])
+        landed_first[n] = lax.ppermute(held, "tensor", in_hops[0]) if in_hops else held
+
+    def sum_side(n):
+        held = parts[n]
         for at, pairs in enumerate(in_hops):
-            landed = lax.ppermute(held, "tensor", pairs)
-            if at == 0:
-                first_landed.append(landed)
-            held = add16(held, landed)
-        mid = add16(held, lax.ppermute(held, "tensor", across))
+            landed = landed_first[n] if at == 0 else lax.ppermute(held, "tensor", pairs)
+            held = add(after(held, last), landed)
+        return held
+
+    def sum_all(n):
+        mid = add(after(sums[n], last), lax.ppermute(sums[n], "tensor", across))
         out = mid
         for pairs in reversed(in_hops):
             back = lax.ppermute(out, "tensor", [(b, a) for a, b in pairs])
             out = back if pairs is in_hops[0] else jnp.where(in_middle, mid, back)
-        return [mid, out]
-
-    def updated(batch, split):
-        rows = len(batch) * piece
-        shape = (replicas // 2 if split else replicas, rows, inner)
-        out_spec = pl.BlockSpec((1 if split else 2, rows, inner), lambda i: (i, 0, 0))
-        count = 2 if split else 1
-        return pl.pallas_call(
-            functools.partial(gradient_kernel, len(batch), split),
-            grid=(replicas // 2,),
-            in_specs=[smem]
-            + [by_chip] * (2 * len(batch))
-            + [normed_spec, pl.BlockSpec((2, rows, inner), lambda i: (i, batch[0] // len(batch), 0))],
-            out_specs=[out_spec] * count,
-            out_shape=[jax.ShapeDtypeStruct(shape, BF16)] * count,
-            cost_estimate=pl.CostEstimate(
-                flops=2 * tokens * replicas * rows * inner,
-                bytes_accessed=2 * (tokens + 2 * replicas * rows) * inner,
-                transcendentals=0,
-            ),
-            compiler_params=params,
-        )(places, *[c for n in batch for c in cots[n]], normed, weight)
+        return mid, out
 
     deltas, gathered = [], []
-    for batch in batches:
-        for n in batch:
-            cots.append(sum_over_heads(n))
-        here = global_weight[batch[0] * piece : (batch[-1] + 1) * piece]
-        if batch is batches[0]:
-            (new,) = updated(batch, False)
-            new = after(new, kept_all)
-            summed = lax.psum_scatter(new.reshape(-1, inner), "replica", scatter_dimension=0, tiled=True).astype(F32)
-            deltas.append(here - summed / replicas)
-            gathered.append(lax.all_gather(deltas[-1].astype(BF16), "replica", axis=0, tiled=True))
-        else:
-            summed = reduce_rows(*updated(batch, True), replicas, me)
-            deltas.append(here - summed / replicas)
-            gathered += gather_rows(deltas[-1].astype(BF16), replicas)
+    pending = list(batches)
+    for n in range(chunks):
+        hop_in(n)
+    for t in range(chunks + 2):
+        if t < chunks:
+            last = sums[t] = sum_side(t)
+        if 1 <= t <= chunks:
+            cots[t - 1] = sum_all(t - 1)
+            last = cots[t - 1][0]
+        if pending and t - 2 == pending[0][-1]:
+            batch = pending.pop(0)
+            if batch[0] == 0:
+                last = after(last, kept_all)
+            elif len(deltas) > 0:
+                last = after(last, deltas[0])
+            cots[batch[0]] = (after(cots[batch[0]][0], last), cots[batch[0]][1])
+            keep, send = updated(batch)
+            last = keep
+            here = global_weight[batch[0] * piece : (batch[-1] + 1) * piece]
+            deltas.append(here - reduce_rows(keep, send, replicas, me) / replicas)
+            if batch[0] == 0:
+                gathered.append(lax.all_gather(deltas[-1].astype(BF16), "replica", axis=0, tiled=True))
+            else:
+                gathered += gather_rows(deltas[-1].astype(BF16), replicas)
 
     (grad_input,) = pl.pallas_call(
         backward_kernel,
         grid=(groups,),
         in_specs=[smem, dt_spec, by_group, inv_spec, by_group, by_state, by_state, gain_spec, smem, smem, smem, weight_spec]
-        + [pl.BlockSpec((span_rows, tokens), lambda g: (0, 0))] * (2 * chunks),
+        + [vmem] * (2 * chunks),
         out_specs=[by_group],
         out_shape=[jax.ShapeDtypeStruct((tokens, inner), BF16)],
         scratch_shapes=[pltpu.VMEM((tokens, width), F32)],
         cost_estimate=cost,
         compiler_params=params,
-    )(places, dt_rows, normed, inv, gate_z, b_proj, c_proj, gain, a_log, dt_bias, skip_d, weight, *[c for p in cots for c in p])
+    )(places, dt_rows, normed, inv, gate_z, b_proj, c_proj, gain, a_log, dt_bias, skip_d, weight, after(cots[0][0], deltas[-1]), *[c for n in range(chunks) for c in cots[n]][1:])
 
     square_sum = functools.reduce(jnp.add, [jnp.sum(d * d) for d in deltas])
     spread = jnp.full((8, LANES), square_sum, F32)

time: 240 us -> 246 us (1.025)
  Pallas kernels: 60.9 us -> 32 us
  local copies, waits for them, and re-layouts: 3.04 us -> 26.5 us
  starting transfers between devices: 35.5 us -> 44.8 us
  waiting for transfers between devices: 104 us -> 109 us
  other arithmetic: 18.3 us -> 15.3 us
    pallas_call x7 -> x13, Pallas kernels: 34.1 us -> 10.4 us  [the longest x3 5.55 us: updated(): pl.pallas_call(functools.partial(gradient_kernel, batch), in_specs=[smem]...]
    unnamed x32 -> x82, local copies, waits for them, and re-layouts: 2.52 us -> 26 us
    ppermute x6 -> x9, waiting for transfers between devices: 7.94 us -> 20.7 us  [reduce_rows(): lax.ppermute(total(mask), 'replica', [(r, r ^ mask << bit) for r in range...]
    reduce_scatter x1 -> x0, waiting for transfers between devices: 10.7 us -> none  [shards(): lax.psum_scatter(new.reshape(-1, inner), 'replica', scatter_dimension=0,...]
    ppermute x12, waiting for transfers between devices: 72.6 us -> 64.5 us  [the longest x4 45.5 us: sum_all(): back = lax.ppermute(out, 'tensor', [(b, a) for a, b in pairs])]
    convert_element_type x9 -> x0, other arithmetic: 6.72 us -> none  [the longest x8 4.2 us: add16(): return (a.astype(F32) + b.astype(F32)).astype(BF16)]
    ppermute x12, starting transfers between devices: 18.3 us -> 23.6 us  [the longest x4 15.3 us: hop_in(): lax.ppermute(held, 'tensor', in_hops[0])]
    ppermute x5, waiting for transfers between devices: 8.77 us -> 13.4 us  [shards(): lax.ppermute(spread, axis, [(r, r ^ 1 << bit) for r in range(size)])]
  transfers between devices with their start and end apart: 36 -> 39, of which waited for: 18 -> 27; matrix products, arithmetic and copies ran while one was open for 7% -> 5% of each run, Pallas kernels for 22% -> 6%
where the time goes in v4:
time: 246 us; the launch traced here: 245 us
  waiting for transfers between devices  109 us (44%)
  starting transfers between devices  44.8 us (18%)
  Pallas kernels  32 us (13%)
  local copies, waits for them, and re-layouts  26.5 us (11%)
  between operations  17.2 us (7%)
  other arithmetic  15.3 us (6%)
    ppermute x4, waiting for transfers between devices, sum_all(): back = lax.ppermute(out, 'tensor', [(b, a) for a, b in pairs])  45.5 us
    unnamed x82, local copies, waits for them, and re-layouts  26 us
    ppermute x9, waiting for transfers between devices, reduce_rows(): lax.ppermute(total(mask), 'replica', [(r, r ^ mask << bit) for r in range...  20.7 us
    ppermute x4, waiting for transfers between devices, hop_in(): lax.ppermute(held, 'tensor', in_hops[0])  19.1 us
    ppermute x4, starting transfers between devices, hop_in(): lax.ppermute(held, 'tensor', in_hops[0])  15.3 us
    ppermute x5, waiting for transfers between devices, shards(): lax.ppermute(spread, axis, [(r, r ^ 1 << bit) for r in range(size)])  13.4 us
    ppermute x9, starting transfers between devices, reduce_rows(): lax.ppermute(total(mask), 'replica', [(r, r ^ mask << bit) for r in range...  9.96 us
    pallas_call x1, Pallas kernels, shards(): pl.pallas_call(backward_kernel, grid=(groups,), in_specs=[smem, dt_spec,...  8.26 us
  transfers between devices with their start and end apart: 39, of which 27 were waited for; matrix products, arithmetic and copies ran while one was open for 5% of the time, Pallas kernels for 6%

profile of v4, /device:TPU:0, one launch (start us, length us, event | category | flops | bytes accessed | tf_op | source)
XLA Modules:
  0.0 245.1 jit_solution(3617420243078779018)
XLA Ops:
  15.1 5.4 %shard_map.156 = (bf16[512,1024]{1,0:T(8,128)(2,1)S(1)}, f32[2,512,1]{2,1,0:T(8,128)S(1)}) custom-call(f32[16,512]{1,0:T(8,128)S(1)} %bitcast.28, bf16[512,1024]{1,0:T(8,128)(2,1)S(1)} %copy-done.36, bf16[512,1024]{1,0:T(8,128)(2,1)S(1)} %copy-done.14, bf16[512,256]{1,0:T(8,128)(2,1)S(1)} %copy-done.22, bf16[512,256]{1,0:T(8,128)(2,1)S(1)} %copy-done.24, ...), custom_call_target="tpu_custom_call" | custom-call | flops 1073741824 | bytes 4194304 | tf_op jit(solution)/shard_map/pallas_call | solution.py:369
  24.3 5.0 %collective-permute-start = (bf16[512,512]{1,0:T(8,128)(2,1)S(1)}, bf16[512,512]{1,0:T(8,128)(2,1)S(1)}, u32[]{:S(2)}, u32[]{:S(2)}) collective-permute-start(bf16[512,512]{1,0:T(8,128)(2,1)S(1)} %shard_map.157.a_ref), channel_id=1, source_target_pairs={{0,1},{3,2},{4,5},{7,6},{8,9},{11,10},{12,13},{15,14},{16,17},{19,... | collective-permute-start | bytes 1572872 | tf_op jit(solution)/shard_map/ppermute | solution.py:422
  29.3 2.5 %shard_map.158 = (bf16[512,512]{1,0:T(8,128)(2,1)S(1)}, bf16[512,512]{1,0:T(8,128)(2,1)S(1)}, bf16[512,512]{1,0:T(8,128)(2,1)S(1)}) custom-call(s32[4]{0:T(128)S(1)} %pad_add_fusion.place_ref, bf16[8,256,1024]{2,1,0:T(8,128)(2,1)S(1)} %bitcast.23, bf16[512,1024]{1,0:T(8,128)(2,1)S(1)} %get-tuple-element.26.normed_ref.refs_4_.refs_2_, ...), custom_call_target="tpu_custom_call" | custom-call | flops 1610612736 | bytes 1048576 | tf_op jit(solution)/shard_map/pallas_call | solution.py:380
  33.5 8.0 %collective-permute-done.b_ref = bf16[512,512]{1,0:T(8,128)(2,1)S(1)} collective-permute-done((bf16[512,512]{1,0:T(8,128)(2,1)S(1)}, bf16[512,512]{1,0:T(8,128)(2,1)S(1)}, u32[]{:S(2)}, u32[]{:S(2)}) %collective-permute-start) | collective-permute-done | bytes 524320 | tf_op jit(solution)/shard_map/ppermute | solution.py:422
  42.4 7.2 %collective-permute-start.3 = (bf16[512,512]{1,0:T(8,128)(2,1)S(1)}, bf16[512,512]{1,0:T(8,128)(2,1)S(1)}, u32[]{:S(2)}, u32[]{:S(2)}) collective-permute-start(bf16[512,512]{1,0:T(8,128)(2,1)S(1)} %get-tuple-element.35.a_ref), channel_id=1, source_target_pairs={{0,1},{3,2},{4,5},{7,6},{8,9},{11,10},{12,13},{15,14},{16,17},{19,... | collective-permute-start | bytes 1572872 | tf_op jit(solution)/shard_map/ppermute | solution.py:422
  49.6 3.2 %collective-permute-done.1.b_ref = bf16[512,512]{1,0:T(8,128)(2,1)S(1)} collective-permute-done((bf16[512,512]{1,0:T(8,128)(2,1)S(1)}, bf16[512,512]{1,0:T(8,128)(2,1)S(1)}, u32[]{:S(2)}, u32[]{:S(2)}) %collective-permute-start.1) | collective-permute-done | bytes 524320 | tf_op jit(solution)/shard_map/ppermute | solution.py:422
  55.1 7.8 %collective-permute-done.3.b_ref = bf16[512,512]{1,0:T(8,128)(2,1)S(1)} collective-permute-done((bf16[512,512]{1,0:T(8,128)(2,1)S(1)}, bf16[512,512]{1,0:T(8,128)(2,1)S(1)}, u32[]{:S(2)}, u32[]{:S(2)}) %collective-permute-start.3) | collective-permute-done | bytes 524320 | tf_op jit(solution)/shard_map/ppermute | solution.py:422
  64.4 7.3 %collective-permute-done.6.refs_1_ = bf16[512,512]{1,0:T(8,128)(2,1)S(1)} collective-permute-done((bf16[512,512]{1,0:T(8,128)(2,1)S(1)}, bf16[512,512]{1,0:T(8,128)(2,1)S(1)}, u32[]{:S(2)}, u32[]{:S(2)}) %collective-permute-start.6) | collective-permute-done | bytes 524320 | tf_op jit(solution)/shard_map/ppermute | solution.py:435
  71.7 9.4 %collective-permute-done.7.refs_3_ = bf16[512,512]{1,0:T(8,128)(2,1)S(1)} collective-permute-done((bf16[512,512]{1,0:T(8,128)(2,1)S(1)}, bf16[512,512]{1,0:T(8,128)(2,1)S(1)}, u32[]{:S(2)}, u32[]{:S(2)}) %collective-permute-start.7) | collective-permute-done | bytes 524320 | tf_op jit(solution)/shard_map/ppermute | solution.py:435
  81.1 2.9 %shard_map.165 = (bf16[4,128,1024]{2,1,0:T(8,128)(2,1)S(1)}, bf16[4,128,1024]{2,1,0:T(8,128)(2,1)}) custom-call(s32[4]{0:T(128)S(1)} %pad_add_fusion.place_ref, bf16[512,512]{1,0:T(8,128)(2,1)S(1)} %shard_map.161.refs_0_, bf16[512,512]{1,0:T(8,128)(2,1)S(1)} %collective-permute-done.6.refs_1_, bf16[512,512]{1,0:T(8,128)(2,1)S(1)} %shard_map.163.refs_2_, ...), custom_call_target="tpu_custom_call" | custom-call | flops 1073741824 | bytes 1048576 | tf_op jit(solution)/shard_map/pallas_call | solution.py:403
  85.0 3.0 %collective-permute-done.16 = bf16[4,128,1024]{2,1,0:T(8,128)(2,1)} collective-permute-done((bf16[4,128,1024]{2,1,0:T(8,128)(2,1)}, bf16[4,128,1024]{2,1,0:T(8,128)(2,1)}, u32[]{:S(2)}, u32[]{:S(2)}) %collective-permute-start.16) | collective-permute-done | bytes 1048608 | tf_op jit(solution)/shard_map/ppermute | solution.py:286
  95.5 4.5 %collective-permute-done.17 = bf16[1,128,1024]{2,1,0:T(8,128)(2,1)} collective-permute-done((bf16[1,128,1024]{2,1,0:T(8,128)(2,1)}, bf16[1,128,1024]{2,1,0:T(8,128)(2,1)}, u32[]{:S(2)}, u32[]{:S(2)}) %collective-permute-start.17) | collective-permute-done | bytes 262176 | tf_op jit(solution)/shard_map/ppermute | solution.py:299
  100.0 5.9 %collective-permute-done.19 = bf16[1,128,1024]{2,1,0:T(8,128)(2,1)} collective-permute-done((bf16[1,128,1024]{2,1,0:T(8,128)(2,1)}, bf16[1,128,1024]{2,1,0:T(8,128)(2,1)}, u32[]{:S(2)}, u32[]{:S(2)}) %collective-permute-start.19) | collective-permute-done | bytes 262176 | tf_op jit(solution)/shard_map/ppermute | solution.py:299
  107.0 2.6 %fusion = (bf16[128,1024]{1,0:T(8,128)(2,1)}, f32[128,1024]{1,0:T(8,128)}) fusion(bf16[1,128,1024]{2,1,0:T(8,128)(2,1)} %collective-permute-done.19, bf16[1,128,1024]{2,1,0:T(8,128)(2,1)} %collective-permute-done.18, bf16[1,128,1024]{2,1,0:T(8,128)(2,1)} %collective-permute-done.17, bf16[4,128,1024]{2,1,0:T(8,128)(2,1)} %collective-permute-done.16, ...), kind=kLoop, calls=%fused_computation.28 | loop fusion | flops 1835008 | bytes 2621444 | tf_op jit(solution)/shard_map/convert_element_type | solution.py:461
  115.8 19.6 %collective-permute-done.15.refs_5_.refs_1_ = bf16[512,512]{1,0:T(8,128)(2,1)S(1)} collective-permute-done((bf16[512,512]{1,0:T(8,128)(2,1)S(1)}, bf16[512,512]{1,0:T(8,128)(2,1)S(1)}, u32[]{:S(2)}, u32[]{:S(2)}) %collective-permute-start.15) | collective-permute-done | bytes 524320 | tf_op jit(solution)/shard_map/ppermute | solution.py:435
  136.8 9.2 %collective-permute-done.9.refs_1_.refs_7_ = bf16[512,512]{1,0:T(8,128)(2,1)S(1)} collective-permute-done((bf16[512,512]{1,0:T(8,128)(2,1)S(1)}, bf16[512,512]{1,0:T(8,128)(2,1)S(1)}, u32[]{:S(2)}, u32[]{:S(2)}) %collective-permute-start.9) | collective-permute-done | bytes 524320 | tf_op jit(solution)/shard_map/ppermute | solution.py:435
  176.2 3.6 %collective-permute-done.27 = f32[8,128]{1,0:T(8,128)S(1)} collective-permute-done((f32[8,128]{1,0:T(8,128)S(1)}, f32[8,128]{1,0:T(8,128)S(1)}, u32[]{:S(2)}, u32[]{:S(2)}) %collective-permute-start.27) | collective-permute-done | bytes 4128 | tf_op jit(solution)/shard_map/ppermute | solution.py:481
  179.8 4.5 %collective-permute-done.28 = f32[8,128]{1,0:T(8,128)S(1)} collective-permute-done((f32[8,128]{1,0:T(8,128)S(1)}, f32[8,128]{1,0:T(8,128)S(1)}, u32[]{:S(2)}, u32[]{:S(2)}) %collective-permute-start.28) | collective-permute-done | bytes 4128 | tf_op jit(solution)/shard_map/ppermute | solution.py:481
  185.6 4.0 %multiply_subtract_fusion = (f32[256,1024]{1,0:T(8,128)}, f32[256,1024]{1,0:T(8,128)}, bf16[256,1024]{1,0:T(8,128)(2,1)}) fusion(f32[256,1024]{1,0:T(8,128)} %param.23, f32[64,1024]{1,0:T(8,128)} %copy-done.40, f32[64,1024]{1,0:T(8,128)} %copy-done.39, f32[128,1024]{1,0:T(8,128)} %get-tuple-element.55, f32[]{:T(128)} %bitcast.10, f32[256,1024]{1,0:T(8,128)} %param.24), kind=kLoop, calls=%fused_computation.1 | loop fusion | flops 3145728 | bytes 5767172 | tf_op jit(solution)/shard_map/sub | solution.py:486
  189.6 2.5 %collective-permute-start.35 = (bf16[1,64,1024]{2,1,0:T(8,128)(2,1)}, bf16[1,64,1024]{2,1,0:T(8,128)(2,1)S(1)}, u32[]{:S(2)}, u32[]{:S(2)}) collective-permute-start(bf16[1,64,1024]{2,1,0:T(8,128)(2,1)} %get-tuple-element.60), channel_id=1, source_target_pairs={{0,24},{4,28},{8,16},{12,20},{16,8},{20,12},{24,0},{28,4},{1,25},{... | collective-permute-start | bytes 393224 | tf_op jit(solution)/shard_map/ppermute | solution.py:311
  193.2 2.5 %collective-permute-start.31 = (bf16[1,64,1024]{2,1,0:T(8,128)(2,1)}, bf16[1,64,1024]{2,1,0:T(8,128)(2,1)S(1)}, u32[]{:S(2)}, u32[]{:S(2)}) collective-permute-start(bf16[1,64,1024]{2,1,0:T(8,128)(2,1)} %get-tuple-element.52), channel_id=1, source_target_pairs={{0,24},{4,28},{8,16},{12,20},{16,8},{20,12},{24,0},{28,4},{1,25},{... | collective-permute-start | bytes 393224 | tf_op jit(solution)/shard_map/ppermute | solution.py:311
  201.1 3.3 %collective-permute-done.30 = bf16[1,64,1024]{2,1,0:T(8,128)(2,1)S(1)} collective-permute-done((bf16[1,64,1024]{2,1,0:T(8,128)(2,1)}, bf16[1,64,1024]{2,1,0:T(8,128)(2,1)S(1)}, u32[]{:S(2)}, u32[]{:S(2)}) %collective-permute-start.30) | collective-permute-done | bytes 131104 | tf_op jit(solution)/shard_map/ppermute | solution.py:311
  216.8 8.3 %shard_map.169 = bf16[512,1024]{1,0:T(8,128)(2,1)} custom-call(s32[4]{0:T(128)S(1)} %pad_add_fusion.place_ref, f32[16,512]{1,0:T(8,128)S(1)} %bitcast.29, bf16[512,1024]{1,0:T(8,128)(2,1)S(1)} %get-tuple-element.26.normed_ref.refs_4_.refs_2_, f32[2,512,1]{2,1,0:T(8,128)S(1)} %copy-done.19, bf16[512,1024]{1,0:T(8,128)(2,1)S(1)} %copy-done.15, ...), custom_call_target="tpu_custom_call" | custom-call | flops 1073741824 | bytes 4194304 | tf_op jit(solution)/shard_map/pallas_call | solution.py:465
  230.4 7.9 %shard_map.171 = bf16[2048,1024]{1,0:T(8,128)(2,1)} custom-call(s32[4]{0:T(128)S(1)} %pad_add_fusion.place_ref, f32[1]{0:T(128)} %bitcast.11.scale_ref, bf16[2048,1024]{1,0:T(8,128)(2,1)S(1)} %copy-done.4, bf16[1024,1024]{1,0:T(8,128)(2,1)S(1)} %copy-done.5, bf16[4,64,1024]{2,1,0:T(8,128)(2,1)} %pad_maximum_fusion.refs_0_, ...), custom_call_target="tpu_custom_call" | custom-call | flops 4194304 | bytes 12582912 | tf_op jit(solution)/shard_map/pallas_call | solution.py:489
  (172 shorter events, 88.0 us)
Async XLA Ops:
  7.2 217.9 %all-gather.5.cloned.1.call-start = ((), (), s32[]{:S(2)}) async-start(), calls=%async_computation.1 | async-start | bytes 2359296 | tf_op jit(solution)/shard_map/all_gather | solution.py:461
  24.3 17.3 %collective-permute-start = (bf16[512,512]{1,0:T(8,128)(2,1)S(1)}, bf16[512,512]{1,0:T(8,128)(2,1)S(1)}, u32[]{:S(2)}, u32[]{:S(2)}) collective-permute-start(bf16[512,512]{1,0:T(8,128)(2,1)S(1)} %shard_map.157.a_ref), channel_id=1, source_target_pairs={{0,1},{3,2},{4,5},{7,6},{8,9},{11,10},{12,13},{15,14},{16,17},{19,... | collective-permute-start | bytes 1572872 | tf_op jit(solution)/shard_map/ppermute | solution.py:422
  31.8 21.0 %collective-permute-start.1 = (bf16[512,512]{1,0:T(8,128)(2,1)S(1)}, bf16[512,512]{1,0:T(8,128)(2,1)S(1)}, u32[]{:S(2)}, u32[]{:S(2)}) collective-permute-start(bf16[512,512]{1,0:T(8,128)(2,1)S(1)} %get-tuple-element.31.a_ref), channel_id=1, source_target_pairs={{0,1},{3,2},{4,5},{7,6},{8,9},{11,10},{12,13},{15,14},{16,17},{19,... | collective-permute-start | bytes 1572872 | tf_op jit(solution)/shard_map/ppermute | solution.py:422
  41.7 11.9 %collective-permute-start.2 = (bf16[512,512]{1,0:T(8,128)(2,1)S(1)}, bf16[512,512]{1,0:T(8,128)(2,1)S(1)}, u32[]{:S(2)}, u32[]{:S(2)}) collective-permute-start(bf16[512,512]{1,0:T(8,128)(2,1)S(1)} %shard_map.159.a_ref), channel_id=1, source_target_pairs={{1,2},{2,1},{5,6},{6,5},{9,10},{10,9},{13,14},{14,13},{17,18},{18,... | collective-permute-start | bytes 1572872 | tf_op jit(solution)/shard_map/ppermute | solution.py:432
  42.4 20.5 %collective-permute-start.3 = (bf16[512,512]{1,0:T(8,128)(2,1)S(1)}, bf16[512,512]{1,0:T(8,128)(2,1)S(1)}, u32[]{:S(2)}, u32[]{:S(2)}) collective-permute-start(bf16[512,512]{1,0:T(8,128)(2,1)S(1)} %get-tuple-element.35.a_ref), channel_id=1, source_target_pairs={{0,1},{3,2},{4,5},{7,6},{8,9},{11,10},{12,13},{15,14},{16,17},{19,... | collective-permute-start | bytes 1572872 | tf_op jit(solution)/shard_map/ppermute | solution.py:422
  52.9 10.1 %collective-permute-start.4 = (bf16[512,512]{1,0:T(8,128)(2,1)S(1)}, bf16[512,512]{1,0:T(8,128)(2,1)S(1)}, u32[]{:S(2)}, u32[]{:S(2)}) collective-permute-start(bf16[512,512]{1,0:T(8,128)(2,1)S(1)} %shard_map.160.a_ref), channel_id=1, source_target_pairs={{1,2},{2,1},{5,6},{6,5},{9,10},{10,9},{13,14},{14,13},{17,18},{18,... | collective-permute-start | bytes 1572872 | tf_op jit(solution)/shard_map/ppermute | solution.py:432
  53.7 17.9 %collective-permute-start.6 = (bf16[512,512]{1,0:T(8,128)(2,1)S(1)}, bf16[512,512]{1,0:T(8,128)(2,1)S(1)}, u32[]{:S(2)}, u32[]{:S(2)}) collective-permute-start(bf16[512,512]{1,0:T(8,128)(2,1)S(1)} %shard_map.161.refs_0_), channel_id=1, source_target_pairs={{1,0},{2,3},{5,4},{6,7},{9,8},{10,11},{13,12},{14,15},{17,16},{18,... | collective-permute-start | bytes 1572872 | tf_op jit(solution)/shard_map/ppermute | solution.py:435
  63.1 18.0 %collective-permute-start.7 = (bf16[512,512]{1,0:T(8,128)(2,1)S(1)}, bf16[512,512]{1,0:T(8,128)(2,1)S(1)}, u32[]{:S(2)}, u32[]{:S(2)}) collective-permute-start(bf16[512,512]{1,0:T(8,128)(2,1)S(1)} %shard_map.163.refs_2_), channel_id=1, source_target_pairs={{1,0},{2,3},{5,4},{6,7},{9,8},{10,11},{13,12},{14,15},{17,16},{18,... | collective-permute-start | bytes 1572872 | tf_op jit(solution)/shard_map/ppermute | solution.py:435
  90.5 9.5 %collective-permute-start.17 = (bf16[1,128,1024]{2,1,0:T(8,128)(2,1)}, bf16[1,128,1024]{2,1,0:T(8,128)(2,1)}, u32[]{:S(2)}, u32[]{:S(2)}) collective-permute-start(bf16[1,128,1024]{2,1,0:T(8,128)(2,1)} %get-tuple-element.57), channel_id=1, source_target_pairs={{0,8},{4,12},{8,0},{12,4},{16,24},{20,28},{24,16},{28,20},{1,9},{5... | collective-permute-start | bytes 786440 | tf_op jit(solution)/shard_map/ppermute | solution.py:299
  92.0 13.9 %collective-permute-start.19 = (bf16[1,128,1024]{2,1,0:T(8,128)(2,1)}, bf16[1,128,1024]{2,1,0:T(8,128)(2,1)}, u32[]{:S(2)}, u32[]{:S(2)}) collective-permute-start(bf16[1,128,1024]{2,1,0:T(8,128)(2,1)} %get-tuple-element.58), channel_id=1, source_target_pairs={{0,24},{4,28},{8,16},{12,20},{16,8},{20,12},{24,0},{28,4},{1,25},{... | collective-permute-start | bytes 786440 | tf_op jit(solution)/shard_map/ppermute | solution.py:299
  93.5 13.5 %collective-permute-start.18 = (bf16[1,128,1024]{2,1,0:T(8,128)(2,1)S(1)}, bf16[1,128,1024]{2,1,0:T(8,128)(2,1)}, u32[]{:S(2)}, u32[]{:S(2)}) collective-permute-start(bf16[1,128,1024]{2,1,0:T(8,128)(2,1)S(1)} %get-tuple-element.59), channel_id=1, source_target_pairs={{0,16},{4,20},{8,24},{12,28},{16,0},{20,4},{24,8},{28,12},{1,17},{... | collective-permute-start | bytes 786440 | tf_op jit(solution)/shard_map/ppermute | solution.py:299
  94.0 16.5 %collective-permute-start.5 = (bf16[512,512]{1,0:T(8,128)(2,1)}, bf16[512,512]{1,0:T(8,128)(2,1)S(1)}, u32[]{:S(2)}, u32[]{:S(2)}) collective-permute-start(bf16[512,512]{1,0:T(8,128)(2,1)} %copy-done.20), channel_id=1, source_target_pairs={{0,1},{3,2},{4,5},{7,6},{8,9},{11,10},{12,13},{15,14},{16,17},{19,... | collective-permute-start | bytes 1572872 | tf_op jit(solution)/shard_map/ppermute | solution.py:422
  109.6 117.0 %all-gather.3.cloned.1.call-start = ((), (), s32[]{:S(2)}) async-start(), calls=%async_computation | async-start | bytes 4718592 | tf_op jit(solution)/shard_map/all_gather | solution.py:367
  112.9 22.5 %collective-permute-start.15 = (bf16[512,512]{1,0:T(8,128)(2,1)S(1)}, bf16[512,512]{1,0:T(8,128)(2,1)S(1)}, u32[]{:S(2)}, u32[]{:S(2)}) collective-permute-start(bf16[512,512]{1,0:T(8,128)(2,1)S(1)} %shard_map.168.refs_4_.refs_0_), channel_id=1, source_target_pairs={{1,0},{2,3},{5,4},{6,7},{9,8},{10,11},{13,12},{14,15},{17,16},{18,... | collective-permute-start | bytes 1572872 | tf_op jit(solution)/shard_map/ppermute | solution.py:435
  114.4 31.6 %collective-permute-start.9 = (bf16[512,512]{1,0:T(8,128)(2,1)S(1)}, bf16[512,512]{1,0:T(8,128)(2,1)S(1)}, u32[]{:S(2)}, u32[]{:S(2)}) collective-permute-start(bf16[512,512]{1,0:T(8,128)(2,1)S(1)} %shard_map.166.refs_0_.refs_6_), channel_id=1, source_target_pairs={{1,0},{2,3},{5,4},{6,7},{9,8},{10,11},{13,12},{14,15},{17,16},{18,... | collective-permute-start | bytes 1572872 | tf_op jit(solution)/shard_map/ppermute | solution.py:435
  136.8 10.7 %collective-permute-start.20 = (bf16[4,64,1024]{2,1,0:T(8,128)(2,1)S(1)}, bf16[4,64,1024]{2,1,0:T(8,128)(2,1)S(1)}, u32[]{:S(2)}, u32[]{:S(2)}) collective-permute-start(bf16[4,64,1024]{2,1,0:T(8,128)(2,1)S(1)} %get-tuple-element.47), channel_id=1, source_target_pairs={{0,4},{4,0},{8,12},{12,8},{16,20},{20,16},{24,28},{28,24},{1,5},{5... | collective-permute-start | bytes 1572872 | tf_op jit(solution)/shard_map/ppermute | solution.py:286
  149.6 9.1 %collective-permute-start.22 = (bf16[1,64,1024]{2,1,0:T(8,128)(2,1)S(1)}, bf16[1,64,1024]{2,1,0:T(8,128)(2,1)S(1)}, u32[]{:S(2)}, u32[]{:S(2)}) collective-permute-start(bf16[1,64,1024]{2,1,0:T(8,128)(2,1)S(1)} %get-tuple-element.64), channel_id=1, source_target_pairs={{0,16},{4,20},{8,24},{12,28},{16,0},{20,4},{24,8},{28,12},{1,17},{... | collective-permute-start | bytes 393224 | tf_op jit(solution)/shard_map/ppermute | solution.py:299
  151.3 8.3 %collective-permute-start.11 = (bf16[1,64,1024]{2,1,0:T(8,128)(2,1)S(1)}, bf16[1,64,1024]{2,1,0:T(8,128)(2,1)S(1)}, u32[]{:S(2)}, u32[]{:S(2)}) collective-permute-start(bf16[1,64,1024]{2,1,0:T(8,128)(2,1)S(1)} %get-tuple-element.65), channel_id=1, source_target_pairs={{0,8},{4,12},{8,0},{12,4},{16,24},{20,28},{24,16},{28,20},{1,9},{5... | collective-permute-start | bytes 393224 | tf_op jit(solution)/shard_map/ppermute | solution.py:299
  152.8 9.2 %collective-permute-start.13 = (bf16[1,64,1024]{2,1,0:T(8,128)(2,1)S(1)}, bf16[1,64,1024]{2,1,0:T(8,128)(2,1)S(1)}, u32[]{:S(2)}, u32[]{:S(2)}) collective-permute-start(bf16[1,64,1024]{2,1,0:T(8,128)(2,1)S(1)} %get-tuple-element.66), channel_id=1, source_target_pairs={{0,24},{4,28},{8,16},{12,20},{16,8},{20,12},{24,0},{28,4},{1,25},{... | collective-permute-start | bytes 393224 | tf_op jit(solution)/shard_map/ppermute | solution.py:299
  153.9 9.4 %collective-permute-start.12 = (bf16[1,64,1024]{2,1,0:T(8,128)(2,1)S(1)}, bf16[1,64,1024]{2,1,0:T(8,128)(2,1)S(1)}, u32[]{:S(2)}, u32[]{:S(2)}) collective-permute-start(bf16[1,64,1024]{2,1,0:T(8,128)(2,1)S(1)} %get-tuple-element.67), channel_id=1, source_target_pairs={{0,16},{4,20},{8,24},{12,28},{16,0},{20,4},{24,8},{28,12},{1,17},{... | collective-permute-start | bytes 393224 | tf_op jit(solution)/shard_map/ppermute | solution.py:299
  195.6 8.8 %collective-permute-start.30 = (bf16[1,64,1024]{2,1,0:T(8,128)(2,1)}, bf16[1,64,1024]{2,1,0:T(8,128)(2,1)S(1)}, u32[]{:S(2)}, u32[]{:S(2)}) collective-permute-start(bf16[1,64,1024]{2,1,0:T(8,128)(2,1)} %get-tuple-element.52), channel_id=1, source_target_pairs={{0,16},{4,20},{8,24},{12,28},{16,0},{20,4},{24,8},{28,12},{1,17},{... | collective-permute-start | bytes 393224 | tf_op jit(solution)/shard_map/ppermute | solution.py:311
  197.0 8.3 %collective-permute-start.29 = (bf16[1,64,1024]{2,1,0:T(8,128)(2,1)}, bf16[1,64,1024]{2,1,0:T(8,128)(2,1)S(1)}, u32[]{:S(2)}, u32[]{:S(2)}) collective-permute-start(bf16[1,64,1024]{2,1,0:T(8,128)(2,1)} %get-tuple-element.52), channel_id=1, source_target_pairs={{0,8},{4,12},{8,0},{12,4},{16,24},{20,28},{24,16},{28,20},{1,9},{5... | collective-permute-start | bytes 393224 | tf_op jit(solution)/shard_map/ppermute | solution.py:311
  200.2 24.8 %collective-permute-start.36 = (bf16[4,64,1024]{2,1,0:T(8,128)(2,1)}, bf16[4,64,1024]{2,1,0:T(8,128)(2,1)}, u32[]{:S(2)}, u32[]{:S(2)}) collective-permute-start(bf16[4,64,1024]{2,1,0:T(8,128)(2,1)} %pad_maximum_fusion.1.refs_2_), channel_id=1, source_target_pairs={{0,4},{4,0},{8,12},{12,8},{16,20},{20,16},{24,28},{28,24},{1,5},{5... | collective-permute-start | bytes 1572872 | tf_op jit(solution)/shard_map/ppermute | solution.py:314
  207.1 17.9 %collective-permute-start.32 = (bf16[4,64,1024]{2,1,0:T(8,128)(2,1)}, bf16[4,64,1024]{2,1,0:T(8,128)(2,1)}, u32[]{:S(2)}, u32[]{:S(2)}) collective-permute-start(bf16[4,64,1024]{2,1,0:T(8,128)(2,1)} %pad_maximum_fusion.refs_0_), channel_id=1, source_target_pairs={{0,4},{4,0},{8,12},{12,8},{16,20},{20,16},{24,28},{28,24},{1,5},{5... | collective-permute-start | bytes 1572872 | tf_op jit(solution)/shard_map/ppermute | solution.py:314
  (56 other events, 426.9 us)
Sparse Core Ops, SparseCore 0:
  109.7 25.9 all-gather.4
  189.7 36.8 all-gather.2

commit v5 on v4

v5 whole, which is shorter than its diff:
```python
import functools

import jax
import jax.numpy as jnp
from jax import lax
from jax.experimental import pallas as pl
from jax.experimental.pallas import tpu as pltpu
from jax.sharding import PartitionSpec as P

HEAD_DIM = 64
STATE = 128
SPAN = 256
HALF = SPAN // 2
LANES = 128

inner_rate = 0.001
outer_rate = 0.7
outer_beta = 0.9
clip_rms = 0.005
LOG2E = 1.4426950408889634
NOTE = 16

F32 = jnp.float32
BF16 = jnp.bfloat16
NN = (((1,), (0,)), ((), ()))
NT = (((1,), (1,)), ((), ()))
TN = (((0,), (0,)), ((), ()))


def dot(a, b, dims):
    return lax.dot_general(a, b, dims, preferred_element_type=F32)


def silu(z):
    return z * (1.0 / (1.0 + jnp.exp(-z)))


def softplus(v):
    return jnp.maximum(v, 0.0) + jnp.log1p(jnp.exp(-jnp.abs(v)))


def iota(shape, axis):
    return lax.broadcasted_iota(jnp.int32, shape, axis)


def thirds(v):
    high = v.astype(BF16).astype(F32)
    middle = (v - high).astype(BF16).astype(F32)
    return jnp.concatenate([high, middle, v - high - middle], axis=0).astype(BF16)


def by_head(refs, first, per_group, tokens):
    row = iota((per_group, tokens), 0)
    rows = []
    for ref in refs:
        value = jnp.zeros((per_group, tokens), F32)
        for h in range(per_group):
            value = jnp.where(row == h, ref[first + h], value)
        rows.append(value)
    return rows


def head_tables(dt_ref, a_ref, bias_ref, first, per_group):
    bias, a_log = by_head([bias_ref, a_ref], first, per_group, dt_ref.shape[1])
    step = softplus(dt_ref[...] + bias)
    return step, -jnp.exp(a_log) * step * LOG2E


def span_tables(step, rate, lo, per_group, width):
    upper = (iota((SPAN, SPAN), 0) <= iota((SPAN, SPAN), 1)).astype(BF16)
    step_k = step[:, lo : lo + SPAN]
    sums = dot(thirds(rate[:, lo : lo + SPAN]), upper, NN)
    cum = sums[:per_group] + sums[per_group : 2 * per_group] + sums[2 * per_group :]
    spread = (iota((3 * per_group, width), 1) // HEAD_DIM == iota((3 * per_group, width), 0) % per_group).astype(BF16)
    turn = (iota((3 * per_group, per_group), 1) == iota((3 * per_group, per_group), 0) % per_group).astype(BF16)
    cum_col = dot(thirds(cum), turn, TN)
    step_x = dot(thirds(step_k), spread, TN)
    fade_x = dot(thirds(jnp.exp2(cum)), spread, TN)
    tail_x = dot(thirds(jnp.exp2(cum[:, SPAN - 1 :] - cum) * step_k), spread, TN)
    return cum, cum_col, step_x, fade_x, tail_x


def skip_row(skip_ref, first, per_group, width):
    head = iota((1, width), 1) // HEAD_DIM
    row = jnp.zeros((1, width), F32)
    for h in range(per_group):
        row = jnp.where(head == h, skip_ref[first + h], row)
    return row


def decay(gap, mask=None):
    return jnp.exp2(gap if mask is None else jnp.where(mask, gap, -1e30))


def even_odd(v):
    first = iota(v.shape, 1) % (2 * HEAD_DIM) < HEAD_DIM
    return jnp.where(first, v, 0.0).astype(BF16), jnp.where(first, 0.0, v).astype(BF16)


def forward_kernel(
    count, dt_ref, x_ref, z_ref, b_ref, c_ref, gain_ref, a_ref, bias_ref, skip_ref, *refs
):
    loads = [pltpu.make_async_copy(refs[n], refs[count + n], refs[-1].at[n]) for n in range(count)]
    normed_ref, inv_ref = refs[2 * count : 2 * count + 2]

    @pl.when(pl.program_id(0) == 0)
    def _():
        for load in loads:
            load.start()

    tokens, width = x_ref.shape
    per_group = width // HEAD_DIM
    first = pl.program_id(0) * per_group
    lanes_here = pl.ds(pl.multiple_of(pl.program_id(0) * width, LANES), width)
    step, rate = head_tables(dt_ref, a_ref, bias_ref, first, per_group)
    skip = skip_row(skip_ref, first, per_group, width)
    causal = iota((HALF, HALF), 0) >= iota((HALF, HALF), 1)
    spans = tokens // SPAN
    entering = None
    for k in range(spans):
        rows = slice(k * SPAN, (k + 1) * SPAN)
        cum, cum_col, step_x, fade_x, tail_x = span_tables(step, rate, k * SPAN, per_group, width)
        x = x_ref[rows, :].astype(F32)
        b, c = b_ref[rows, :], c_ref[rows, :]
        scores = dot(c, b, NT)
        values = even_odd(x * step_x)
        pieces = []
        for pair in range(per_group // 2):
            lanes = slice(2 * pair * HEAD_DIM, 2 * (pair + 1) * HEAD_DIM)
            tops, bottoms = [], []
            for h in (2 * pair, 2 * pair + 1):
                col, line = cum_col[:, h : h + 1], cum[h : h + 1, :]
                top = decay(col[:HALF] - line[:, :HALF], causal) * scores[:HALF, :HALF]
                left = decay(col[HALF:] - line[:, :HALF]) * scores[HALF:, :HALF]
                low = decay(col[HALF:] - line[:, HALF:], causal) * scores[HALF:, HALF:]
                tops.append(top.astype(BF16))
                bottoms += [left.astype(BF16), low.astype(BF16)]
            upper_values = jnp.concatenate([v[:HALF, lanes] for v in values], axis=0)
            all_values = jnp.concatenate([v[:, lanes] for v in values], axis=0)
            pieces.append(
                jnp.concatenate(
                    [
                        dot(jnp.concatenate(tops, axis=1), upper_values, NN),
                        dot(jnp.concatenate(bottoms, axis=1), all_values, NN),
                    ],
                    axis=0,
                )
            )
        ssd = jnp.concatenate(pieces, axis=1) + skip * x
        if entering is not None:
            ssd = ssd + dot(c, entering.astype(BF16), NN) * fade_x
        if k + 1 < spans:
            state = dot(b, (x * tail_x).astype(BF16), TN)
            entering = state if entering is None else entering * fade_x[SPAN - 1 :, :] + state
        gated = ssd * silu(z_ref[rows, :].astype(F32))
        inv = lax.rsqrt(jnp.mean(gated * gated, axis=1, keepdims=True) + 1e-05)
        normed_ref[rows, lanes_here] = (gated * inv * gain_ref[...]).astype(BF16)
        inv_ref[pl.program_id(0), rows, :] = inv

    @pl.when(pl.program_id(0) == pl.num_programs(0) - 1)
    def _():
        for load in loads:
            load.wait()


def project_kernel(chunks, place_ref, weight_ref, normed_ref, target_ref, *part_refs):
    replicas, owned, inner = weight_ref.shape
    held, features = target_ref.shape
    piece = part_refs[0].shape[0] // replicas
    tokens = normed_ref.shape[0]
    eye = (iota((held, held), 0) == iota((held, held), 1)).astype(BF16)
    turned = dot(target_ref[...], eye, TN).reshape(replicas, owned, held)
    here = iota((replicas * piece, tokens), 1) // held == place_ref[0]
    for n, part_ref in zip(chunks, part_refs):
        at = slice(n * piece, (n + 1) * piece)
        part = dot(weight_ref[:, at, :].reshape(replicas * piece, inner), normed_ref[...], NT)
        goal = jnp.concatenate([turned[:, at, :].reshape(replicas * piece, held)] * (tokens // held), axis=1)
        part_ref[...] = (part - jnp.where(here, goal, 0.0)).astype(BF16)


def add_kernel(a_ref, b_ref, sum_ref):
    sum_ref[...] = (a_ref[...].astype(F32) + b_ref[...].astype(F32)).astype(BF16)


def gradient_kernel(batch, place_ref, *refs):
    count = len(batch)
    cot_refs, (normed_ref, weight_ref, keep_ref, send_ref) = refs[: 2 * count], refs[2 * count :]
    middle = place_ref[1] == 1
    odd = place_ref[2] == 1
    replicas, _, inner = weight_ref.shape
    piece = keep_ref.shape[1] // count
    tile = min(inner, 512)
    for n, chunk in enumerate(batch):
        cot = jnp.where(middle, cot_refs[2 * n][...], cot_refs[2 * n + 1][...])
        rows = slice(chunk * piece, (chunk + 1) * piece)
        at = slice(n * piece, (n + 1) * piece)
        for lo in range(0, inner, tile):
            cols = slice(lo, lo + tile)
            weight = weight_ref[:, rows, cols].reshape(replicas * piece, tile).astype(F32)
            new = weight - inner_rate * dot(cot, normed_ref[:, cols], NN)
            new = new.astype(BF16).reshape(replicas // 2, 2, piece, tile)
            keep_ref[:, at, cols] = jnp.where(odd, new[:, 1], new[:, 0])
            send_ref[:, at, cols] = jnp.where(odd, new[:, 0], new[:, 1])


def backward_kernel(
    begin, place_ref, dt_ref, z_ref, b_ref, c_ref, gain_ref, a_ref, bias_ref, skip_ref, normed_ref, inv_ref, weight_ref, *refs
):
    *cot_refs, dx_ref, dn_ref = refs
    if len(cot_refs) % 2:
        cot_refs = cot_refs[:-1]
    tokens, width = z_ref.shape
    per_group = width // HEAD_DIM
    group = pl.program_id(0) + begin
    first = group * per_group
    here = pl.ds(pl.multiple_of(group * width, LANES), width)
    replicas, owned, _ = weight_ref.shape
    chunks = len(cot_refs) // 2
    piece = owned // chunks
    middle = place_ref[1] == 1
    for n in range(chunks):
        weight = weight_ref[:, n * piece : (n + 1) * piece, here].reshape(replicas * piece, width)
        term = dot(jnp.where(middle, cot_refs[2 * n][...], cot_refs[2 * n + 1][...]), weight, TN)
        dn_ref[...] = term if n == 0 else dn_ref[...] + term
    step, rate = head_tables(dt_ref, a_ref, bias_ref, first, per_group)
    skip = skip_row(skip_ref, first, per_group, width)
    causal = iota((HALF, HALF), 1) >= iota((HALF, HALF), 0)
    spans = tokens // SPAN
    d_state = None
    for k in reversed(range(spans)):
        rows = slice(k * SPAN, (k + 1) * SPAN)
        cum, cum_col, step_x, fade_x, tail_x = span_tables(step, rate, k * SPAN, per_group, width)
        dn = dn_ref[rows, :]
        gain = gain_ref[...]
        normed = normed_ref[rows, here].astype(F32)
        shared = jnp.mean(normed * dn, axis=1, keepdims=True)
        d_gated = inv_ref[group, rows, :] * (gain * dn - (normed / gain) * shared)
        d_ssd = d_gated * silu(z_ref[rows, :].astype(F32))
        values = even_odd(d_ssd)
        b, c = b_ref[rows, :], c_ref[rows, :]
        scores = dot(b, c, NT)
        pieces = []
        for pair in range(per_group // 2):
            lanes = slice(2 * pair * HEAD_DIM, 2 * (pair + 1) * HEAD_DIM)
            tops, bottoms = [], []
            for h in (2 * pair, 2 * pair + 1):
                col, line = cum_col[:, h : h + 1], cum[h : h + 1, :]
                high = decay(line[:, :HALF] - col[:HALF], causal) * scores[:HALF, :HALF]
                right = decay(line[:, HALF:] - col[:HALF]) * scores[:HALF, HALF:]
                low = decay(line[:, HALF:] - col[HALF:], causal) * scores[HALF:, HALF:]
                tops += [high.astype(BF16), right.astype(BF16)]
                bottoms.append(low.astype(BF16))
            lower_values = jnp.concatenate([v[HALF:, lanes] for v in values], axis=0)
            all_values = jnp.concatenate([v[:, lanes] for v in values], axis=0)
            pieces.append(
                jnp.concatenate(
                    [
                        dot(jnp.concatenate(tops, axis=1), all_values, NN),
                        dot(jnp.concatenate(bottoms, axis=1), lower_values, NN),
                    ],
                    axis=0,
                )
            )
        dx = jnp.concatenate(pieces, axis=1) * step_x + skip * d_ssd
        if d_state is not None:
            dx = dx + dot(b, d_state.astype(BF16), NN) * tail_x
        dx_ref[rows, :] = dx.astype(BF16)
        if k > 0:
            own = dot(c, (d_ssd * fade_x).astype(BF16), TN)
            d_state = own if d_state is None else own + d_state * fade_x[SPAN - 1 :, :]


def pick_kernel(count, place_ref, *refs):
    terms, outs = refs[:count], refs[count:]
    my = lax.rem(lax.div(place_ref[3], place_ref[4]), len(outs))
    for mask, out_ref in enumerate(outs):
        at = lax.bitwise_xor(my, jnp.int32(mask))
        total = terms[0][:, at].astype(F32)
        for term in terms[1:]:
            total = total + term[:, at].astype(F32)
        out_ref[...] = total.astype(BF16)


def delta_kernel(count, lo, replicas, global_ref, before_ref, *refs):
    terms, (delta_ref, sent_ref, squares_ref) = refs[:count], refs[count:]
    rows, inner = delta_ref.shape
    total = terms[0][0].astype(F32)
    for term in terms[1:]:
        total = total + term[0].astype(F32)
    delta = global_ref[lo : lo + rows, :] - total / replicas
    delta_ref[...] = delta
    sent_ref[:rows, :] = delta.astype(BF16)
    squares = jnp.sum(delta * delta, axis=0, keepdims=True)
    squares = before_ref[...] + jnp.broadcast_to(jnp.sum(squares, axis=1, keepdims=True), before_ref.shape)
    squares_ref[...] = squares
    if sent_ref.shape[0] > rows:
        at = iota((NOTE, LANES), 0)
        value = jnp.broadcast_to(squares[:1, :], (NOTE, LANES))
        high = value.astype(BF16).astype(F32)
        middle = (value - high).astype(BF16).astype(F32)
        note = jnp.where(at == 0, high, jnp.where(at == 1, middle, jnp.where(at == 2, value - high - middle, 0.0)))
        sent_ref[rows:, :] = jnp.concatenate([note] * (inner // LANES), axis=1).astype(BF16)


def join_kernel(*refs):
    *parts, out_ref = refs
    lo = 0
    for part in parts:
        out_ref[lo : lo + part.shape[0]] = part[...]
        lo += part.shape[0]


def tree(values):
    while len(values) > 1:
        values = [a + b for a, b in zip(values[::2], values[1::2])]
    return values[0]


def squares_kernel(own_ref, other_ref, out_ref):
    sides = []
    for ref in (own_ref, other_ref):
        rows = ref.shape[1] - NOTE
        notes = [ref[p, rows:, :LANES].astype(F32) for p in range(ref.shape[0])]
        sides.append(tree([note[0:1] + note[1:2] + note[2:3] for note in notes]))
    out_ref[...] = jnp.broadcast_to(sides[0] + sides[1], out_ref.shape)


def weight_kernel(sizes, entries, place_ref, kept_ref, whole_ref, global_ref, momentum_ref, *refs):
    count = len(sizes)
    pairs, deltas, squares = refs[: 2 * count - 2], refs[2 * count - 2 : 3 * count - 2], refs[3 * count - 2 : -3]
    new_ref, new_global_ref, new_momentum_ref = refs[-3:]
    mean = tree([ref[:1, :1] for ref in squares]) / entries
    factor = jnp.minimum(1.0, clip_rms / jnp.sqrt(mean + 1e-06))
    r = pl.program_id(0)
    owned = new_ref.shape[0]
    at_chip = lax.bitwise_xor(lax.div(r, 2), place_ref[3])
    mine = lax.rem(r, 2) == place_ref[2]
    scale = (outer_rate * (1.0 + outer_beta)) * factor
    lo = 0
    for n, size in enumerate(sizes):
        if n == 0:
            piece = whole_ref[...]
        else:
            piece = jnp.where(mine, pairs[2 * n - 2][at_chip, :size, :], pairs[2 * n - 1][at_chip, :size, :])
        kept = kept_ref[pl.ds(pl.multiple_of(r * owned + lo, 16), size), :]
        new_ref[lo : lo + size, :] = (kept.astype(F32) - scale * piece.astype(F32)).astype(BF16)
        lo += size

    @pl.when(r == 0)
    def _():
        lo = 0
        for n, size in enumerate(sizes):
            rows = slice(lo, lo + size)
            lo += size
            clipped = factor * deltas[n][...]
            new_momentum = outer_beta * momentum_ref[rows, :] + clipped
            new_momentum_ref[rows, :] = new_momentum
            new_global_ref[rows, :] = global_ref[rows, :] - outer_rate * (clipped + outer_beta * new_momentum)


def inward(axis_size):
    half = axis_size // 2
    hops = [[(s, s + 1), (axis_size - 1 - s, axis_size - 2 - s)] for s in range(half - 1)]
    return hops, [(half - 1, half), (half, half - 1)]


def in_turn(kernel, inputs, waits, outs):
    def body(*refs):
        end = inputs + waits + outs
        refs[end][...] = jnp.zeros_like(refs[end])
        kernel(*refs[:inputs], *refs[inputs + waits : end], *refs[end + 1 :])

    return body


def stages(replicas):
    bit, left, found = 1, replicas // 2, []
    while left > 1:
        bits = 2 if left >= 4 else 1
        found.append((bit, bits))
        bit, left = bit + bits, left >> bits
    return found


def shards(
    x_in,
    gate_z,
    b_proj,
    c_proj,
    dt_raw,
    a_log,
    dt_bias,
    skip_d,
    norm_gain,
    out_weight,
    global_weight,
    momentum,
    target,
):
    tokens, inner = x_in.shape
    features = out_weight.shape[1]
    replicas = lax.axis_size("replica")
    heads_over = lax.axis_size("tensor")
    groups = b_proj.shape[1] // STATE
    heads = dt_raw.shape[1]
    width = inner // groups
    owned = features // replicas
    chunks = max(2, min(4, owned // 16))
    batches = [list(range(max(1, chunks - 2)))] + [[n] for n in range(max(1, chunks - 2), chunks)]
    piece = owned // chunks
    span_rows = replicas * piece
    place = lax.axis_index("tensor")
    me = lax.axis_index("replica")
    in_middle = (place == heads_over // 2 - 1) | (place == heads_over // 2)
    one = jnp.int32(1)
    places = jnp.stack([place, in_middle.astype(jnp.int32), lax.rem(me, 2), lax.div(me, 2), one]).astype(jnp.int32)
    stored = out_weight[0].reshape(replicas, owned, inner)
    gain = norm_gain.reshape(1, inner)
    dt_rows = dt_raw.T

    smem = pl.BlockSpec(memory_space=pltpu.SMEM)
    vmem = pl.BlockSpec(memory_space=pltpu.VMEM)
    anywhere = pl.BlockSpec(memory_space=pl.ANY)
    inv_spec = pl.BlockSpec((1, tokens, 1), lambda g: (g, 0, 0))
    large = pltpu.CompilerParams(vmem_limit_bytes=30 * 1024 * 1024)
    small = pltpu.CompilerParams(vmem_limit_bytes=16 * 1024 * 1024)
    cost = pl.CostEstimate(
        flops=2 * tokens * inner * 4 * SPAN, bytes_accessed=8 * inner * tokens, transcendentals=tokens * SPAN * heads
    )

    turn = []

    def run(kernel, inputs, in_specs, outs, out_specs, waits=(), **options):
        waits = [*turn[-1:], *waits]
        done = jax.ShapeDtypeStruct((8, LANES), F32)
        *results, ran = pl.pallas_call(
            in_turn(kernel, len(inputs), len(waits), len(outs)),
            in_specs=[*in_specs, *[vmem] * len(waits)],
            out_specs=[*out_specs, vmem],
            out_shape=[*outs, done],
            **options,
        )(*inputs, *waits)
        turn.append(ran)
        return results

    def step(kernel, operands, outs, flops, waits=(), out_specs=None, scalars=()):
        return run(
            kernel,
            [*scalars, *operands],
            [smem] * len(scalars) + [vmem] * len(operands),
            outs,
            out_specs or [vmem] * len(outs),
            waits,
            cost_estimate=pl.CostEstimate(flops=flops, bytes_accessed=4 * sum(o.size for o in outs), transcendentals=0),
            compiler_params=small,
        )

    def shape(*dims, dtype=BF16):
        return jax.ShapeDtypeStruct(dims, dtype)

    def in_hbm(*arrays):
        return [pltpu.with_memory_space_constraint(a, pltpu.HBM) for a in arrays]

    kept = global_weight - outer_rate * outer_beta * outer_beta * momentum
    kept_all = lax.all_gather(kept.astype(BF16), "replica", axis=0, tiled=True)

    def group_specs(begin):
        wide = pl.BlockSpec((tokens, width), lambda g: (0, g + begin))
        state = pl.BlockSpec((tokens, STATE), lambda g: (0, g + begin))
        dt = pl.BlockSpec((heads // groups, tokens), lambda g: (g + begin, 0))
        return wide, state, dt, pl.BlockSpec((1, width), lambda g: (0, g + begin))

    by_group, by_state, dt_spec, gain_spec = group_specs(0)
    shared = in_hbm(dt_rows, gate_z, b_proj, c_proj, gain, a_log, dt_bias, skip_d)
    later = [stored, target, global_weight, momentum]
    weight, goal, own_global, own_momentum, normed, inv = run(
        functools.partial(forward_kernel, len(later)),
        [shared[0], *in_hbm(x_in), *shared[1:], *in_hbm(*later)],
        [dt_spec, by_group, by_group, by_state, by_state, gain_spec, smem, smem, smem] + [anywhere] * len(later),
        [pltpu.VMEM(v.shape, v.dtype) for v in later] + [pltpu.VMEM((tokens, inner), BF16), pltpu.VMEM((groups, tokens, 1), F32)],
        [vmem] * (len(later) + 2),
        grid=(groups,),
        scratch_shapes=[pltpu.SemaphoreType.DMA((len(later),))],
        cost_estimate=cost,
        compiler_params=large,
    )

    part = shape(span_rows, tokens)
    chunk_flops = 2 * tokens * span_rows * inner

    def project(picked):
        return step(
            functools.partial(project_kernel, picked),
            [weight, normed, goal],
            [part] * len(picked),
            len(picked) * chunk_flops,
            scalars=[places],
        )

    in_hops, across = inward(heads_over)
    parts = project([0])
    parts += project(list(range(1, chunks)))
    first_landed = [lax.ppermute(p, "tensor", in_hops[0]) if in_hops else None for p in parts]
    sums, cots = {}, {}

    def sum_side(n):
        held = parts[n]
        for at, pairs in enumerate(in_hops):
            landed = first_landed[n] if at == 0 else lax.ppermute(held, "tensor", pairs)
            (held,) = step(add_kernel, [held, landed], [part], part.size)
        sums[n] = held

    def sum_all(n):
        (mid,) = step(add_kernel, [sums[n], lax.ppermute(sums[n], "tensor", across)], [part], part.size)
        out = mid
        for pairs in reversed(in_hops):
            back = lax.ppermute(out, "tensor", [(b, a) for a, b in pairs])
            out = back if pairs is in_hops[0] else jnp.where(in_middle, mid, back)
        cots[n] = (mid, out)

    def exchange(value, mask):
        return lax.ppermute(value, "replica", [(r, r ^ mask) for r in range(replicas)])

    terms, deltas, gathered = {}, {}, {}
    squares = {-1: jnp.zeros((8, LANES), F32)}

    def send_rows(b):
        batch = batches[b]
        rows = len(batch) * piece
        keep, send = step(
            functools.partial(gradient_kernel, batch),
            [c for n in batch for c in cots[n]] + [normed, weight],
            [shape(replicas // 2, rows, inner)] * 2,
            len(batch) * chunk_flops,
            waits=[kept_all[:NOTE, :LANES]] if b == 0 else [],
            scalars=[places],
        )
        held, left = [keep, exchange(send, 1)], replicas // 2
        for bit, bits in stages(replicas):
            ways = 1 << bits
            left //= ways
            cut = [h.reshape(left, ways, rows, inner) for h in held]
            picked = step(
                functools.partial(pick_kernel, len(cut)),
                cut,
                [shape(left, rows, inner)] * ways,
                replicas * rows * inner,
                scalars=[places.at[4].set(1 << (bit - 1))] if bit > 1 else [places],
            )
            held = [picked[0]] + [exchange(picked[mask], mask << bit) for mask in range(1, ways)]
        terms[b] = held

    def own_rows(b):
        batch = batches[b]
        rows = len(batch) * piece
        sent_rows = rows + NOTE if b == len(batches) - 1 else rows
        delta, sent, total = step(
            functools.partial(delta_kernel, len(terms[b]), batch[0] * piece, replicas),
            [own_global, squares[b - 1], *terms[b]],
            [shape(rows, inner, dtype=F32), shape(sent_rows, inner), shape(8, LANES, dtype=F32)],
            4 * rows * inner,
            out_specs=[vmem, vmem if b else pl.BlockSpec((rows, inner)), vmem],
        )
        deltas[b], squares[b] = delta, total
        if b == 0:
            gathered[b] = [lax.all_gather(sent, "replica", axis=0, tiled=True)]
        else:
            gathered[b] = [sent[None]]
            (bit, bits), *_ = stages(replicas)
            gathered[b] += [exchange(gathered[b][0], mask << bit) for mask in range(1, 1 << bits)]

    def join(b):
        for at, (bit, bits) in enumerate(stages(replicas)):
            if at > 0:
                gathered[b] = [held] + [exchange(held, mask << bit) for mask in range(1, 1 << bits)]
            one = gathered[b][0]
            (held,) = step(join_kernel, gathered[b], [shape(len(gathered[b]) * one.shape[0], *one.shape[1:])], one.size)
        gathered[b] = [held, exchange(held, 1)]

    def backward(begin, count, so_far):
        wide, state, dt, gain_here = group_specs(begin)
        operands = [places, *shared, normed, inv, weight] + [c for n in range(chunks) for c in cots[n]]
        specs = [smem, dt, wide, state, state, gain_here, smem, smem, smem, vmem, vmem, vmem] + [vmem] * (2 * chunks)
        aliases = {}
        if so_far is not None:
            aliases = {len(operands): 0}
            operands.append(so_far)
            specs.append(anywhere)
        (grad,) = run(
            functools.partial(backward_kernel, begin),
            operands,
            specs,
            [shape(tokens, inner)],
            [wide],
            grid=(count,),
            scratch_shapes=[pltpu.VMEM((tokens, width), F32)],
            input_output_aliases=aliases,
            cost_estimate=cost,
            compiler_params=large,
        )
        return grad

    begun = 0
    for t in range(chunks + 2):
        if t < chunks:
            sum_side(t)
        if 1 <= t <= chunks:
            sum_all(t - 1)
        if begun < len(batches) and t - 2 == batches[begun][-1]:
            send_rows(begun)
            if begun > 0:
                own_rows(begun - 1)
            begun += 1
    half = groups // 2
    end = len(batches) - 1
    grad_input = backward(0, half, None) if half else None
    own_rows(end)
    for b in range(1, end):
        join(b)
    grad_input = backward(half, groups - half, grad_input)
    join(end)
    (column,) = step(squares_kernel, gathered[end], [shape(8, LANES, dtype=F32)], NOTE * inner)
    columns = [column] + [
        lax.ppermute(column, "tensor", [(t, t ^ mask) for t in range(heads_over)]) for mask in range(1, heads_over)
    ]

    sizes = [len(batch) * piece for batch in batches]
    row_spec = pl.BlockSpec((owned, inner), lambda r: (r, 0))
    held_spec = pl.BlockSpec((owned, inner), lambda r: (0, 0))
    pairs = [v for b in range(1, end + 1) for v in gathered[b]]
    new_weight, new_global, new_momentum = run(
        functools.partial(weight_kernel, sizes, features * inner * heads_over),
        [places, kept_all, *in_hbm(*gathered[0]), own_global, own_momentum, *pairs, *[deltas[b] for b in range(end + 1)], *columns],
        [smem, vmem, pl.BlockSpec((sizes[0], inner), lambda r: (r, 0)), vmem, vmem]
        + [vmem] * (len(pairs) + len(sizes) + len(columns)),
        [shape(features, inner), shape(owned, inner, dtype=F32), shape(owned, inner, dtype=F32)],
        [row_spec, held_spec, held_spec],
        grid=(replicas,),
        cost_estimate=pl.CostEstimate(flops=2 * features * inner, bytes_accessed=6 * features * inner, transcendentals=0),
        compiler_params=pltpu.CompilerParams(vmem_limit_bytes=24 * 1024 * 1024),
    )
    return (grad_input, new_weight, new_global, new_momentum)


def solution(mesh):
    placed = (
        P("replica", "tensor"),
        P("replica", "tensor"),
        P("replica", "tensor"),
        P("replica", "tensor"),
        P("replica", "tensor"),
        P("tensor"),
        P("tensor"),
        P("tensor"),
        P("tensor"),
        P("replica", None, "tensor"),
        P("replica", "tensor"),
        P("replica", "tensor"),
        P(("replica", "tensor"), None),
    )
    return jax.shard_map(
        shards,
        mesh=mesh,
        in_specs=placed,
        out_specs=(
            P("replica", "tensor"),
            P(None, "tensor"),
            P("replica", "tensor"),
            P("replica", "tensor"),
        ),
        check_vma=False,
    )
```

time: 246 us -> 217 us (0.88)
  waiting for transfers between devices: 109 us -> 85.3 us
  other arithmetic: 15.3 us -> 2.54 us
  Pallas kernels: 32 us -> 40.5 us
  starting transfers between devices: 44.8 us -> 51.2 us
  local copies, waits for them, and re-layouts: 26.5 us -> 22 us
  between operations: 17.2 us -> 14.5 us
    ppermute x33 -> x31, waiting for transfers between devices: 62.2 us -> 43 us  [the longest x4 21.2 us: shards(): lax.ppermute(p, 'tensor', in_hops[0])]
    pallas_call x16 -> x26, Pallas kernels: 32 us -> 40.5 us  [run(): pl.pallas_call(in_turn(kernel, len(inputs), len(waits), len(outs)), in_sp...]
    ppermute x33 -> x31, starting transfers between devices: 39.4 us -> 45.8 us  [the longest x4 20.7 us: shards(): lax.ppermute(p, 'tensor', in_hops[0])]
    unnamed x82 -> x68, local copies, waits for them, and re-layouts: 26 us -> 21.2 us
    sub x1 -> x0, other arithmetic: 3.98 us -> none  [shards(): global_weight - outer_rate * (clipped + outer_beta * new_momentum)]
    concatenate x2 -> x0, other arithmetic: 3.57 us -> none  [gather_rows(): held = jnp.concatenate(parts, axis=0)]
    ppermute x4, waiting for transfers between devices: 45.5 us -> 42.2 us  [sum_all(): back = lax.ppermute(out, 'tensor', [(b, a) for a, b in pairs])]
    convert_element_type x4 -> x1, other arithmetic: 5.27 us -> 2.54 us  [shards(): kept_all = lax.all_gather(kept.astype(BF16), 'replica', axis=0, tiled=True)]
  transfers between devices with their start and end apart: 39 -> 37, of which waited for: 27 -> 18; matrix products, arithmetic and copies ran while one was open for 5% -> 0% of each run, Pallas kernels for 6% -> 13%
where the time goes in v5:
time: 217 us; the launch traced here: 216 us
  waiting for transfers between devices  85.3 us (39%)
  starting transfers between devices  51.2 us (24%)
  Pallas kernels  40.5 us (19%)
  local copies, waits for them, and re-layouts  22 us (10%)
  between operations  14.5 us (7%)
  other arithmetic  2.54 us (1%)
    ppermute x4, waiting for transfers between devices, sum_all(): back = lax.ppermute(out, 'tensor', [(b, a) for a, b in pairs])  42.2 us
    pallas_call x26, Pallas kernels, run(): pl.pallas_call(in_turn(kernel, len(inputs), len(waits), len(outs)), in_sp...  40.5 us
    unnamed x68, local copies, waits for them, and re-layouts  21.2 us
    ppermute x4, waiting for transfers between devices, shards(): lax.ppermute(p, 'tensor', in_hops[0])  21.2 us
    ppermute x4, starting transfers between devices, shards(): lax.ppermute(p, 'tensor', in_hops[0])  20.7 us
    ppermute x20, starting transfers between devices, exchange(): lax.ppermute(value, 'replica', [(r, r ^ mask) for r in range(replicas)])  17.8 us
    ppermute x20, waiting for transfers between devices, exchange(): lax.ppermute(value, 'replica', [(r, r ^ mask) for r in range(replicas)])  17.8 us
    ppermute x4, starting transfers between devices, sum_all(): back = lax.ppermute(out, 'tensor', [(b, a) for a, b in pairs])  5.35 us
  transfers between devices with their start and end apart: 37, of which 18 were waited for; matrix products, arithmetic and copies ran while one was open for 0% of the time, Pallas kernels for 13%

profile of v5, /device:TPU:0, one launch (start us, length us, event | category | flops | bytes accessed | tf_op | source)
XLA Modules:
  0.0 216.0 jit_solution(16897191776824270554)
XLA Ops:
  7.2 2.5 %subtract_convert_fusion = bf16[256,1024]{1,0:T(8,128)(2,1)} fusion(f32[256,1024]{1,0:T(8,128)} %refs_11_.1, f32[256,1024]{1,0:T(8,128)} %refs_12_.1), kind=kLoop, calls=%fused_computation | loop fusion | flops 786432 | bytes 2621440 | tf_op jit(solution)/shard_map/convert_element_type | solution.py:465
  9.9 6.2 %shard_map.156 = (bf16[8,256,1024]{2,1,0:T(8,128)(2,1)S(1)}, bf16[128,2048]{1,0:T(8,128)(2,1)S(1)}, f32[256,1024]{1,0:T(8,128)S(1)}, f32[256,1024]{1,0:T(8,128)S...) custom-call(f32[16,512]{1,0:T(8,128)} %bitcast.30, bf16[512,1024]{1,0:T(8,128)(2,1)} %refs_1_.1, ...), custom_call_target="tpu_custom_call" | custom-call | flops 1073741824 | bytes 4194304 | tf_op jit(solution)/shard_map/pallas_call | solution.py:436
  18.5 5.0 %collective-permute-start = (bf16[512,512]{1,0:T(8,128)(2,1)S(1)}, bf16[512,512]{1,0:T(8,128)(2,1)S(1)}, u32[]{:S(2)}, u32[]{:S(2)}) collective-permute-start(bf16[512,512]{1,0:T(8,128)(2,1)S(1)} %get-tuple-element.86.refs_0_), channel_id=1, source_target_pairs={{0,1},{3,2},{4,5},{7,6},{8,9},{11,10},{12,13},{15,14},{16,17},{19,... | collective-permute-start | bytes 1572872 | tf_op jit(solution)/shard_map/ppermute | solution.py:503
  23.5 2.5 %shard_map.158 = (bf16[512,512]{1,0:T(8,128)(2,1)S(1)}, bf16[512,512]{1,0:T(8,128)(2,1)S(1)}, bf16[512,512]{1,0:T(8,128)(2,1)S(1)}, f32[8,128]{1,0:T(8,128)S(1)}) custom-call(s32[5]{0:T(128)S(1)} %stack.23.refs_0_, bf16[8,256,1024]{2,1,0:T(8,128)(2,1)S(1)} %get-tuple-element.83.refs_1_.refs_6_.refs_4_.refs_11_, ...), custom_call_target="tpu_custom_call" | custom-call | flops 1610612736 | bytes 3145728 | tf_op jit(solution)/shard_map/pallas_call | solution.py:436
  27.4 8.4 %collective-permute-done.refs_1_ = bf16[512,512]{1,0:T(8,128)(2,1)S(1)} collective-permute-done((bf16[512,512]{1,0:T(8,128)(2,1)S(1)}, bf16[512,512]{1,0:T(8,128)(2,1)S(1)}, u32[]{:S(2)}, u32[]{:S(2)}) %collective-permute-start) | collective-permute-done | bytes 524320 | tf_op jit(solution)/shard_map/ppermute | solution.py:503
  36.6 7.2 %collective-permute-start.5 = (bf16[512,512]{1,0:T(8,128)(2,1)S(1)}, bf16[512,512]{1,0:T(8,128)(2,1)S(1)}, u32[]{:S(2)}, u32[]{:S(2)}) collective-permute-start(bf16[512,512]{1,0:T(8,128)(2,1)S(1)} %get-tuple-element.95.refs_0_), channel_id=1, source_target_pairs={{0,1},{3,2},{4,5},{7,6},{8,9},{11,10},{12,13},{15,14},{16,17},{19,... | collective-permute-start | bytes 1572872 | tf_op jit(solution)/shard_map/ppermute | solution.py:503
  43.8 3.2 %collective-permute-done.2.refs_1_ = bf16[512,512]{1,0:T(8,128)(2,1)S(1)} collective-permute-done((bf16[512,512]{1,0:T(8,128)(2,1)S(1)}, bf16[512,512]{1,0:T(8,128)(2,1)S(1)}, u32[]{:S(2)}, u32[]{:S(2)}) %collective-permute-start.2) | collective-permute-done | bytes 524320 | tf_op jit(solution)/shard_map/ppermute | solution.py:503
  47.8 7.2 %collective-permute-start.8 = (bf16[512,512]{1,0:T(8,128)(2,1)S(1)}, bf16[512,512]{1,0:T(8,128)(2,1)S(1)}, u32[]{:S(2)}, u32[]{:S(2)}) collective-permute-start(bf16[512,512]{1,0:T(8,128)(2,1)S(1)} %get-tuple-element.100.refs_0_), channel_id=1, source_target_pairs={{0,1},{3,2},{4,5},{7,6},{8,9},{11,10},{12,13},{15,14},{16,17},{19,... | collective-permute-start | bytes 1572872 | tf_op jit(solution)/shard_map/ppermute | solution.py:503
  55.2 3.0 %collective-permute-done.5.refs_1_ = bf16[512,512]{1,0:T(8,128)(2,1)S(1)} collective-permute-done((bf16[512,512]{1,0:T(8,128)(2,1)S(1)}, bf16[512,512]{1,0:T(8,128)(2,1)S(1)}, u32[]{:S(2)}, u32[]{:S(2)}) %collective-permute-start.5) | collective-permute-done | bytes 524320 | tf_op jit(solution)/shard_map/ppermute | solution.py:503
  61.8 6.5 %collective-permute-done.8.refs_1_ = bf16[512,512]{1,0:T(8,128)(2,1)S(1)} collective-permute-done((bf16[512,512]{1,0:T(8,128)(2,1)S(1)}, bf16[512,512]{1,0:T(8,128)(2,1)S(1)}, u32[]{:S(2)}, u32[]{:S(2)}) %collective-permute-start.8) | collective-permute-done | bytes 524320 | tf_op jit(solution)/shard_map/ppermute | solution.py:503
  70.9 7.8 %collective-permute-done.6.refs_4_.refs_15_ = bf16[512,512]{1,0:T(8,128)(2,1)} collective-permute-done((bf16[512,512]{1,0:T(8,128)(2,1)S(1)}, bf16[512,512]{1,0:T(8,128)(2,1)}, u32[]{:S(2)}, u32[]{:S(2)}) %collective-permute-start.6) | collective-permute-done | bytes 524320 | tf_op jit(solution)/shard_map/ppermute | solution.py:517
  78.7 8.0 %collective-permute-done.3.refs_2_.refs_13_ = bf16[512,512]{1,0:T(8,128)(2,1)} collective-permute-done((bf16[512,512]{1,0:T(8,128)(2,1)S(1)}, bf16[512,512]{1,0:T(8,128)(2,1)}, u32[]{:S(2)}, u32[]{:S(2)}) %collective-permute-start.3) | collective-permute-done | bytes 524320 | tf_op jit(solution)/shard_map/ppermute | solution.py:517
  88.9 2.8 %shard_map.166 = (bf16[4,128,1024]{2,1,0:T(8,128)(2,1)S(1)}, bf16[4,128,1024]{2,1,0:T(8,128)(2,1)S(1)}, f32[8,128]{1,0:T(8,128)S(1)}) custom-call(s32[5]{0:T(128)S(1)} %stack.23.refs_0_, bf16[512,512]{1,0:T(8,128)(2,1)S(1)} %get-tuple-element.93.refs_1_.refs_12_, bf16[512,512]{1,0:T(8,128)(2,1)} %collective-permute-done.3.refs_2_.refs_13_, ...), custom_call_target="tpu_custom_call" | custom-call | flops 1073741824 | bytes 4194304 | tf_op jit(solution)/shard_map/pallas_call | solution.py:436
  96.2 12.5 %collective-permute-done.9.refs_2_.refs_17_ = bf16[512,512]{1,0:T(8,128)(2,1)S(1)} collective-permute-done((bf16[512,512]{1,0:T(8,128)(2,1)S(1)}, bf16[512,512]{1,0:T(8,128)(2,1)S(1)}, u32[]{:S(2)}, u32[]{:S(2)}) %collective-permute-start.9) | collective-permute-done | bytes 524320 | tf_op jit(solution)/shard_map/ppermute | solution.py:517
  114.4 4.9 %collective-permute-done.13.refs_3_ = bf16[1,128,1024]{2,1,0:T(8,128)(2,1)S(1)} collective-permute-done((bf16[1,128,1024]{2,1,0:T(8,128)(2,1)S(1)}, bf16[1,128,1024]{2,1,0:T(8,128)(2,1)S(1)}, u32[]{:S(2)}, u32[]{:S(2)}) %collective-permute-start.13) | collective-permute-done | bytes 262176 | tf_op jit(solution)/shard_map/ppermute | solution.py:522
  119.3 6.4 %collective-permute-done.14.refs_4_ = bf16[1,128,1024]{2,1,0:T(8,128)(2,1)S(1)} collective-permute-done((bf16[1,128,1024]{2,1,0:T(8,128)(2,1)S(1)}, bf16[1,128,1024]{2,1,0:T(8,128)(2,1)S(1)}, u32[]{:S(2)}, u32[]{:S(2)}) %collective-permute-start.14) | collective-permute-done | bytes 262176 | tf_op jit(solution)/shard_map/ppermute | solution.py:522
  129.1 13.9 %collective-permute-done.12.refs_2_.refs_19_ = bf16[512,512]{1,0:T(8,128)(2,1)S(1)} collective-permute-done((bf16[512,512]{1,0:T(8,128)(2,1)}, bf16[512,512]{1,0:T(8,128)(2,1)S(1)}, u32[]{:S(2)}, u32[]{:S(2)}) %collective-permute-start.12) | collective-permute-done | bytes 524320 | tf_op jit(solution)/shard_map/ppermute | solution.py:517
  143.0 2.5 %copy-done.3 = bf16[8,256,1024]{2,1,0:T(8,128)(2,1)S(1)} copy-done((bf16[8,256,1024]{2,1,0:T(8,128)(2,1)S(1)}, bf16[8,256,1024]{2,1,0:T(8,128)(2,1)}, u32[]{:S(2)}) %copy-start.3) | copy-done | bytes 4194328
  156.6 2.3 %collective-permute-done.19.refs_5_ = bf16[1,64,1024]{2,1,0:T(8,128)(2,1)S(1)} collective-permute-done((bf16[1,64,1024]{2,1,0:T(8,128)(2,1)S(1)}, bf16[1,64,1024]{2,1,0:T(8,128)(2,1)S(1)}, u32[]{:S(2)}, u32[]{:S(2)}) %collective-permute-start.19) | collective-permute-done | bytes 131104 | tf_op jit(solution)/shard_map/ppermute | solution.py:522
  162.6 5.6 %shard_map.175 = (bf16[512,1024]{1,0:T(8,128)(2,1)}, f32[8,128]{1,0:T(8,128)S(1)}) custom-call(s32[5]{0:T(128)S(1)} %stack.23.refs_0_, f32[16,512]{1,0:T(8,128)} %bitcast.31, bf16[512,1024]{1,0:T(8,128)(2,1)} %refs_2_.5, bf16[512,256]{1,0:T(8,128)(2,1)} %refs_3_.5, bf16[512,256]{1,0:T(8,128)(2,1)} %refs_4_.5, f32[1,1024]{1,0:T(1,128)} %bitcast.34, ...), custom_call_target="tpu_custom_call" | custom-call | flops 1073741824 | bytes 4194304 | tf_op jit(solution)/shard_map/pallas_call | solution.py:436
  173.3 5.8 %shard_map.178 = (bf16[512,1024]{1,0:T(8,128)(2,1)}, f32[8,128]{1,0:T(8,128)S(1)}) custom-call(s32[5]{0:T(128)S(1)} %stack.23.refs_0_, f32[16,512]{1,0:T(8,128)} %bitcast.32, bf16[512,1024]{1,0:T(8,128)(2,1)} %refs_2_.5, bf16[512,256]{1,0:T(8,128)(2,1)} %refs_3_.5, bf16[512,256]{1,0:T(8,128)(2,1)} %refs_4_.5, ...), custom_call_target="tpu_custom_call", output_to_operand_aliasing={{0}: (20, {})} | custom-call | flops 1073741824 | bytes 4194304 | tf_op jit(solution)/shard_map/pallas_call | solution.py:436
  183.5 2.4 %collective-permute-start.33 = (f32[8,128]{1,0:T(8,128)S(1)}, f32[8,128]{1,0:T(8,128)S(1)}, u32[]{:S(2)}, u32[]{:S(2)}) collective-permute-start(f32[8,128]{1,0:T(8,128)S(1)} %get-tuple-element.153.refs_12_), channel_id=1, source_target_pairs={{0,2},{1,3},{2,0},{3,1},{4,6},{5,7},{6,4},{7,5},{8,10},{9,11},{10,... | collective-permute-start | bytes 12296 | tf_op jit(solution)/shard_map/ppermute | solution.py:624
  188.0 3.3 %collective-permute-done.34.refs_15_ = f32[8,128]{1,0:T(8,128)S(1)} collective-permute-done((f32[8,128]{1,0:T(8,128)S(1)}, f32[8,128]{1,0:T(8,128)S(1)}, u32[]{:S(2)}, u32[]{:S(2)}) %collective-permute-start.34) | collective-permute-done | bytes 4128 | tf_op jit(solution)/shard_map/ppermute | solution.py:624
  201.0 8.2 %shard_map.181 = (bf16[2048,1024]{1,0:T(8,128)(2,1)}, f32[256,1024]{1,0:T(8,128)}, f32[256,1024]{1,0:T(8,128)}, f32[8,128]{1,0:T(8,128)}) custom-call(s32[5]{0:T(128)S(1)} %stack.23.refs_0_, bf16[2048,1024]{1,0:T(8,128)(2,1)S(1)} %copy-done.13, bf16[1024,1024]{1,0:T(8,128)(2,1)} %all-gather.5.cloned.1.call-done.refs_2_, ...), custom_call_target="tpu_custom_call" | custom-call | flops 4194304 | bytes 12582912 | tf_op jit(solution)/shard_map/pallas_call | solution.py:436
  (150 shorter events, 63.2 us)
Async XLA Ops:
  7.2 63.0 %all-gather.3.cloned.1.call-start = ((), (), s32[]{:S(2)}) async-start(), calls=%async_computation | async-start | bytes 4718592 | tf_op jit(solution)/shard_map/all_gather | solution.py:465
  9.8 181.5 %all-gather.5.cloned.1.call-start = ((), (), s32[]{:S(2)}) async-start(), calls=%async_computation.1 | async-start | bytes 2359296 | tf_op jit(solution)/shard_map/all_gather | solution.py:566
  18.5 17.3 %collective-permute-start = (bf16[512,512]{1,0:T(8,128)(2,1)S(1)}, bf16[512,512]{1,0:T(8,128)(2,1)S(1)}, u32[]{:S(2)}, u32[]{:S(2)}) collective-permute-start(bf16[512,512]{1,0:T(8,128)(2,1)S(1)} %get-tuple-element.86.refs_0_), channel_id=1, source_target_pairs={{0,1},{3,2},{4,5},{7,6},{8,9},{11,10},{12,13},{15,14},{16,17},{19,... | collective-permute-start | bytes 1572872 | tf_op jit(solution)/shard_map/ppermute | solution.py:503
  26.0 21.0 %collective-permute-start.2 = (bf16[512,512]{1,0:T(8,128)(2,1)S(1)}, bf16[512,512]{1,0:T(8,128)(2,1)S(1)}, u32[]{:S(2)}, u32[]{:S(2)}) collective-permute-start(bf16[512,512]{1,0:T(8,128)(2,1)S(1)} %get-tuple-element.90.refs_0_), channel_id=1, source_target_pairs={{0,1},{3,2},{4,5},{7,6},{8,9},{11,10},{12,13},{15,14},{16,17},{19,... | collective-permute-start | bytes 1572872 | tf_op jit(solution)/shard_map/ppermute | solution.py:503
  35.9 19.2 %collective-permute-start.1 = (bf16[512,512]{1,0:T(8,128)(2,1)S(1)}, bf16[512,512]{1,0:T(8,128)(2,1)S(1)}, u32[]{:S(2)}, u32[]{:S(2)}) collective-permute-start(bf16[512,512]{1,0:T(8,128)(2,1)S(1)} %get-tuple-element.89.refs_0_), channel_id=1, source_target_pairs={{1,2},{2,1},{5,6},{6,5},{9,10},{10,9},{13,14},{14,13},{17,18},{18,... | collective-permute-start | bytes 1572872 | tf_op jit(solution)/shard_map/ppermute | solution.py:514
  36.6 21.6 %collective-permute-start.5 = (bf16[512,512]{1,0:T(8,128)(2,1)S(1)}, bf16[512,512]{1,0:T(8,128)(2,1)S(1)}, u32[]{:S(2)}, u32[]{:S(2)}) collective-permute-start(bf16[512,512]{1,0:T(8,128)(2,1)S(1)} %get-tuple-element.95.refs_0_), channel_id=1, source_target_pairs={{0,1},{3,2},{4,5},{7,6},{8,9},{11,10},{12,13},{15,14},{16,17},{19,... | collective-permute-start | bytes 1572872 | tf_op jit(solution)/shard_map/ppermute | solution.py:503
  47.1 11.9 %collective-permute-start.4 = (bf16[512,512]{1,0:T(8,128)(2,1)S(1)}, bf16[512,512]{1,0:T(8,128)(2,1)S(1)}, u32[]{:S(2)}, u32[]{:S(2)}) collective-permute-start(bf16[512,512]{1,0:T(8,128)(2,1)S(1)} %get-tuple-element.94.refs_0_), channel_id=1, source_target_pairs={{1,2},{2,1},{5,6},{6,5},{9,10},{10,9},{13,14},{14,13},{17,18},{18,... | collective-permute-start | bytes 1572872 | tf_op jit(solution)/shard_map/ppermute | solution.py:514
  47.8 20.5 %collective-permute-start.8 = (bf16[512,512]{1,0:T(8,128)(2,1)S(1)}, bf16[512,512]{1,0:T(8,128)(2,1)S(1)}, u32[]{:S(2)}, u32[]{:S(2)}) collective-permute-start(bf16[512,512]{1,0:T(8,128)(2,1)S(1)} %get-tuple-element.100.refs_0_), channel_id=1, source_target_pairs={{0,1},{3,2},{4,5},{7,6},{8,9},{11,10},{12,13},{15,14},{16,17},{19,... | collective-permute-start | bytes 1572872 | tf_op jit(solution)/shard_map/ppermute | solution.py:503
  58.4 10.9 %collective-permute-start.7 = (bf16[512,512]{1,0:T(8,128)(2,1)S(1)}, bf16[512,512]{1,0:T(8,128)(2,1)S(1)}, u32[]{:S(2)}, u32[]{:S(2)}) collective-permute-start(bf16[512,512]{1,0:T(8,128)(2,1)S(1)} %get-tuple-element.99.refs_0_), channel_id=1, source_target_pairs={{1,2},{2,1},{5,6},{6,5},{9,10},{10,9},{13,14},{14,13},{17,18},{18,... | collective-permute-start | bytes 1572872 | tf_op jit(solution)/shard_map/ppermute | solution.py:514
  59.2 19.5 %collective-permute-start.6 = (bf16[512,512]{1,0:T(8,128)(2,1)S(1)}, bf16[512,512]{1,0:T(8,128)(2,1)}, u32[]{:S(2)}, u32[]{:S(2)}) collective-permute-start(bf16[512,512]{1,0:T(8,128)(2,1)S(1)} %get-tuple-element.98.refs_3_.refs_14_), channel_id=1, source_target_pairs={{1,0},{2,3},{5,4},{6,7},{9,8},{10,11},{13,12},{14,15},{17,16},{18,... | collective-permute-start | bytes 1572872 | tf_op jit(solution)/shard_map/ppermute | solution.py:517
  60.5 26.2 %collective-permute-start.3 = (bf16[512,512]{1,0:T(8,128)(2,1)S(1)}, bf16[512,512]{1,0:T(8,128)(2,1)}, u32[]{:S(2)}, u32[]{:S(2)}) collective-permute-start(bf16[512,512]{1,0:T(8,128)(2,1)S(1)} %get-tuple-element.93.refs_1_.refs_12_), channel_id=1, source_target_pairs={{1,0},{2,3},{5,4},{6,7},{9,8},{10,11},{13,12},{14,15},{17,16},{18,... | collective-permute-start | bytes 1572872 | tf_op jit(solution)/shard_map/ppermute | solution.py:517
  92.6 16.2 %collective-permute-start.9 = (bf16[512,512]{1,0:T(8,128)(2,1)S(1)}, bf16[512,512]{1,0:T(8,128)(2,1)S(1)}, u32[]{:S(2)}, u32[]{:S(2)}) collective-permute-start(bf16[512,512]{1,0:T(8,128)(2,1)S(1)} %copy-done.6), channel_id=1, source_target_pairs={{1,0},{2,3},{5,4},{6,7},{9,8},{10,11},{13,12},{14,15},{17,16},{18,... | collective-permute-start | bytes 1572872 | tf_op jit(solution)/shard_map/ppermute | solution.py:517
  110.2 9.2 %collective-permute-start.13 = (bf16[1,128,1024]{2,1,0:T(8,128)(2,1)S(1)}, bf16[1,128,1024]{2,1,0:T(8,128)(2,1)S(1)}, u32[]{:S(2)}, u32[]{:S(2)}) collective-permute-start(bf16[1,128,1024]{2,1,0:T(8,128)(2,1)S(1)} %get-tuple-element.113), channel_id=1, source_target_pairs={{0,8},{4,12},{8,0},{12,4},{16,24},{20,28},{24,16},{28,20},{1,9},{5... | collective-permute-start | bytes 786440 | tf_op jit(solution)/shard_map/ppermute | solution.py:522
  111.7 14.0 %collective-permute-start.14 = (bf16[1,128,1024]{2,1,0:T(8,128)(2,1)S(1)}, bf16[1,128,1024]{2,1,0:T(8,128)(2,1)S(1)}, u32[]{:S(2)}, u32[]{:S(2)}) collective-permute-start(bf16[1,128,1024]{2,1,0:T(8,128)(2,1)S(1)} %get-tuple-element.114), channel_id=1, source_target_pairs={{0,16},{4,20},{8,24},{12,28},{16,0},{20,4},{24,8},{28,12},{1,17},{... | collective-permute-start | bytes 786440 | tf_op jit(solution)/shard_map/ppermute | solution.py:522
  113.3 12.5 %collective-permute-start.15 = (bf16[1,128,1024]{2,1,0:T(8,128)(2,1)S(1)}, bf16[1,128,1024]{2,1,0:T(8,128)(2,1)S(1)}, u32[]{:S(2)}, u32[]{:S(2)}) collective-permute-start(bf16[1,128,1024]{2,1,0:T(8,128)(2,1)S(1)} %get-tuple-element.115), channel_id=1, source_target_pairs={{0,24},{4,28},{8,16},{12,20},{16,8},{20,12},{24,0},{28,4},{1,25},{... | collective-permute-start | bytes 786440 | tf_op jit(solution)/shard_map/ppermute | solution.py:522
  127.6 15.4 %collective-permute-start.12 = (bf16[512,512]{1,0:T(8,128)(2,1)}, bf16[512,512]{1,0:T(8,128)(2,1)S(1)}, u32[]{:S(2)}, u32[]{:S(2)}) collective-permute-start(bf16[512,512]{1,0:T(8,128)(2,1)} %copy-done.10), channel_id=1, source_target_pairs={{1,0},{2,3},{5,4},{6,7},{9,8},{10,11},{13,12},{14,15},{17,16},{18,... | collective-permute-start | bytes 1572872 | tf_op jit(solution)/shard_map/ppermute | solution.py:517
  149.8 9.0 %collective-permute-start.19 = (bf16[1,64,1024]{2,1,0:T(8,128)(2,1)S(1)}, bf16[1,64,1024]{2,1,0:T(8,128)(2,1)S(1)}, u32[]{:S(2)}, u32[]{:S(2)}) collective-permute-start(bf16[1,64,1024]{2,1,0:T(8,128)(2,1)S(1)} %get-tuple-element.125), channel_id=1, source_target_pairs={{0,24},{4,28},{8,16},{12,20},{16,8},{20,12},{24,0},{28,4},{1,25},{... | collective-permute-start | bytes 393224 | tf_op jit(solution)/shard_map/ppermute | solution.py:522
  153.6 14.6 %collective-permute-start.25 = (bf16[1,64,1024]{2,1,0:T(8,128)(2,1)S(1)}, bf16[1,64,1024]{2,1,0:T(8,128)(2,1)S(1)}, u32[]{:S(2)}, u32[]{:S(2)}) collective-permute-start(bf16[1,64,1024]{2,1,0:T(8,128)(2,1)S(1)} %get-tuple-element.137), channel_id=1, source_target_pairs={{0,16},{4,20},{8,24},{12,28},{16,0},{20,4},{24,8},{28,12},{1,17},{... | collective-permute-start | bytes 393224 | tf_op jit(solution)/shard_map/ppermute | solution.py:522
  155.1 13.1 %collective-permute-start.26 = (bf16[1,64,1024]{2,1,0:T(8,128)(2,1)S(1)}, bf16[1,64,1024]{2,1,0:T(8,128)(2,1)S(1)}, u32[]{:S(2)}, u32[]{:S(2)}) collective-permute-start(bf16[1,64,1024]{2,1,0:T(8,128)(2,1)S(1)} %get-tuple-element.138), channel_id=1, source_target_pairs={{0,24},{4,28},{8,16},{12,20},{16,8},{20,12},{24,0},{28,4},{1,25},{... | collective-permute-start | bytes 393224 | tf_op jit(solution)/shard_map/ppermute | solution.py:522
  159.1 12.3 %collective-permute-start.21 = (bf16[1,64,1024]{2,1,0:T(8,128)(2,1)S(1)}, bf16[1,64,1024]{2,1,0:T(8,128)(2,1)S(1)}, u32[]{:S(2)}, u32[]{:S(2)}) collective-permute-start(bf16[1,64,1024]{2,1,0:T(8,128)(2,1)S(1)} %bitcast.25), channel_id=1, source_target_pairs={{0,8},{4,12},{8,0},{12,4},{16,24},{20,28},{24,16},{28,20},{1,9},{5... | collective-permute-start | bytes 393224 | tf_op jit(solution)/shard_map/ppermute | solution.py:522
  159.7 13.6 %collective-permute-start.22 = (bf16[1,64,1024]{2,1,0:T(8,128)(2,1)S(1)}, bf16[1,64,1024]{2,1,0:T(8,128)(2,1)S(1)}, u32[]{:S(2)}, u32[]{:S(2)}) collective-permute-start(bf16[1,64,1024]{2,1,0:T(8,128)(2,1)S(1)} %bitcast.26), channel_id=1, source_target_pairs={{0,16},{4,20},{8,24},{12,28},{16,0},{20,4},{24,8},{28,12},{1,17},{... | collective-permute-start | bytes 393224 | tf_op jit(solution)/shard_map/ppermute | solution.py:522
  160.8 12.5 %collective-permute-start.23 = (bf16[1,64,1024]{2,1,0:T(8,128)(2,1)S(1)}, bf16[1,64,1024]{2,1,0:T(8,128)(2,1)S(1)}, u32[]{:S(2)}, u32[]{:S(2)}) collective-permute-start(bf16[1,64,1024]{2,1,0:T(8,128)(2,1)S(1)} %bitcast.27), channel_id=1, source_target_pairs={{0,24},{4,28},{8,16},{12,20},{16,8},{20,12},{24,0},{28,4},{1,25},{... | collective-permute-start | bytes 393224 | tf_op jit(solution)/shard_map/ppermute | solution.py:522
  169.8 9.3 %collective-permute-start.28 = (bf16[1,80,1024]{2,1,0:T(8,128)(2,1)S(1)}, bf16[1,80,1024]{2,1,0:T(8,128)(2,1)S(1)}, u32[]{:S(2)}, u32[]{:S(2)}) collective-permute-start(bf16[1,80,1024]{2,1,0:T(8,128)(2,1)S(1)} %bitcast.21), channel_id=1, source_target_pairs={{0,8},{4,12},{8,0},{12,4},{16,24},{20,28},{24,16},{28,20},{1,9},{5... | collective-permute-start | bytes 491528 | tf_op jit(solution)/shard_map/ppermute | solution.py:522
  170.9 8.8 %collective-permute-start.29 = (bf16[1,80,1024]{2,1,0:T(8,128)(2,1)S(1)}, bf16[1,80,1024]{2,1,0:T(8,128)(2,1)S(1)}, u32[]{:S(2)}, u32[]{:S(2)}) collective-permute-start(bf16[1,80,1024]{2,1,0:T(8,128)(2,1)S(1)} %bitcast.22), channel_id=1, source_target_pairs={{0,16},{4,20},{8,24},{12,28},{16,0},{20,4},{24,8},{28,12},{1,17},{... | collective-permute-start | bytes 491528 | tf_op jit(solution)/shard_map/ppermute | solution.py:522
  (47 other events, 284.2 us)
Sparse Core Ops, SparseCore 0:
  9.9 39.4 all-gather.2
  127.7 26.8 all-gather.4

commit v6 on v5

--- a/solution.py
+++ b/solution.py
@@ -161,6 +161,13 @@
     def _():
         for load in loads:
             load.wait()
+
+
+def kept_kernel(chunks, place_ref, weight_ref, normed_ref, target_ref, global_ref, momentum_ref, *refs):
+    *part_refs, kept_ref = refs
+    kept = global_ref[...] - outer_rate * outer_beta * outer_beta * momentum_ref[...]
+    kept_ref[...] = kept.astype(BF16)
+    project_kernel(chunks, place_ref, weight_ref, normed_ref, target_ref, *part_refs)
 
 
 def project_kernel(chunks, place_ref, weight_ref, normed_ref, target_ref, *part_refs):
@@ -325,28 +332,32 @@
     out_ref[...] = jnp.broadcast_to(sides[0] + sides[1], out_ref.shape)
 
 
-def weight_kernel(sizes, entries, place_ref, kept_ref, whole_ref, global_ref, momentum_ref, *refs):
+def weight_kernel(sizes, entries, place_ref, global_ref, momentum_ref, *refs):
     count = len(sizes)
-    pairs, deltas, squares = refs[: 2 * count - 2], refs[2 * count - 2 : 3 * count - 2], refs[3 * count - 2 : -3]
+    pairs, deltas, squares = refs[: 2 * count + 2], refs[2 * count + 2 : 3 * count + 2], refs[3 * count + 2 : -3]
     new_ref, new_global_ref, new_momentum_ref = refs[-3:]
     mean = tree([ref[:1, :1] for ref in squares]) / entries
     factor = jnp.minimum(1.0, clip_rms / jnp.sqrt(mean + 1e-06))
-    r = pl.program_id(0)
-    owned = new_ref.shape[0]
-    at_chip = lax.bitwise_xor(lax.div(r, 2), place_ref[3])
-    mine = lax.rem(r, 2) == place_ref[2]
+    at_chip = lax.bitwise_xor(pl.program_id(0), place_ref[3])
+    owned = new_ref.shape[0] // 2
     scale = (outer_rate * (1.0 + outer_beta)) * factor
-    lo = 0
-    for n, size in enumerate(sizes):
-        if n == 0:
-            piece = whole_ref[...]
-        else:
-            piece = jnp.where(mine, pairs[2 * n - 2][at_chip, :size, :], pairs[2 * n - 1][at_chip, :size, :])
-        kept = kept_ref[pl.ds(pl.multiple_of(r * owned + lo, 16), size), :]
-        new_ref[lo : lo + size, :] = (kept.astype(F32) - scale * piece.astype(F32)).astype(BF16)
-        lo += size
-
-    @pl.when(r == 0)
+
+    def one_core(core, side):
+        lo = 0
+        for n, size in enumerate(sizes):
+            kept = pairs[side][at_chip, lo : lo + size, :].astype(F32)
+            delta = pairs[2 * n + 2 + side][at_chip, :size, :].astype(F32)
+            new_ref[core * owned + lo : core * owned + lo + size, :] = (kept - scale * delta).astype(BF16)
+            lo += size
+
+    for own_core in range(2):
+
+        @pl.when(place_ref[2] == own_core)
+        def _():
+            one_core(own_core, 0)
+            one_core(1 - own_core, 1)
+
+    @pl.when(pl.program_id(0) == 0)
     def _():
         lo = 0
         for n, size in enumerate(sizes):
@@ -422,16 +433,14 @@
     vmem = pl.BlockSpec(memory_space=pltpu.VMEM)
     anywhere = pl.BlockSpec(memory_space=pl.ANY)
     inv_spec = pl.BlockSpec((1, tokens, 1), lambda g: (g, 0, 0))
-    large = pltpu.CompilerParams(vmem_limit_bytes=30 * 1024 * 1024)
-    small = pltpu.CompilerParams(vmem_limit_bytes=16 * 1024 * 1024)
-    cost = pl.CostEstimate(
-        flops=2 * tokens * inner * 4 * SPAN, bytes_accessed=8 * inner * tokens, transcendentals=tokens * SPAN * heads
-    )
+    large = pltpu.CompilerParams(vmem_limit_bytes=20 * 1024 * 1024)
+    small = pltpu.CompilerParams(vmem_limit_bytes=12 * 1024 * 1024)
+    small_cost = pl.CostEstimate(flops=1, bytes_accessed=1, transcendentals=0)
 
     turn = []
 
-    def run(kernel, inputs, in_specs, outs, out_specs, waits=(), **options):
-        waits = [*turn[-1:], *waits]
+    def run(kernel, inputs, in_specs, outs, out_specs, **options):
+        waits = turn[-1:]
         done = jax.ShapeDtypeStruct((8, LANES), F32)
         *results, ran = pl.pallas_call(
             in_turn(kernel, len(inputs), len(waits), len(outs)),
@@ -443,15 +452,14 @@
         turn.append(ran)
         return results
 
-    def step(kernel, operands, outs, flops, waits=(), out_specs=None, scalars=()):
+    def step(kernel, operands, outs, flops, scalars=()):
         return run(
             kernel,
             [*scalars, *operands],
             [smem] * len(scalars) + [vmem] * len(operands),
             outs,
-            out_specs or [vmem] * len(outs),
-            waits,
-            cost_estimate=pl.CostEstimate(flops=flops, bytes_accessed=4 * sum(o.size for o in outs), transcendentals=0),
+            [vmem] * len(outs),
+            cost_estimate=small_cost,
             compiler_params=small,
         )
 
@@ -460,9 +468,6 @@
 
     def in_hbm(*arrays):
         return [pltpu.with_memory_space_constraint(a, pltpu.HBM) for a in arrays]
-
-    kept = global_weight - outer_rate * outer_beta * outer_beta * momentum
-    kept_all = lax.all_gather(kept.astype(BF16), "replica", axis=0, tiled=True)
 
     def group_specs(begin):
         wide = pl.BlockSpec((tokens, width), lambda g: (0, g + begin))
@@ -481,7 +486,7 @@
         [vmem] * (len(later) + 2),
         grid=(groups,),
         scratch_shapes=[pltpu.SemaphoreType.DMA((len(later),))],
-        cost_estimate=cost,
+        cost_estimate=small_cost,
         compiler_params=large,
     )
 
@@ -499,7 +504,14 @@
 
     in_hops, across = inward(heads_over)
     parts = project([0])
-    parts += project(list(range(1, chunks)))
+    *others, kept = step(
+        functools.partial(kept_kernel, list(range(1, chunks))),
+        [weight, normed, goal, own_global, own_momentum],
+        [part] * (chunks - 1) + [shape(owned, inner)],
+        (chunks - 1) * chunk_flops,
+        scalars=[places],
+    )
+    parts += others
     first_landed = [lax.ppermute(p, "tensor", in_hops[0]) if in_hops else None for p in parts]
     sums, cots = {}, {}
 
@@ -532,7 +544,6 @@
             [c for n in batch for c in cots[n]] + [normed, weight],
             [shape(replicas // 2, rows, inner)] * 2,
             len(batch) * chunk_flops,
-            waits=[kept_all[:NOTE, :LANES]] if b == 0 else [],
             scalars=[places],
         )
         held, left = [keep, exchange(send, 1)], replicas // 2
@@ -559,15 +570,13 @@
             [own_global, squares[b - 1], *terms[b]],
             [shape(rows, inner, dtype=F32), shape(sent_rows, inner), shape(8, LANES, dtype=F32)],
             4 * rows * inner,
-            out_specs=[vmem, vmem if b else pl.BlockSpec((rows, inner)), vmem],
         )
         deltas[b], squares[b] = delta, total
-        if b == 0:
-            gathered[b] = [lax.all_gather(sent, "replica", axis=0, tiled=True)]
-        else:
-            gathered[b] = [sent[None]]
-            (bit, bits), *_ = stages(replicas)
-            gathered[b] += [exchange(gathered[b][0], mask << bit) for mask in range(1, 1 << bits)]
+        spread_rows(b, sent)
+
+    def spread_rows(b, sent):
+        (bit, bits), *_ = stages(replicas)
+        gathered[b] = [sent[None]] + [exchange(sent[None], mask << bit) for mask in range(1, 1 << bits)]
 
     def join(b):
         for at, (bit, bits) in enumerate(stages(replicas)):
@@ -595,17 +604,20 @@
             grid=(count,),
             scratch_shapes=[pltpu.VMEM((tokens, width), F32)],
             input_output_aliases=aliases,
-            cost_estimate=cost,
+            cost_estimate=small_cost,
             compiler_params=large,
         )
         return grad
 
+    spread_rows("kept", kept)
     begun = 0
     for t in range(chunks + 2):
         if t < chunks:
             sum_side(t)
         if 1 <= t <= chunks:
             sum_all(t - 1)
+        if t == chunks - 2:
+            join("kept")
         if begun < len(batches) and t - 2 == batches[begun][-1]:
             send_rows(begun)
             if begun > 0:
@@ -613,9 +625,11 @@
             begun += 1
     half = groups // 2
     end = len(batches) - 1
+    if end > 1:
+        join(0)
     grad_input = backward(0, half, None) if half else None
     own_rows(end)
-    for b in range(1, end):
+    for b in range(1 if end > 1 else 0, end):
         join(b)
     grad_input = backward(half, groups - half, grad_input)
     join(end)
@@ -625,19 +639,19 @@
     ]
 
     sizes = [len(batch) * piece for batch in batches]
-    row_spec = pl.BlockSpec((owned, inner), lambda r: (r, 0))
+    pair_spec = pl.BlockSpec((2 * owned, inner), lambda r: (r, 0))
     held_spec = pl.BlockSpec((owned, inner), lambda r: (0, 0))
-    pairs = [v for b in range(1, end + 1) for v in gathered[b]]
+    inputs = [own_global, own_momentum, *gathered["kept"], *[v for b in range(end + 1) for v in gathered[b]]]
+    inputs += [*[deltas[b] for b in range(end + 1)], *columns]
     new_weight, new_global, new_momentum = run(
         functools.partial(weight_kernel, sizes, features * inner * heads_over),
-        [places, kept_all, *in_hbm(*gathered[0]), own_global, own_momentum, *pairs, *[deltas[b] for b in range(end + 1)], *columns],
-        [smem, vmem, pl.BlockSpec((sizes[0], inner), lambda r: (r, 0)), vmem, vmem]
-        + [vmem] * (len(pairs) + len(sizes) + len(columns)),
+        [places, *inputs],
+        [smem] + [vmem] * len(inputs),
         [shape(features, inner), shape(owned, inner, dtype=F32), shape(owned, inner, dtype=F32)],
-        [row_spec, held_spec, held_spec],
-        grid=(replicas,),
-        cost_estimate=pl.CostEstimate(flops=2 * features * inner, bytes_accessed=6 * features * inner, transcendentals=0),
-        compiler_params=pltpu.CompilerParams(vmem_limit_bytes=24 * 1024 * 1024),
+        [pair_spec, held_spec, held_spec],
+        grid=(replicas // 2,),
+        cost_estimate=small_cost,
+        compiler_params=small,
     )
     return (grad_input, new_weight, new_global, new_momentum)
 

time: 217 us -> 181 us (0.83)
  local copies, waits for them, and re-layouts: 22 us -> 0.09 us
  between operations: 14.5 us -> 0.99 us
  Pallas kernels: 40.5 us -> 35.6 us
  waiting for transfers between devices: 85.3 us -> 89.1 us
  starting transfers between devices: 51.2 us -> 54.4 us
  other arithmetic: 2.54 us -> 0 us
    unnamed x68 -> x0, local copies, waits for them, and re-layouts: 21.2 us -> none
    ppermute x20 -> x28, waiting for transfers between devices: 17.8 us -> 38.7 us  [exchange(): lax.ppermute(value, 'replica', [(r, r ^ mask) for r in range(replicas)])]
    ppermute x4, waiting for transfers between devices: 42.2 us -> 30 us  [sum_all(): back = lax.ppermute(out, 'tensor', [(b, a) for a, b in pairs])]
    ppermute x20 -> x28, starting transfers between devices: 17.8 us -> 23.9 us  [exchange(): lax.ppermute(value, 'replica', [(r, r ^ mask) for r in range(replicas)])]
    pallas_call x26 -> x28, Pallas kernels: 40.5 us -> 35.6 us  [run(): pl.pallas_call(in_turn(kernel, len(inputs), len(waits), len(outs)), in_sp...]
    ppermute x4, waiting for transfers between devices: 21.2 us -> 17 us  [shards(): lax.ppermute(p, 'tensor', in_hops[0])]
    ppermute x4, starting transfers between devices: 20.7 us -> 17.9 us  [shards(): lax.ppermute(p, 'tensor', in_hops[0])]
    convert_element_type x1 -> x0, other arithmetic: 2.54 us -> none  [shards(): kept_all = lax.all_gather(kept.astype(BF16), 'replica', axis=0, tiled=True)]
  transfers between devices with their start and end apart: 37 -> 43, of which waited for: 18 -> 20; matrix products, arithmetic and copies ran while one was open for 0% -> 0% of each run, Pallas kernels for 13% -> 11%
where the time goes in v6:
time: 181 us; the launch traced here: 180 us
  waiting for transfers between devices  89.1 us (49%)
  starting transfers between devices  54.4 us (30%)
  Pallas kernels  35.6 us (20%)
    ppermute x28, waiting for transfers between devices, exchange(): lax.ppermute(value, 'replica', [(r, r ^ mask) for r in range(replicas)])  38.7 us
    pallas_call x28, Pallas kernels, run(): pl.pallas_call(in_turn(kernel, len(inputs), len(waits), len(outs)), in_sp...  35.6 us
    ppermute x4, waiting for transfers between devices, sum_all(): back = lax.ppermute(out, 'tensor', [(b, a) for a, b in pairs])  30 us
    ppermute x28, starting transfers between devices, exchange(): lax.ppermute(value, 'replica', [(r, r ^ mask) for r in range(replicas)])  23.9 us
    ppermute x4, starting transfers between devices, shards(): lax.ppermute(p, 'tensor', in_hops[0])  17.9 us
    ppermute x4, waiting for transfers between devices, shards(): lax.ppermute(p, 'tensor', in_hops[0])  17 us
    ppermute x4, starting transfers between devices, sum_all(): back = lax.ppermute(out, 'tensor', [(b, a) for a, b in pairs])  5.33 us
    ppermute x3, starting transfers between devices, shards(): lax.ppermute(column, 'tensor', [(t, t ^ mask) for t in range(heads_over)])  4.45 us
  transfers between devices with their start and end apart: 43, of which 20 were waited for; matrix products, arithmetic and copies ran while one was open for 0% of the time, Pallas kernels for 11%

profile of v6, /device:TPU:0, one launch (start us, length us, event | category | flops | bytes accessed | tf_op | source)
XLA Modules:
  0.0 180.2 jit_solution(15737901304905161243)
XLA Ops:
  0.7 6.2 %shard_map.156 = (bf16[8,256,1024]{2,1,0:T(8,128)(2,1)S(1)}, bf16[128,2048]{1,0:T(8,128)(2,1)S(1)}, f32[256,1024]{1,0:T(8,128)S(1)}, f32[256,1024]{1,0:T(8,128)S...) custom-call(f32[16,512]{1,0:T(8,128)} %bitcast.40, bf16[512,1024]{1,0:T(8,128)(2,1)} %refs_1_.1, ...), custom_call_target="tpu_custom_call" | custom-call | flops 1 | bytes 1 | tf_op jit(solution)/shard_map/pallas_call | solution.py:445
  8.4 5.0 %collective-permute-start = (bf16[512,512]{1,0:T(8,128)(2,1)S(1)}, bf16[512,512]{1,0:T(8,128)(2,1)S(1)}, u32[]{:S(2)}, u32[]{:S(2)}) collective-permute-start(bf16[512,512]{1,0:T(8,128)(2,1)S(1)} %get-tuple-element.91.refs_0_), channel_id=1, source_target_pairs={{0,1},{3,2},{4,5},{7,6},{8,9},{11,10},{12,13},{15,14},{16,17},{19,... | collective-permute-start | bytes 1572872 | tf_op jit(solution)/shard_map/ppermute | solution.py:515
  13.3 2.7 %shard_map.158 = (bf16[512,512]{1,0:T(8,128)(2,1)S(1)}, bf16[512,512]{1,0:T(8,128)(2,1)S(1)}, bf16[512,512]{1,0:T(8,128)(2,1)S(1)}, bf16[256,1024]{1,0:T(8,128)(2,1)S(1)}, f32[8,128]{1,0:T(8,128)S(1)}) custom-call(s32[5]{0:T(128)S(1)} %stack.23.refs_0_, bf16[8,256,1024]{2,1,0:T(8,128)(2,1)S(1)} %get-tuple-element.88.refs_1_.refs_6_.refs_4_.refs_11_, ...), custom_call_target="tpu_custom_call" | custom-call | flops 1 | bytes 1 | tf_op jit(solution)/shard_map/pallas_call | solution.py:445
  17.4 8.2 %collective-permute-done.refs_1_ = bf16[512,512]{1,0:T(8,128)(2,1)S(1)} collective-permute-done((bf16[512,512]{1,0:T(8,128)(2,1)S(1)}, bf16[512,512]{1,0:T(8,128)(2,1)S(1)}, u32[]{:S(2)}, u32[]{:S(2)}) %collective-permute-start) | collective-permute-done | bytes 524320 | tf_op jit(solution)/shard_map/ppermute | solution.py:515
  26.4 7.2 %collective-permute-start.5 = (bf16[512,512]{1,0:T(8,128)(2,1)S(1)}, bf16[512,512]{1,0:T(8,128)(2,1)S(1)}, u32[]{:S(2)}, u32[]{:S(2)}) collective-permute-start(bf16[512,512]{1,0:T(8,128)(2,1)S(1)} %get-tuple-element.102.refs_0_), channel_id=1, source_target_pairs={{0,1},{3,2},{4,5},{7,6},{8,9},{11,10},{12,13},{15,14},{16,17},{19,... | collective-permute-start | bytes 1572872 | tf_op jit(solution)/shard_map/ppermute | solution.py:515
  33.7 3.2 %collective-permute-done.2.refs_1_ = bf16[512,512]{1,0:T(8,128)(2,1)S(1)} collective-permute-done((bf16[512,512]{1,0:T(8,128)(2,1)S(1)}, bf16[512,512]{1,0:T(8,128)(2,1)S(1)}, u32[]{:S(2)}, u32[]{:S(2)}) %collective-permute-start.2) | collective-permute-done | bytes 524320 | tf_op jit(solution)/shard_map/ppermute | solution.py:515
  37.7 2.5 %collective-permute-start.11 = (bf16[1,256,1024]{2,1,0:T(8,128)(2,1)S(1)}, bf16[1,256,1024]{2,1,0:T(8,128)(2,1)S(1)}, u32[]{:S(2)}, u32[]{:S(2)}) collective-permute-start(bf16[1,256,1024]{2,1,0:T(8,128)(2,1)S(1)} %bitcast.23), channel_id=1, source_target_pairs={{0,24},{4,28},{8,16},{12,20},{16,8},{20,12},{24,0},{28,4},{1,25},{... | collective-permute-start | bytes 1572872 | tf_op jit(solution)/shard_map/ppermute | solution.py:534
  41.4 5.6 %collective-permute-done.5.refs_1_ = bf16[512,512]{1,0:T(8,128)(2,1)S(1)} collective-permute-done((bf16[512,512]{1,0:T(8,128)(2,1)S(1)}, bf16[512,512]{1,0:T(8,128)(2,1)S(1)}, u32[]{:S(2)}, u32[]{:S(2)}) %collective-permute-start.5) | collective-permute-done | bytes 524320 | tf_op jit(solution)/shard_map/ppermute | solution.py:515
  46.9 4.4 %collective-permute-start.8 = (bf16[512,512]{1,0:T(8,128)(2,1)S(1)}, bf16[512,512]{1,0:T(8,128)(2,1)S(1)}, u32[]{:S(2)}, u32[]{:S(2)}) collective-permute-start(bf16[512,512]{1,0:T(8,128)(2,1)S(1)} %get-tuple-element.107.refs_0_), channel_id=1, source_target_pairs={{0,1},{3,2},{4,5},{7,6},{8,9},{11,10},{12,13},{15,14},{16,17},{19,... | collective-permute-start | bytes 1572872 | tf_op jit(solution)/shard_map/ppermute | solution.py:515
  54.8 6.7 %collective-permute-done.10.refs_2_ = bf16[1,256,1024]{2,1,0:T(8,128)(2,1)S(1)} collective-permute-done((bf16[1,256,1024]{2,1,0:T(8,128)(2,1)S(1)}, bf16[1,256,1024]{2,1,0:T(8,128)(2,1)S(1)}, u32[]{:S(2)}, u32[]{:S(2)}) %collective-permute-start.10) | collective-permute-done | bytes 524320 | tf_op jit(solution)/shard_map/ppermute | solution.py:534
  63.3 3.9 %collective-permute-done.3.refs_2_.refs_13_ = bf16[512,512]{1,0:T(8,128)(2,1)S(1)} collective-permute-done((bf16[512,512]{1,0:T(8,128)(2,1)S(1)}, bf16[512,512]{1,0:T(8,128)(2,1)S(1)}, u32[]{:S(2)}, u32[]{:S(2)}) %collective-permute-start.3) | collective-permute-done | bytes 524320 | tf_op jit(solution)/shard_map/ppermute | solution.py:529
  67.2 12.7 %collective-permute-done.6.refs_4_.refs_15_ = bf16[512,512]{1,0:T(8,128)(2,1)S(1)} collective-permute-done((bf16[512,512]{1,0:T(8,128)(2,1)S(1)}, bf16[512,512]{1,0:T(8,128)(2,1)S(1)}, u32[]{:S(2)}, u32[]{:S(2)}) %collective-permute-start.6) | collective-permute-done | bytes 524320 | tf_op jit(solution)/shard_map/ppermute | solution.py:529
  85.5 13.3 %collective-permute-done.12.refs_2_.refs_17_ = bf16[512,512]{1,0:T(8,128)(2,1)S(1)} collective-permute-done((bf16[512,512]{1,0:T(8,128)(2,1)S(1)}, bf16[512,512]{1,0:T(8,128)(2,1)S(1)}, u32[]{:S(2)}, u32[]{:S(2)}) %collective-permute-start.12) | collective-permute-done | bytes 524320 | tf_op jit(solution)/shard_map/ppermute | solution.py:529
  106.5 5.0 %collective-permute-done.16.refs_3_ = bf16[1,128,1024]{2,1,0:T(8,128)(2,1)S(1)} collective-permute-done((bf16[1,128,1024]{2,1,0:T(8,128)(2,1)S(1)}, bf16[1,128,1024]{2,1,0:T(8,128)(2,1)S(1)}, u32[]{:S(2)}, u32[]{:S(2)}) %collective-permute-start.16) | collective-permute-done | bytes 262176 | tf_op jit(solution)/shard_map/ppermute | solution.py:534
  111.5 5.9 %collective-permute-done.17.refs_4_ = bf16[1,128,1024]{2,1,0:T(8,128)(2,1)S(1)} collective-permute-done((bf16[1,128,1024]{2,1,0:T(8,128)(2,1)S(1)}, bf16[1,128,1024]{2,1,0:T(8,128)(2,1)S(1)}, u32[]{:S(2)}, u32[]{:S(2)}) %collective-permute-start.17) | collective-permute-done | bytes 262176 | tf_op jit(solution)/shard_map/ppermute | solution.py:534
  122.9 2.8 %collective-permute-done.23.refs_3_ = bf16[1,64,1024]{2,1,0:T(8,128)(2,1)S(1)} collective-permute-done((bf16[1,64,1024]{2,1,0:T(8,128)(2,1)S(1)}, bf16[1,64,1024]{2,1,0:T(8,128)(2,1)S(1)}, u32[]{:S(2)}, u32[]{:S(2)}) %collective-permute-start.23) | collective-permute-done | bytes 131104 | tf_op jit(solution)/shard_map/ppermute | solution.py:534
  125.8 5.4 %collective-permute-done.24.refs_4_ = bf16[1,64,1024]{2,1,0:T(8,128)(2,1)S(1)} collective-permute-done((bf16[1,64,1024]{2,1,0:T(8,128)(2,1)S(1)}, bf16[1,64,1024]{2,1,0:T(8,128)(2,1)S(1)}, u32[]{:S(2)}, u32[]{:S(2)}) %collective-permute-start.24) | collective-permute-done | bytes 131104 | tf_op jit(solution)/shard_map/ppermute | solution.py:534
  134.9 6.1 %collective-permute-done.25.refs_5_ = bf16[1,64,1024]{2,1,0:T(8,128)(2,1)S(1)} collective-permute-done((bf16[1,64,1024]{2,1,0:T(8,128)(2,1)S(1)}, bf16[1,64,1024]{2,1,0:T(8,128)(2,1)S(1)}, u32[]{:S(2)}, u32[]{:S(2)}) %collective-permute-start.25) | collective-permute-done | bytes 131104 | tf_op jit(solution)/shard_map/ppermute | solution.py:534
  142.3 2.2 %collective-permute-start.32 = (bf16[1,64,1024]{2,1,0:T(8,128)(2,1)S(1)}, bf16[1,64,1024]{2,1,0:T(8,128)(2,1)S(1)}, u32[]{:S(2)}, u32[]{:S(2)}) collective-permute-start(bf16[1,64,1024]{2,1,0:T(8,128)(2,1)S(1)} %get-tuple-element.148), channel_id=1, source_target_pairs={{0,24},{4,28},{8,16},{12,20},{16,8},{20,12},{24,0},{28,4},{1,25},{... | collective-permute-start | bytes 393224 | tf_op jit(solution)/shard_map/ppermute | solution.py:534
  146.5 2.2 %collective-permute-done.31.refs_4_ = bf16[1,64,1024]{2,1,0:T(8,128)(2,1)S(1)} collective-permute-done((bf16[1,64,1024]{2,1,0:T(8,128)(2,1)S(1)}, bf16[1,64,1024]{2,1,0:T(8,128)(2,1)S(1)}, u32[]{:S(2)}, u32[]{:S(2)}) %collective-permute-start.31) | collective-permute-done | bytes 131104 | tf_op jit(solution)/shard_map/ppermute | solution.py:534
  149.9 5.2 %shard_map.177 = (bf16[512,1024]{1,0:T(8,128)(2,1)}, f32[8,128]{1,0:T(8,128)S(1)}) custom-call(s32[5]{0:T(128)S(1)} %stack.23.refs_0_, f32[16,512]{1,0:T(8,128)} %bitcast.41, bf16[512,1024]{1,0:T(8,128)(2,1)} %refs_2_.5, bf16[512,256]{1,0:T(8,128)(2,1)} %refs_3_.5, bf16[512,256]{1,0:T(8,128)(2,1)} %refs_4_.5, f32[1,1024]{1,0:T(1,128)} %bitcast.44, ...), custom_call_target="tpu_custom_call" | custom-call | flops 1 | bytes 1 | tf_op jit(solution)/shard_map/pallas_call | solution.py:445
  156.0 2.2 %collective-permute-start.38 = (bf16[1,80,1024]{2,1,0:T(8,128)(2,1)S(1)}, bf16[1,80,1024]{2,1,0:T(8,128)(2,1)S(1)}, u32[]{:S(2)}, u32[]{:S(2)}) collective-permute-start(bf16[1,80,1024]{2,1,0:T(8,128)(2,1)S(1)} %bitcast.31), channel_id=1, source_target_pairs={{0,24},{4,28},{8,16},{12,20},{16,8},{20,12},{24,0},{28,4},{1,25},{... | collective-permute-start | bytes 491528 | tf_op jit(solution)/shard_map/ppermute | solution.py:534
  159.5 5.3 %shard_map.180 = (bf16[512,1024]{1,0:T(8,128)(2,1)}, f32[8,128]{1,0:T(8,128)S(1)}) custom-call(s32[5]{0:T(128)S(1)} %stack.23.refs_0_, f32[16,512]{1,0:T(8,128)} %bitcast.42, bf16[512,1024]{1,0:T(8,128)(2,1)} %refs_2_.5, bf16[512,256]{1,0:T(8,128)(2,1)} %refs_3_.5, bf16[512,256]{1,0:T(8,128)(2,1)} %refs_4_.5, ...), custom_call_target="tpu_custom_call", output_to_operand_aliasing={{0}: (20, {})} | custom-call | flops 1 | bytes 1 | tf_op jit(solution)/shard_map/pallas_call | solution.py:445
  175.0 5.2 %shard_map.183 = (bf16[2048,1024]{1,0:T(8,128)(2,1)}, f32[256,1024]{1,0:T(8,128)}, f32[256,1024]{1,0:T(8,128)}, f32[8,128]{1,0:T(8,128)}) custom-call(s32[5]{0:T(128)S(1)} %stack.23.refs_0_, f32[256,1024]{1,0:T(8,128)S(1)} %get-tuple-element.92.refs_4_.refs_0_.refs_1_, f32[256,1024]{1,0:T(8,128)S(1)} %get-tuple-element.93.refs_5_.refs_2_, ...), custom_call_target="tpu_custom_call" | custom-call | flops 1 | bytes 1 | tf_op jit(solution)/shard_map/pallas_call | solution.py:445
  (92 shorter events, 49.9 us)
Async XLA Ops:
  8.4 17.2 %collective-permute-start = (bf16[512,512]{1,0:T(8,128)(2,1)S(1)}, bf16[512,512]{1,0:T(8,128)(2,1)S(1)}, u32[]{:S(2)}, u32[]{:S(2)}) collective-permute-start(bf16[512,512]{1,0:T(8,128)(2,1)S(1)} %get-tuple-element.91.refs_0_), channel_id=1, source_target_pairs={{0,1},{3,2},{4,5},{7,6},{8,9},{11,10},{12,13},{15,14},{16,17},{19,... | collective-permute-start | bytes 1572872 | tf_op jit(solution)/shard_map/ppermute | solution.py:515
  16.0 20.8 %collective-permute-start.2 = (bf16[512,512]{1,0:T(8,128)(2,1)S(1)}, bf16[512,512]{1,0:T(8,128)(2,1)S(1)}, u32[]{:S(2)}, u32[]{:S(2)}) collective-permute-start(bf16[512,512]{1,0:T(8,128)(2,1)S(1)} %get-tuple-element.97.refs_0_), channel_id=1, source_target_pairs={{0,1},{3,2},{4,5},{7,6},{8,9},{11,10},{12,13},{15,14},{16,17},{19,... | collective-permute-start | bytes 1572872 | tf_op jit(solution)/shard_map/ppermute | solution.py:515
  25.7 15.0 %collective-permute-start.1 = (bf16[512,512]{1,0:T(8,128)(2,1)S(1)}, bf16[512,512]{1,0:T(8,128)(2,1)S(1)}, u32[]{:S(2)}, u32[]{:S(2)}) collective-permute-start(bf16[512,512]{1,0:T(8,128)(2,1)S(1)} %get-tuple-element.96.refs_0_), channel_id=1, source_target_pairs={{1,2},{2,1},{5,6},{6,5},{9,10},{10,9},{13,14},{14,13},{17,18},{18,... | collective-permute-start | bytes 1572872 | tf_op jit(solution)/shard_map/ppermute | solution.py:526
  26.4 20.5 %collective-permute-start.5 = (bf16[512,512]{1,0:T(8,128)(2,1)S(1)}, bf16[512,512]{1,0:T(8,128)(2,1)S(1)}, u32[]{:S(2)}, u32[]{:S(2)}) collective-permute-start(bf16[512,512]{1,0:T(8,128)(2,1)S(1)} %get-tuple-element.102.refs_0_), channel_id=1, source_target_pairs={{0,1},{3,2},{4,5},{7,6},{8,9},{11,10},{12,13},{15,14},{16,17},{19,... | collective-permute-start | bytes 1572872 | tf_op jit(solution)/shard_map/ppermute | solution.py:515
  37.0 14.5 %collective-permute-start.4 = (bf16[512,512]{1,0:T(8,128)(2,1)S(1)}, bf16[512,512]{1,0:T(8,128)(2,1)S(1)}, u32[]{:S(2)}, u32[]{:S(2)}) collective-permute-start(bf16[512,512]{1,0:T(8,128)(2,1)S(1)} %get-tuple-element.101.refs_0_), channel_id=1, source_target_pairs={{1,2},{2,1},{5,6},{6,5},{9,10},{10,9},{13,14},{14,13},{17,18},{18,... | collective-permute-start | bytes 1572872 | tf_op jit(solution)/shard_map/ppermute | solution.py:526
  37.7 15.8 %collective-permute-start.11 = (bf16[1,256,1024]{2,1,0:T(8,128)(2,1)S(1)}, bf16[1,256,1024]{2,1,0:T(8,128)(2,1)S(1)}, u32[]{:S(2)}, u32[]{:S(2)}) collective-permute-start(bf16[1,256,1024]{2,1,0:T(8,128)(2,1)S(1)} %bitcast.23), channel_id=1, source_target_pairs={{0,24},{4,28},{8,16},{12,20},{16,8},{20,12},{24,0},{28,4},{1,25},{... | collective-permute-start | bytes 1572872 | tf_op jit(solution)/shard_map/ppermute | solution.py:534
  40.2 21.3 %collective-permute-start.10 = (bf16[1,256,1024]{2,1,0:T(8,128)(2,1)S(1)}, bf16[1,256,1024]{2,1,0:T(8,128)(2,1)S(1)}, u32[]{:S(2)}, u32[]{:S(2)}) collective-permute-start(bf16[1,256,1024]{2,1,0:T(8,128)(2,1)S(1)} %bitcast.24), channel_id=1, source_target_pairs={{0,16},{4,20},{8,24},{12,28},{16,0},{20,4},{24,8},{28,12},{1,17},{... | collective-permute-start | bytes 1572872 | tf_op jit(solution)/shard_map/ppermute | solution.py:534
  40.7 22.1 %collective-permute-start.9 = (bf16[1,256,1024]{2,1,0:T(8,128)(2,1)S(1)}, bf16[1,256,1024]{2,1,0:T(8,128)(2,1)S(1)}, u32[]{:S(2)}, u32[]{:S(2)}) collective-permute-start(bf16[1,256,1024]{2,1,0:T(8,128)(2,1)S(1)} %bitcast.25), channel_id=1, source_target_pairs={{0,8},{4,12},{8,0},{12,4},{16,24},{20,28},{24,16},{28,20},{1,9},{5... | collective-permute-start | bytes 1572872 | tf_op jit(solution)/shard_map/ppermute | solution.py:534
  46.9 16.0 %collective-permute-start.8 = (bf16[512,512]{1,0:T(8,128)(2,1)S(1)}, bf16[512,512]{1,0:T(8,128)(2,1)S(1)}, u32[]{:S(2)}, u32[]{:S(2)}) collective-permute-start(bf16[512,512]{1,0:T(8,128)(2,1)S(1)} %get-tuple-element.107.refs_0_), channel_id=1, source_target_pairs={{0,1},{3,2},{4,5},{7,6},{8,9},{11,10},{12,13},{15,14},{16,17},{19,... | collective-permute-start | bytes 1572872 | tf_op jit(solution)/shard_map/ppermute | solution.py:515
  51.5 11.6 %collective-permute-start.7 = (bf16[512,512]{1,0:T(8,128)(2,1)S(1)}, bf16[512,512]{1,0:T(8,128)(2,1)S(1)}, u32[]{:S(2)}, u32[]{:S(2)}) collective-permute-start(bf16[512,512]{1,0:T(8,128)(2,1)S(1)} %get-tuple-element.106.refs_0_), channel_id=1, source_target_pairs={{1,2},{2,1},{5,6},{6,5},{9,10},{10,9},{13,14},{14,13},{17,18},{18,... | collective-permute-start | bytes 1572872 | tf_op jit(solution)/shard_map/ppermute | solution.py:526
  53.5 13.7 %collective-permute-start.3 = (bf16[512,512]{1,0:T(8,128)(2,1)S(1)}, bf16[512,512]{1,0:T(8,128)(2,1)S(1)}, u32[]{:S(2)}, u32[]{:S(2)}) collective-permute-start(bf16[512,512]{1,0:T(8,128)(2,1)S(1)} %get-tuple-element.100.refs_1_.refs_12_), channel_id=1, source_target_pairs={{1,0},{2,3},{5,4},{6,7},{9,8},{10,11},{13,12},{14,15},{17,16},{18,... | collective-permute-start | bytes 1572872 | tf_op jit(solution)/shard_map/ppermute | solution.py:529
  61.5 18.4 %collective-permute-start.6 = (bf16[512,512]{1,0:T(8,128)(2,1)S(1)}, bf16[512,512]{1,0:T(8,128)(2,1)S(1)}, u32[]{:S(2)}, u32[]{:S(2)}) collective-permute-start(bf16[512,512]{1,0:T(8,128)(2,1)S(1)} %get-tuple-element.105.refs_3_.refs_14_), channel_id=1, source_target_pairs={{1,0},{2,3},{5,4},{6,7},{9,8},{10,11},{13,12},{14,15},{17,16},{18,... | collective-permute-start | bytes 1572872 | tf_op jit(solution)/shard_map/ppermute | solution.py:529
  82.7 16.2 %collective-permute-start.12 = (bf16[512,512]{1,0:T(8,128)(2,1)S(1)}, bf16[512,512]{1,0:T(8,128)(2,1)S(1)}, u32[]{:S(2)}, u32[]{:S(2)}) collective-permute-start(bf16[512,512]{1,0:T(8,128)(2,1)S(1)} %get-tuple-element.112.refs_1_.refs_16_), channel_id=1, source_target_pairs={{1,0},{2,3},{5,4},{6,7},{9,8},{10,11},{13,12},{14,15},{17,16},{18,... | collective-permute-start | bytes 1572872 | tf_op jit(solution)/shard_map/ppermute | solution.py:529
  100.3 17.6 %collective-permute-start.15 = (bf16[512,512]{1,0:T(8,128)(2,1)S(1)}, bf16[512,512]{1,0:T(8,128)(2,1)S(1)}, u32[]{:S(2)}, u32[]{:S(2)}) collective-permute-start(bf16[512,512]{1,0:T(8,128)(2,1)S(1)} %get-tuple-element.119.refs_1_.refs_18_), channel_id=1, source_target_pairs={{1,0},{2,3},{5,4},{6,7},{9,8},{10,11},{13,12},{14,15},{17,16},{18,... | collective-permute-start | bytes 1572872 | tf_op jit(solution)/shard_map/ppermute | solution.py:529
  101.8 69.6 %collective-permute-start.33 = (bf16[4,256,1024]{2,1,0:T(8,128)(2,1)S(1)}, bf16[4,256,1024]{2,1,0:T(8,128)(2,1)S(1)}, u32[]{:S(2)}, u32[]{:S(2)}) collective-permute-start(bf16[4,256,1024]{2,1,0:T(8,128)(2,1)S(1)} %get-tuple-element.153.refs_3_), channel_id=1, source_target_pairs={{0,4},{4,0},{8,12},{12,8},{16,20},{20,16},{24,28},{28,24},{1,5},{5... | collective-permute-start | bytes 6291464 | tf_op jit(solution)/shard_map/ppermute | solution.py:534
  103.8 13.6 %collective-permute-start.17 = (bf16[1,128,1024]{2,1,0:T(8,128)(2,1)S(1)}, bf16[1,128,1024]{2,1,0:T(8,128)(2,1)S(1)}, u32[]{:S(2)}, u32[]{:S(2)}) collective-permute-start(bf16[1,128,1024]{2,1,0:T(8,128)(2,1)S(1)} %get-tuple-element.122), channel_id=1, source_target_pairs={{0,16},{4,20},{8,24},{12,28},{16,0},{20,4},{24,8},{28,12},{1,17},{... | collective-permute-start | bytes 786440 | tf_op jit(solution)/shard_map/ppermute | solution.py:534
  103.9 13.5 %collective-permute-start.18 = (bf16[1,128,1024]{2,1,0:T(8,128)(2,1)S(1)}, bf16[1,128,1024]{2,1,0:T(8,128)(2,1)S(1)}, u32[]{:S(2)}, u32[]{:S(2)}) collective-permute-start(bf16[1,128,1024]{2,1,0:T(8,128)(2,1)S(1)} %get-tuple-element.123), channel_id=1, source_target_pairs={{0,24},{4,28},{8,16},{12,20},{16,8},{20,12},{24,0},{28,4},{1,25},{... | collective-permute-start | bytes 786440 | tf_op jit(solution)/shard_map/ppermute | solution.py:534
  119.2 13.3 %collective-permute-start.26 = (bf16[4,64,1024]{2,1,0:T(8,128)(2,1)S(1)}, bf16[4,64,1024]{2,1,0:T(8,128)(2,1)S(1)}, u32[]{:S(2)}, u32[]{:S(2)}) collective-permute-start(bf16[4,64,1024]{2,1,0:T(8,128)(2,1)S(1)} %get-tuple-element.137), channel_id=1, source_target_pairs={{0,4},{4,0},{8,12},{12,8},{16,20},{20,16},{24,28},{28,24},{1,5},{5... | collective-permute-start | bytes 1572872 | tf_op jit(solution)/shard_map/ppermute | solution.py:534
  119.9 11.2 %collective-permute-start.24 = (bf16[1,64,1024]{2,1,0:T(8,128)(2,1)S(1)}, bf16[1,64,1024]{2,1,0:T(8,128)(2,1)S(1)}, u32[]{:S(2)}, u32[]{:S(2)}) collective-permute-start(bf16[1,64,1024]{2,1,0:T(8,128)(2,1)S(1)} %get-tuple-element.133), channel_id=1, source_target_pairs={{0,16},{4,20},{8,24},{12,28},{16,0},{20,4},{24,8},{28,12},{1,17},{... | collective-permute-start | bytes 393224 | tf_op jit(solution)/shard_map/ppermute | solution.py:534
  121.4 20.9 %collective-permute-start.22 = (bf16[1,128,1024]{2,1,0:T(8,128)(2,1)S(1)}, bf16[1,128,1024]{2,1,0:T(8,128)(2,1)S(1)}, u32[]{:S(2)}, u32[]{:S(2)}) collective-permute-start(bf16[1,128,1024]{2,1,0:T(8,128)(2,1)S(1)} %bitcast.27), channel_id=1, source_target_pairs={{0,24},{4,28},{8,16},{12,20},{16,8},{20,12},{24,0},{28,4},{1,25},{... | collective-permute-start | bytes 786440 | tf_op jit(solution)/shard_map/ppermute | solution.py:534
  125.7 16.7 %collective-permute-start.21 = (bf16[1,128,1024]{2,1,0:T(8,128)(2,1)S(1)}, bf16[1,128,1024]{2,1,0:T(8,128)(2,1)S(1)}, u32[]{:S(2)}, u32[]{:S(2)}) collective-permute-start(bf16[1,128,1024]{2,1,0:T(8,128)(2,1)S(1)} %bitcast.28), channel_id=1, source_target_pairs={{0,16},{4,20},{8,24},{12,28},{16,0},{20,4},{24,8},{28,12},{1,17},{... | collective-permute-start | bytes 786440 | tf_op jit(solution)/shard_map/ppermute | solution.py:534
  131.1 13.6 %collective-permute-start.20 = (bf16[1,128,1024]{2,1,0:T(8,128)(2,1)S(1)}, bf16[1,128,1024]{2,1,0:T(8,128)(2,1)S(1)}, u32[]{:S(2)}, u32[]{:S(2)}) collective-permute-start(bf16[1,128,1024]{2,1,0:T(8,128)(2,1)S(1)} %bitcast.29), channel_id=1, source_target_pairs={{0,8},{4,12},{8,0},{12,4},{16,24},{20,28},{24,16},{28,20},{1,9},{5... | collective-permute-start | bytes 786440 | tf_op jit(solution)/shard_map/ppermute | solution.py:534
  144.8 30.1 %collective-permute-start.34 = (bf16[4,128,1024]{2,1,0:T(8,128)(2,1)S(1)}, bf16[4,128,1024]{2,1,0:T(8,128)(2,1)S(1)}, u32[]{:S(2)}, u32[]{:S(2)}) collective-permute-start(bf16[4,128,1024]{2,1,0:T(8,128)(2,1)S(1)} %get-tuple-element.154.refs_5_), channel_id=1, source_target_pairs={{0,4},{4,0},{8,12},{12,8},{16,20},{20,16},{24,28},{28,24},{1,5},{5... | collective-permute-start | bytes 3145736 | tf_op jit(solution)/shard_map/ppermute | solution.py:534
  146.0 10.0 %collective-permute-start.29 = (bf16[1,64,1024]{2,1,0:T(8,128)(2,1)S(1)}, bf16[1,64,1024]{2,1,0:T(8,128)(2,1)S(1)}, u32[]{:S(2)}, u32[]{:S(2)}) collective-permute-start(bf16[1,64,1024]{2,1,0:T(8,128)(2,1)S(1)} %bitcast.35), channel_id=1, source_target_pairs={{0,24},{4,28},{8,16},{12,20},{16,8},{20,12},{24,0},{28,4},{1,25},{... | collective-permute-start | bytes 393224 | tf_op jit(solution)/shard_map/ppermute | solution.py:534
  (19 other events, 115.0 us)

commit v7 on v6

--- a/solution.py
+++ b/solution.py
@@ -18,7 +18,6 @@
 outer_beta = 0.9
 clip_rms = 0.005
 LOG2E = 1.4426950408889634
-NOTE = 16
 
 F32 = jnp.float32
 BF16 = jnp.bfloat16
@@ -163,11 +162,8 @@
             load.wait()
 
 
-def kept_kernel(chunks, place_ref, weight_ref, normed_ref, target_ref, global_ref, momentum_ref, *refs):
-    *part_refs, kept_ref = refs
-    kept = global_ref[...] - outer_rate * outer_beta * outer_beta * momentum_ref[...]
-    kept_ref[...] = kept.astype(BF16)
-    project_kernel(chunks, place_ref, weight_ref, normed_ref, target_ref, *part_refs)
+def kept_kernel(global_ref, momentum_ref, kept_ref):
+    kept_ref[...] = (global_ref[...] - outer_rate * outer_beta * outer_beta * momentum_ref[...]).astype(BF16)
 
 
 def project_kernel(chunks, place_ref, weight_ref, normed_ref, target_ref, *part_refs):
@@ -187,6 +183,10 @@
 
 def add_kernel(a_ref, b_ref, sum_ref):
     sum_ref[...] = (a_ref[...].astype(F32) + b_ref[...].astype(F32)).astype(BF16)
+
+
+def add_squares_kernel(a_ref, b_ref, sum_ref):
+    sum_ref[...] = a_ref[...] + b_ref[...]
 
 
 def gradient_kernel(batch, place_ref, *refs):
@@ -296,17 +296,10 @@
         total = total + term[0].astype(F32)
     delta = global_ref[lo : lo + rows, :] - total / replicas
     delta_ref[...] = delta
-    sent_ref[:rows, :] = delta.astype(BF16)
+    sent_ref[...] = delta.astype(BF16)
     squares = jnp.sum(delta * delta, axis=0, keepdims=True)
     squares = before_ref[...] + jnp.broadcast_to(jnp.sum(squares, axis=1, keepdims=True), before_ref.shape)
     squares_ref[...] = squares
-    if sent_ref.shape[0] > rows:
-        at = iota((NOTE, LANES), 0)
-        value = jnp.broadcast_to(squares[:1, :], (NOTE, LANES))
-        high = value.astype(BF16).astype(F32)
-        middle = (value - high).astype(BF16).astype(F32)
-        note = jnp.where(at == 0, high, jnp.where(at == 1, middle, jnp.where(at == 2, value - high - middle, 0.0)))
-        sent_ref[rows:, :] = jnp.concatenate([note] * (inner // LANES), axis=1).astype(BF16)
 
 
 def join_kernel(*refs):
@@ -317,26 +310,11 @@
         lo += part.shape[0]
 
 
-def tree(values):
-    while len(values) > 1:
-        values = [a + b for a, b in zip(values[::2], values[1::2])]
-    return values[0]
-
-
-def squares_kernel(own_ref, other_ref, out_ref):
-    sides = []
-    for ref in (own_ref, other_ref):
-        rows = ref.shape[1] - NOTE
-        notes = [ref[p, rows:, :LANES].astype(F32) for p in range(ref.shape[0])]
-        sides.append(tree([note[0:1] + note[1:2] + note[2:3] for note in notes]))
-    out_ref[...] = jnp.broadcast_to(sides[0] + sides[1], out_ref.shape)
-
-
 def weight_kernel(sizes, entries, place_ref, global_ref, momentum_ref, *refs):
     count = len(sizes)
     pairs, deltas, squares = refs[: 2 * count + 2], refs[2 * count + 2 : 3 * count + 2], refs[3 * count + 2 : -3]
     new_ref, new_global_ref, new_momentum_ref = refs[-3:]
-    mean = tree([ref[:1, :1] for ref in squares]) / entries
+    mean = (squares[0][:1, :1] + squares[1][:1, :1]) / entries
     factor = jnp.minimum(1.0, clip_rms / jnp.sqrt(mean + 1e-06))
     at_chip = lax.bitwise_xor(pl.program_id(0), place_ref[3])
     owned = new_ref.shape[0] // 2
@@ -417,7 +395,7 @@
     width = inner // groups
     owned = features // replicas
     chunks = max(2, min(4, owned // 16))
-    batches = [list(range(max(1, chunks - 2)))] + [[n] for n in range(max(1, chunks - 2), chunks)]
+    batches = [list(range(chunks // 2)), list(range(chunks // 2, chunks))]
     piece = owned // chunks
     span_rows = replicas * piece
     place = lax.axis_index("tensor")
@@ -439,8 +417,8 @@
 
     turn = []
 
-    def run(kernel, inputs, in_specs, outs, out_specs, **options):
-        waits = turn[-1:]
+    def run(kernel, inputs, in_specs, outs, out_specs, waits=(), **options):
+        waits = [*turn[-1:], *waits]
         done = jax.ShapeDtypeStruct((8, LANES), F32)
         *results, ran = pl.pallas_call(
             in_turn(kernel, len(inputs), len(waits), len(outs)),
@@ -452,13 +430,14 @@
         turn.append(ran)
         return results
 
-    def step(kernel, operands, outs, flops, scalars=()):
+    def step(kernel, operands, outs, scalars=(), waits=()):
         return run(
             kernel,
             [*scalars, *operands],
             [smem] * len(scalars) + [vmem] * len(operands),
             outs,
             [vmem] * len(outs),
+            waits,
             cost_estimate=small_cost,
             compiler_params=small,
         )
@@ -475,9 +454,29 @@
         dt = pl.BlockSpec((heads // groups, tokens), lambda g: (g + begin, 0))
         return wide, state, dt, pl.BlockSpec((1, width), lambda g: (0, g + begin))
 
+    def exchange(value, mask):
+        return lax.ppermute(value, "replica", [(r, r ^ mask) for r in range(replicas)])
+
+    gathered = {}
+
+    def spread_rows(b, sent):
+        (bit, bits), *_ = stages(replicas)
+        gathered[b] = [sent[None]] + [exchange(sent[None], mask << bit) for mask in range(1, 1 << bits)]
+
+    def join(b, waits=()):
+        for at, (bit, bits) in enumerate(stages(replicas)):
+            if at > 0:
+                gathered[b] = [held] + [exchange(held, mask << bit) for mask in range(1, 1 << bits)]
+            one = gathered[b][0]
+            out = shape(len(gathered[b]) * one.shape[0], *one.shape[1:])
+            (held,) = step(join_kernel, gathered[b], [out], waits=waits if at == 0 else ())
+        gathered[b] = [held, exchange(held, 1)]
+
     by_group, by_state, dt_spec, gain_spec = group_specs(0)
     shared = in_hbm(dt_rows, gate_z, b_proj, c_proj, gain, a_log, dt_bias, skip_d)
     later = [stored, target, global_weight, momentum]
+    (kept,) = step(kept_kernel, in_hbm(global_weight, momentum), [shape(owned, inner)])
+    spread_rows("kept", kept)
     weight, goal, own_global, own_momentum, normed, inv = run(
         functools.partial(forward_kernel, len(later)),
         [shared[0], *in_hbm(x_in), *shared[1:], *in_hbm(*later)],
@@ -491,27 +490,14 @@
     )
 
     part = shape(span_rows, tokens)
-    chunk_flops = 2 * tokens * span_rows * inner
 
     def project(picked):
-        return step(
-            functools.partial(project_kernel, picked),
-            [weight, normed, goal],
-            [part] * len(picked),
-            len(picked) * chunk_flops,
-            scalars=[places],
-        )
+        kernel = functools.partial(project_kernel, picked)
+        return step(kernel, [weight, normed, goal], [part] * len(picked), scalars=[places])
 
     in_hops, across = inward(heads_over)
     parts = project([0])
-    *others, kept = step(
-        functools.partial(kept_kernel, list(range(1, chunks))),
-        [weight, normed, goal, own_global, own_momentum],
-        [part] * (chunks - 1) + [shape(owned, inner)],
-        (chunks - 1) * chunk_flops,
-        scalars=[places],
-    )
-    parts += others
+    parts += project(list(range(1, chunks)))
     first_landed = [lax.ppermute(p, "tensor", in_hops[0]) if in_hops else None for p in parts]
     sums, cots = {}, {}
 
@@ -519,21 +505,19 @@
         held = parts[n]
         for at, pairs in enumerate(in_hops):
             landed = first_landed[n] if at == 0 else lax.ppermute(held, "tensor", pairs)
-            (held,) = step(add_kernel, [held, landed], [part], part.size)
+            (held,) = step(add_kernel, [held, landed], [part])
         sums[n] = held
 
     def sum_all(n):
-        (mid,) = step(add_kernel, [sums[n], lax.ppermute(sums[n], "tensor", across)], [part], part.size)
+        (mid,) = step(add_kernel, [sums[n], lax.ppermute(sums[n], "tensor", across)], [part])
         out = mid
         for pairs in reversed(in_hops):
             back = lax.ppermute(out, "tensor", [(b, a) for a, b in pairs])
             out = back if pairs is in_hops[0] else jnp.where(in_middle, mid, back)
         cots[n] = (mid, out)
 
-    def exchange(value, mask):
-        return lax.ppermute(value, "replica", [(r, r ^ mask) for r in range(replicas)])
-
-    terms, deltas, gathered = {}, {}, {}
+    terms, deltas = {}, {}
+    tile = shape(8, LANES, dtype=F32)
     squares = {-1: jnp.zeros((8, LANES), F32)}
 
     def send_rows(b):
@@ -543,7 +527,6 @@
             functools.partial(gradient_kernel, batch),
             [c for n in batch for c in cots[n]] + [normed, weight],
             [shape(replicas // 2, rows, inner)] * 2,
-            len(batch) * chunk_flops,
             scalars=[places],
         )
         held, left = [keep, exchange(send, 1)], replicas // 2
@@ -555,36 +538,21 @@
                 functools.partial(pick_kernel, len(cut)),
                 cut,
                 [shape(left, rows, inner)] * ways,
-                replicas * rows * inner,
                 scalars=[places.at[4].set(1 << (bit - 1))] if bit > 1 else [places],
             )
             held = [picked[0]] + [exchange(picked[mask], mask << bit) for mask in range(1, ways)]
         terms[b] = held
 
-    def own_rows(b):
+    def own_rows(b, waits=()):
         batch = batches[b]
         rows = len(batch) * piece
-        sent_rows = rows + NOTE if b == len(batches) - 1 else rows
-        delta, sent, total = step(
+        deltas[b], sent, squares[b] = step(
             functools.partial(delta_kernel, len(terms[b]), batch[0] * piece, replicas),
             [own_global, squares[b - 1], *terms[b]],
-            [shape(rows, inner, dtype=F32), shape(sent_rows, inner), shape(8, LANES, dtype=F32)],
-            4 * rows * inner,
+            [shape(rows, inner, dtype=F32), shape(rows, inner), tile],
+            waits=waits,
         )
-        deltas[b], squares[b] = delta, total
         spread_rows(b, sent)
-
-    def spread_rows(b, sent):
-        (bit, bits), *_ = stages(replicas)
-        gathered[b] = [sent[None]] + [exchange(sent[None], mask << bit) for mask in range(1, 1 << bits)]
-
-    def join(b):
-        for at, (bit, bits) in enumerate(stages(replicas)):
-            if at > 0:
-                gathered[b] = [held] + [exchange(held, mask << bit) for mask in range(1, 1 << bits)]
-            one = gathered[b][0]
-            (held,) = step(join_kernel, gathered[b], [shape(len(gathered[b]) * one.shape[0], *one.shape[1:])], one.size)
-        gathered[b] = [held, exchange(held, 1)]
 
     def backward(begin, count, so_far):
         wide, state, dt, gain_here = group_specs(begin)
@@ -609,40 +577,36 @@
         )
         return grad
 
-    spread_rows("kept", kept)
-    begun = 0
+    first, second = range(2)
     for t in range(chunks + 2):
         if t < chunks:
             sum_side(t)
+        if t == 0:
+            join("kept")
         if 1 <= t <= chunks:
             sum_all(t - 1)
-        if t == chunks - 2:
-            join("kept")
-        if begun < len(batches) and t - 2 == batches[begun][-1]:
-            send_rows(begun)
-            if begun > 0:
-                own_rows(begun - 1)
-            begun += 1
+        if t - 2 == batches[first][-1]:
+            send_rows(first)
+    own_rows(first, gathered["kept"][1:])
+    send_rows(second)
     half = groups // 2
-    end = len(batches) - 1
-    if end > 1:
-        join(0)
     grad_input = backward(0, half, None) if half else None
-    own_rows(end)
-    for b in range(1 if end > 1 else 0, end):
-        join(b)
+    join(first)
     grad_input = backward(half, groups - half, grad_input)
-    join(end)
-    (column,) = step(squares_kernel, gathered[end], [shape(8, LANES, dtype=F32)], NOTE * inner)
-    columns = [column] + [
-        lax.ppermute(column, "tensor", [(t, t ^ mask) for t in range(heads_over)]) for mask in range(1, heads_over)
-    ]
+    own_rows(second, gathered[first][1:])
+    total = squares[second]
+    for axis, bits in (("tensor", range(heads_over.bit_length() - 1)), ("replica", range(1, replicas.bit_length() - 1))):
+        for bit in bits:
+            pairs = [(r, r ^ (1 << bit)) for r in range(lax.axis_size(axis))]
+            (total,) = step(add_squares_kernel, [total, lax.ppermute(total, axis, pairs)], [tile])
+    join(second)
+    columns = [total, exchange(total, 1)]
 
     sizes = [len(batch) * piece for batch in batches]
     pair_spec = pl.BlockSpec((2 * owned, inner), lambda r: (r, 0))
     held_spec = pl.BlockSpec((owned, inner), lambda r: (0, 0))
-    inputs = [own_global, own_momentum, *gathered["kept"], *[v for b in range(end + 1) for v in gathered[b]]]
-    inputs += [*[deltas[b] for b in range(end + 1)], *columns]
+    inputs = [own_global, own_momentum, *gathered["kept"], *gathered[first], *gathered[second]]
+    inputs += [deltas[first], deltas[second], *columns]
     new_weight, new_global, new_momentum = run(
         functools.partial(weight_kernel, sizes, features * inner * heads_over),
         [places, *inputs],

time: 181 us -> 167 us (0.923)
  waiting for transfers between devices: 89.1 us -> 79.4 us
  starting transfers between devices: 54.4 us -> 50.7 us
    ppermute x4, waiting for transfers between devices: 30 us -> 22 us  [sum_all(): back = lax.ppermute(out, 'tensor', [(b, a) for a, b in pairs])]
    ppermute x28 -> x21, starting transfers between devices: 23.9 us -> 18.6 us  [exchange(): lax.ppermute(value, 'replica', [(r, r ^ mask) for r in range(replicas)])]
    ppermute x3 -> x4, waiting for transfers between devices: 3.45 us -> 8.64 us  [shards(): lax.ppermute(total, axis, pairs)]
    ppermute x28 -> x21, waiting for transfers between devices: 38.7 us -> 34.3 us  [exchange(): lax.ppermute(value, 'replica', [(r, r ^ mask) for r in range(replicas)])]
    ppermute x3 -> x4, starting transfers between devices: 4.45 us -> 7.67 us  [shards(): lax.ppermute(total, axis, pairs)]
    ppermute x4, waiting for transfers between devices: 17 us -> 14.3 us  [shards(): lax.ppermute(p, 'tensor', in_hops[0])]
  transfers between devices with their start and end apart: 43 -> 37, of which waited for: 20 -> 20; matrix products, arithmetic and copies ran while one was open for 0% -> 0% of each run, Pallas kernels for 11% -> 11%
where the time goes in v7:
time: 167 us
  waiting for transfers between devices  79.4 us (48%)
  starting transfers between devices  50.7 us (30%)
  Pallas kernels  35.4 us (21%)
    pallas_call x28, Pallas kernels, run(): pl.pallas_call(in_turn(kernel, len(inputs), len(waits), len(outs)), in_sp...  35.4 us
    ppermute x21, waiting for transfers between devices, exchange(): lax.ppermute(value, 'replica', [(r, r ^ mask) for r in range(replicas)])  34.3 us
    ppermute x4, waiting for transfers between devices, sum_all(): back = lax.ppermute(out, 'tensor', [(b, a) for a, b in pairs])  22 us
    ppermute x21, starting transfers between devices, exchange(): lax.ppermute(value, 'replica', [(r, r ^ mask) for r in range(replicas)])  18.6 us
    ppermute x4, starting transfers between devices, shards(): lax.ppermute(p, 'tensor', in_hops[0])  16.4 us
    ppermute x4, waiting for transfers between devices, shards(): lax.ppermute(p, 'tensor', in_hops[0])  14.3 us
    ppermute x4, waiting for transfers between devices, shards(): lax.ppermute(total, axis, pairs)  8.64 us
    ppermute x4, starting transfers between devices, shards(): lax.ppermute(total, axis, pairs)  7.67 us
  transfers between devices with their start and end apart: 37, of which 20 were waited for; matrix products, arithmetic and copies ran while one was open for 0% of the time, Pallas kernels for 11%

profile of v7, /device:TPU:0, one launch (start us, length us, event | category | flops | bytes accessed | tf_op | source)
XLA Modules:
  0.0 166.6 jit_solution(8942734425764338736)
XLA Ops:
  2.4 6.2 %shard_map.157 = (bf16[8,256,1024]{2,1,0:T(8,128)(2,1)S(1)}, bf16[128,2048]{1,0:T(8,128)(2,1)S(1)}, f32[256,1024]{1,0:T(8,128)S(1)}, f32[256,1024]{1,0:T(8,128)S...) custom-call(f32[16,512]{1,0:T(8,128)} %bitcast.31, bf16[512,1024]{1,0:T(8,128)(2,1)} %refs_1_.3, ...), custom_call_target="tpu_custom_call" | custom-call | flops 1 | bytes 1 | tf_op jit(solution)/shard_map/pallas_call | solution.py:423
  10.0 5.0 %collective-permute-start = (bf16[512,512]{1,0:T(8,128)(2,1)S(1)}, bf16[512,512]{1,0:T(8,128)(2,1)S(1)}, u32[]{:S(2)}, u32[]{:S(2)}) collective-permute-start(bf16[512,512]{1,0:T(8,128)(2,1)S(1)} %get-tuple-element.86.refs_0_), channel_id=1, source_target_pairs={{0,1},{3,2},{4,5},{7,6},{8,9},{11,10},{12,13},{15,14},{16,17},{19,... | collective-permute-start | bytes 1572872 | tf_op jit(solution)/shard_map/ppermute | solution.py:501
  18.6 2.5 %shard_map.159 = (bf16[512,512]{1,0:T(8,128)(2,1)S(1)}, bf16[512,512]{1,0:T(8,128)(2,1)S(1)}, bf16[512,512]{1,0:T(8,128)(2,1)S(1)}, f32[8,128]{1,0:T(8,128)S(1)}) custom-call(s32[5]{0:T(128)S(1)} %stack.23.refs_0_, bf16[8,256,1024]{2,1,0:T(8,128)(2,1)S(1)} %get-tuple-element.83.refs_1_.refs_6_.refs_11_, ...), custom_call_target="tpu_custom_call" | custom-call | flops 1 | bytes 1 | tf_op jit(solution)/shard_map/pallas_call | solution.py:423
  22.4 4.9 %collective-permute-done.refs_1_ = bf16[512,512]{1,0:T(8,128)(2,1)S(1)} collective-permute-done((bf16[512,512]{1,0:T(8,128)(2,1)S(1)}, bf16[512,512]{1,0:T(8,128)(2,1)S(1)}, u32[]{:S(2)}, u32[]{:S(2)}) %collective-permute-start) | collective-permute-done | bytes 524320 | tf_op jit(solution)/shard_map/ppermute | solution.py:501
  29.9 5.4 %collective-permute-start.8 = (bf16[512,512]{1,0:T(8,128)(2,1)S(1)}, bf16[512,512]{1,0:T(8,128)(2,1)S(1)}, u32[]{:S(2)}, u32[]{:S(2)}) collective-permute-start(bf16[512,512]{1,0:T(8,128)(2,1)S(1)} %get-tuple-element.97.refs_0_), channel_id=1, source_target_pairs={{0,1},{3,2},{4,5},{7,6},{8,9},{11,10},{12,13},{15,14},{16,17},{19,... | collective-permute-start | bytes 1572872 | tf_op jit(solution)/shard_map/ppermute | solution.py:501
  35.3 5.6 %collective-permute-done.4.refs_2_ = bf16[1,256,1024]{2,1,0:T(8,128)(2,1)S(1)} collective-permute-done((bf16[1,256,1024]{2,1,0:T(8,128)(2,1)S(1)}, bf16[1,256,1024]{2,1,0:T(8,128)(2,1)S(1)}, u32[]{:S(2)}, u32[]{:S(2)}) %collective-permute-start.4) | collective-permute-done | bytes 524320 | tf_op jit(solution)/shard_map/ppermute | solution.py:458
  42.0 4.7 %collective-permute-start.11 = (bf16[512,512]{1,0:T(8,128)(2,1)S(1)}, bf16[512,512]{1,0:T(8,128)(2,1)S(1)}, u32[]{:S(2)}, u32[]{:S(2)}) collective-permute-start(bf16[512,512]{1,0:T(8,128)(2,1)S(1)} %get-tuple-element.102.refs_0_), channel_id=1, source_target_pairs={{0,1},{3,2},{4,5},{7,6},{8,9},{11,10},{12,13},{15,14},{16,17},{19,... | collective-permute-start | bytes 1572872 | tf_op jit(solution)/shard_map/ppermute | solution.py:501
  52.0 7.8 %collective-permute-done.11.refs_1_ = bf16[512,512]{1,0:T(8,128)(2,1)S(1)} collective-permute-done((bf16[512,512]{1,0:T(8,128)(2,1)S(1)}, bf16[512,512]{1,0:T(8,128)(2,1)S(1)}, u32[]{:S(2)}, u32[]{:S(2)}) %collective-permute-start.11) | collective-permute-done | bytes 524320 | tf_op jit(solution)/shard_map/ppermute | solution.py:501
  60.1 3.3 %collective-permute-done.6.refs_2_.refs_13_ = bf16[512,512]{1,0:T(8,128)(2,1)S(1)} collective-permute-done((bf16[512,512]{1,0:T(8,128)(2,1)S(1)}, bf16[512,512]{1,0:T(8,128)(2,1)S(1)}, u32[]{:S(2)}, u32[]{:S(2)}) %collective-permute-start.6) | collective-permute-done | bytes 524320 | tf_op jit(solution)/shard_map/ppermute | solution.py:515
  63.5 10.5 %collective-permute-done.9.refs_4_.refs_15_ = bf16[512,512]{1,0:T(8,128)(2,1)S(1)} collective-permute-done((bf16[512,512]{1,0:T(8,128)(2,1)S(1)}, bf16[512,512]{1,0:T(8,128)(2,1)S(1)}, u32[]{:S(2)}, u32[]{:S(2)}) %collective-permute-start.9) | collective-permute-done | bytes 524320 | tf_op jit(solution)/shard_map/ppermute | solution.py:515
  84.7 5.7 %collective-permute-done.16.refs_3_ = bf16[1,128,1024]{2,1,0:T(8,128)(2,1)S(1)} collective-permute-done((bf16[1,128,1024]{2,1,0:T(8,128)(2,1)S(1)}, bf16[1,128,1024]{2,1,0:T(8,128)(2,1)S(1)}, u32[]{:S(2)}, u32[]{:S(2)}) %collective-permute-start.16) | collective-permute-done | bytes 262176 | tf_op jit(solution)/shard_map/ppermute | solution.py:458
  90.3 6.0 %collective-permute-done.17.refs_4_ = bf16[1,128,1024]{2,1,0:T(8,128)(2,1)S(1)} collective-permute-done((bf16[1,128,1024]{2,1,0:T(8,128)(2,1)S(1)}, bf16[1,128,1024]{2,1,0:T(8,128)(2,1)S(1)}, u32[]{:S(2)}, u32[]{:S(2)}) %collective-permute-start.17) | collective-permute-done | bytes 262176 | tf_op jit(solution)/shard_map/ppermute | solution.py:458
  96.8 8.2 %collective-permute-done.15.refs_4_.refs_19_ = bf16[512,512]{1,0:T(8,128)(2,1)S(1)} collective-permute-done((bf16[512,512]{1,0:T(8,128)(2,1)S(1)}, bf16[512,512]{1,0:T(8,128)(2,1)S(1)}, u32[]{:S(2)}, u32[]{:S(2)}) %collective-permute-start.15) | collective-permute-done | bytes 524320 | tf_op jit(solution)/shard_map/ppermute | solution.py:515
  105.0 2.0 %shard_map.172 = (bf16[4,128,1024]{2,1,0:T(8,128)(2,1)S(1)}, bf16[4,128,1024]{2,1,0:T(8,128)(2,1)S(1)}, f32[8,128]{1,0:T(8,128)S(1)}) custom-call(s32[5]{0:T(128)S(1)} %stack.23.refs_0_, bf16[512,512]{1,0:T(8,128)(2,1)S(1)} %get-tuple-element.105.refs_1_.refs_16_, bf16[512,512]{1,0:T(8,128)(2,1)S(1)} %collective-permute-done.12.refs_2_.refs_17_, ...), custom_call_target="tpu_custom_call" | custom-call | flops 1 | bytes 1 | tf_op jit(solution)/shard_map/pallas_call | solution.py:423
  111.4 5.3 %shard_map.174 = (bf16[512,1024]{1,0:T(8,128)(2,1)}, f32[8,128]{1,0:T(8,128)S(1)}) custom-call(s32[5]{0:T(128)S(1)} %stack.23.refs_0_, f32[16,512]{1,0:T(8,128)} %bitcast.32, bf16[512,1024]{1,0:T(8,128)(2,1)} %refs_2_.5, bf16[512,256]{1,0:T(8,128)(2,1)} %refs_3_.5, bf16[512,256]{1,0:T(8,128)(2,1)} %refs_4_.5, f32[1,1024]{1,0:T(1,128)} %bitcast.35, ...), custom_call_target="tpu_custom_call" | custom-call | flops 1 | bytes 1 | tf_op jit(solution)/shard_map/pallas_call | solution.py:423
  116.7 5.9 %collective-permute-done.22.refs_2_ = bf16[1,128,1024]{2,1,0:T(8,128)(2,1)S(1)} collective-permute-done((bf16[1,128,1024]{2,1,0:T(8,128)(2,1)S(1)}, bf16[1,128,1024]{2,1,0:T(8,128)(2,1)S(1)}, u32[]{:S(2)}, u32[]{:S(2)}) %collective-permute-start.22) | collective-permute-done | bytes 262176 | tf_op jit(solution)/shard_map/ppermute | solution.py:458
  126.3 5.2 %shard_map.176 = (bf16[512,1024]{1,0:T(8,128)(2,1)}, f32[8,128]{1,0:T(8,128)S(1)}) custom-call(s32[5]{0:T(128)S(1)} %stack.23.refs_0_, f32[16,512]{1,0:T(8,128)} %bitcast.33, bf16[512,1024]{1,0:T(8,128)(2,1)} %refs_2_.5, bf16[512,256]{1,0:T(8,128)(2,1)} %refs_3_.5, bf16[512,256]{1,0:T(8,128)(2,1)} %refs_4_.5, ...), custom_call_target="tpu_custom_call", output_to_operand_aliasing={{0}: (20, {})} | custom-call | flops 1 | bytes 1 | tf_op jit(solution)/shard_map/pallas_call | solution.py:423
  132.0 4.5 %collective-permute-done.26.refs_4_ = bf16[1,128,1024]{2,1,0:T(8,128)(2,1)S(1)} collective-permute-done((bf16[1,128,1024]{2,1,0:T(8,128)(2,1)S(1)}, bf16[1,128,1024]{2,1,0:T(8,128)(2,1)S(1)}, u32[]{:S(2)}, u32[]{:S(2)}) %collective-permute-start.26) | collective-permute-done | bytes 262176 | tf_op jit(solution)/shard_map/ppermute | solution.py:458
  142.0 3.0 %collective-permute-start.31 = (f32[8,128]{1,0:T(8,128)S(1)}, f32[8,128]{1,0:T(8,128)S(1)}, u32[]{:S(2)}, u32[]{:S(2)}) collective-permute-start(f32[8,128]{1,0:T(8,128)S(1)} %get-tuple-element.139.refs_0_), channel_id=1, source_target_pairs={{0,1},{1,0},{2,3},{3,2},{4,5},{5,4},{6,7},{7,6},{8,9},{9,8},{10,11... | collective-permute-start | bytes 12296 | tf_op jit(solution)/shard_map/ppermute | solution.py:601
  148.5 2.6 %collective-permute-done.32.refs_1_ = f32[8,128]{1,0:T(8,128)S(1)} collective-permute-done((f32[8,128]{1,0:T(8,128)S(1)}, f32[8,128]{1,0:T(8,128)S(1)}, u32[]{:S(2)}, u32[]{:S(2)}) %collective-permute-start.32) | collective-permute-done | bytes 4128 | tf_op jit(solution)/shard_map/ppermute | solution.py:601
  152.4 2.4 %collective-permute-done.33.refs_1_ = f32[8,128]{1,0:T(8,128)S(1)} collective-permute-done((f32[8,128]{1,0:T(8,128)S(1)}, f32[8,128]{1,0:T(8,128)S(1)}, u32[]{:S(2)}, u32[]{:S(2)}) %collective-permute-start.33) | collective-permute-done | bytes 4128 | tf_op jit(solution)/shard_map/ppermute | solution.py:601
  156.2 2.1 %collective-permute-done.34.refs_1_ = f32[8,128]{1,0:T(8,128)S(1)} collective-permute-done((f32[8,128]{1,0:T(8,128)S(1)}, f32[8,128]{1,0:T(8,128)S(1)}, u32[]{:S(2)}, u32[]{:S(2)}) %collective-permute-start.34) | collective-permute-done | bytes 4128 | tf_op jit(solution)/shard_map/ppermute | solution.py:601
  159.0 2.2 %collective-permute-done.36.refs_12_ = f32[8,128]{1,0:T(8,128)S(1)} collective-permute-done((f32[8,128]{1,0:T(8,128)S(1)}, f32[8,128]{1,0:T(8,128)S(1)}, u32[]{:S(2)}, u32[]{:S(2)}) %collective-permute-start.36) | collective-permute-done | bytes 4128 | tf_op jit(solution)/shard_map/ppermute | solution.py:458
  161.2 5.4 %shard_map.183 = (bf16[2048,1024]{1,0:T(8,128)(2,1)}, f32[256,1024]{1,0:T(8,128)}, f32[256,1024]{1,0:T(8,128)}, f32[8,128]{1,0:T(8,128)}) custom-call(s32[5]{0:T(128)S(1)} %stack.23.refs_0_, f32[256,1024]{1,0:T(8,128)S(1)} %get-tuple-element.113.refs_0_.refs_1_, f32[256,1024]{1,0:T(8,128)S(1)} %get-tuple-element.130.refs_2_, ...), custom_call_target="tpu_custom_call" | custom-call | flops 1 | bytes 1 | tf_op jit(solution)/shard_map/pallas_call | solution.py:423
  (80 shorter events, 49.3 us)
Async XLA Ops:
  10.0 17.2 %collective-permute-start = (bf16[512,512]{1,0:T(8,128)(2,1)S(1)}, bf16[512,512]{1,0:T(8,128)(2,1)S(1)}, u32[]{:S(2)}, u32[]{:S(2)}) collective-permute-start(bf16[512,512]{1,0:T(8,128)(2,1)S(1)} %get-tuple-element.86.refs_0_), channel_id=1, source_target_pairs={{0,1},{3,2},{4,5},{7,6},{8,9},{11,10},{12,13},{15,14},{16,17},{19,... | collective-permute-start | bytes 1572872 | tf_op jit(solution)/shard_map/ppermute | solution.py:501
  15.0 14.9 %collective-permute-start.3 = (bf16[1,256,1024]{2,1,0:T(8,128)(2,1)S(1)}, bf16[1,256,1024]{2,1,0:T(8,128)(2,1)S(1)}, u32[]{:S(2)}, u32[]{:S(2)}) collective-permute-start(bf16[1,256,1024]{2,1,0:T(8,128)(2,1)S(1)} %bitcast.18), channel_id=1, source_target_pairs={{0,8},{4,12},{8,0},{12,4},{16,24},{20,28},{24,16},{28,20},{1,9},{5... | collective-permute-start | bytes 1572872 | tf_op jit(solution)/shard_map/ppermute | solution.py:458
  16.6 24.3 %collective-permute-start.4 = (bf16[1,256,1024]{2,1,0:T(8,128)(2,1)S(1)}, bf16[1,256,1024]{2,1,0:T(8,128)(2,1)S(1)}, u32[]{:S(2)}, u32[]{:S(2)}) collective-permute-start(bf16[1,256,1024]{2,1,0:T(8,128)(2,1)S(1)} %bitcast.19), channel_id=1, source_target_pairs={{0,16},{4,20},{8,24},{12,28},{16,0},{20,4},{24,8},{28,12},{1,17},{... | collective-permute-start | bytes 1572872 | tf_op jit(solution)/shard_map/ppermute | solution.py:458
  18.1 22.8 %collective-permute-start.5 = (bf16[1,256,1024]{2,1,0:T(8,128)(2,1)S(1)}, bf16[1,256,1024]{2,1,0:T(8,128)(2,1)S(1)}, u32[]{:S(2)}, u32[]{:S(2)}) collective-permute-start(bf16[1,256,1024]{2,1,0:T(8,128)(2,1)S(1)} %bitcast.20), channel_id=1, source_target_pairs={{0,24},{4,28},{8,16},{12,20},{16,8},{20,12},{24,0},{28,4},{1,25},{... | collective-permute-start | bytes 1572872 | tf_op jit(solution)/shard_map/ppermute | solution.py:458
  21.1 20.0 %collective-permute-start.2 = (bf16[512,512]{1,0:T(8,128)(2,1)S(1)}, bf16[512,512]{1,0:T(8,128)(2,1)S(1)}, u32[]{:S(2)}, u32[]{:S(2)}) collective-permute-start(bf16[512,512]{1,0:T(8,128)(2,1)S(1)} %get-tuple-element.90.refs_0_), channel_id=1, source_target_pairs={{0,1},{3,2},{4,5},{7,6},{8,9},{11,10},{12,13},{15,14},{16,17},{19,... | collective-permute-start | bytes 1572872 | tf_op jit(solution)/shard_map/ppermute | solution.py:501
  27.4 19.3 %collective-permute-start.1 = (bf16[512,512]{1,0:T(8,128)(2,1)S(1)}, bf16[512,512]{1,0:T(8,128)(2,1)S(1)}, u32[]{:S(2)}, u32[]{:S(2)}) collective-permute-start(bf16[512,512]{1,0:T(8,128)(2,1)S(1)} %get-tuple-element.89.refs_0_), channel_id=1, source_target_pairs={{1,2},{2,1},{5,6},{6,5},{9,10},{10,9},{13,14},{14,13},{17,18},{18,... | collective-permute-start | bytes 1572872 | tf_op jit(solution)/shard_map/ppermute | solution.py:512
  29.9 19.8 %collective-permute-start.8 = (bf16[512,512]{1,0:T(8,128)(2,1)S(1)}, bf16[512,512]{1,0:T(8,128)(2,1)S(1)}, u32[]{:S(2)}, u32[]{:S(2)}) collective-permute-start(bf16[512,512]{1,0:T(8,128)(2,1)S(1)} %get-tuple-element.97.refs_0_), channel_id=1, source_target_pairs={{0,1},{3,2},{4,5},{7,6},{8,9},{11,10},{12,13},{15,14},{16,17},{19,... | collective-permute-start | bytes 1572872 | tf_op jit(solution)/shard_map/ppermute | solution.py:501
  41.9 42.3 %collective-permute-start.19 = (bf16[4,256,1024]{2,1,0:T(8,128)(2,1)S(1)}, bf16[4,256,1024]{2,1,0:T(8,128)(2,1)S(1)}, u32[]{:S(2)}, u32[]{:S(2)}) collective-permute-start(bf16[4,256,1024]{2,1,0:T(8,128)(2,1)S(1)} %get-tuple-element.119.refs_3_), channel_id=1, source_target_pairs={{0,4},{4,0},{8,12},{12,8},{16,20},{20,16},{24,28},{28,24},{1,5},{5... | collective-permute-start | bytes 6291464 | tf_op jit(solution)/shard_map/ppermute | solution.py:458
  42.0 17.9 %collective-permute-start.11 = (bf16[512,512]{1,0:T(8,128)(2,1)S(1)}, bf16[512,512]{1,0:T(8,128)(2,1)S(1)}, u32[]{:S(2)}, u32[]{:S(2)}) collective-permute-start(bf16[512,512]{1,0:T(8,128)(2,1)S(1)} %get-tuple-element.102.refs_0_), channel_id=1, source_target_pairs={{0,1},{3,2},{4,5},{7,6},{8,9},{11,10},{12,13},{15,14},{16,17},{19,... | collective-permute-start | bytes 1572872 | tf_op jit(solution)/shard_map/ppermute | solution.py:501
  46.8 16.7 %collective-permute-start.6 = (bf16[512,512]{1,0:T(8,128)(2,1)S(1)}, bf16[512,512]{1,0:T(8,128)(2,1)S(1)}, u32[]{:S(2)}, u32[]{:S(2)}) collective-permute-start(bf16[512,512]{1,0:T(8,128)(2,1)S(1)} %get-tuple-element.95.refs_1_.refs_12_), channel_id=1, source_target_pairs={{1,0},{2,3},{5,4},{6,7},{9,8},{10,11},{13,12},{14,15},{17,16},{18,... | collective-permute-start | bytes 1572872 | tf_op jit(solution)/shard_map/ppermute | solution.py:515
  49.9 10.1 %collective-permute-start.10 = (bf16[512,512]{1,0:T(8,128)(2,1)S(1)}, bf16[512,512]{1,0:T(8,128)(2,1)S(1)}, u32[]{:S(2)}, u32[]{:S(2)}) collective-permute-start(bf16[512,512]{1,0:T(8,128)(2,1)S(1)} %get-tuple-element.101.refs_0_), channel_id=1, source_target_pairs={{1,2},{2,1},{5,6},{6,5},{9,10},{10,9},{13,14},{14,13},{17,18},{18,... | collective-permute-start | bytes 1572872 | tf_op jit(solution)/shard_map/ppermute | solution.py:512
  50.7 23.2 %collective-permute-start.9 = (bf16[512,512]{1,0:T(8,128)(2,1)S(1)}, bf16[512,512]{1,0:T(8,128)(2,1)S(1)}, u32[]{:S(2)}, u32[]{:S(2)}) collective-permute-start(bf16[512,512]{1,0:T(8,128)(2,1)S(1)} %get-tuple-element.100.refs_3_.refs_14_), channel_id=1, source_target_pairs={{1,0},{2,3},{5,4},{6,7},{9,8},{10,11},{13,12},{14,15},{17,16},{18,... | collective-permute-start | bytes 1572872 | tf_op jit(solution)/shard_map/ppermute | solution.py:515
  76.7 20.1 %collective-permute-start.12 = (bf16[512,512]{1,0:T(8,128)(2,1)S(1)}, bf16[512,512]{1,0:T(8,128)(2,1)S(1)}, u32[]{:S(2)}, u32[]{:S(2)}) collective-permute-start(bf16[512,512]{1,0:T(8,128)(2,1)S(1)} %get-tuple-element.105.refs_1_.refs_16_), channel_id=1, source_target_pairs={{1,0},{2,3},{5,4},{6,7},{9,8},{10,11},{13,12},{14,15},{17,16},{18,... | collective-permute-start | bytes 1572872 | tf_op jit(solution)/shard_map/ppermute | solution.py:515
  79.6 25.4 %collective-permute-start.15 = (bf16[512,512]{1,0:T(8,128)(2,1)S(1)}, bf16[512,512]{1,0:T(8,128)(2,1)S(1)}, u32[]{:S(2)}, u32[]{:S(2)}) collective-permute-start(bf16[512,512]{1,0:T(8,128)(2,1)S(1)} %get-tuple-element.112.refs_3_.refs_18_), channel_id=1, source_target_pairs={{1,0},{2,3},{5,4},{6,7},{9,8},{10,11},{13,12},{14,15},{17,16},{18,... | collective-permute-start | bytes 1572872 | tf_op jit(solution)/shard_map/ppermute | solution.py:515
  82.7 13.7 %collective-permute-start.17 = (bf16[1,128,1024]{2,1,0:T(8,128)(2,1)S(1)}, bf16[1,128,1024]{2,1,0:T(8,128)(2,1)S(1)}, u32[]{:S(2)}, u32[]{:S(2)}) collective-permute-start(bf16[1,128,1024]{2,1,0:T(8,128)(2,1)S(1)} %get-tuple-element.116), channel_id=1, source_target_pairs={{0,16},{4,20},{8,24},{12,28},{16,0},{20,4},{24,8},{28,12},{1,17},{... | collective-permute-start | bytes 786440 | tf_op jit(solution)/shard_map/ppermute | solution.py:458
  84.2 12.2 %collective-permute-start.18 = (bf16[1,128,1024]{2,1,0:T(8,128)(2,1)S(1)}, bf16[1,128,1024]{2,1,0:T(8,128)(2,1)S(1)}, u32[]{:S(2)}, u32[]{:S(2)}) collective-permute-start(bf16[1,128,1024]{2,1,0:T(8,128)(2,1)S(1)} %get-tuple-element.117), channel_id=1, source_target_pairs={{0,24},{4,28},{8,16},{12,20},{16,8},{20,12},{24,0},{28,4},{1,25},{... | collective-permute-start | bytes 786440 | tf_op jit(solution)/shard_map/ppermute | solution.py:458
  108.6 14.0 %collective-permute-start.22 = (bf16[1,128,1024]{2,1,0:T(8,128)(2,1)S(1)}, bf16[1,128,1024]{2,1,0:T(8,128)(2,1)S(1)}, u32[]{:S(2)}, u32[]{:S(2)}) collective-permute-start(bf16[1,128,1024]{2,1,0:T(8,128)(2,1)S(1)} %bitcast.27), channel_id=1, source_target_pairs={{0,16},{4,20},{8,24},{12,28},{16,0},{20,4},{24,8},{28,12},{1,17},{... | collective-permute-start | bytes 786440 | tf_op jit(solution)/shard_map/ppermute | solution.py:458
  110.2 12.5 %collective-permute-start.23 = (bf16[1,128,1024]{2,1,0:T(8,128)(2,1)S(1)}, bf16[1,128,1024]{2,1,0:T(8,128)(2,1)S(1)}, u32[]{:S(2)}, u32[]{:S(2)}) collective-permute-start(bf16[1,128,1024]{2,1,0:T(8,128)(2,1)S(1)} %bitcast.28), channel_id=1, source_target_pairs={{0,24},{4,28},{8,16},{12,20},{16,8},{20,12},{24,0},{28,4},{1,25},{... | collective-permute-start | bytes 786440 | tf_op jit(solution)/shard_map/ppermute | solution.py:458
  122.7 15.4 %collective-permute-start.24 = (bf16[4,128,1024]{2,1,0:T(8,128)(2,1)S(1)}, bf16[4,128,1024]{2,1,0:T(8,128)(2,1)S(1)}, u32[]{:S(2)}, u32[]{:S(2)}) collective-permute-start(bf16[4,128,1024]{2,1,0:T(8,128)(2,1)S(1)} %get-tuple-element.131.refs_5_), channel_id=1, source_target_pairs={{0,4},{4,0},{8,12},{12,8},{16,20},{20,16},{24,28},{28,24},{1,5},{5... | collective-permute-start | bytes 3145736 | tf_op jit(solution)/shard_map/ppermute | solution.py:458
  124.1 12.4 %collective-permute-start.26 = (bf16[1,128,1024]{2,1,0:T(8,128)(2,1)S(1)}, bf16[1,128,1024]{2,1,0:T(8,128)(2,1)S(1)}, u32[]{:S(2)}, u32[]{:S(2)}) collective-permute-start(bf16[1,128,1024]{2,1,0:T(8,128)(2,1)S(1)} %get-tuple-element.135), channel_id=1, source_target_pairs={{0,16},{4,20},{8,24},{12,28},{16,0},{20,4},{24,8},{28,12},{1,17},{... | collective-permute-start | bytes 786440 | tf_op jit(solution)/shard_map/ppermute | solution.py:458
  124.9 13.2 %collective-permute-start.27 = (bf16[1,128,1024]{2,1,0:T(8,128)(2,1)S(1)}, bf16[1,128,1024]{2,1,0:T(8,128)(2,1)S(1)}, u32[]{:S(2)}, u32[]{:S(2)}) collective-permute-start(bf16[1,128,1024]{2,1,0:T(8,128)(2,1)S(1)} %get-tuple-element.136), channel_id=1, source_target_pairs={{0,24},{4,28},{8,16},{12,20},{16,8},{20,12},{24,0},{28,4},{1,25},{... | collective-permute-start | bytes 786440 | tf_op jit(solution)/shard_map/ppermute | solution.py:458
  138.5 19.8 %collective-permute-start.28 = (bf16[1,128,1024]{2,1,0:T(8,128)(2,1)S(1)}, bf16[1,128,1024]{2,1,0:T(8,128)(2,1)S(1)}, u32[]{:S(2)}, u32[]{:S(2)}) collective-permute-start(bf16[1,128,1024]{2,1,0:T(8,128)(2,1)S(1)} %bitcast.22), channel_id=1, source_target_pairs={{0,8},{4,12},{8,0},{12,4},{16,24},{20,28},{24,16},{28,20},{1,9},{5... | collective-permute-start | bytes 786440 | tf_op jit(solution)/shard_map/ppermute | solution.py:458
  139.3 19.0 %collective-permute-start.29 = (bf16[1,128,1024]{2,1,0:T(8,128)(2,1)S(1)}, bf16[1,128,1024]{2,1,0:T(8,128)(2,1)S(1)}, u32[]{:S(2)}, u32[]{:S(2)}) collective-permute-start(bf16[1,128,1024]{2,1,0:T(8,128)(2,1)S(1)} %bitcast.23), channel_id=1, source_target_pairs={{0,16},{4,20},{8,24},{12,28},{16,0},{20,4},{24,8},{28,12},{1,17},{... | collective-permute-start | bytes 786440 | tf_op jit(solution)/shard_map/ppermute | solution.py:458
  140.8 17.5 %collective-permute-start.30 = (bf16[1,128,1024]{2,1,0:T(8,128)(2,1)S(1)}, bf16[1,128,1024]{2,1,0:T(8,128)(2,1)S(1)}, u32[]{:S(2)}, u32[]{:S(2)}) collective-permute-start(bf16[1,128,1024]{2,1,0:T(8,128)(2,1)S(1)} %bitcast.24), channel_id=1, source_target_pairs={{0,24},{4,28},{8,16},{12,20},{16,8},{20,12},{24,0},{28,4},{1,25},{... | collective-permute-start | bytes 786440 | tf_op jit(solution)/shard_map/ppermute | solution.py:458
  (13 other events, 68.9 us)

commit v8 on v7

--- a/solution.py
+++ b/solution.py
@@ -414,6 +414,7 @@
     large = pltpu.CompilerParams(vmem_limit_bytes=20 * 1024 * 1024)
     small = pltpu.CompilerParams(vmem_limit_bytes=12 * 1024 * 1024)
     small_cost = pl.CostEstimate(flops=1, bytes_accessed=1, transcendentals=0)
+    large_cost = pl.CostEstimate(flops=30_000_000_000, bytes_accessed=1, transcendentals=0)
 
     turn = []
 
@@ -430,7 +431,7 @@
         turn.append(ran)
         return results
 
-    def step(kernel, operands, outs, scalars=(), waits=()):
+    def step(kernel, operands, outs, scalars=(), waits=(), cost=small_cost):
         return run(
             kernel,
             [*scalars, *operands],
@@ -438,7 +439,7 @@
             outs,
             [vmem] * len(outs),
             waits,
-            cost_estimate=small_cost,
+            cost_estimate=cost,
             compiler_params=small,
         )
 
@@ -508,8 +509,9 @@
             (held,) = step(add_kernel, [held, landed], [part])
         sums[n] = held
 
-    def sum_all(n):
-        (mid,) = step(add_kernel, [sums[n], lax.ppermute(sums[n], "tensor", across)], [part])
+    def sum_all(n, waits=(), cost=small_cost):
+        landed = lax.ppermute(sums[n], "tensor", across)
+        (mid,) = step(add_kernel, [sums[n], landed], [part], waits=waits, cost=cost)
         out = mid
         for pairs in reversed(in_hops):
             back = lax.ppermute(out, "tensor", [(b, a) for a, b in pairs])
@@ -520,7 +522,7 @@
     tile = shape(8, LANES, dtype=F32)
     squares = {-1: jnp.zeros((8, LANES), F32)}
 
-    def send_rows(b):
+    def new_rows(b, waits=()):
         batch = batches[b]
         rows = len(batch) * piece
         keep, send = step(
@@ -528,8 +530,12 @@
             [c for n in batch for c in cots[n]] + [normed, weight],
             [shape(replicas // 2, rows, inner)] * 2,
             scalars=[places],
+            waits=waits,
         )
-        held, left = [keep, exchange(send, 1)], replicas // 2
+        return [keep, exchange(send, 1)]
+
+    def send_rows(b, held):
+        rows, left = len(batches[b]) * piece, replicas // 2
         for bit, bits in stages(replicas):
             ways = 1 << bits
             left //= ways
@@ -543,14 +549,14 @@
             held = [picked[0]] + [exchange(picked[mask], mask << bit) for mask in range(1, ways)]
         terms[b] = held
 
-    def own_rows(b, waits=()):
+    def own_rows(b, cost=small_cost):
         batch = batches[b]
         rows = len(batch) * piece
         deltas[b], sent, squares[b] = step(
             functools.partial(delta_kernel, len(terms[b]), batch[0] * piece, replicas),
             [own_global, squares[b - 1], *terms[b]],
             [shape(rows, inner, dtype=F32), shape(rows, inner), tile],
-            waits=waits,
+            cost=cost,
         )
         spread_rows(b, sent)
 
@@ -572,34 +578,35 @@
             grid=(count,),
             scratch_shapes=[pltpu.VMEM((tokens, width), F32)],
             input_output_aliases=aliases,
-            cost_estimate=small_cost,
+            cost_estimate=large_cost,
             compiler_params=large,
         )
         return grad
 
     first, second = range(2)
-    for t in range(chunks + 2):
-        if t < chunks:
-            sum_side(t)
+    for t in range(chunks):
+        sum_side(t)
         if t == 0:
             join("kept")
-        if 1 <= t <= chunks:
+        else:
             sum_all(t - 1)
-        if t - 2 == batches[first][-1]:
-            send_rows(first)
-    own_rows(first, gathered["kept"][1:])
-    send_rows(second)
+    held_first = new_rows(first)
+    sum_all(chunks - 1, [cots[chunks - 2][1], gathered["kept"][1]], large_cost)
+    send_rows(first, held_first)
+    held_second = new_rows(second)
+    own_rows(first, large_cost)
+    send_rows(second, held_second)
     half = groups // 2
     grad_input = backward(0, half, None) if half else None
     join(first)
     grad_input = backward(half, groups - half, grad_input)
-    own_rows(second, gathered[first][1:])
+    own_rows(second)
     total = squares[second]
     for axis, bits in (("tensor", range(heads_over.bit_length() - 1)), ("replica", range(1, replicas.bit_length() - 1))):
         for bit in bits:
             pairs = [(r, r ^ (1 << bit)) for r in range(lax.axis_size(axis))]
             (total,) = step(add_squares_kernel, [total, lax.ppermute(total, axis, pairs)], [tile])
-    join(second)
+    join(second, gathered[first][1:])
     columns = [total, exchange(total, 1)]
 
     sizes = [len(batch) * piece for batch in batches]

time: 167 us -> 178 us (1.066)
  waiting for transfers between devices: 79.4 us -> 94.9 us
  starting transfers between devices: 50.7 us -> 46.4 us
    ppermute x4, waiting for transfers between devices: 22 us -> 33.9 us  [sum_all(): back = lax.ppermute(out, 'tensor', [(b, a) for a, b in pairs])]
    ppermute x21, waiting for transfers between devices: 34.3 us -> 24.8 us  [exchange(): lax.ppermute(value, 'replica', [(r, r ^ mask) for r in range(replicas)])]
    ppermute x4, waiting for transfers between devices: 14.3 us -> 22.8 us  [shards(): lax.ppermute(p, 'tensor', in_hops[0])]
    ppermute x4, starting transfers between devices: 7.67 us -> 1.96 us  [shards(): lax.ppermute(total, axis, pairs)]
    ppermute x4, waiting for transfers between devices: 8.64 us -> 13.4 us  [shards(): lax.ppermute(total, axis, pairs)]
  transfers between devices with their start and end apart: 37 -> 37, of which waited for: 20 -> 17; matrix products, arithmetic and copies ran while one was open for 0% -> 0% of each run, Pallas kernels for 11% -> 12%
where the time goes in v8:
time: 178 us
  waiting for transfers between devices  94.9 us (53%)
  starting transfers between devices  46.4 us (26%)
  Pallas kernels  35.4 us (20%)
    pallas_call x28, Pallas kernels, run(): pl.pallas_call(in_turn(kernel, len(inputs), len(waits), len(outs)), in_sp...  35.4 us
    ppermute x4, waiting for transfers between devices, sum_all(): back = lax.ppermute(out, 'tensor', [(b, a) for a, b in pairs])  33.9 us
    ppermute x21, waiting for transfers between devices, exchange(): lax.ppermute(value, 'replica', [(r, r ^ mask) for r in range(replicas)])  24.8 us
    ppermute x4, waiting for transfers between devices, shards(): lax.ppermute(p, 'tensor', in_hops[0])  22.8 us
    ppermute x21, starting transfers between devices, exchange(): lax.ppermute(value, 'replica', [(r, r ^ mask) for r in range(replicas)])  18.5 us
    ppermute x4, starting transfers between devices, shards(): lax.ppermute(p, 'tensor', in_hops[0])  17.8 us
    ppermute x4, waiting for transfers between devices, shards(): lax.ppermute(total, axis, pairs)  13.4 us
    ppermute x4, starting transfers between devices, sum_all(): back = lax.ppermute(out, 'tensor', [(b, a) for a, b in pairs])  5.35 us
  transfers between devices with their start and end apart: 37, of which 17 were waited for; matrix products, arithmetic and copies ran while one was open for 0% of the time, Pallas kernels for 12%

profile of v8, /device:TPU:0, one launch (start us, length us, event | category | flops | bytes accessed | tf_op | source)
XLA Modules:
  0.0 177.9 jit_solution(9748104051835722147)
XLA Ops:
  2.4 6.2 %shard_map.157 = (bf16[8,256,1024]{2,1,0:T(8,128)(2,1)S(1)}, bf16[128,2048]{1,0:T(8,128)(2,1)S(1)}, f32[256,1024]{1,0:T(8,128)S(1)}, f32[256,1024]{1,0:T(8,128)S...) custom-call(f32[16,512]{1,0:T(8,128)} %bitcast.31, bf16[512,1024]{1,0:T(8,128)(2,1)} %refs_1_.3, ...), custom_call_target="tpu_custom_call" | custom-call | flops 1 | bytes 1 | tf_op jit(solution)/shard_map/pallas_call | solution.py:424
  10.0 5.0 %collective-permute-start = (bf16[512,512]{1,0:T(8,128)(2,1)S(1)}, bf16[512,512]{1,0:T(8,128)(2,1)S(1)}, u32[]{:S(2)}, u32[]{:S(2)}) collective-permute-start(bf16[512,512]{1,0:T(8,128)(2,1)S(1)} %get-tuple-element.86.refs_0_), channel_id=1, source_target_pairs={{0,1},{3,2},{4,5},{7,6},{8,9},{11,10},{12,13},{15,14},{16,17},{19,... | collective-permute-start | bytes 1572872 | tf_op jit(solution)/shard_map/ppermute | solution.py:502
  18.6 2.5 %shard_map.159 = (bf16[512,512]{1,0:T(8,128)(2,1)S(1)}, bf16[512,512]{1,0:T(8,128)(2,1)S(1)}, bf16[512,512]{1,0:T(8,128)(2,1)S(1)}, f32[8,128]{1,0:T(8,128)S(1)}) custom-call(s32[5]{0:T(128)S(1)} %stack.23.refs_0_, bf16[8,256,1024]{2,1,0:T(8,128)(2,1)S(1)} %get-tuple-element.83.refs_1_.refs_6_.refs_11_, ...), custom_call_target="tpu_custom_call" | custom-call | flops 1 | bytes 1 | tf_op jit(solution)/shard_map/pallas_call | solution.py:424
  21.1 5.1 %collective-permute-done.refs_1_ = bf16[512,512]{1,0:T(8,128)(2,1)S(1)} collective-permute-done((bf16[512,512]{1,0:T(8,128)(2,1)S(1)}, bf16[512,512]{1,0:T(8,128)(2,1)S(1)}, u32[]{:S(2)}, u32[]{:S(2)}) %collective-permute-start) | collective-permute-done | bytes 524320 | tf_op jit(solution)/shard_map/ppermute | solution.py:502
  26.3 3.7 %collective-permute-done.3.refs_1_ = bf16[1,256,1024]{2,1,0:T(8,128)(2,1)S(1)} collective-permute-done((bf16[1,256,1024]{2,1,0:T(8,128)(2,1)S(1)}, bf16[1,256,1024]{2,1,0:T(8,128)(2,1)S(1)}, u32[]{:S(2)}, u32[]{:S(2)}) %collective-permute-start.3) | collective-permute-done | bytes 524320 | tf_op jit(solution)/shard_map/ppermute | solution.py:459
  29.9 11.0 %collective-permute-done.4.refs_2_ = bf16[1,256,1024]{2,1,0:T(8,128)(2,1)S(1)} collective-permute-done((bf16[1,256,1024]{2,1,0:T(8,128)(2,1)S(1)}, bf16[1,256,1024]{2,1,0:T(8,128)(2,1)S(1)}, u32[]{:S(2)}, u32[]{:S(2)}) %collective-permute-start.4) | collective-permute-done | bytes 524320 | tf_op jit(solution)/shard_map/ppermute | solution.py:459
  43.4 4.1 %collective-permute-start.8 = (bf16[512,512]{1,0:T(8,128)(2,1)S(1)}, bf16[512,512]{1,0:T(8,128)(2,1)S(1)}, u32[]{:S(2)}, u32[]{:S(2)}) collective-permute-start(bf16[512,512]{1,0:T(8,128)(2,1)S(1)} %get-tuple-element.97.refs_0_), channel_id=1, source_target_pairs={{0,1},{3,2},{4,5},{7,6},{8,9},{11,10},{12,13},{15,14},{16,17},{19,... | collective-permute-start | bytes 1572872 | tf_op jit(solution)/shard_map/ppermute | solution.py:502
  47.5 7.4 %collective-permute-done.2.refs_1_ = bf16[512,512]{1,0:T(8,128)(2,1)S(1)} collective-permute-done((bf16[512,512]{1,0:T(8,128)(2,1)S(1)}, bf16[512,512]{1,0:T(8,128)(2,1)S(1)}, u32[]{:S(2)}, u32[]{:S(2)}) %collective-permute-start.2) | collective-permute-done | bytes 524320 | tf_op jit(solution)/shard_map/ppermute | solution.py:502
  55.7 7.2 %collective-permute-start.11 = (bf16[512,512]{1,0:T(8,128)(2,1)S(1)}, bf16[512,512]{1,0:T(8,128)(2,1)S(1)}, u32[]{:S(2)}, u32[]{:S(2)}) collective-permute-start(bf16[512,512]{1,0:T(8,128)(2,1)S(1)} %get-tuple-element.102.refs_0_), channel_id=1, source_target_pairs={{0,1},{3,2},{4,5},{7,6},{8,9},{11,10},{12,13},{15,14},{16,17},{19,... | collective-permute-start | bytes 1572872 | tf_op jit(solution)/shard_map/ppermute | solution.py:502
  63.1 3.0 %collective-permute-done.8.refs_1_ = bf16[512,512]{1,0:T(8,128)(2,1)S(1)} collective-permute-done((bf16[512,512]{1,0:T(8,128)(2,1)S(1)}, bf16[512,512]{1,0:T(8,128)(2,1)S(1)}, u32[]{:S(2)}, u32[]{:S(2)}) %collective-permute-start.8) | collective-permute-done | bytes 524320 | tf_op jit(solution)/shard_map/ppermute | solution.py:502
  69.7 7.3 %collective-permute-done.11.refs_1_ = bf16[512,512]{1,0:T(8,128)(2,1)S(1)} collective-permute-done((bf16[512,512]{1,0:T(8,128)(2,1)S(1)}, bf16[512,512]{1,0:T(8,128)(2,1)S(1)}, u32[]{:S(2)}, u32[]{:S(2)}) %collective-permute-start.11) | collective-permute-done | bytes 524320 | tf_op jit(solution)/shard_map/ppermute | solution.py:502
  79.3 7.6 %collective-permute-done.9.refs_4_.refs_15_ = bf16[512,512]{1,0:T(8,128)(2,1)S(1)} collective-permute-done((bf16[512,512]{1,0:T(8,128)(2,1)S(1)}, bf16[512,512]{1,0:T(8,128)(2,1)S(1)}, u32[]{:S(2)}, u32[]{:S(2)}) %collective-permute-start.9) | collective-permute-done | bytes 524320 | tf_op jit(solution)/shard_map/ppermute | solution.py:517
  86.8 11.2 %collective-permute-done.6.refs_2_.refs_13_ = bf16[512,512]{1,0:T(8,128)(2,1)S(1)} collective-permute-done((bf16[512,512]{1,0:T(8,128)(2,1)S(1)}, bf16[512,512]{1,0:T(8,128)(2,1)S(1)}, u32[]{:S(2)}, u32[]{:S(2)}) %collective-permute-start.6) | collective-permute-done | bytes 524320 | tf_op jit(solution)/shard_map/ppermute | solution.py:517
  100.2 7.1 %collective-permute-done.12.refs_3_.refs_2_.refs_17_ = bf16[512,512]{1,0:T(8,128)(2,1)S(1)} collective-permute-done((bf16[512,512]{1,0:T(8,128)(2,1)S(1)}, bf16[512,512]{1,0:T(8,128)(2,1)S(1)}, u32[]{:S(2)}, u32[]{:S(2)}) %collective-permute-start.12) | collective-permute-done | bytes 524320 | tf_op jit(solution)/shard_map/ppermute | solution.py:517
  113.3 8.0 %collective-permute-done.15.refs_4_.refs_19_ = bf16[512,512]{1,0:T(8,128)(2,1)S(1)} collective-permute-done((bf16[512,512]{1,0:T(8,128)(2,1)S(1)}, bf16[512,512]{1,0:T(8,128)(2,1)S(1)}, u32[]{:S(2)}, u32[]{:S(2)}) %collective-permute-start.15) | collective-permute-done | bytes 524320 | tf_op jit(solution)/shard_map/ppermute | solution.py:517
  130.2 5.2 %shard_map.174 = (bf16[512,1024]{1,0:T(8,128)(2,1)}, f32[8,128]{1,0:T(8,128)S(1)}) custom-call(s32[5]{0:T(128)S(1)} %stack.23.refs_0_, f32[16,512]{1,0:T(8,128)} %bitcast.32, bf16[512,1024]{1,0:T(8,128)(2,1)} %refs_2_.5, bf16[512,256]{1,0:T(8,128)(2,1)} %refs_3_.5, bf16[512,256]{1,0:T(8,128)(2,1)} %refs_4_.5, f32[1,1024]{1,0:T(1,128)} %bitcast.35, ...), custom_call_target="tpu_custom_call" | custom-call | flops 30000001024 | bytes 1 | tf_op jit(solution)/shard_map/pallas_call | solution.py:424
  136.9 2.9 %collective-permute-done.22.refs_2_ = bf16[1,128,1024]{2,1,0:T(8,128)(2,1)S(1)} collective-permute-done((bf16[1,128,1024]{2,1,0:T(8,128)(2,1)S(1)}, bf16[1,128,1024]{2,1,0:T(8,128)(2,1)S(1)}, u32[]{:S(2)}, u32[]{:S(2)}) %collective-permute-start.22) | collective-permute-done | bytes 262176 | tf_op jit(solution)/shard_map/ppermute | solution.py:459
  139.9 5.3 %shard_map.176 = (bf16[512,1024]{1,0:T(8,128)(2,1)}, f32[8,128]{1,0:T(8,128)S(1)}) custom-call(s32[5]{0:T(128)S(1)} %stack.23.refs_0_, f32[16,512]{1,0:T(8,128)} %bitcast.33, bf16[512,1024]{1,0:T(8,128)(2,1)} %refs_2_.5, bf16[512,256]{1,0:T(8,128)(2,1)} %refs_3_.5, bf16[512,256]{1,0:T(8,128)(2,1)} %refs_4_.5, ...), custom_call_target="tpu_custom_call", output_to_operand_aliasing={{0}: (20, {})} | custom-call | flops 30000001024 | bytes 1 | tf_op jit(solution)/shard_map/pallas_call | solution.py:424
  145.2 5.1 %collective-permute-done.27.refs_5_ = bf16[1,128,1024]{2,1,0:T(8,128)(2,1)S(1)} collective-permute-done((bf16[1,128,1024]{2,1,0:T(8,128)(2,1)S(1)}, bf16[1,128,1024]{2,1,0:T(8,128)(2,1)S(1)}, u32[]{:S(2)}, u32[]{:S(2)}) %collective-permute-start.27) | collective-permute-done | bytes 262176 | tf_op jit(solution)/shard_map/ppermute | solution.py:459
  154.3 3.6 %collective-permute-done.31.refs_1_ = f32[8,128]{1,0:T(8,128)S(1)} collective-permute-done((f32[8,128]{1,0:T(8,128)S(1)}, f32[8,128]{1,0:T(8,128)S(1)}, u32[]{:S(2)}, u32[]{:S(2)}) %collective-permute-start.31) | collective-permute-done | bytes 4128 | tf_op jit(solution)/shard_map/ppermute | solution.py:608
  158.3 4.1 %collective-permute-done.32.refs_1_ = f32[8,128]{1,0:T(8,128)S(1)} collective-permute-done((f32[8,128]{1,0:T(8,128)S(1)}, f32[8,128]{1,0:T(8,128)S(1)}, u32[]{:S(2)}, u32[]{:S(2)}) %collective-permute-start.32) | collective-permute-done | bytes 4128 | tf_op jit(solution)/shard_map/ppermute | solution.py:608
  163.1 2.9 %collective-permute-done.33.refs_1_ = f32[8,128]{1,0:T(8,128)S(1)} collective-permute-done((f32[8,128]{1,0:T(8,128)S(1)}, f32[8,128]{1,0:T(8,128)S(1)}, u32[]{:S(2)}, u32[]{:S(2)}) %collective-permute-start.33) | collective-permute-done | bytes 4128 | tf_op jit(solution)/shard_map/ppermute | solution.py:608
  166.8 2.8 %collective-permute-done.34.refs_1_ = f32[8,128]{1,0:T(8,128)S(1)} collective-permute-done((f32[8,128]{1,0:T(8,128)S(1)}, f32[8,128]{1,0:T(8,128)S(1)}, u32[]{:S(2)}, u32[]{:S(2)}) %collective-permute-start.34) | collective-permute-done | bytes 4128 | tf_op jit(solution)/shard_map/ppermute | solution.py:608
  172.5 5.4 %shard_map.183 = (bf16[2048,1024]{1,0:T(8,128)(2,1)}, f32[256,1024]{1,0:T(8,128)}, f32[256,1024]{1,0:T(8,128)}, f32[8,128]{1,0:T(8,128)}) custom-call(s32[5]{0:T(128)S(1)} %stack.23.refs_0_, f32[256,1024]{1,0:T(8,128)S(1)} %get-tuple-element.117.refs_0_.refs_1_, f32[256,1024]{1,0:T(8,128)S(1)} %get-tuple-element.130.refs_2_, ...), custom_call_target="tpu_custom_call" | custom-call | flops 1 | bytes 1 | tf_op jit(solution)/shard_map/pallas_call | solution.py:424
  (80 shorter events, 43.2 us)
Async XLA Ops:
  10.0 16.1 %collective-permute-start = (bf16[512,512]{1,0:T(8,128)(2,1)S(1)}, bf16[512,512]{1,0:T(8,128)(2,1)S(1)}, u32[]{:S(2)}, u32[]{:S(2)}) collective-permute-start(bf16[512,512]{1,0:T(8,128)(2,1)S(1)} %get-tuple-element.86.refs_0_), channel_id=1, source_target_pairs={{0,1},{3,2},{4,5},{7,6},{8,9},{11,10},{12,13},{15,14},{16,17},{19,... | collective-permute-start | bytes 1572872 | tf_op jit(solution)/shard_map/ppermute | solution.py:502
  15.0 14.9 %collective-permute-start.3 = (bf16[1,256,1024]{2,1,0:T(8,128)(2,1)S(1)}, bf16[1,256,1024]{2,1,0:T(8,128)(2,1)S(1)}, u32[]{:S(2)}, u32[]{:S(2)}) collective-permute-start(bf16[1,256,1024]{2,1,0:T(8,128)(2,1)S(1)} %bitcast.18), channel_id=1, source_target_pairs={{0,8},{4,12},{8,0},{12,4},{16,24},{20,28},{24,16},{28,20},{1,9},{5... | collective-permute-start | bytes 1572872 | tf_op jit(solution)/shard_map/ppermute | solution.py:459
  16.6 24.3 %collective-permute-start.4 = (bf16[1,256,1024]{2,1,0:T(8,128)(2,1)S(1)}, bf16[1,256,1024]{2,1,0:T(8,128)(2,1)S(1)}, u32[]{:S(2)}, u32[]{:S(2)}) collective-permute-start(bf16[1,256,1024]{2,1,0:T(8,128)(2,1)S(1)} %bitcast.19), channel_id=1, source_target_pairs={{0,16},{4,20},{8,24},{12,28},{16,0},{20,4},{24,8},{28,12},{1,17},{... | collective-permute-start | bytes 1572872 | tf_op jit(solution)/shard_map/ppermute | solution.py:459
  18.1 22.8 %collective-permute-start.5 = (bf16[1,256,1024]{2,1,0:T(8,128)(2,1)S(1)}, bf16[1,256,1024]{2,1,0:T(8,128)(2,1)S(1)}, u32[]{:S(2)}, u32[]{:S(2)}) collective-permute-start(bf16[1,256,1024]{2,1,0:T(8,128)(2,1)S(1)} %bitcast.20), channel_id=1, source_target_pairs={{0,24},{4,28},{8,16},{12,20},{16,8},{20,12},{24,0},{28,4},{1,25},{... | collective-permute-start | bytes 1572872 | tf_op jit(solution)/shard_map/ppermute | solution.py:459
  41.1 66.2 %collective-permute-start.14 = (bf16[4,256,1024]{2,1,0:T(8,128)(2,1)S(1)}, bf16[4,256,1024]{2,1,0:T(8,128)(2,1)S(1)}, u32[]{:S(2)}, u32[]{:S(2)}) collective-permute-start(bf16[4,256,1024]{2,1,0:T(8,128)(2,1)S(1)} %get-tuple-element.109.refs_3_), channel_id=1, source_target_pairs={{0,4},{4,0},{8,12},{12,8},{16,20},{20,16},{24,28},{28,24},{1,5},{5... | collective-permute-start | bytes 6291464 | tf_op jit(solution)/shard_map/ppermute | solution.py:459
  41.1 13.8 %collective-permute-start.2 = (bf16[512,512]{1,0:T(8,128)(2,1)S(1)}, bf16[512,512]{1,0:T(8,128)(2,1)S(1)}, u32[]{:S(2)}, u32[]{:S(2)}) collective-permute-start(bf16[512,512]{1,0:T(8,128)(2,1)S(1)} %get-tuple-element.90.refs_0_), channel_id=1, source_target_pairs={{0,1},{3,2},{4,5},{7,6},{8,9},{11,10},{12,13},{15,14},{16,17},{19,... | collective-permute-start | bytes 1572872 | tf_op jit(solution)/shard_map/ppermute | solution.py:502
  42.7 20.2 %collective-permute-start.1 = (bf16[512,512]{1,0:T(8,128)(2,1)S(1)}, bf16[512,512]{1,0:T(8,128)(2,1)S(1)}, u32[]{:S(2)}, u32[]{:S(2)}) collective-permute-start(bf16[512,512]{1,0:T(8,128)(2,1)S(1)} %get-tuple-element.89.refs_0_), channel_id=1, source_target_pairs={{1,2},{2,1},{5,6},{6,5},{9,10},{10,9},{13,14},{14,13},{17,18},{18,... | collective-permute-start | bytes 1572872 | tf_op jit(solution)/shard_map/ppermute | solution.py:513
  43.4 22.7 %collective-permute-start.8 = (bf16[512,512]{1,0:T(8,128)(2,1)S(1)}, bf16[512,512]{1,0:T(8,128)(2,1)S(1)}, u32[]{:S(2)}, u32[]{:S(2)}) collective-permute-start(bf16[512,512]{1,0:T(8,128)(2,1)S(1)} %get-tuple-element.97.refs_0_), channel_id=1, source_target_pairs={{0,1},{3,2},{4,5},{7,6},{8,9},{11,10},{12,13},{15,14},{16,17},{19,... | collective-permute-start | bytes 1572872 | tf_op jit(solution)/shard_map/ppermute | solution.py:502
  55.7 21.3 %collective-permute-start.11 = (bf16[512,512]{1,0:T(8,128)(2,1)S(1)}, bf16[512,512]{1,0:T(8,128)(2,1)S(1)}, u32[]{:S(2)}, u32[]{:S(2)}) collective-permute-start(bf16[512,512]{1,0:T(8,128)(2,1)S(1)} %get-tuple-element.102.refs_0_), channel_id=1, source_target_pairs={{0,1},{3,2},{4,5},{7,6},{8,9},{11,10},{12,13},{15,14},{16,17},{19,... | collective-permute-start | bytes 1572872 | tf_op jit(solution)/shard_map/ppermute | solution.py:502
  67.1 19.7 %collective-permute-start.9 = (bf16[512,512]{1,0:T(8,128)(2,1)S(1)}, bf16[512,512]{1,0:T(8,128)(2,1)S(1)}, u32[]{:S(2)}, u32[]{:S(2)}) collective-permute-start(bf16[512,512]{1,0:T(8,128)(2,1)S(1)} %get-tuple-element.100.refs_3_.refs_14_), channel_id=1, source_target_pairs={{1,0},{2,3},{5,4},{6,7},{9,8},{10,11},{13,12},{14,15},{17,16},{18,... | collective-permute-start | bytes 1572872 | tf_op jit(solution)/shard_map/ppermute | solution.py:517
  68.4 29.7 %collective-permute-start.6 = (bf16[512,512]{1,0:T(8,128)(2,1)S(1)}, bf16[512,512]{1,0:T(8,128)(2,1)S(1)}, u32[]{:S(2)}, u32[]{:S(2)}) collective-permute-start(bf16[512,512]{1,0:T(8,128)(2,1)S(1)} %get-tuple-element.95.refs_1_.refs_12_), channel_id=1, source_target_pairs={{1,0},{2,3},{5,4},{6,7},{9,8},{10,11},{13,12},{14,15},{17,16},{18,... | collective-permute-start | bytes 1572872 | tf_op jit(solution)/shard_map/ppermute | solution.py:517
  77.1 23.0 %collective-permute-start.13 = (bf16[512,512]{1,0:T(8,128)(2,1)S(1)}, bf16[512,512]{1,0:T(8,128)(2,1)S(1)}, u32[]{:S(2)}, u32[]{:S(2)}) collective-permute-start(bf16[512,512]{1,0:T(8,128)(2,1)S(1)} %get-tuple-element.106.refs_0_), channel_id=1, source_target_pairs={{1,2},{2,1},{5,6},{6,5},{9,10},{10,9},{13,14},{14,13},{17,18},{18,... | collective-permute-start | bytes 1572872 | tf_op jit(solution)/shard_map/ppermute | solution.py:513
  78.0 29.3 %collective-permute-start.12 = (bf16[512,512]{1,0:T(8,128)(2,1)S(1)}, bf16[512,512]{1,0:T(8,128)(2,1)S(1)}, u32[]{:S(2)}, u32[]{:S(2)}) collective-permute-start(bf16[512,512]{1,0:T(8,128)(2,1)S(1)} %get-tuple-element.105.refs_1_.refs_16_), channel_id=1, source_target_pairs={{1,0},{2,3},{5,4},{6,7},{9,8},{10,11},{13,12},{14,15},{17,16},{18,... | collective-permute-start | bytes 1572872 | tf_op jit(solution)/shard_map/ppermute | solution.py:517
  107.4 13.8 %collective-permute-start.15 = (bf16[512,512]{1,0:T(8,128)(2,1)S(1)}, bf16[512,512]{1,0:T(8,128)(2,1)S(1)}, u32[]{:S(2)}, u32[]{:S(2)}) collective-permute-start(bf16[512,512]{1,0:T(8,128)(2,1)S(1)} %get-tuple-element.110.refs_3_.refs_18_), channel_id=1, source_target_pairs={{1,0},{2,3},{5,4},{6,7},{9,8},{10,11},{13,12},{14,15},{17,16},{18,... | collective-permute-start | bytes 1572872 | tf_op jit(solution)/shard_map/ppermute | solution.py:517
  109.7 13.6 %collective-permute-start.18 = (bf16[1,128,1024]{2,1,0:T(8,128)(2,1)S(1)}, bf16[1,128,1024]{2,1,0:T(8,128)(2,1)S(1)}, u32[]{:S(2)}, u32[]{:S(2)}) collective-permute-start(bf16[1,128,1024]{2,1,0:T(8,128)(2,1)S(1)} %get-tuple-element.119), channel_id=1, source_target_pairs={{0,8},{4,12},{8,0},{12,4},{16,24},{20,28},{24,16},{28,20},{1,9},{5... | collective-permute-start | bytes 786440 | tf_op jit(solution)/shard_map/ppermute | solution.py:459
  125.0 14.8 %collective-permute-start.22 = (bf16[1,128,1024]{2,1,0:T(8,128)(2,1)S(1)}, bf16[1,128,1024]{2,1,0:T(8,128)(2,1)S(1)}, u32[]{:S(2)}, u32[]{:S(2)}) collective-permute-start(bf16[1,128,1024]{2,1,0:T(8,128)(2,1)S(1)} %bitcast.23), channel_id=1, source_target_pairs={{0,16},{4,20},{8,24},{12,28},{16,0},{20,4},{24,8},{28,12},{1,17},{... | collective-permute-start | bytes 786440 | tf_op jit(solution)/shard_map/ppermute | solution.py:459
  125.8 13.9 %collective-permute-start.23 = (bf16[1,128,1024]{2,1,0:T(8,128)(2,1)S(1)}, bf16[1,128,1024]{2,1,0:T(8,128)(2,1)S(1)}, u32[]{:S(2)}, u32[]{:S(2)}) collective-permute-start(bf16[1,128,1024]{2,1,0:T(8,128)(2,1)S(1)} %bitcast.24), channel_id=1, source_target_pairs={{0,24},{4,28},{8,16},{12,20},{16,8},{20,12},{24,0},{28,4},{1,25},{... | collective-permute-start | bytes 786440 | tf_op jit(solution)/shard_map/ppermute | solution.py:459
  128.1 17.1 %collective-permute-start.25 = (bf16[1,128,1024]{2,1,0:T(8,128)(2,1)S(1)}, bf16[1,128,1024]{2,1,0:T(8,128)(2,1)S(1)}, u32[]{:S(2)}, u32[]{:S(2)}) collective-permute-start(bf16[1,128,1024]{2,1,0:T(8,128)(2,1)S(1)} %get-tuple-element.134), channel_id=1, source_target_pairs={{0,8},{4,12},{8,0},{12,4},{16,24},{20,28},{24,16},{28,20},{1,9},{5... | collective-permute-start | bytes 786440 | tf_op jit(solution)/shard_map/ppermute | solution.py:459
  129.4 15.8 %collective-permute-start.26 = (bf16[1,128,1024]{2,1,0:T(8,128)(2,1)S(1)}, bf16[1,128,1024]{2,1,0:T(8,128)(2,1)S(1)}, u32[]{:S(2)}, u32[]{:S(2)}) collective-permute-start(bf16[1,128,1024]{2,1,0:T(8,128)(2,1)S(1)} %get-tuple-element.135), channel_id=1, source_target_pairs={{0,16},{4,20},{8,24},{12,28},{16,0},{20,4},{24,8},{28,12},{1,17},{... | collective-permute-start | bytes 786440 | tf_op jit(solution)/shard_map/ppermute | solution.py:459
  135.5 14.9 %collective-permute-start.27 = (bf16[1,128,1024]{2,1,0:T(8,128)(2,1)S(1)}, bf16[1,128,1024]{2,1,0:T(8,128)(2,1)S(1)}, u32[]{:S(2)}, u32[]{:S(2)}) collective-permute-start(bf16[1,128,1024]{2,1,0:T(8,128)(2,1)S(1)} %get-tuple-element.136), channel_id=1, source_target_pairs={{0,24},{4,28},{8,16},{12,20},{16,8},{20,12},{24,0},{28,4},{1,25},{... | collective-permute-start | bytes 786440 | tf_op jit(solution)/shard_map/ppermute | solution.py:459
  139.9 29.8 %collective-permute-start.24 = (bf16[4,128,1024]{2,1,0:T(8,128)(2,1)S(1)}, bf16[4,128,1024]{2,1,0:T(8,128)(2,1)S(1)}, u32[]{:S(2)}, u32[]{:S(2)}) collective-permute-start(bf16[4,128,1024]{2,1,0:T(8,128)(2,1)S(1)} %get-tuple-element.131.refs_5_), channel_id=1, source_target_pairs={{0,4},{4,0},{8,12},{12,8},{16,20},{20,16},{24,28},{28,24},{1,5},{5... | collective-permute-start | bytes 3145736 | tf_op jit(solution)/shard_map/ppermute | solution.py:459
  150.8 18.8 %collective-permute-start.28 = (bf16[1,128,1024]{2,1,0:T(8,128)(2,1)S(1)}, bf16[1,128,1024]{2,1,0:T(8,128)(2,1)S(1)}, u32[]{:S(2)}, u32[]{:S(2)}) collective-permute-start(bf16[1,128,1024]{2,1,0:T(8,128)(2,1)S(1)} %bitcast.26), channel_id=1, source_target_pairs={{0,8},{4,12},{8,0},{12,4},{16,24},{20,28},{24,16},{28,20},{1,9},{5... | collective-permute-start | bytes 786440 | tf_op jit(solution)/shard_map/ppermute | solution.py:459
  151.5 18.1 %collective-permute-start.29 = (bf16[1,128,1024]{2,1,0:T(8,128)(2,1)S(1)}, bf16[1,128,1024]{2,1,0:T(8,128)(2,1)S(1)}, u32[]{:S(2)}, u32[]{:S(2)}) collective-permute-start(bf16[1,128,1024]{2,1,0:T(8,128)(2,1)S(1)} %bitcast.27), channel_id=1, source_target_pairs={{0,16},{4,20},{8,24},{12,28},{16,0},{20,4},{24,8},{28,12},{1,17},{... | collective-permute-start | bytes 786440 | tf_op jit(solution)/shard_map/ppermute | solution.py:459
  153.0 16.6 %collective-permute-start.30 = (bf16[1,128,1024]{2,1,0:T(8,128)(2,1)S(1)}, bf16[1,128,1024]{2,1,0:T(8,128)(2,1)S(1)}, u32[]{:S(2)}, u32[]{:S(2)}) collective-permute-start(bf16[1,128,1024]{2,1,0:T(8,128)(2,1)S(1)} %bitcast.28), channel_id=1, source_target_pairs={{0,24},{4,28},{8,16},{12,20},{16,8},{20,12},{24,0},{28,4},{1,25},{... | collective-permute-start | bytes 786440 | tf_op jit(solution)/shard_map/ppermute | solution.py:459
  (13 other events, 92.6 us)

commit v9 on v8

--- a/solution.py
+++ b/solution.py
@@ -189,25 +189,21 @@
     sum_ref[...] = a_ref[...] + b_ref[...]
 
 
-def gradient_kernel(batch, place_ref, *refs):
-    count = len(batch)
+def gradient_kernel(count, place_ref, *refs):
     cot_refs, (normed_ref, weight_ref, keep_ref, send_ref) = refs[: 2 * count], refs[2 * count :]
     middle = place_ref[1] == 1
     odd = place_ref[2] == 1
-    replicas, _, inner = weight_ref.shape
-    piece = keep_ref.shape[1] // count
-    tile = min(inner, 512)
-    for n, chunk in enumerate(batch):
+    replicas, rows, tile = weight_ref.shape
+    piece = rows // count
+    cols = pl.ds(pl.multiple_of(pl.program_id(0) * tile, LANES), tile)
+    for n in range(count):
         cot = jnp.where(middle, cot_refs[2 * n][...], cot_refs[2 * n + 1][...])
-        rows = slice(chunk * piece, (chunk + 1) * piece)
         at = slice(n * piece, (n + 1) * piece)
-        for lo in range(0, inner, tile):
-            cols = slice(lo, lo + tile)
-            weight = weight_ref[:, rows, cols].reshape(replicas * piece, tile).astype(F32)
-            new = weight - inner_rate * dot(cot, normed_ref[:, cols], NN)
-            new = new.astype(BF16).reshape(replicas // 2, 2, piece, tile)
-            keep_ref[:, at, cols] = jnp.where(odd, new[:, 1], new[:, 0])
-            send_ref[:, at, cols] = jnp.where(odd, new[:, 0], new[:, 1])
+        weight = weight_ref[:, at, :].reshape(replicas * piece, tile).astype(F32)
+        new = weight - inner_rate * dot(cot, normed_ref[:, cols], NN)
+        new = new.astype(BF16).reshape(replicas // 2, 2, piece, tile)
+        keep_ref[:, at, cols] = jnp.where(odd, new[:, 1], new[:, 0])
+        send_ref[:, at, cols] = jnp.where(odd, new[:, 0], new[:, 1])
 
 
 def backward_kernel(
@@ -226,7 +222,7 @@
     piece = owned // chunks
     middle = place_ref[1] == 1
     for n in range(chunks):
-        weight = weight_ref[:, n * piece : (n + 1) * piece, here].reshape(replicas * piece, width)
+        weight = weight_ref[:, n * piece : (n + 1) * piece, :].reshape(replicas * piece, width)
         term = dot(jnp.where(middle, cot_refs[2 * n][...], cot_refs[2 * n + 1][...]), weight, TN)
         dn_ref[...] = term if n == 0 else dn_ref[...] + term
     step, rate = head_tables(dt_ref, a_ref, bias_ref, first, per_group)
@@ -288,13 +284,13 @@
         out_ref[...] = total.astype(BF16)
 
 
-def delta_kernel(count, lo, replicas, global_ref, before_ref, *refs):
+def delta_kernel(count, replicas, global_ref, before_ref, *refs):
     terms, (delta_ref, sent_ref, squares_ref) = refs[:count], refs[count:]
     rows, inner = delta_ref.shape
     total = terms[0][0].astype(F32)
     for term in terms[1:]:
         total = total + term[0].astype(F32)
-    delta = global_ref[lo : lo + rows, :] - total / replicas
+    delta = global_ref[...] - total / replicas
     delta_ref[...] = delta
     sent_ref[...] = delta.astype(BF16)
     squares = jnp.sum(delta * delta, axis=0, keepdims=True)
@@ -310,9 +306,9 @@
         lo += part.shape[0]
 
 
-def weight_kernel(sizes, entries, place_ref, global_ref, momentum_ref, *refs):
+def weight_kernel(sizes, entries, place_ref, kept_ref, global_ref, momentum_ref, *refs):
     count = len(sizes)
-    pairs, deltas, squares = refs[: 2 * count + 2], refs[2 * count + 2 : 3 * count + 2], refs[3 * count + 2 : -3]
+    pairs, deltas, squares = refs[: 2 * count], refs[2 * count : 3 * count], refs[3 * count : -3]
     new_ref, new_global_ref, new_momentum_ref = refs[-3:]
     mean = (squares[0][:1, :1] + squares[1][:1, :1]) / entries
     factor = jnp.minimum(1.0, clip_rms / jnp.sqrt(mean + 1e-06))
@@ -323,9 +319,9 @@
     def one_core(core, side):
         lo = 0
         for n, size in enumerate(sizes):
-            kept = pairs[side][at_chip, lo : lo + size, :].astype(F32)
-            delta = pairs[2 * n + 2 + side][at_chip, :size, :].astype(F32)
-            new_ref[core * owned + lo : core * owned + lo + size, :] = (kept - scale * delta).astype(BF16)
+            rows = slice(core * owned + lo, core * owned + lo + size)
+            delta = pairs[2 * n + side][at_chip].astype(F32)
+            new_ref[rows, :] = (kept_ref[rows, :].astype(F32) - scale * delta).astype(BF16)
             lo += size
 
     for own_core in range(2):
@@ -423,7 +419,7 @@
         done = jax.ShapeDtypeStruct((8, LANES), F32)
         *results, ran = pl.pallas_call(
             in_turn(kernel, len(inputs), len(waits), len(outs)),
-            in_specs=[*in_specs, *[vmem] * len(waits)],
+            in_specs=[*in_specs, *[vmem if v.size <= 8 * LANES or v.shape == (span_rows, tokens) else anywhere for v in waits]],
             out_specs=[*out_specs, vmem],
             out_shape=[*outs, done],
             **options,
@@ -475,10 +471,19 @@
 
     by_group, by_state, dt_spec, gain_spec = group_specs(0)
     shared = in_hbm(dt_rows, gate_z, b_proj, c_proj, gain, a_log, dt_bias, skip_d)
-    later = [stored, target, global_weight, momentum]
-    (kept,) = step(kept_kernel, in_hbm(global_weight, momentum), [shape(owned, inner)])
-    spread_rows("kept", kept)
-    weight, goal, own_global, own_momentum, normed, inv = run(
+    later = [stored, target]
+    (kept,) = run(
+        kept_kernel,
+        in_hbm(global_weight, momentum),
+        [pl.BlockSpec((owned, inner), lambda i: (0, 0))] * 2,
+        [shape(owned, inner)],
+        [pl.BlockSpec((owned, inner), lambda i: (0, 0))],
+        grid=(1,),
+        cost_estimate=small_cost,
+        compiler_params=small,
+    )
+    (kept_all,) = in_hbm(lax.all_gather(kept, "replica", axis=0, tiled=True))
+    weight, goal, normed, inv = run(
         functools.partial(forward_kernel, len(later)),
         [shared[0], *in_hbm(x_in), *shared[1:], *in_hbm(*later)],
         [dt_spec, by_group, by_group, by_state, by_state, gain_spec, smem, smem, smem] + [anywhere] * len(later),
@@ -502,11 +507,11 @@
     first_landed = [lax.ppermute(p, "tensor", in_hops[0]) if in_hops else None for p in parts]
     sums, cots = {}, {}
 
-    def sum_side(n):
+    def sum_side(n, waits=()):
         held = parts[n]
         for at, pairs in enumerate(in_hops):
             landed = first_landed[n] if at == 0 else lax.ppermute(held, "tensor", pairs)
-            (held,) = step(add_kernel, [held, landed], [part])
+            (held,) = step(add_kernel, [held, landed], [part], waits=waits)
         sums[n] = held
 
     def sum_all(n, waits=(), cost=small_cost):
@@ -525,12 +530,17 @@
     def new_rows(b, waits=()):
         batch = batches[b]
         rows = len(batch) * piece
-        keep, send = step(
-            functools.partial(gradient_kernel, batch),
-            [c for n in batch for c in cots[n]] + [normed, weight],
+        col_tile = min(inner, 512)
+        keep, send = run(
+            functools.partial(gradient_kernel, len(batch)),
+            [places, *[c for n in batch for c in cots[n]], normed, *in_hbm(stored)],
+            [smem] + [vmem] * (2 * len(batch) + 1) + [pl.BlockSpec((replicas, rows, col_tile), lambda i: (0, b, i))],
             [shape(replicas // 2, rows, inner)] * 2,
-            scalars=[places],
-            waits=waits,
+            [vmem] * 2,
+            waits,
+            grid=(inner // col_tile,),
+            cost_estimate=small_cost,
+            compiler_params=small,
         )
         return [keep, exchange(send, 1)]
 
@@ -552,18 +562,23 @@
     def own_rows(b, cost=small_cost):
         batch = batches[b]
         rows = len(batch) * piece
-        deltas[b], sent, squares[b] = step(
-            functools.partial(delta_kernel, len(terms[b]), batch[0] * piece, replicas),
-            [own_global, squares[b - 1], *terms[b]],
+        deltas[b], sent, squares[b] = run(
+            functools.partial(delta_kernel, len(terms[b]), replicas),
+            [*in_hbm(global_weight), squares[b - 1], *terms[b]],
+            [pl.BlockSpec((rows, inner), lambda i: (b, 0))] + [vmem] * (1 + len(terms[b])),
             [shape(rows, inner, dtype=F32), shape(rows, inner), tile],
-            cost=cost,
+            [vmem] * 3,
+            grid=(1,),
+            cost_estimate=cost,
+            compiler_params=small,
         )
         spread_rows(b, sent)
 
     def backward(begin, count, so_far):
         wide, state, dt, gain_here = group_specs(begin)
-        operands = [places, *shared, normed, inv, weight] + [c for n in range(chunks) for c in cots[n]]
-        specs = [smem, dt, wide, state, state, gain_here, smem, smem, smem, vmem, vmem, vmem] + [vmem] * (2 * chunks)
+        operands = [places, *shared, normed, inv, *in_hbm(stored)] + [c for n in range(chunks) for c in cots[n]]
+        specs = [smem, dt, wide, state, state, gain_here, smem, smem, smem, vmem, vmem]
+        specs += [pl.BlockSpec((replicas, owned, width), lambda g: (0, 0, g + begin))] + [vmem] * (2 * chunks)
         aliases = {}
         if so_far is not None:
             aliases = {len(operands): 0}
@@ -585,13 +600,11 @@
 
     first, second = range(2)
     for t in range(chunks):
-        sum_side(t)
-        if t == 0:
-            join("kept")
-        else:
+        sum_side(t, [cots[t - 3][1], kept_all] if t >= 3 else [kept_all] if t == chunks - 1 else [])
+        if t > 0:
             sum_all(t - 1)
     held_first = new_rows(first)
-    sum_all(chunks - 1, [cots[chunks - 2][1], gathered["kept"][1]], large_cost)
+    sum_all(chunks - 1, [cots[chunks - 2][1]], large_cost)
     send_rows(first, held_first)
     held_second = new_rows(second)
     own_rows(first, large_cost)
@@ -612,12 +625,11 @@
     sizes = [len(batch) * piece for batch in batches]
     pair_spec = pl.BlockSpec((2 * owned, inner), lambda r: (r, 0))
     held_spec = pl.BlockSpec((owned, inner), lambda r: (0, 0))
-    inputs = [own_global, own_momentum, *gathered["kept"], *gathered[first], *gathered[second]]
-    inputs += [deltas[first], deltas[second], *columns]
+    inputs = [*gathered[first], *gathered[second], deltas[first], deltas[second], *columns]
     new_weight, new_global, new_momentum = run(
         functools.partial(weight_kernel, sizes, features * inner * heads_over),
-        [places, *inputs],
-        [smem] + [vmem] * len(inputs),
+        [places, kept_all, *in_hbm(global_weight, momentum), *inputs],
+        [smem, pair_spec, held_spec, held_spec] + [vmem] * len(inputs),
         [shape(features, inner), shape(owned, inner, dtype=F32), shape(owned, inner, dtype=F32)],
         [pair_spec, held_spec, held_spec],
         grid=(replicas // 2,),

time: 178 us -> 175 us (0.983)
  waiting for transfers between devices: 94.9 us -> 63.1 us
  between operations: 1 us -> 14.4 us
  Pallas kernels: 35.4 us -> 45.5 us
  local copies, waits for them, and re-layouts: 0.09 us -> 8.25 us
  starting transfers between devices: 46.4 us -> 42.6 us
    ppermute x4, waiting for transfers between devices: 33.9 us -> 17.6 us  [sum_all(): back = lax.ppermute(out, 'tensor', [(b, a) for a, b in pairs])]
    ppermute x21 -> x17, waiting for transfers between devices: 24.8 us -> 8.64 us  [exchange(): lax.ppermute(value, 'replica', [(r, r ^ mask) for r in range(replicas)])]
    pallas_call x28 -> x27, Pallas kernels: 35.4 us -> 45.5 us  [run(): pl.pallas_call(in_turn(kernel, len(inputs), len(waits), len(outs)), in_sp...]
    unnamed x0 -> x16, local copies, waits for them, and re-layouts: none -> 8.16 us
    ppermute x21 -> x17, starting transfers between devices: 18.5 us -> 14.9 us  [exchange(): lax.ppermute(value, 'replica', [(r, r ^ mask) for r in range(replicas)])]
    ppermute x4, starting transfers between devices: 17.8 us -> 14.8 us  [shards(): lax.ppermute(p, 'tensor', in_hops[0])]
    ppermute x4, waiting for transfers between devices: 22.8 us -> 25.5 us  [shards(): lax.ppermute(p, 'tensor', in_hops[0])]
    ppermute x4, starting transfers between devices: 1.96 us -> 3.99 us  [shards(): lax.ppermute(total, axis, pairs)]
  transfers between devices with their start and end apart: 37 -> 34, of which waited for: 17 -> 15; matrix products, arithmetic and copies ran while one was open for 0% -> 0% of each run, Pallas kernels for 12% -> 20%
where the time goes in v9:
time: 175 us; the launch traced here: 174 us
  waiting for transfers between devices  63.1 us (36%)
  Pallas kernels  45.5 us (26%)
  starting transfers between devices  42.6 us (24%)
  between operations  14.4 us (8%)
  local copies, waits for them, and re-layouts  8.25 us (5%)
    pallas_call x27, Pallas kernels, run(): pl.pallas_call(in_turn(kernel, len(inputs), len(waits), len(outs)), in_sp...  45.5 us
    ppermute x4, waiting for transfers between devices, shards(): lax.ppermute(p, 'tensor', in_hops[0])  25.5 us
    ppermute x4, waiting for transfers between devices, sum_all(): back = lax.ppermute(out, 'tensor', [(b, a) for a, b in pairs])  17.6 us
    ppermute x17, starting transfers between devices, exchange(): lax.ppermute(value, 'replica', [(r, r ^ mask) for r in range(replicas)])  14.9 us
    ppermute x4, starting transfers between devices, shards(): lax.ppermute(p, 'tensor', in_hops[0])  14.8 us
    ppermute x4, waiting for transfers between devices, shards(): lax.ppermute(total, axis, pairs)  11.3 us
    ppermute x17, waiting for transfers between devices, exchange(): lax.ppermute(value, 'replica', [(r, r ^ mask) for r in range(replicas)])  8.64 us
    unnamed x16, local copies, waits for them, and re-layouts  8.16 us
  transfers between devices with their start and end apart: 34, of which 15 were waited for; matrix products, arithmetic and copies ran while one was open for 0% of the time, Pallas kernels for 20%

profile of v9, /device:TPU:0, one launch (start us, length us, event | category | flops | bytes accessed | tf_op | source)
XLA Modules:
  0.0 173.8 jit_solution(14116889180308362653)
XLA Ops:
  7.2 2.5 %shard_map.156 = (bf16[256,1024]{1,0:T(8,128)(2,1)}, f32[8,128]{1,0:T(8,128)S(1)}) custom-call(f32[256,1024]{1,0:T(8,128)} %refs_2_.7, f32[256,1024]{1,0:T(8,128)} %refs_3_.7), custom_call_target="tpu_custom_call" | custom-call | flops 1 | bytes 1 | tf_op jit(solution)/shard_map/pallas_call | solution.py:420
  9.7 6.0 %shard_map.157 = (bf16[8,256,1024]{2,1,0:T(8,128)(2,1)S(1)}, bf16[128,2048]{1,0:T(8,128)(2,1)S(1)}, bf16[512,1024]{1,0:T(8,128)(2,1)S(1)}, f32[2,512,1]{2,1,0:T(8,128)S(1)}, f32[8,128]{1,0:T(8,128)S(1)}) custom-call(f32[16,512]{1,0:T(8,128)} %bitcast.30, bf16[512,1024]{1,0:T(8,128)(2,1)} %refs_1_.3, bf16[512,1024]{1,0:T(8,128)(2,1)} %refs_2_.6, ...), custom_call_target="tpu_custom_call" | custom-call | flops 1 | bytes 1 | tf_op jit(solution)/shard_map/pallas_call | solution.py:420
  18.6 2.5 %copy-done.1 = bf16[8,256,1024]{2,1,0:T(8,128)(2,1)S(1)} copy-done((bf16[8,256,1024]{2,1,0:T(8,128)(2,1)S(1)}, bf16[8,256,1024]{2,1,0:T(8,128)(2,1)}, u32[]{:S(2)}) %copy-start.1) | copy-done | bytes 4194328
  22.5 5.0 %collective-permute-start = (bf16[512,512]{1,0:T(8,128)(2,1)S(1)}, bf16[512,512]{1,0:T(8,128)(2,1)S(1)}, u32[]{:S(2)}, u32[]{:S(2)}) collective-permute-start(bf16[512,512]{1,0:T(8,128)(2,1)S(1)} %get-tuple-element.82.refs_0_), channel_id=1, source_target_pairs={{0,1},{3,2},{4,5},{7,6},{8,9},{11,10},{12,13},{15,14},{16,17},{19,... | collective-permute-start | bytes 1572872 | tf_op jit(solution)/shard_map/ppermute | solution.py:507
  27.4 2.5 %shard_map.159 = (bf16[512,512]{1,0:T(8,128)(2,1)S(1)}, bf16[512,512]{1,0:T(8,128)(2,1)S(1)}, bf16[512,512]{1,0:T(8,128)(2,1)S(1)}, f32[8,128]{1,0:T(8,128)S(1)}) custom-call(s32[5]{0:T(128)S(1)} %stack.23.refs_0_, bf16[8,256,1024]{2,1,0:T(8,128)(2,1)S(1)} %copy-done.1, bf16[512,1024]{1,0:T(8,128)(2,1)S(1)} %get-tuple-element.77.refs_2_.refs_5_.refs_9_, ...), custom_call_target="tpu_custom_call" | custom-call | flops 1 | bytes 1 | tf_op jit(solution)/shard_map/pallas_call | solution.py:420
  31.3 8.4 %collective-permute-done.refs_1_ = bf16[512,512]{1,0:T(8,128)(2,1)S(1)} collective-permute-done((bf16[512,512]{1,0:T(8,128)(2,1)S(1)}, bf16[512,512]{1,0:T(8,128)(2,1)S(1)}, u32[]{:S(2)}, u32[]{:S(2)}) %collective-permute-start) | collective-permute-done | bytes 524320 | tf_op jit(solution)/shard_map/ppermute | solution.py:507
  40.6 7.2 %collective-permute-start.5 = (bf16[512,512]{1,0:T(8,128)(2,1)S(1)}, bf16[512,512]{1,0:T(8,128)(2,1)S(1)}, u32[]{:S(2)}, u32[]{:S(2)}) collective-permute-start(bf16[512,512]{1,0:T(8,128)(2,1)S(1)} %get-tuple-element.91.refs_0_), channel_id=1, source_target_pairs={{0,1},{3,2},{4,5},{7,6},{8,9},{11,10},{12,13},{15,14},{16,17},{19,... | collective-permute-start | bytes 1572872 | tf_op jit(solution)/shard_map/ppermute | solution.py:507
  53.2 9.0 %collective-permute-done.5.refs_1_ = bf16[512,512]{1,0:T(8,128)(2,1)S(1)} collective-permute-done((bf16[512,512]{1,0:T(8,128)(2,1)S(1)}, bf16[512,512]{1,0:T(8,128)(2,1)S(1)}, u32[]{:S(2)}, u32[]{:S(2)}) %collective-permute-start.5) | collective-permute-done | bytes 524320 | tf_op jit(solution)/shard_map/ppermute | solution.py:507
  66.0 6.2 %collective-permute-done.8.refs_1_ = bf16[512,512]{1,0:T(8,128)(2,1)S(1)} collective-permute-done((bf16[512,512]{1,0:T(8,128)(2,1)S(1)}, bf16[512,512]{1,0:T(8,128)(2,1)S(1)}, u32[]{:S(2)}, u32[]{:S(2)}) %collective-permute-start.8) | collective-permute-done | bytes 524320 | tf_op jit(solution)/shard_map/ppermute | solution.py:507
  80.0 2.9 %shard_map.167 = (bf16[4,128,1024]{2,1,0:T(8,128)(2,1)S(1)}, bf16[4,128,1024]{2,1,0:T(8,128)(2,1)S(1)}, f32[8,128]{1,0:T(8,128)S(1)}) custom-call(s32[5]{0:T(128)S(1)} %stack.23.refs_0_, bf16[512,512]{1,0:T(8,128)(2,1)S(1)} %get-tuple-element.89.refs_1_.refs_12_, bf16[512,512]{1,0:T(8,128)(2,1)S(1)} %collective-permute-done.3.refs_3_.refs_2_.refs_13_, ...), custom_call_target="tpu_custom_call" | custom-call | flops 1 | bytes 1 | tf_op jit(solution)/shard_map/pallas_call | solution.py:420
  82.9 8.5 %collective-permute-done.9.refs_3_.refs_2_.refs_17_ = bf16[512,512]{1,0:T(8,128)(2,1)S(1)} collective-permute-done((bf16[512,512]{1,0:T(8,128)(2,1)S(1)}, bf16[512,512]{1,0:T(8,128)(2,1)S(1)}, u32[]{:S(2)}, u32[]{:S(2)}) %collective-permute-start.9) | collective-permute-done | bytes 524320 | tf_op jit(solution)/shard_map/ppermute | solution.py:522
  97.4 7.7 %collective-permute-done.11.refs_4_.refs_19_ = bf16[512,512]{1,0:T(8,128)(2,1)S(1)} collective-permute-done((bf16[512,512]{1,0:T(8,128)(2,1)S(1)}, bf16[512,512]{1,0:T(8,128)(2,1)S(1)}, u32[]{:S(2)}, u32[]{:S(2)}) %collective-permute-start.11) | collective-permute-done | bytes 524320 | tf_op jit(solution)/shard_map/ppermute | solution.py:522
  105.1 2.9 %shard_map.170 = (bf16[4,128,1024]{2,1,0:T(8,128)(2,1)S(1)}, bf16[4,128,1024]{2,1,0:T(8,128)(2,1)S(1)}, f32[8,128]{1,0:T(8,128)S(1)}) custom-call(s32[5]{0:T(128)S(1)} %stack.23.refs_0_, bf16[512,512]{1,0:T(8,128)(2,1)S(1)} %get-tuple-element.100.refs_1_.refs_16_, bf16[512,512]{1,0:T(8,128)(2,1)S(1)} %collective-permute-done.9.refs_3_.refs_2_.refs_17_, ...), custom_call_target="tpu_custom_call" | custom-call | flops 1 | bytes 1 | tf_op jit(solution)/shard_map/pallas_call | solution.py:420
  109.7 2.4 %collective-permute-start.19 = (bf16[1,128,1024]{2,1,0:T(8,128)(2,1)S(1)}, bf16[1,128,1024]{2,1,0:T(8,128)(2,1)S(1)}, u32[]{:S(2)}, u32[]{:S(2)}) collective-permute-start(bf16[1,128,1024]{2,1,0:T(8,128)(2,1)S(1)} %bitcast.17), channel_id=1, source_target_pairs={{0,24},{4,28},{8,16},{12,20},{16,8},{20,12},{24,0},{28,4},{1,25},{... | collective-permute-start | bytes 786440 | tf_op jit(solution)/shard_map/ppermute | solution.py:455
  117.1 6.0 %shard_map.173 = (bf16[512,1024]{1,0:T(8,128)(2,1)}, f32[8,128]{1,0:T(8,128)S(1)}) custom-call(s32[5]{0:T(128)S(1)} %stack.23.refs_0_, f32[16,512]{1,0:T(8,128)} %bitcast.31, bf16[512,1024]{1,0:T(8,128)(2,1)} %refs_2_.6, bf16[512,256]{1,0:T(8,128)(2,1)} %refs_3_.6, bf16[512,256]{1,0:T(8,128)(2,1)} %refs_4_.5, f32[1,1024]{1,0:T(1,128)} %bitcast.34, ...), custom_call_target="tpu_custom_call" | custom-call | flops 30000001024 | bytes 1 | tf_op jit(solution)/shard_map/pallas_call | solution.py:420
  125.6 6.0 %shard_map.175 = (bf16[512,1024]{1,0:T(8,128)(2,1)}, f32[8,128]{1,0:T(8,128)S(1)}) custom-call(s32[5]{0:T(128)S(1)} %stack.23.refs_0_, f32[16,512]{1,0:T(8,128)} %bitcast.32, bf16[512,1024]{1,0:T(8,128)(2,1)} %refs_2_.6, bf16[512,256]{1,0:T(8,128)(2,1)} %refs_3_.6, bf16[512,256]{1,0:T(8,128)(2,1)} %refs_4_.5, ...), custom_call_target="tpu_custom_call", output_to_operand_aliasing={{0}: (20, {})} | custom-call | flops 30000001024 | bytes 1 | tf_op jit(solution)/shard_map/pallas_call | solution.py:420
  131.6 4.6 %collective-permute-done.23.refs_5_ = bf16[1,128,1024]{2,1,0:T(8,128)(2,1)S(1)} collective-permute-done((bf16[1,128,1024]{2,1,0:T(8,128)(2,1)S(1)}, bf16[1,128,1024]{2,1,0:T(8,128)(2,1)S(1)}, u32[]{:S(2)}, u32[]{:S(2)}) %collective-permute-start.23) | collective-permute-done | bytes 262176 | tf_op jit(solution)/shard_map/ppermute | solution.py:455
  137.7 2.4 %collective-permute-start.26 = (bf16[1,128,1024]{2,1,0:T(8,128)(2,1)S(1)}, bf16[1,128,1024]{2,1,0:T(8,128)(2,1)S(1)}, u32[]{:S(2)}, u32[]{:S(2)}) collective-permute-start(bf16[1,128,1024]{2,1,0:T(8,128)(2,1)S(1)} %bitcast.21), channel_id=1, source_target_pairs={{0,24},{4,28},{8,16},{12,20},{16,8},{20,12},{24,0},{28,4},{1,25},{... | collective-permute-start | bytes 786440 | tf_op jit(solution)/shard_map/ppermute | solution.py:455
  141.2 3.6 %collective-permute-done.27.refs_1_ = f32[8,128]{1,0:T(8,128)S(1)} collective-permute-done((f32[8,128]{1,0:T(8,128)S(1)}, f32[8,128]{1,0:T(8,128)S(1)}, u32[]{:S(2)}, u32[]{:S(2)}) %collective-permute-start.27) | collective-permute-done | bytes 4128 | tf_op jit(solution)/shard_map/ppermute | solution.py:621
  145.8 3.5 %collective-permute-done.28.refs_1_ = f32[8,128]{1,0:T(8,128)S(1)} collective-permute-done((f32[8,128]{1,0:T(8,128)S(1)}, f32[8,128]{1,0:T(8,128)S(1)}, u32[]{:S(2)}, u32[]{:S(2)}) %collective-permute-start.28) | collective-permute-done | bytes 4128 | tf_op jit(solution)/shard_map/ppermute | solution.py:621
  150.8 2.1 %collective-permute-done.29.refs_1_ = f32[8,128]{1,0:T(8,128)S(1)} collective-permute-done((f32[8,128]{1,0:T(8,128)S(1)}, f32[8,128]{1,0:T(8,128)S(1)}, u32[]{:S(2)}, u32[]{:S(2)}) %collective-permute-start.29) | collective-permute-done | bytes 4128 | tf_op jit(solution)/shard_map/ppermute | solution.py:621
  154.4 2.1 %collective-permute-done.30.refs_1_ = f32[8,128]{1,0:T(8,128)S(1)} collective-permute-done((f32[8,128]{1,0:T(8,128)S(1)}, f32[8,128]{1,0:T(8,128)S(1)}, u32[]{:S(2)}, u32[]{:S(2)}) %collective-permute-start.30) | collective-permute-done | bytes 4128 | tf_op jit(solution)/shard_map/ppermute | solution.py:621
  157.2 2.2 %collective-permute-done.32.refs_11_ = f32[8,128]{1,0:T(8,128)S(1)} collective-permute-done((f32[8,128]{1,0:T(8,128)S(1)}, f32[8,128]{1,0:T(8,128)S(1)}, u32[]{:S(2)}, u32[]{:S(2)}) %collective-permute-start.32) | collective-permute-done | bytes 4128 | tf_op jit(solution)/shard_map/ppermute | solution.py:455
  159.3 7.6 %shard_map.182 = (bf16[2048,1024]{1,0:T(8,128)(2,1)}, f32[256,1024]{1,0:T(8,128)}, f32[256,1024]{1,0:T(8,128)}, f32[8,128]{1,0:T(8,128)}) custom-call(s32[5]{0:T(128)S(1)} %stack.23.refs_0_, bf16[2048,1024]{1,0:T(8,128)(2,1)} %all-gather.2.cloned.1.call-done.refs_4_.refs_1_, f32[256,1024]{1,0:T(8,128)} %refs_2_.7, f32[256,1024]{1,0:T(8,128)} %refs_3_.7, ...), custom_call_target="tpu_custom_call" | custom-call | flops 1 | bytes 1 | tf_op jit(solution)/shard_map/pallas_call | solution.py:420
  (90 shorter events, 45.6 us)
Async XLA Ops:
  7.2 65.9 %all-gather.2.cloned.1.call-start = ((), (), s32[]{:S(2)}) async-start(), calls=%async_computation | async-start | bytes 4718592 | tf_op jit(solution)/shard_map/all_gather | solution.py:485
  22.5 17.3 %collective-permute-start = (bf16[512,512]{1,0:T(8,128)(2,1)S(1)}, bf16[512,512]{1,0:T(8,128)(2,1)S(1)}, u32[]{:S(2)}, u32[]{:S(2)}) collective-permute-start(bf16[512,512]{1,0:T(8,128)(2,1)S(1)} %get-tuple-element.82.refs_0_), channel_id=1, source_target_pairs={{0,1},{3,2},{4,5},{7,6},{8,9},{11,10},{12,13},{15,14},{16,17},{19,... | collective-permute-start | bytes 1572872 | tf_op jit(solution)/shard_map/ppermute | solution.py:507
  30.0 21.0 %collective-permute-start.2 = (bf16[512,512]{1,0:T(8,128)(2,1)S(1)}, bf16[512,512]{1,0:T(8,128)(2,1)S(1)}, u32[]{:S(2)}, u32[]{:S(2)}) collective-permute-start(bf16[512,512]{1,0:T(8,128)(2,1)S(1)} %get-tuple-element.86.refs_0_), channel_id=1, source_target_pairs={{0,1},{3,2},{4,5},{7,6},{8,9},{11,10},{12,13},{15,14},{16,17},{19,... | collective-permute-start | bytes 1572872 | tf_op jit(solution)/shard_map/ppermute | solution.py:507
  40.6 21.6 %collective-permute-start.5 = (bf16[512,512]{1,0:T(8,128)(2,1)S(1)}, bf16[512,512]{1,0:T(8,128)(2,1)S(1)}, u32[]{:S(2)}, u32[]{:S(2)}) collective-permute-start(bf16[512,512]{1,0:T(8,128)(2,1)S(1)} %get-tuple-element.91.refs_0_), channel_id=1, source_target_pairs={{0,1},{3,2},{4,5},{7,6},{8,9},{11,10},{12,13},{15,14},{16,17},{19,... | collective-permute-start | bytes 1572872 | tf_op jit(solution)/shard_map/ppermute | solution.py:507
  47.8 24.4 %collective-permute-start.8 = (bf16[512,512]{1,0:T(8,128)(2,1)S(1)}, bf16[512,512]{1,0:T(8,128)(2,1)S(1)}, u32[]{:S(2)}, u32[]{:S(2)}) collective-permute-start(bf16[512,512]{1,0:T(8,128)(2,1)S(1)} %get-tuple-element.96.refs_0_), channel_id=1, source_target_pairs={{0,1},{3,2},{4,5},{7,6},{8,9},{11,10},{12,13},{15,14},{16,17},{19,... | collective-permute-start | bytes 1572872 | tf_op jit(solution)/shard_map/ppermute | solution.py:507
  51.1 13.5 %collective-permute-start.4 = (bf16[512,512]{1,0:T(8,128)(2,1)S(1)}, bf16[512,512]{1,0:T(8,128)(2,1)S(1)}, u32[]{:S(2)}, u32[]{:S(2)}) collective-permute-start(bf16[512,512]{1,0:T(8,128)(2,1)S(1)} %get-tuple-element.90.refs_0_), channel_id=1, source_target_pairs={{1,2},{2,1},{5,6},{6,5},{9,10},{10,9},{13,14},{14,13},{17,18},{18,... | collective-permute-start | bytes 1572872 | tf_op jit(solution)/shard_map/ppermute | solution.py:518
  51.9 21.1 %collective-permute-start.3 = (bf16[512,512]{1,0:T(8,128)(2,1)S(1)}, bf16[512,512]{1,0:T(8,128)(2,1)S(1)}, u32[]{:S(2)}, u32[]{:S(2)}) collective-permute-start(bf16[512,512]{1,0:T(8,128)(2,1)S(1)} %get-tuple-element.89.refs_1_.refs_12_), channel_id=1, source_target_pairs={{1,0},{2,3},{5,4},{6,7},{9,8},{10,11},{13,12},{14,15},{17,16},{18,... | collective-permute-start | bytes 1572872 | tf_op jit(solution)/shard_map/ppermute | solution.py:522
  63.1 12.1 %collective-permute-start.7 = (bf16[512,512]{1,0:T(8,128)(2,1)}, bf16[512,512]{1,0:T(8,128)(2,1)}, u32[]{:S(2)}, u32[]{:S(2)}) collective-permute-start(bf16[512,512]{1,0:T(8,128)(2,1)} %get-tuple-element.95.refs_0_), channel_id=1, source_target_pairs={{1,2},{2,1},{5,6},{6,5},{9,10},{10,9},{13,14},{14,13},{17,18},{18,... | collective-permute-start | bytes 1572872 | tf_op jit(solution)/shard_map/ppermute | solution.py:518
  64.7 15.3 %collective-permute-start.6 = (bf16[512,512]{1,0:T(8,128)(2,1)S(1)}, bf16[512,512]{1,0:T(8,128)(2,1)S(1)}, u32[]{:S(2)}, u32[]{:S(2)}) collective-permute-start(bf16[512,512]{1,0:T(8,128)(2,1)S(1)} %get-tuple-element.94.refs_3_.refs_14_), channel_id=1, source_target_pairs={{1,0},{2,3},{5,4},{6,7},{9,8},{10,11},{13,12},{14,15},{17,16},{18,... | collective-permute-start | bytes 1572872 | tf_op jit(solution)/shard_map/ppermute | solution.py:522
  76.6 14.9 %collective-permute-start.9 = (bf16[512,512]{1,0:T(8,128)(2,1)S(1)}, bf16[512,512]{1,0:T(8,128)(2,1)S(1)}, u32[]{:S(2)}, u32[]{:S(2)}) collective-permute-start(bf16[512,512]{1,0:T(8,128)(2,1)S(1)} %get-tuple-element.100.refs_1_.refs_16_), channel_id=1, source_target_pairs={{1,0},{2,3},{5,4},{6,7},{9,8},{10,11},{13,12},{14,15},{17,16},{18,... | collective-permute-start | bytes 1572872 | tf_op jit(solution)/shard_map/ppermute | solution.py:522
  77.9 13.6 %collective-permute-start.10 = (bf16[512,512]{1,0:T(8,128)(2,1)S(1)}, bf16[512,512]{1,0:T(8,128)(2,1)S(1)}, u32[]{:S(2)}, u32[]{:S(2)}) collective-permute-start(bf16[512,512]{1,0:T(8,128)(2,1)S(1)} %get-tuple-element.101.refs_0_), channel_id=1, source_target_pairs={{1,2},{2,1},{5,6},{6,5},{9,10},{10,9},{13,14},{14,13},{17,18},{18,... | collective-permute-start | bytes 1572872 | tf_op jit(solution)/shard_map/ppermute | solution.py:518
  91.6 13.6 %collective-permute-start.11 = (bf16[512,512]{1,0:T(8,128)(2,1)S(1)}, bf16[512,512]{1,0:T(8,128)(2,1)S(1)}, u32[]{:S(2)}, u32[]{:S(2)}) collective-permute-start(bf16[512,512]{1,0:T(8,128)(2,1)S(1)} %get-tuple-element.104.refs_3_.refs_18_), channel_id=1, source_target_pairs={{1,0},{2,3},{5,4},{6,7},{9,8},{10,11},{13,12},{14,15},{17,16},{18,... | collective-permute-start | bytes 1572872 | tf_op jit(solution)/shard_map/ppermute | solution.py:522
  93.9 14.3 %collective-permute-start.14 = (bf16[1,128,1024]{2,1,0:T(8,128)(2,1)S(1)}, bf16[1,128,1024]{2,1,0:T(8,128)(2,1)S(1)}, u32[]{:S(2)}, u32[]{:S(2)}) collective-permute-start(bf16[1,128,1024]{2,1,0:T(8,128)(2,1)S(1)} %get-tuple-element.112), channel_id=1, source_target_pairs={{0,8},{4,12},{8,0},{12,4},{16,24},{20,28},{24,16},{28,20},{1,9},{5... | collective-permute-start | bytes 786440 | tf_op jit(solution)/shard_map/ppermute | solution.py:455
  95.4 12.7 %collective-permute-start.15 = (bf16[1,128,1024]{2,1,0:T(8,128)(2,1)S(1)}, bf16[1,128,1024]{2,1,0:T(8,128)(2,1)S(1)}, u32[]{:S(2)}, u32[]{:S(2)}) collective-permute-start(bf16[1,128,1024]{2,1,0:T(8,128)(2,1)S(1)} %get-tuple-element.113), channel_id=1, source_target_pairs={{0,16},{4,20},{8,24},{12,28},{16,0},{20,4},{24,8},{28,12},{1,17},{... | collective-permute-start | bytes 786440 | tf_op jit(solution)/shard_map/ppermute | solution.py:455
  109.7 13.4 %collective-permute-start.19 = (bf16[1,128,1024]{2,1,0:T(8,128)(2,1)S(1)}, bf16[1,128,1024]{2,1,0:T(8,128)(2,1)S(1)}, u32[]{:S(2)}, u32[]{:S(2)}) collective-permute-start(bf16[1,128,1024]{2,1,0:T(8,128)(2,1)S(1)} %bitcast.17), channel_id=1, source_target_pairs={{0,24},{4,28},{8,16},{12,20},{16,8},{20,12},{24,0},{28,4},{1,25},{... | collective-permute-start | bytes 786440 | tf_op jit(solution)/shard_map/ppermute | solution.py:455
  112.1 12.8 %collective-permute-start.18 = (bf16[1,128,1024]{2,1,0:T(8,128)(2,1)S(1)}, bf16[1,128,1024]{2,1,0:T(8,128)(2,1)S(1)}, u32[]{:S(2)}, u32[]{:S(2)}) collective-permute-start(bf16[1,128,1024]{2,1,0:T(8,128)(2,1)S(1)} %bitcast.18), channel_id=1, source_target_pairs={{0,16},{4,20},{8,24},{12,28},{16,0},{20,4},{24,8},{28,12},{1,17},{... | collective-permute-start | bytes 786440 | tf_op jit(solution)/shard_map/ppermute | solution.py:455
  112.7 12.8 %collective-permute-start.17 = (bf16[1,128,1024]{2,1,0:T(8,128)(2,1)S(1)}, bf16[1,128,1024]{2,1,0:T(8,128)(2,1)S(1)}, u32[]{:S(2)}, u32[]{:S(2)}) collective-permute-start(bf16[1,128,1024]{2,1,0:T(8,128)(2,1)S(1)} %bitcast.19), channel_id=1, source_target_pairs={{0,8},{4,12},{8,0},{12,4},{16,24},{20,28},{24,16},{28,20},{1,9},{5... | collective-permute-start | bytes 786440 | tf_op jit(solution)/shard_map/ppermute | solution.py:455
  114.0 17.6 %collective-permute-start.21 = (bf16[1,128,1024]{2,1,0:T(8,128)(2,1)S(1)}, bf16[1,128,1024]{2,1,0:T(8,128)(2,1)S(1)}, u32[]{:S(2)}, u32[]{:S(2)}) collective-permute-start(bf16[1,128,1024]{2,1,0:T(8,128)(2,1)S(1)} %get-tuple-element.126), channel_id=1, source_target_pairs={{0,8},{4,12},{8,0},{12,4},{16,24},{20,28},{24,16},{28,20},{1,9},{5... | collective-permute-start | bytes 786440 | tf_op jit(solution)/shard_map/ppermute | solution.py:455
  115.6 16.0 %collective-permute-start.22 = (bf16[1,128,1024]{2,1,0:T(8,128)(2,1)S(1)}, bf16[1,128,1024]{2,1,0:T(8,128)(2,1)S(1)}, u32[]{:S(2)}, u32[]{:S(2)}) collective-permute-start(bf16[1,128,1024]{2,1,0:T(8,128)(2,1)S(1)} %get-tuple-element.127), channel_id=1, source_target_pairs={{0,16},{4,20},{8,24},{12,28},{16,0},{20,4},{24,8},{28,12},{1,17},{... | collective-permute-start | bytes 786440 | tf_op jit(solution)/shard_map/ppermute | solution.py:455
  123.1 13.1 %collective-permute-start.23 = (bf16[1,128,1024]{2,1,0:T(8,128)(2,1)S(1)}, bf16[1,128,1024]{2,1,0:T(8,128)(2,1)S(1)}, u32[]{:S(2)}, u32[]{:S(2)}) collective-permute-start(bf16[1,128,1024]{2,1,0:T(8,128)(2,1)S(1)} %get-tuple-element.128), channel_id=1, source_target_pairs={{0,24},{4,28},{8,16},{12,20},{16,8},{20,12},{24,0},{28,4},{1,25},{... | collective-permute-start | bytes 786440 | tf_op jit(solution)/shard_map/ppermute | solution.py:455
  125.5 31.0 %collective-permute-start.20 = (bf16[4,128,1024]{2,1,0:T(8,128)(2,1)S(1)}, bf16[4,128,1024]{2,1,0:T(8,128)(2,1)S(1)}, u32[]{:S(2)}, u32[]{:S(2)}) collective-permute-start(bf16[4,128,1024]{2,1,0:T(8,128)(2,1)S(1)} %get-tuple-element.123.refs_4_), channel_id=1, source_target_pairs={{0,4},{4,0},{8,12},{12,8},{16,20},{20,16},{24,28},{28,24},{1,5},{5... | collective-permute-start | bytes 3145736 | tf_op jit(solution)/shard_map/ppermute | solution.py:455
  137.7 18.8 %collective-permute-start.26 = (bf16[1,128,1024]{2,1,0:T(8,128)(2,1)S(1)}, bf16[1,128,1024]{2,1,0:T(8,128)(2,1)S(1)}, u32[]{:S(2)}, u32[]{:S(2)}) collective-permute-start(bf16[1,128,1024]{2,1,0:T(8,128)(2,1)S(1)} %bitcast.21), channel_id=1, source_target_pairs={{0,24},{4,28},{8,16},{12,20},{16,8},{20,12},{24,0},{28,4},{1,25},{... | collective-permute-start | bytes 786440 | tf_op jit(solution)/shard_map/ppermute | solution.py:455
  140.1 16.4 %collective-permute-start.25 = (bf16[1,128,1024]{2,1,0:T(8,128)(2,1)S(1)}, bf16[1,128,1024]{2,1,0:T(8,128)(2,1)S(1)}, u32[]{:S(2)}, u32[]{:S(2)}) collective-permute-start(bf16[1,128,1024]{2,1,0:T(8,128)(2,1)S(1)} %bitcast.22), channel_id=1, source_target_pairs={{0,16},{4,20},{8,24},{12,28},{16,0},{20,4},{24,8},{28,12},{1,17},{... | collective-permute-start | bytes 786440 | tf_op jit(solution)/shard_map/ppermute | solution.py:455
  140.6 15.9 %collective-permute-start.24 = (bf16[1,128,1024]{2,1,0:T(8,128)(2,1)S(1)}, bf16[1,128,1024]{2,1,0:T(8,128)(2,1)S(1)}, u32[]{:S(2)}, u32[]{:S(2)}) collective-permute-start(bf16[1,128,1024]{2,1,0:T(8,128)(2,1)S(1)} %bitcast.23), channel_id=1, source_target_pairs={{0,8},{4,12},{8,0},{12,4},{16,24},{20,28},{24,16},{28,20},{1,9},{5... | collective-permute-start | bytes 786440 | tf_op jit(solution)/shard_map/ppermute | solution.py:455
  (18 other events, 112.4 us)
Sparse Core Ops, SparseCore 0:
  10.5 39.4 all-gather.1

commit v10 on v8

--- a/solution.py
+++ b/solution.py
@@ -179,6 +179,10 @@
         part = dot(weight_ref[:, at, :].reshape(replicas * piece, inner), normed_ref[...], NT)
         goal = jnp.concatenate([turned[:, at, :].reshape(replicas * piece, held)] * (tokens // held), axis=1)
         part_ref[...] = (part - jnp.where(here, goal, 0.0)).astype(BF16)
+
+
+def gate_kernel(out_ref):
+    out_ref[...] = jnp.zeros_like(out_ref)
 
 
 def add_kernel(a_ref, b_ref, sum_ref):
@@ -414,6 +418,7 @@
     large = pltpu.CompilerParams(vmem_limit_bytes=20 * 1024 * 1024)
     small = pltpu.CompilerParams(vmem_limit_bytes=12 * 1024 * 1024)
     small_cost = pl.CostEstimate(flops=1, bytes_accessed=1, transcendentals=0)
+    some_cost = pl.CostEstimate(flops=2_000_000_000, bytes_accessed=1, transcendentals=0)
     large_cost = pl.CostEstimate(flops=30_000_000_000, bytes_accessed=1, transcendentals=0)
 
     turn = []
@@ -476,8 +481,6 @@
     by_group, by_state, dt_spec, gain_spec = group_specs(0)
     shared = in_hbm(dt_rows, gate_z, b_proj, c_proj, gain, a_log, dt_bias, skip_d)
     later = [stored, target, global_weight, momentum]
-    (kept,) = step(kept_kernel, in_hbm(global_weight, momentum), [shape(owned, inner)])
-    spread_rows("kept", kept)
     weight, goal, own_global, own_momentum, normed, inv = run(
         functools.partial(forward_kernel, len(later)),
         [shared[0], *in_hbm(x_in), *shared[1:], *in_hbm(*later)],
@@ -498,15 +501,17 @@
 
     in_hops, across = inward(heads_over)
     parts = project([0])
+    (kept,) = step(kept_kernel, [own_global, own_momentum], [shape(owned, inner)])
+    spread_rows("kept", kept)
     parts += project(list(range(1, chunks)))
     first_landed = [lax.ppermute(p, "tensor", in_hops[0]) if in_hops else None for p in parts]
     sums, cots = {}, {}
 
-    def sum_side(n):
+    def sum_side(n, waits=()):
         held = parts[n]
         for at, pairs in enumerate(in_hops):
             landed = first_landed[n] if at == 0 else lax.ppermute(held, "tensor", pairs)
-            (held,) = step(add_kernel, [held, landed], [part])
+            (held,) = step(add_kernel, [held, landed], [part], waits=waits)
         sums[n] = held
 
     def sum_all(n, waits=(), cost=small_cost):
@@ -578,34 +583,37 @@
             grid=(count,),
             scratch_shapes=[pltpu.VMEM((tokens, width), F32)],
             input_output_aliases=aliases,
-            cost_estimate=large_cost,
+            cost_estimate=small_cost,
             compiler_params=large,
         )
         return grad
 
     first, second = range(2)
     for t in range(chunks):
-        sum_side(t)
+        sum_side(t, [cots[t - 3][1]] if t >= 3 else [])
         if t == 0:
             join("kept")
         else:
             sum_all(t - 1)
     held_first = new_rows(first)
-    sum_all(chunks - 1, [cots[chunks - 2][1], gathered["kept"][1]], large_cost)
+    sum_all(chunks - 1, cost=large_cost)
+    step(gate_kernel, [], [tile], waits=[cots[chunks - 2][1]])
     send_rows(first, held_first)
-    held_second = new_rows(second)
+    held_second = new_rows(second, gathered["kept"][1:])
     own_rows(first, large_cost)
     send_rows(second, held_second)
     half = groups // 2
     grad_input = backward(0, half, None) if half else None
-    join(first)
     grad_input = backward(half, groups - half, grad_input)
-    own_rows(second)
+    own_rows(second, some_cost)
     total = squares[second]
-    for axis, bits in (("tensor", range(heads_over.bit_length() - 1)), ("replica", range(1, replicas.bit_length() - 1))):
-        for bit in bits:
-            pairs = [(r, r ^ (1 << bit)) for r in range(lax.axis_size(axis))]
-            (total,) = step(add_squares_kernel, [total, lax.ppermute(total, axis, pairs)], [tile])
+    hops = [("tensor", bit) for bit in range(heads_over.bit_length() - 1)]
+    hops += [("replica", bit) for bit in range(1, replicas.bit_length() - 1)]
+    for at, (axis, bit) in enumerate(hops):
+        if at == len(hops) // 2:
+            join(first)
+        pairs = [(r, r ^ (1 << bit)) for r in range(lax.axis_size(axis))]
+        (total,) = step(add_squares_kernel, [total, lax.ppermute(total, axis, pairs)], [tile])
     join(second, gathered[first][1:])
     columns = [total, exchange(total, 1)]
 

time: 178 us -> 155 us (0.87)
  waiting for transfers between devices: 94.9 us -> 73.9 us
    ppermute x4, waiting for transfers between devices: 33.9 us -> 23.3 us  [sum_all(): back = lax.ppermute(out, 'tensor', [(b, a) for a, b in pairs])]
    ppermute x21, waiting for transfers between devices: 24.8 us -> 15.4 us  [exchange(): lax.ppermute(value, 'replica', [(r, r ^ mask) for r in range(replicas)])]
    ppermute x4, waiting for transfers between devices: 22.8 us -> 14.3 us  [shards(): lax.ppermute(p, 'tensor', in_hops[0])]
    ppermute x4, waiting for transfers between devices: 13.4 us -> 20.8 us  [shards(): lax.ppermute(total, axis, pairs)]
    pallas_call x28 -> x29, Pallas kernels: 35.4 us -> 34.4 us  [run(): pl.pallas_call(in_turn(kernel, len(inputs), len(waits), len(outs)), in_sp...]
  transfers between devices with their start and end apart: 37 -> 37, of which waited for: 17 -> 17; matrix products, arithmetic and copies ran while one was open for 0% -> 0% of each run, Pallas kernels for 12% -> 13%
where the time goes in v10:
time: 155 us; the launch traced here: 154 us
  waiting for transfers between devices  73.9 us (48%)
  starting transfers between devices  45 us (29%)
  Pallas kernels  34.4 us (22%)
    pallas_call x29, Pallas kernels, run(): pl.pallas_call(in_turn(kernel, len(inputs), len(waits), len(outs)), in_sp...  34.4 us
    ppermute x4, waiting for transfers between devices, sum_all(): back = lax.ppermute(out, 'tensor', [(b, a) for a, b in pairs])  23.3 us
    ppermute x4, waiting for transfers between devices, shards(): lax.ppermute(total, axis, pairs)  20.8 us
    ppermute x21, starting transfers between devices, exchange(): lax.ppermute(value, 'replica', [(r, r ^ mask) for r in range(replicas)])  19 us
    ppermute x4, starting transfers between devices, shards(): lax.ppermute(p, 'tensor', in_hops[0])  16.1 us
    ppermute x21, waiting for transfers between devices, exchange(): lax.ppermute(value, 'replica', [(r, r ^ mask) for r in range(replicas)])  15.4 us
    ppermute x4, waiting for transfers between devices, shards(): lax.ppermute(p, 'tensor', in_hops[0])  14.3 us
    ppermute x4, starting transfers between devices, sum_all(): back = lax.ppermute(out, 'tensor', [(b, a) for a, b in pairs])  5.35 us
  transfers between devices with their start and end apart: 37, of which 17 were waited for; matrix products, arithmetic and copies ran while one was open for 0% of the time, Pallas kernels for 13%

profile of v10, /device:TPU:0, one launch (start us, length us, event | category | flops | bytes accessed | tf_op | source)
XLA Modules:
  0.0 154.4 jit_solution(2244749191425492268)
XLA Ops:
  0.7 6.2 %shard_map.156 = (bf16[8,256,1024]{2,1,0:T(8,128)(2,1)S(1)}, bf16[128,2048]{1,0:T(8,128)(2,1)S(1)}, f32[256,1024]{1,0:T(8,128)S(1)}, f32[256,1024]{1,0:T(8,128)S...) custom-call(f32[16,512]{1,0:T(8,128)} %bitcast.31, bf16[512,1024]{1,0:T(8,128)(2,1)} %refs_1_.1, ...), custom_call_target="tpu_custom_call" | custom-call | flops 1 | bytes 1 | tf_op jit(solution)/shard_map/pallas_call | solution.py:429
  8.4 5.0 %collective-permute-start = (bf16[512,512]{1,0:T(8,128)(2,1)S(1)}, bf16[512,512]{1,0:T(8,128)(2,1)S(1)}, u32[]{:S(2)}, u32[]{:S(2)}) collective-permute-start(bf16[512,512]{1,0:T(8,128)(2,1)S(1)} %get-tuple-element.86.refs_0_), channel_id=1, source_target_pairs={{0,1},{3,2},{4,5},{7,6},{8,9},{11,10},{12,13},{15,14},{16,17},{19,... | collective-permute-start | bytes 1572872 | tf_op jit(solution)/shard_map/ppermute | solution.py:507
  17.0 2.5 %shard_map.159 = (bf16[512,512]{1,0:T(8,128)(2,1)S(1)}, bf16[512,512]{1,0:T(8,128)(2,1)S(1)}, bf16[512,512]{1,0:T(8,128)(2,1)S(1)}, f32[8,128]{1,0:T(8,128)S(1)}) custom-call(s32[5]{0:T(128)S(1)} %stack.23.refs_0_, bf16[8,256,1024]{2,1,0:T(8,128)(2,1)S(1)} %get-tuple-element.83.refs_1_.refs_6_.refs_11_, ...), custom_call_target="tpu_custom_call" | custom-call | flops 1 | bytes 1 | tf_op jit(solution)/shard_map/pallas_call | solution.py:429
  20.9 4.8 %collective-permute-done.refs_1_ = bf16[512,512]{1,0:T(8,128)(2,1)S(1)} collective-permute-done((bf16[512,512]{1,0:T(8,128)(2,1)S(1)}, bf16[512,512]{1,0:T(8,128)(2,1)S(1)}, u32[]{:S(2)}, u32[]{:S(2)}) %collective-permute-start) | collective-permute-done | bytes 524320 | tf_op jit(solution)/shard_map/ppermute | solution.py:507
  26.4 1.9 %collective-permute-done.3.refs_1_ = bf16[1,256,1024]{2,1,0:T(8,128)(2,1)S(1)} collective-permute-done((bf16[1,256,1024]{2,1,0:T(8,128)(2,1)S(1)}, bf16[1,256,1024]{2,1,0:T(8,128)(2,1)S(1)}, u32[]{:S(2)}, u32[]{:S(2)}) %collective-permute-start.3) | collective-permute-done | bytes 524320 | tf_op jit(solution)/shard_map/ppermute | solution.py:464
  28.4 5.3 %collective-permute-start.8 = (bf16[512,512]{1,0:T(8,128)(2,1)S(1)}, bf16[512,512]{1,0:T(8,128)(2,1)S(1)}, u32[]{:S(2)}, u32[]{:S(2)}) collective-permute-start(bf16[512,512]{1,0:T(8,128)(2,1)S(1)} %get-tuple-element.100.refs_0_), channel_id=1, source_target_pairs={{0,1},{3,2},{4,5},{7,6},{8,9},{11,10},{12,13},{15,14},{16,17},{19,... | collective-permute-start | bytes 1572872 | tf_op jit(solution)/shard_map/ppermute | solution.py:507
  33.7 5.7 %collective-permute-done.4.refs_2_ = bf16[1,256,1024]{2,1,0:T(8,128)(2,1)S(1)} collective-permute-done((bf16[1,256,1024]{2,1,0:T(8,128)(2,1)S(1)}, bf16[1,256,1024]{2,1,0:T(8,128)(2,1)S(1)}, u32[]{:S(2)}, u32[]{:S(2)}) %collective-permute-start.4) | collective-permute-done | bytes 524320 | tf_op jit(solution)/shard_map/ppermute | solution.py:464
  40.4 4.5 %collective-permute-start.11 = (bf16[512,512]{1,0:T(8,128)(2,1)S(1)}, bf16[512,512]{1,0:T(8,128)(2,1)S(1)}, u32[]{:S(2)}, u32[]{:S(2)}) collective-permute-start(bf16[512,512]{1,0:T(8,128)(2,1)S(1)} %get-tuple-element.105.refs_0_), channel_id=1, source_target_pairs={{0,1},{3,2},{4,5},{7,6},{8,9},{11,10},{12,13},{15,14},{16,17},{19,... | collective-permute-start | bytes 1572872 | tf_op jit(solution)/shard_map/ppermute | solution.py:507
  50.4 7.8 %collective-permute-done.11.refs_1_ = bf16[512,512]{1,0:T(8,128)(2,1)S(1)} collective-permute-done((bf16[512,512]{1,0:T(8,128)(2,1)S(1)}, bf16[512,512]{1,0:T(8,128)(2,1)S(1)}, u32[]{:S(2)}, u32[]{:S(2)}) %collective-permute-start.11) | collective-permute-done | bytes 524320 | tf_op jit(solution)/shard_map/ppermute | solution.py:507
  58.2 3.6 %collective-permute-done.6.refs_3_.refs_2_.refs_13_ = bf16[512,512]{1,0:T(8,128)(2,1)S(1)} collective-permute-done((bf16[512,512]{1,0:T(8,128)(2,1)S(1)}, bf16[512,512]{1,0:T(8,128)(2,1)S(1)}, u32[]{:S(2)}, u32[]{:S(2)}) %collective-permute-start.6) | collective-permute-done | bytes 524320 | tf_op jit(solution)/shard_map/ppermute | solution.py:522
  64.1 8.0 %collective-permute-done.9.refs_4_.refs_15_ = bf16[512,512]{1,0:T(8,128)(2,1)S(1)} collective-permute-done((bf16[512,512]{1,0:T(8,128)(2,1)S(1)}, bf16[512,512]{1,0:T(8,128)(2,1)S(1)}, u32[]{:S(2)}, u32[]{:S(2)}) %collective-permute-start.9) | collective-permute-done | bytes 524320 | tf_op jit(solution)/shard_map/ppermute | solution.py:522
  72.1 2.0 %shard_map.168 = (bf16[4,128,1024]{2,1,0:T(8,128)(2,1)S(1)}, bf16[4,128,1024]{2,1,0:T(8,128)(2,1)S(1)}, f32[8,128]{1,0:T(8,128)S(1)}) custom-call(s32[5]{0:T(128)S(1)} %stack.23.refs_0_, bf16[512,512]{1,0:T(8,128)(2,1)S(1)} %get-tuple-element.98.refs_1_.refs_12_, bf16[512,512]{1,0:T(8,128)(2,1)S(1)} %collective-permute-done.6.refs_3_.refs_2_.refs_13_, ...), custom_call_target="tpu_custom_call" | custom-call | flops 1 | bytes 1 | tf_op jit(solution)/shard_map/pallas_call | solution.py:429
  75.8 7.3 %collective-permute-done.12.refs_1_.refs_2_.refs_17_ = bf16[512,512]{1,0:T(8,128)(2,1)S(1)} collective-permute-done((bf16[512,512]{1,0:T(8,128)(2,1)S(1)}, bf16[512,512]{1,0:T(8,128)(2,1)S(1)}, u32[]{:S(2)}, u32[]{:S(2)}) %collective-permute-start.12) | collective-permute-done | bytes 524320 | tf_op jit(solution)/shard_map/ppermute | solution.py:522
  88.0 4.4 %collective-permute-done.14.refs_4_.refs_19_ = bf16[512,512]{1,0:T(8,128)(2,1)S(1)} collective-permute-done((bf16[512,512]{1,0:T(8,128)(2,1)S(1)}, bf16[512,512]{1,0:T(8,128)(2,1)S(1)}, u32[]{:S(2)}, u32[]{:S(2)}) %collective-permute-start.14) | collective-permute-done | bytes 524320 | tf_op jit(solution)/shard_map/ppermute | solution.py:522
  92.5 2.0 %shard_map.172 = (bf16[4,128,1024]{2,1,0:T(8,128)(2,1)S(1)}, bf16[4,128,1024]{2,1,0:T(8,128)(2,1)S(1)}, f32[8,128]{1,0:T(8,128)S(1)}) custom-call(s32[5]{0:T(128)S(1)} %stack.23.refs_0_, bf16[512,512]{1,0:T(8,128)(2,1)S(1)} %get-tuple-element.108.refs_1_.refs_16_, bf16[512,512]{1,0:T(8,128)(2,1)S(1)} %collective-permute-done.12.refs_1_.refs_2_.refs_17_, ...), custom_call_target="tpu_custom_call" | custom-call | flops 1 | bytes 1 | tf_op jit(solution)/shard_map/pallas_call | solution.py:429
  103.8 3.4 %collective-permute-done.24.refs_3_ = bf16[1,128,1024]{2,1,0:T(8,128)(2,1)S(1)} collective-permute-done((bf16[1,128,1024]{2,1,0:T(8,128)(2,1)S(1)}, bf16[1,128,1024]{2,1,0:T(8,128)(2,1)S(1)}, u32[]{:S(2)}, u32[]{:S(2)}) %collective-permute-start.24) | collective-permute-done | bytes 262176 | tf_op jit(solution)/shard_map/ppermute | solution.py:464
  108.9 5.2 %shard_map.175 = (bf16[512,1024]{1,0:T(8,128)(2,1)}, f32[8,128]{1,0:T(8,128)S(1)}) custom-call(s32[5]{0:T(128)S(1)} %stack.23.refs_0_, f32[16,512]{1,0:T(8,128)} %bitcast.32, bf16[512,1024]{1,0:T(8,128)(2,1)} %refs_2_.5, bf16[512,256]{1,0:T(8,128)(2,1)} %refs_3_.5, bf16[512,256]{1,0:T(8,128)(2,1)} %refs_4_.5, f32[1,1024]{1,0:T(1,128)} %bitcast.35, ...), custom_call_target="tpu_custom_call" | custom-call | flops 1 | bytes 1 | tf_op jit(solution)/shard_map/pallas_call | solution.py:429
  114.1 5.2 %shard_map.176 = (bf16[512,1024]{1,0:T(8,128)(2,1)}, f32[8,128]{1,0:T(8,128)S(1)}) custom-call(s32[5]{0:T(128)S(1)} %stack.23.refs_0_, f32[16,512]{1,0:T(8,128)} %bitcast.33, bf16[512,1024]{1,0:T(8,128)(2,1)} %refs_2_.5, bf16[512,256]{1,0:T(8,128)(2,1)} %refs_3_.5, bf16[512,256]{1,0:T(8,128)(2,1)} %refs_4_.5, ...), custom_call_target="tpu_custom_call", output_to_operand_aliasing={{0}: (20, {})} | custom-call | flops 1 | bytes 1 | tf_op jit(solution)/shard_map/pallas_call | solution.py:429
  119.8 3.6 %collective-permute-done.27.refs_1_ = f32[8,128]{1,0:T(8,128)S(1)} collective-permute-done((f32[8,128]{1,0:T(8,128)S(1)}, f32[8,128]{1,0:T(8,128)S(1)}, u32[]{:S(2)}, u32[]{:S(2)}) %collective-permute-start.27) | collective-permute-done | bytes 4128 | tf_op jit(solution)/shard_map/ppermute | solution.py:616
  123.4 4.5 %collective-permute-done.28.refs_1_ = f32[8,128]{1,0:T(8,128)S(1)} collective-permute-done((f32[8,128]{1,0:T(8,128)S(1)}, f32[8,128]{1,0:T(8,128)S(1)}, u32[]{:S(2)}, u32[]{:S(2)}) %collective-permute-start.28) | collective-permute-done | bytes 4128 | tf_op jit(solution)/shard_map/ppermute | solution.py:616
  132.2 10.3 %collective-permute-done.33.refs_1_ = f32[8,128]{1,0:T(8,128)S(1)} collective-permute-done((f32[8,128]{1,0:T(8,128)S(1)}, f32[8,128]{1,0:T(8,128)S(1)}, u32[]{:S(2)}, u32[]{:S(2)}) %collective-permute-start.33) | collective-permute-done | bytes 4128 | tf_op jit(solution)/shard_map/ppermute | solution.py:616
  143.8 2.4 %collective-permute-done.34.refs_1_ = f32[8,128]{1,0:T(8,128)S(1)} collective-permute-done((f32[8,128]{1,0:T(8,128)S(1)}, f32[8,128]{1,0:T(8,128)S(1)}, u32[]{:S(2)}, u32[]{:S(2)}) %collective-permute-start.34) | collective-permute-done | bytes 4128 | tf_op jit(solution)/shard_map/ppermute | solution.py:616
  146.9 2.2 %collective-permute-done.36.refs_12_ = f32[8,128]{1,0:T(8,128)S(1)} collective-permute-done((f32[8,128]{1,0:T(8,128)S(1)}, f32[8,128]{1,0:T(8,128)S(1)}, u32[]{:S(2)}, u32[]{:S(2)}) %collective-permute-start.36) | collective-permute-done | bytes 4128 | tf_op jit(solution)/shard_map/ppermute | solution.py:464
  149.0 5.4 %shard_map.184 = (bf16[2048,1024]{1,0:T(8,128)(2,1)}, f32[256,1024]{1,0:T(8,128)}, f32[256,1024]{1,0:T(8,128)}, f32[8,128]{1,0:T(8,128)}) custom-call(s32[5]{0:T(128)S(1)} %stack.23.refs_0_, f32[256,1024]{1,0:T(8,128)S(1)} %get-tuple-element.87.refs_0_.refs_1_, f32[256,1024]{1,0:T(8,128)S(1)} %get-tuple-element.88.refs_1_.refs_2_, ...), custom_call_target="tpu_custom_call" | custom-call | flops 1 | bytes 1 | tf_op jit(solution)/shard_map/pallas_call | solution.py:429
  (81 shorter events, 40.2 us)
Async XLA Ops:
  8.4 17.2 %collective-permute-start = (bf16[512,512]{1,0:T(8,128)(2,1)S(1)}, bf16[512,512]{1,0:T(8,128)(2,1)S(1)}, u32[]{:S(2)}, u32[]{:S(2)}) collective-permute-start(bf16[512,512]{1,0:T(8,128)(2,1)S(1)} %get-tuple-element.86.refs_0_), channel_id=1, source_target_pairs={{0,1},{3,2},{4,5},{7,6},{8,9},{11,10},{12,13},{15,14},{16,17},{19,... | collective-permute-start | bytes 1572872 | tf_op jit(solution)/shard_map/ppermute | solution.py:507
  13.5 14.9 %collective-permute-start.3 = (bf16[1,256,1024]{2,1,0:T(8,128)(2,1)S(1)}, bf16[1,256,1024]{2,1,0:T(8,128)(2,1)S(1)}, u32[]{:S(2)}, u32[]{:S(2)}) collective-permute-start(bf16[1,256,1024]{2,1,0:T(8,128)(2,1)S(1)} %bitcast.18), channel_id=1, source_target_pairs={{0,8},{4,12},{8,0},{12,4},{16,24},{20,28},{24,16},{28,20},{1,9},{5... | collective-permute-start | bytes 1572872 | tf_op jit(solution)/shard_map/ppermute | solution.py:464
  15.0 24.3 %collective-permute-start.4 = (bf16[1,256,1024]{2,1,0:T(8,128)(2,1)S(1)}, bf16[1,256,1024]{2,1,0:T(8,128)(2,1)S(1)}, u32[]{:S(2)}, u32[]{:S(2)}) collective-permute-start(bf16[1,256,1024]{2,1,0:T(8,128)(2,1)S(1)} %bitcast.19), channel_id=1, source_target_pairs={{0,16},{4,20},{8,24},{12,28},{16,0},{20,4},{24,8},{28,12},{1,17},{... | collective-permute-start | bytes 1572872 | tf_op jit(solution)/shard_map/ppermute | solution.py:464
  16.6 22.8 %collective-permute-start.5 = (bf16[1,256,1024]{2,1,0:T(8,128)(2,1)S(1)}, bf16[1,256,1024]{2,1,0:T(8,128)(2,1)S(1)}, u32[]{:S(2)}, u32[]{:S(2)}) collective-permute-start(bf16[1,256,1024]{2,1,0:T(8,128)(2,1)S(1)} %bitcast.20), channel_id=1, source_target_pairs={{0,24},{4,28},{8,16},{12,20},{16,8},{20,12},{24,0},{28,4},{1,25},{... | collective-permute-start | bytes 1572872 | tf_op jit(solution)/shard_map/ppermute | solution.py:464
  19.5 20.0 %collective-permute-start.2 = (bf16[512,512]{1,0:T(8,128)(2,1)S(1)}, bf16[512,512]{1,0:T(8,128)(2,1)S(1)}, u32[]{:S(2)}, u32[]{:S(2)}) collective-permute-start(bf16[512,512]{1,0:T(8,128)(2,1)S(1)} %get-tuple-element.93.refs_0_), channel_id=1, source_target_pairs={{0,1},{3,2},{4,5},{7,6},{8,9},{11,10},{12,13},{15,14},{16,17},{19,... | collective-permute-start | bytes 1572872 | tf_op jit(solution)/shard_map/ppermute | solution.py:507
  25.7 19.2 %collective-permute-start.1 = (bf16[512,512]{1,0:T(8,128)(2,1)S(1)}, bf16[512,512]{1,0:T(8,128)(2,1)S(1)}, u32[]{:S(2)}, u32[]{:S(2)}) collective-permute-start(bf16[512,512]{1,0:T(8,128)(2,1)S(1)} %get-tuple-element.92.refs_0_), channel_id=1, source_target_pairs={{1,2},{2,1},{5,6},{6,5},{9,10},{10,9},{13,14},{14,13},{17,18},{18,... | collective-permute-start | bytes 1572872 | tf_op jit(solution)/shard_map/ppermute | solution.py:518
  28.4 19.7 %collective-permute-start.8 = (bf16[512,512]{1,0:T(8,128)(2,1)S(1)}, bf16[512,512]{1,0:T(8,128)(2,1)S(1)}, u32[]{:S(2)}, u32[]{:S(2)}) collective-permute-start(bf16[512,512]{1,0:T(8,128)(2,1)S(1)} %get-tuple-element.100.refs_0_), channel_id=1, source_target_pairs={{0,1},{3,2},{4,5},{7,6},{8,9},{11,10},{12,13},{15,14},{16,17},{19,... | collective-permute-start | bytes 1572872 | tf_op jit(solution)/shard_map/ppermute | solution.py:507
  40.4 17.8 %collective-permute-start.11 = (bf16[512,512]{1,0:T(8,128)(2,1)S(1)}, bf16[512,512]{1,0:T(8,128)(2,1)S(1)}, u32[]{:S(2)}, u32[]{:S(2)}) collective-permute-start(bf16[512,512]{1,0:T(8,128)(2,1)S(1)} %get-tuple-element.105.refs_0_), channel_id=1, source_target_pairs={{0,1},{3,2},{4,5},{7,6},{8,9},{11,10},{12,13},{15,14},{16,17},{19,... | collective-permute-start | bytes 1572872 | tf_op jit(solution)/shard_map/ppermute | solution.py:507
  45.0 16.8 %collective-permute-start.6 = (bf16[512,512]{1,0:T(8,128)(2,1)S(1)}, bf16[512,512]{1,0:T(8,128)(2,1)S(1)}, u32[]{:S(2)}, u32[]{:S(2)}) collective-permute-start(bf16[512,512]{1,0:T(8,128)(2,1)S(1)} %get-tuple-element.98.refs_1_.refs_12_), channel_id=1, source_target_pairs={{1,0},{2,3},{5,4},{6,7},{9,8},{10,11},{13,12},{14,15},{17,16},{18,... | collective-permute-start | bytes 1572872 | tf_op jit(solution)/shard_map/ppermute | solution.py:522
  48.2 14.5 %collective-permute-start.10 = (bf16[512,512]{1,0:T(8,128)(2,1)S(1)}, bf16[512,512]{1,0:T(8,128)(2,1)S(1)}, u32[]{:S(2)}, u32[]{:S(2)}) collective-permute-start(bf16[512,512]{1,0:T(8,128)(2,1)S(1)} %get-tuple-element.104.refs_0_), channel_id=1, source_target_pairs={{1,2},{2,1},{5,6},{6,5},{9,10},{10,9},{13,14},{14,13},{17,18},{18,... | collective-permute-start | bytes 1572872 | tf_op jit(solution)/shard_map/ppermute | solution.py:518
  49.1 23.1 %collective-permute-start.9 = (bf16[512,512]{1,0:T(8,128)(2,1)S(1)}, bf16[512,512]{1,0:T(8,128)(2,1)S(1)}, u32[]{:S(2)}, u32[]{:S(2)}) collective-permute-start(bf16[512,512]{1,0:T(8,128)(2,1)S(1)} %get-tuple-element.103.refs_3_.refs_14_), channel_id=1, source_target_pairs={{1,0},{2,3},{5,4},{6,7},{9,8},{10,11},{13,12},{14,15},{17,16},{18,... | collective-permute-start | bytes 1572872 | tf_op jit(solution)/shard_map/ppermute | solution.py:522
  61.9 12.3 %collective-permute-start.13 = (bf16[512,512]{1,0:T(8,128)(2,1)S(1)}, bf16[512,512]{1,0:T(8,128)(2,1)S(1)}, u32[]{:S(2)}, u32[]{:S(2)}) collective-permute-start(bf16[512,512]{1,0:T(8,128)(2,1)S(1)} %get-tuple-element.109.refs_0_), channel_id=1, source_target_pairs={{1,2},{2,1},{5,6},{6,5},{9,10},{10,9},{13,14},{14,13},{17,18},{18,... | collective-permute-start | bytes 1572872 | tf_op jit(solution)/shard_map/ppermute | solution.py:518
  62.6 29.9 %collective-permute-start.16 = (bf16[4,256,1024]{2,1,0:T(8,128)(2,1)S(1)}, bf16[4,256,1024]{2,1,0:T(8,128)(2,1)S(1)}, u32[]{:S(2)}, u32[]{:S(2)}) collective-permute-start(bf16[4,256,1024]{2,1,0:T(8,128)(2,1)S(1)} %get-tuple-element.118.refs_3_), channel_id=1, source_target_pairs={{0,4},{4,0},{8,12},{12,8},{16,20},{20,16},{24,28},{28,24},{1,5},{5... | collective-permute-start | bytes 6291464 | tf_op jit(solution)/shard_map/ppermute | solution.py:464
  62.8 20.3 %collective-permute-start.12 = (bf16[512,512]{1,0:T(8,128)(2,1)S(1)}, bf16[512,512]{1,0:T(8,128)(2,1)S(1)}, u32[]{:S(2)}, u32[]{:S(2)}) collective-permute-start(bf16[512,512]{1,0:T(8,128)(2,1)S(1)} %get-tuple-element.108.refs_1_.refs_16_), channel_id=1, source_target_pairs={{1,0},{2,3},{5,4},{6,7},{9,8},{10,11},{13,12},{14,15},{17,16},{18,... | collective-permute-start | bytes 1572872 | tf_op jit(solution)/shard_map/ppermute | solution.py:522
  74.4 18.1 %collective-permute-start.14 = (bf16[512,512]{1,0:T(8,128)(2,1)S(1)}, bf16[512,512]{1,0:T(8,128)(2,1)S(1)}, u32[]{:S(2)}, u32[]{:S(2)}) collective-permute-start(bf16[512,512]{1,0:T(8,128)(2,1)S(1)} %get-tuple-element.112.refs_3_.refs_18_), channel_id=1, source_target_pairs={{1,0},{2,3},{5,4},{6,7},{9,8},{10,11},{13,12},{14,15},{17,16},{18,... | collective-permute-start | bytes 1572872 | tf_op jit(solution)/shard_map/ppermute | solution.py:522
  99.5 19.9 %collective-permute-start.25 = (bf16[1,128,1024]{2,1,0:T(8,128)(2,1)S(1)}, bf16[1,128,1024]{2,1,0:T(8,128)(2,1)S(1)}, u32[]{:S(2)}, u32[]{:S(2)}) collective-permute-start(bf16[1,128,1024]{2,1,0:T(8,128)(2,1)S(1)} %get-tuple-element.135), channel_id=1, source_target_pairs={{0,16},{4,20},{8,24},{12,28},{16,0},{20,4},{24,8},{28,12},{1,17},{... | collective-permute-start | bytes 786440 | tf_op jit(solution)/shard_map/ppermute | solution.py:464
  100.3 19.1 %collective-permute-start.26 = (bf16[1,128,1024]{2,1,0:T(8,128)(2,1)S(1)}, bf16[1,128,1024]{2,1,0:T(8,128)(2,1)S(1)}, u32[]{:S(2)}, u32[]{:S(2)}) collective-permute-start(bf16[1,128,1024]{2,1,0:T(8,128)(2,1)S(1)} %get-tuple-element.136), channel_id=1, source_target_pairs={{0,24},{4,28},{8,16},{12,20},{16,8},{20,12},{24,0},{28,4},{1,25},{... | collective-permute-start | bytes 786440 | tf_op jit(solution)/shard_map/ppermute | solution.py:464
  101.6 26.4 %collective-permute-start.21 = (bf16[1,128,1024]{2,1,0:T(8,128)(2,1)S(1)}, bf16[1,128,1024]{2,1,0:T(8,128)(2,1)S(1)}, u32[]{:S(2)}, u32[]{:S(2)}) collective-permute-start(bf16[1,128,1024]{2,1,0:T(8,128)(2,1)S(1)} %bitcast.22), channel_id=1, source_target_pairs={{0,8},{4,12},{8,0},{12,4},{16,24},{20,28},{24,16},{28,20},{1,9},{5... | collective-permute-start | bytes 786440 | tf_op jit(solution)/shard_map/ppermute | solution.py:464
  103.0 24.9 %collective-permute-start.22 = (bf16[1,128,1024]{2,1,0:T(8,128)(2,1)S(1)}, bf16[1,128,1024]{2,1,0:T(8,128)(2,1)S(1)}, u32[]{:S(2)}, u32[]{:S(2)}) collective-permute-start(bf16[1,128,1024]{2,1,0:T(8,128)(2,1)S(1)} %bitcast.23), channel_id=1, source_target_pairs={{0,16},{4,20},{8,24},{12,28},{16,0},{20,4},{24,8},{28,12},{1,17},{... | collective-permute-start | bytes 786440 | tf_op jit(solution)/shard_map/ppermute | solution.py:464
  107.2 20.7 %collective-permute-start.23 = (bf16[1,128,1024]{2,1,0:T(8,128)(2,1)S(1)}, bf16[1,128,1024]{2,1,0:T(8,128)(2,1)S(1)}, u32[]{:S(2)}, u32[]{:S(2)}) collective-permute-start(bf16[1,128,1024]{2,1,0:T(8,128)(2,1)S(1)} %bitcast.24), channel_id=1, source_target_pairs={{0,24},{4,28},{8,16},{12,20},{16,8},{20,12},{24,0},{28,4},{1,25},{... | collective-permute-start | bytes 786440 | tf_op jit(solution)/shard_map/ppermute | solution.py:464
  128.0 18.1 %collective-permute-start.29 = (bf16[4,128,1024]{2,1,0:T(8,128)(2,1)S(1)}, bf16[4,128,1024]{2,1,0:T(8,128)(2,1)S(1)}, u32[]{:S(2)}, u32[]{:S(2)}) collective-permute-start(bf16[4,128,1024]{2,1,0:T(8,128)(2,1)S(1)} %get-tuple-element.143.refs_5_), channel_id=1, source_target_pairs={{0,4},{4,0},{8,12},{12,8},{16,20},{20,16},{24,28},{28,24},{1,5},{5... | collective-permute-start | bytes 3145736 | tf_op jit(solution)/shard_map/ppermute | solution.py:464
  128.1 18.0 %collective-permute-start.30 = (bf16[1,128,1024]{2,1,0:T(8,128)(2,1)S(1)}, bf16[1,128,1024]{2,1,0:T(8,128)(2,1)S(1)}, u32[]{:S(2)}, u32[]{:S(2)}) collective-permute-start(bf16[1,128,1024]{2,1,0:T(8,128)(2,1)S(1)} %bitcast.26), channel_id=1, source_target_pairs={{0,8},{4,12},{8,0},{12,4},{16,24},{20,28},{24,16},{28,20},{1,9},{5... | collective-permute-start | bytes 786440 | tf_op jit(solution)/shard_map/ppermute | solution.py:464
  128.7 17.5 %collective-permute-start.31 = (bf16[1,128,1024]{2,1,0:T(8,128)(2,1)S(1)}, bf16[1,128,1024]{2,1,0:T(8,128)(2,1)S(1)}, u32[]{:S(2)}, u32[]{:S(2)}) collective-permute-start(bf16[1,128,1024]{2,1,0:T(8,128)(2,1)S(1)} %bitcast.27), channel_id=1, source_target_pairs={{0,16},{4,20},{8,24},{12,28},{16,0},{20,4},{24,8},{28,12},{1,17},{... | collective-permute-start | bytes 786440 | tf_op jit(solution)/shard_map/ppermute | solution.py:464
  130.0 16.2 %collective-permute-start.32 = (bf16[1,128,1024]{2,1,0:T(8,128)(2,1)S(1)}, bf16[1,128,1024]{2,1,0:T(8,128)(2,1)S(1)}, u32[]{:S(2)}, u32[]{:S(2)}) collective-permute-start(bf16[1,128,1024]{2,1,0:T(8,128)(2,1)S(1)} %bitcast.28), channel_id=1, source_target_pairs={{0,24},{4,28},{8,16},{12,20},{16,8},{20,12},{24,0},{28,4},{1,25},{... | collective-permute-start | bytes 786440 | tf_op jit(solution)/shard_map/ppermute | solution.py:464
  (13 other events, 89.1 us)

commit v11 on v10

--- a/solution.py
+++ b/solution.py
@@ -189,8 +189,12 @@
     sum_ref[...] = (a_ref[...].astype(F32) + b_ref[...].astype(F32)).astype(BF16)
 
 
-def add_squares_kernel(a_ref, b_ref, sum_ref):
-    sum_ref[...] = a_ref[...] + b_ref[...]
+def add_squares_kernel(*refs):
+    *term_refs, sum_ref = refs
+    values = [ref[...] for ref in term_refs]
+    while len(values) > 1:
+        values = [a + b for a, b in zip(values[::2], values[1::2])]
+    sum_ref[...] = values[0]
 
 
 def gradient_kernel(batch, place_ref, *refs):
@@ -605,16 +609,16 @@
     half = groups // 2
     grad_input = backward(0, half, None) if half else None
     grad_input = backward(half, groups - half, grad_input)
-    own_rows(second, some_cost)
+    join(first)
+    own_rows(second, large_cost)
     total = squares[second]
-    hops = [("tensor", bit) for bit in range(heads_over.bit_length() - 1)]
-    hops += [("replica", bit) for bit in range(1, replicas.bit_length() - 1)]
-    for at, (axis, bit) in enumerate(hops):
-        if at == len(hops) // 2:
-            join(first)
-        pairs = [(r, r ^ (1 << bit)) for r in range(lax.axis_size(axis))]
-        (total,) = step(add_squares_kernel, [total, lax.ppermute(total, axis, pairs)], [tile])
-    join(second, gathered[first][1:])
+    for bit in range(heads_over.bit_length() - 1):
+        pairs = [(t, t ^ (1 << bit)) for t in range(heads_over)]
+        (total,) = step(add_squares_kernel, [total, lax.ppermute(total, "tensor", pairs)], [tile], waits=gathered[first][1:])
+    for bit, bits in stages(replicas):
+        landed = [exchange(total, mask << bit) for mask in range(1, 1 << bits)]
+        (total,) = step(add_squares_kernel, [total, *landed], [tile])
+    join(second)
     columns = [total, exchange(total, 1)]
 
     sizes = [len(batch) * piece for batch in batches]

time: 155 us -> 151 us (0.974)
  waiting for transfers between devices: 73.9 us -> 70.1 us
    ppermute x4 -> x2, waiting for transfers between devices: 20.8 us -> 8.1 us  [shards(): lax.ppermute(total, 'tensor', pairs)]
    ppermute x21 -> x24, waiting for transfers between devices: 15.4 us -> 24.3 us  [exchange(): lax.ppermute(value, 'replica', [(r, r ^ mask) for r in range(replicas)])]
    ppermute x4 -> x2, starting transfers between devices: 1.75 us -> 0.01 us  [shards(): lax.ppermute(total, 'tensor', pairs)]
    ppermute x21 -> x24, starting transfers between devices: 19 us -> 20.4 us  [exchange(): lax.ppermute(value, 'replica', [(r, r ^ mask) for r in range(replicas)])]
    pallas_call x29 -> x28, Pallas kernels: 34.4 us -> 34.4 us  [run(): pl.pallas_call(in_turn(kernel, len(inputs), len(waits), len(outs)), in_sp...]
  transfers between devices with their start and end apart: 37 -> 38, of which waited for: 17 -> 17; matrix products, arithmetic and copies ran while one was open for 0% -> 0% of each run, Pallas kernels for 13% -> 14%
where the time goes in v11:
time: 151 us; the launch traced here: 150 us
  waiting for transfers between devices  70.1 us (46%)
  starting transfers between devices  44.6 us (30%)
  Pallas kernels  34.4 us (23%)
    pallas_call x28, Pallas kernels, run(): pl.pallas_call(in_turn(kernel, len(inputs), len(waits), len(outs)), in_sp...  34.4 us
    ppermute x24, waiting for transfers between devices, exchange(): lax.ppermute(value, 'replica', [(r, r ^ mask) for r in range(replicas)])  24.3 us
    ppermute x4, waiting for transfers between devices, sum_all(): back = lax.ppermute(out, 'tensor', [(b, a) for a, b in pairs])  23.3 us
    ppermute x24, starting transfers between devices, exchange(): lax.ppermute(value, 'replica', [(r, r ^ mask) for r in range(replicas)])  20.4 us
    ppermute x4, starting transfers between devices, shards(): lax.ppermute(p, 'tensor', in_hops[0])  16.1 us
    ppermute x4, waiting for transfers between devices, shards(): lax.ppermute(p, 'tensor', in_hops[0])  14.3 us
    ppermute x2, waiting for transfers between devices, shards(): lax.ppermute(total, 'tensor', pairs)  8.1 us
    ppermute x4, starting transfers between devices, sum_all(): back = lax.ppermute(out, 'tensor', [(b, a) for a, b in pairs])  5.35 us
  transfers between devices with their start and end apart: 38, of which 17 were waited for; matrix products, arithmetic and copies ran while one was open for 0% of the time, Pallas kernels for 14%

profile of v11, /device:TPU:0, one launch (start us, length us, event | category | flops | bytes accessed | tf_op | source)
XLA Modules:
  0.0 150.2 jit_solution(17722155690885281392)
XLA Ops:
  0.7 6.2 %shard_map.156 = (bf16[8,256,1024]{2,1,0:T(8,128)(2,1)S(1)}, bf16[128,2048]{1,0:T(8,128)(2,1)S(1)}, f32[256,1024]{1,0:T(8,128)S(1)}, f32[256,1024]{1,0:T(8,128)S...) custom-call(f32[16,512]{1,0:T(8,128)} %bitcast.31, bf16[512,1024]{1,0:T(8,128)(2,1)} %refs_1_.1, ...), custom_call_target="tpu_custom_call" | custom-call | flops 1 | bytes 1 | tf_op jit(solution)/shard_map/pallas_call | solution.py:433
  8.4 5.0 %collective-permute-start = (bf16[512,512]{1,0:T(8,128)(2,1)S(1)}, bf16[512,512]{1,0:T(8,128)(2,1)S(1)}, u32[]{:S(2)}, u32[]{:S(2)}) collective-permute-start(bf16[512,512]{1,0:T(8,128)(2,1)S(1)} %get-tuple-element.84.refs_0_), channel_id=1, source_target_pairs={{0,1},{3,2},{4,5},{7,6},{8,9},{11,10},{12,13},{15,14},{16,17},{19,... | collective-permute-start | bytes 1572872 | tf_op jit(solution)/shard_map/ppermute | solution.py:511
  17.0 2.5 %shard_map.159 = (bf16[512,512]{1,0:T(8,128)(2,1)S(1)}, bf16[512,512]{1,0:T(8,128)(2,1)S(1)}, bf16[512,512]{1,0:T(8,128)(2,1)S(1)}, f32[8,128]{1,0:T(8,128)S(1)}) custom-call(s32[5]{0:T(128)S(1)} %stack.23.refs_0_, bf16[8,256,1024]{2,1,0:T(8,128)(2,1)S(1)} %get-tuple-element.81.refs_1_.refs_6_.refs_11_, ...), custom_call_target="tpu_custom_call" | custom-call | flops 1 | bytes 1 | tf_op jit(solution)/shard_map/pallas_call | solution.py:433
  20.9 4.8 %collective-permute-done.refs_1_ = bf16[512,512]{1,0:T(8,128)(2,1)S(1)} collective-permute-done((bf16[512,512]{1,0:T(8,128)(2,1)S(1)}, bf16[512,512]{1,0:T(8,128)(2,1)S(1)}, u32[]{:S(2)}, u32[]{:S(2)}) %collective-permute-start) | collective-permute-done | bytes 524320 | tf_op jit(solution)/shard_map/ppermute | solution.py:511
  28.4 5.3 %collective-permute-start.8 = (bf16[512,512]{1,0:T(8,128)(2,1)S(1)}, bf16[512,512]{1,0:T(8,128)(2,1)S(1)}, u32[]{:S(2)}, u32[]{:S(2)}) collective-permute-start(bf16[512,512]{1,0:T(8,128)(2,1)S(1)} %get-tuple-element.98.refs_0_), channel_id=1, source_target_pairs={{0,1},{3,2},{4,5},{7,6},{8,9},{11,10},{12,13},{15,14},{16,17},{19,... | collective-permute-start | bytes 1572872 | tf_op jit(solution)/shard_map/ppermute | solution.py:511
  33.7 5.7 %collective-permute-done.4.refs_2_ = bf16[1,256,1024]{2,1,0:T(8,128)(2,1)S(1)} collective-permute-done((bf16[1,256,1024]{2,1,0:T(8,128)(2,1)S(1)}, bf16[1,256,1024]{2,1,0:T(8,128)(2,1)S(1)}, u32[]{:S(2)}, u32[]{:S(2)}) %collective-permute-start.4) | collective-permute-done | bytes 524320 | tf_op jit(solution)/shard_map/ppermute | solution.py:468
  40.4 4.5 %collective-permute-start.11 = (bf16[512,512]{1,0:T(8,128)(2,1)S(1)}, bf16[512,512]{1,0:T(8,128)(2,1)S(1)}, u32[]{:S(2)}, u32[]{:S(2)}) collective-permute-start(bf16[512,512]{1,0:T(8,128)(2,1)S(1)} %get-tuple-element.103.refs_0_), channel_id=1, source_target_pairs={{0,1},{3,2},{4,5},{7,6},{8,9},{11,10},{12,13},{15,14},{16,17},{19,... | collective-permute-start | bytes 1572872 | tf_op jit(solution)/shard_map/ppermute | solution.py:511
  50.4 7.8 %collective-permute-done.11.refs_1_ = bf16[512,512]{1,0:T(8,128)(2,1)S(1)} collective-permute-done((bf16[512,512]{1,0:T(8,128)(2,1)S(1)}, bf16[512,512]{1,0:T(8,128)(2,1)S(1)}, u32[]{:S(2)}, u32[]{:S(2)}) %collective-permute-start.11) | collective-permute-done | bytes 524320 | tf_op jit(solution)/shard_map/ppermute | solution.py:511
  58.2 3.6 %collective-permute-done.6.refs_3_.refs_2_.refs_13_ = bf16[512,512]{1,0:T(8,128)(2,1)S(1)} collective-permute-done((bf16[512,512]{1,0:T(8,128)(2,1)S(1)}, bf16[512,512]{1,0:T(8,128)(2,1)S(1)}, u32[]{:S(2)}, u32[]{:S(2)}) %collective-permute-start.6) | collective-permute-done | bytes 524320 | tf_op jit(solution)/shard_map/ppermute | solution.py:526
  64.1 8.0 %collective-permute-done.9.refs_4_.refs_15_ = bf16[512,512]{1,0:T(8,128)(2,1)S(1)} collective-permute-done((bf16[512,512]{1,0:T(8,128)(2,1)S(1)}, bf16[512,512]{1,0:T(8,128)(2,1)S(1)}, u32[]{:S(2)}, u32[]{:S(2)}) %collective-permute-start.9) | collective-permute-done | bytes 524320 | tf_op jit(solution)/shard_map/ppermute | solution.py:526
  72.1 2.0 %shard_map.168 = (bf16[4,128,1024]{2,1,0:T(8,128)(2,1)S(1)}, bf16[4,128,1024]{2,1,0:T(8,128)(2,1)S(1)}, f32[8,128]{1,0:T(8,128)S(1)}) custom-call(s32[5]{0:T(128)S(1)} %stack.23.refs_0_, bf16[512,512]{1,0:T(8,128)(2,1)S(1)} %get-tuple-element.96.refs_1_.refs_12_, bf16[512,512]{1,0:T(8,128)(2,1)S(1)} %collective-permute-done.6.refs_3_.refs_2_.refs_13_, ...), custom_call_target="tpu_custom_call" | custom-call | flops 1 | bytes 1 | tf_op jit(solution)/shard_map/pallas_call | solution.py:433
  75.8 7.3 %collective-permute-done.12.refs_1_.refs_2_.refs_17_ = bf16[512,512]{1,0:T(8,128)(2,1)S(1)} collective-permute-done((bf16[512,512]{1,0:T(8,128)(2,1)S(1)}, bf16[512,512]{1,0:T(8,128)(2,1)S(1)}, u32[]{:S(2)}, u32[]{:S(2)}) %collective-permute-start.12) | collective-permute-done | bytes 524320 | tf_op jit(solution)/shard_map/ppermute | solution.py:526
  88.0 4.4 %collective-permute-done.14.refs_4_.refs_19_ = bf16[512,512]{1,0:T(8,128)(2,1)S(1)} collective-permute-done((bf16[512,512]{1,0:T(8,128)(2,1)S(1)}, bf16[512,512]{1,0:T(8,128)(2,1)S(1)}, u32[]{:S(2)}, u32[]{:S(2)}) %collective-permute-start.14) | collective-permute-done | bytes 524320 | tf_op jit(solution)/shard_map/ppermute | solution.py:526
  92.5 2.0 %shard_map.172 = (bf16[4,128,1024]{2,1,0:T(8,128)(2,1)S(1)}, bf16[4,128,1024]{2,1,0:T(8,128)(2,1)S(1)}, f32[8,128]{1,0:T(8,128)S(1)}) custom-call(s32[5]{0:T(128)S(1)} %stack.23.refs_0_, bf16[512,512]{1,0:T(8,128)(2,1)S(1)} %get-tuple-element.106.refs_1_.refs_16_, bf16[512,512]{1,0:T(8,128)(2,1)S(1)} %collective-permute-done.12.refs_1_.refs_2_.refs_17_, ...), custom_call_target="tpu_custom_call" | custom-call | flops 1 | bytes 1 | tf_op jit(solution)/shard_map/pallas_call | solution.py:433
  98.2 2.0 %collective-permute-start.23 = (bf16[1,128,1024]{2,1,0:T(8,128)(2,1)S(1)}, bf16[1,128,1024]{2,1,0:T(8,128)(2,1)S(1)}, u32[]{:S(2)}, u32[]{:S(2)}) collective-permute-start(bf16[1,128,1024]{2,1,0:T(8,128)(2,1)S(1)} %bitcast.28), channel_id=1, source_target_pairs={{0,24},{4,28},{8,16},{12,20},{16,8},{20,12},{24,0},{28,4},{1,25},{... | collective-permute-start | bytes 786440 | tf_op jit(solution)/shard_map/ppermute | solution.py:468
  102.6 3.4 %collective-permute-done.21.refs_1_ = bf16[1,128,1024]{2,1,0:T(8,128)(2,1)S(1)} collective-permute-done((bf16[1,128,1024]{2,1,0:T(8,128)(2,1)S(1)}, bf16[1,128,1024]{2,1,0:T(8,128)(2,1)S(1)}, u32[]{:S(2)}, u32[]{:S(2)}) %collective-permute-start.21) | collective-permute-done | bytes 262176 | tf_op jit(solution)/shard_map/ppermute | solution.py:468
  106.9 5.2 %shard_map.175 = (bf16[512,1024]{1,0:T(8,128)(2,1)}, f32[8,128]{1,0:T(8,128)S(1)}) custom-call(s32[5]{0:T(128)S(1)} %stack.23.refs_0_, f32[16,512]{1,0:T(8,128)} %bitcast.32, bf16[512,1024]{1,0:T(8,128)(2,1)} %refs_2_.5, bf16[512,256]{1,0:T(8,128)(2,1)} %refs_3_.5, bf16[512,256]{1,0:T(8,128)(2,1)} %refs_4_.5, f32[1,1024]{1,0:T(1,128)} %bitcast.35, ...), custom_call_target="tpu_custom_call" | custom-call | flops 1 | bytes 1 | tf_op jit(solution)/shard_map/pallas_call | solution.py:433
  112.1 5.2 %shard_map.176 = (bf16[512,1024]{1,0:T(8,128)(2,1)}, f32[8,128]{1,0:T(8,128)S(1)}) custom-call(s32[5]{0:T(128)S(1)} %stack.23.refs_0_, f32[16,512]{1,0:T(8,128)} %bitcast.33, bf16[512,1024]{1,0:T(8,128)(2,1)} %refs_2_.5, bf16[512,256]{1,0:T(8,128)(2,1)} %refs_3_.5, bf16[512,256]{1,0:T(8,128)(2,1)} %refs_4_.5, ...), custom_call_target="tpu_custom_call", output_to_operand_aliasing={{0}: (20, {})} | custom-call | flops 1 | bytes 1 | tf_op jit(solution)/shard_map/pallas_call | solution.py:433
  117.5 4.2 %collective-permute-done.26.refs_4_ = bf16[1,128,1024]{2,1,0:T(8,128)(2,1)S(1)} collective-permute-done((bf16[1,128,1024]{2,1,0:T(8,128)(2,1)S(1)}, bf16[1,128,1024]{2,1,0:T(8,128)(2,1)S(1)}, u32[]{:S(2)}, u32[]{:S(2)}) %collective-permute-start.26) | collective-permute-done | bytes 262176 | tf_op jit(solution)/shard_map/ppermute | solution.py:468
  125.7 3.6 %collective-permute-done.31.refs_1_ = f32[8,128]{1,0:T(8,128)S(1)} collective-permute-done((f32[8,128]{1,0:T(8,128)S(1)}, f32[8,128]{1,0:T(8,128)S(1)}, u32[]{:S(2)}, u32[]{:S(2)}) %collective-permute-start.31) | collective-permute-done | bytes 4128 | tf_op jit(solution)/shard_map/ppermute | solution.py:617
  129.3 4.5 %collective-permute-done.32.refs_1_ = f32[8,128]{1,0:T(8,128)S(1)} collective-permute-done((f32[8,128]{1,0:T(8,128)S(1)}, f32[8,128]{1,0:T(8,128)S(1)}, u32[]{:S(2)}, u32[]{:S(2)}) %collective-permute-start.32) | collective-permute-done | bytes 4128 | tf_op jit(solution)/shard_map/ppermute | solution.py:617
  138.6 3.3 %collective-permute-done.35.refs_3_ = f32[8,128]{1,0:T(8,128)S(1)} collective-permute-done((f32[8,128]{1,0:T(8,128)S(1)}, f32[8,128]{1,0:T(8,128)S(1)}, u32[]{:S(2)}, u32[]{:S(2)}) %collective-permute-start.35) | collective-permute-done | bytes 4128 | tf_op jit(solution)/shard_map/ppermute | solution.py:468
  142.6 2.2 %collective-permute-done.37.refs_12_ = f32[8,128]{1,0:T(8,128)S(1)} collective-permute-done((f32[8,128]{1,0:T(8,128)S(1)}, f32[8,128]{1,0:T(8,128)S(1)}, u32[]{:S(2)}, u32[]{:S(2)}) %collective-permute-start.37) | collective-permute-done | bytes 4128 | tf_op jit(solution)/shard_map/ppermute | solution.py:468
  144.8 5.4 %shard_map.183 = (bf16[2048,1024]{1,0:T(8,128)(2,1)}, f32[256,1024]{1,0:T(8,128)}, f32[256,1024]{1,0:T(8,128)}, f32[8,128]{1,0:T(8,128)}) custom-call(s32[5]{0:T(128)S(1)} %stack.23.refs_0_, f32[256,1024]{1,0:T(8,128)S(1)} %get-tuple-element.85.refs_0_.refs_1_, f32[256,1024]{1,0:T(8,128)S(1)} %get-tuple-element.86.refs_1_.refs_2_, ...), custom_call_target="tpu_custom_call" | custom-call | flops 1 | bytes 1 | tf_op jit(solution)/shard_map/pallas_call | solution.py:433
  (82 shorter events, 41.0 us)
Async XLA Ops:
  8.4 17.2 %collective-permute-start = (bf16[512,512]{1,0:T(8,128)(2,1)S(1)}, bf16[512,512]{1,0:T(8,128)(2,1)S(1)}, u32[]{:S(2)}, u32[]{:S(2)}) collective-permute-start(bf16[512,512]{1,0:T(8,128)(2,1)S(1)} %get-tuple-element.84.refs_0_), channel_id=1, source_target_pairs={{0,1},{3,2},{4,5},{7,6},{8,9},{11,10},{12,13},{15,14},{16,17},{19,... | collective-permute-start | bytes 1572872 | tf_op jit(solution)/shard_map/ppermute | solution.py:511
  13.5 14.9 %collective-permute-start.3 = (bf16[1,256,1024]{2,1,0:T(8,128)(2,1)S(1)}, bf16[1,256,1024]{2,1,0:T(8,128)(2,1)S(1)}, u32[]{:S(2)}, u32[]{:S(2)}) collective-permute-start(bf16[1,256,1024]{2,1,0:T(8,128)(2,1)S(1)} %bitcast.18), channel_id=1, source_target_pairs={{0,8},{4,12},{8,0},{12,4},{16,24},{20,28},{24,16},{28,20},{1,9},{5... | collective-permute-start | bytes 1572872 | tf_op jit(solution)/shard_map/ppermute | solution.py:468
  15.0 24.3 %collective-permute-start.4 = (bf16[1,256,1024]{2,1,0:T(8,128)(2,1)S(1)}, bf16[1,256,1024]{2,1,0:T(8,128)(2,1)S(1)}, u32[]{:S(2)}, u32[]{:S(2)}) collective-permute-start(bf16[1,256,1024]{2,1,0:T(8,128)(2,1)S(1)} %bitcast.19), channel_id=1, source_target_pairs={{0,16},{4,20},{8,24},{12,28},{16,0},{20,4},{24,8},{28,12},{1,17},{... | collective-permute-start | bytes 1572872 | tf_op jit(solution)/shard_map/ppermute | solution.py:468
  16.6 22.8 %collective-permute-start.5 = (bf16[1,256,1024]{2,1,0:T(8,128)(2,1)S(1)}, bf16[1,256,1024]{2,1,0:T(8,128)(2,1)S(1)}, u32[]{:S(2)}, u32[]{:S(2)}) collective-permute-start(bf16[1,256,1024]{2,1,0:T(8,128)(2,1)S(1)} %bitcast.20), channel_id=1, source_target_pairs={{0,24},{4,28},{8,16},{12,20},{16,8},{20,12},{24,0},{28,4},{1,25},{... | collective-permute-start | bytes 1572872 | tf_op jit(solution)/shard_map/ppermute | solution.py:468
  19.5 20.0 %collective-permute-start.2 = (bf16[512,512]{1,0:T(8,128)(2,1)S(1)}, bf16[512,512]{1,0:T(8,128)(2,1)S(1)}, u32[]{:S(2)}, u32[]{:S(2)}) collective-permute-start(bf16[512,512]{1,0:T(8,128)(2,1)S(1)} %get-tuple-element.91.refs_0_), channel_id=1, source_target_pairs={{0,1},{3,2},{4,5},{7,6},{8,9},{11,10},{12,13},{15,14},{16,17},{19,... | collective-permute-start | bytes 1572872 | tf_op jit(solution)/shard_map/ppermute | solution.py:511
  25.7 19.2 %collective-permute-start.1 = (bf16[512,512]{1,0:T(8,128)(2,1)S(1)}, bf16[512,512]{1,0:T(8,128)(2,1)S(1)}, u32[]{:S(2)}, u32[]{:S(2)}) collective-permute-start(bf16[512,512]{1,0:T(8,128)(2,1)S(1)} %get-tuple-element.90.refs_0_), channel_id=1, source_target_pairs={{1,2},{2,1},{5,6},{6,5},{9,10},{10,9},{13,14},{14,13},{17,18},{18,... | collective-permute-start | bytes 1572872 | tf_op jit(solution)/shard_map/ppermute | solution.py:522
  28.4 19.7 %collective-permute-start.8 = (bf16[512,512]{1,0:T(8,128)(2,1)S(1)}, bf16[512,512]{1,0:T(8,128)(2,1)S(1)}, u32[]{:S(2)}, u32[]{:S(2)}) collective-permute-start(bf16[512,512]{1,0:T(8,128)(2,1)S(1)} %get-tuple-element.98.refs_0_), channel_id=1, source_target_pairs={{0,1},{3,2},{4,5},{7,6},{8,9},{11,10},{12,13},{15,14},{16,17},{19,... | collective-permute-start | bytes 1572872 | tf_op jit(solution)/shard_map/ppermute | solution.py:511
  40.4 17.8 %collective-permute-start.11 = (bf16[512,512]{1,0:T(8,128)(2,1)S(1)}, bf16[512,512]{1,0:T(8,128)(2,1)S(1)}, u32[]{:S(2)}, u32[]{:S(2)}) collective-permute-start(bf16[512,512]{1,0:T(8,128)(2,1)S(1)} %get-tuple-element.103.refs_0_), channel_id=1, source_target_pairs={{0,1},{3,2},{4,5},{7,6},{8,9},{11,10},{12,13},{15,14},{16,17},{19,... | collective-permute-start | bytes 1572872 | tf_op jit(solution)/shard_map/ppermute | solution.py:511
  45.0 16.8 %collective-permute-start.6 = (bf16[512,512]{1,0:T(8,128)(2,1)S(1)}, bf16[512,512]{1,0:T(8,128)(2,1)S(1)}, u32[]{:S(2)}, u32[]{:S(2)}) collective-permute-start(bf16[512,512]{1,0:T(8,128)(2,1)S(1)} %get-tuple-element.96.refs_1_.refs_12_), channel_id=1, source_target_pairs={{1,0},{2,3},{5,4},{6,7},{9,8},{10,11},{13,12},{14,15},{17,16},{18,... | collective-permute-start | bytes 1572872 | tf_op jit(solution)/shard_map/ppermute | solution.py:526
  48.2 14.5 %collective-permute-start.10 = (bf16[512,512]{1,0:T(8,128)(2,1)S(1)}, bf16[512,512]{1,0:T(8,128)(2,1)S(1)}, u32[]{:S(2)}, u32[]{:S(2)}) collective-permute-start(bf16[512,512]{1,0:T(8,128)(2,1)S(1)} %get-tuple-element.102.refs_0_), channel_id=1, source_target_pairs={{1,2},{2,1},{5,6},{6,5},{9,10},{10,9},{13,14},{14,13},{17,18},{18,... | collective-permute-start | bytes 1572872 | tf_op jit(solution)/shard_map/ppermute | solution.py:522
  49.1 23.1 %collective-permute-start.9 = (bf16[512,512]{1,0:T(8,128)(2,1)S(1)}, bf16[512,512]{1,0:T(8,128)(2,1)S(1)}, u32[]{:S(2)}, u32[]{:S(2)}) collective-permute-start(bf16[512,512]{1,0:T(8,128)(2,1)S(1)} %get-tuple-element.101.refs_3_.refs_14_), channel_id=1, source_target_pairs={{1,0},{2,3},{5,4},{6,7},{9,8},{10,11},{13,12},{14,15},{17,16},{18,... | collective-permute-start | bytes 1572872 | tf_op jit(solution)/shard_map/ppermute | solution.py:526
  61.9 12.3 %collective-permute-start.13 = (bf16[512,512]{1,0:T(8,128)(2,1)S(1)}, bf16[512,512]{1,0:T(8,128)(2,1)S(1)}, u32[]{:S(2)}, u32[]{:S(2)}) collective-permute-start(bf16[512,512]{1,0:T(8,128)(2,1)S(1)} %get-tuple-element.107.refs_0_), channel_id=1, source_target_pairs={{1,2},{2,1},{5,6},{6,5},{9,10},{10,9},{13,14},{14,13},{17,18},{18,... | collective-permute-start | bytes 1572872 | tf_op jit(solution)/shard_map/ppermute | solution.py:522
  62.6 29.9 %collective-permute-start.16 = (bf16[4,256,1024]{2,1,0:T(8,128)(2,1)S(1)}, bf16[4,256,1024]{2,1,0:T(8,128)(2,1)S(1)}, u32[]{:S(2)}, u32[]{:S(2)}) collective-permute-start(bf16[4,256,1024]{2,1,0:T(8,128)(2,1)S(1)} %get-tuple-element.116.refs_3_), channel_id=1, source_target_pairs={{0,4},{4,0},{8,12},{12,8},{16,20},{20,16},{24,28},{28,24},{1,5},{5... | collective-permute-start | bytes 6291464 | tf_op jit(solution)/shard_map/ppermute | solution.py:468
  62.8 20.3 %collective-permute-start.12 = (bf16[512,512]{1,0:T(8,128)(2,1)S(1)}, bf16[512,512]{1,0:T(8,128)(2,1)S(1)}, u32[]{:S(2)}, u32[]{:S(2)}) collective-permute-start(bf16[512,512]{1,0:T(8,128)(2,1)S(1)} %get-tuple-element.106.refs_1_.refs_16_), channel_id=1, source_target_pairs={{1,0},{2,3},{5,4},{6,7},{9,8},{10,11},{13,12},{14,15},{17,16},{18,... | collective-permute-start | bytes 1572872 | tf_op jit(solution)/shard_map/ppermute | solution.py:526
  74.4 18.1 %collective-permute-start.14 = (bf16[512,512]{1,0:T(8,128)(2,1)S(1)}, bf16[512,512]{1,0:T(8,128)(2,1)S(1)}, u32[]{:S(2)}, u32[]{:S(2)}) collective-permute-start(bf16[512,512]{1,0:T(8,128)(2,1)S(1)} %get-tuple-element.110.refs_3_.refs_18_), channel_id=1, source_target_pairs={{1,0},{2,3},{5,4},{6,7},{9,8},{10,11},{13,12},{14,15},{17,16},{18,... | collective-permute-start | bytes 1572872 | tf_op jit(solution)/shard_map/ppermute | solution.py:526
  97.8 19.6 %collective-permute-start.22 = (bf16[1,128,1024]{2,1,0:T(8,128)(2,1)S(1)}, bf16[1,128,1024]{2,1,0:T(8,128)(2,1)S(1)}, u32[]{:S(2)}, u32[]{:S(2)}) collective-permute-start(bf16[1,128,1024]{2,1,0:T(8,128)(2,1)S(1)} %bitcast.27), channel_id=1, source_target_pairs={{0,16},{4,20},{8,24},{12,28},{16,0},{20,4},{24,8},{28,12},{1,17},{... | collective-permute-start | bytes 786440 | tf_op jit(solution)/shard_map/ppermute | solution.py:468
  98.2 19.1 %collective-permute-start.23 = (bf16[1,128,1024]{2,1,0:T(8,128)(2,1)S(1)}, bf16[1,128,1024]{2,1,0:T(8,128)(2,1)S(1)}, u32[]{:S(2)}, u32[]{:S(2)}) collective-permute-start(bf16[1,128,1024]{2,1,0:T(8,128)(2,1)S(1)} %bitcast.28), channel_id=1, source_target_pairs={{0,24},{4,28},{8,16},{12,20},{16,8},{20,12},{24,0},{28,4},{1,25},{... | collective-permute-start | bytes 786440 | tf_op jit(solution)/shard_map/ppermute | solution.py:468
  101.1 16.5 %collective-permute-start.25 = (bf16[1,128,1024]{2,1,0:T(8,128)(2,1)S(1)}, bf16[1,128,1024]{2,1,0:T(8,128)(2,1)S(1)}, u32[]{:S(2)}, u32[]{:S(2)}) collective-permute-start(bf16[1,128,1024]{2,1,0:T(8,128)(2,1)S(1)} %get-tuple-element.134), channel_id=1, source_target_pairs={{0,8},{4,12},{8,0},{12,4},{16,24},{20,28},{24,16},{28,20},{1,9},{5... | collective-permute-start | bytes 786440 | tf_op jit(solution)/shard_map/ppermute | solution.py:468
  102.1 19.6 %collective-permute-start.26 = (bf16[1,128,1024]{2,1,0:T(8,128)(2,1)S(1)}, bf16[1,128,1024]{2,1,0:T(8,128)(2,1)S(1)}, u32[]{:S(2)}, u32[]{:S(2)}) collective-permute-start(bf16[1,128,1024]{2,1,0:T(8,128)(2,1)S(1)} %get-tuple-element.135), channel_id=1, source_target_pairs={{0,16},{4,20},{8,24},{12,28},{16,0},{20,4},{24,8},{28,12},{1,17},{... | collective-permute-start | bytes 786440 | tf_op jit(solution)/shard_map/ppermute | solution.py:468
  106.0 15.7 %collective-permute-start.27 = (bf16[1,128,1024]{2,1,0:T(8,128)(2,1)S(1)}, bf16[1,128,1024]{2,1,0:T(8,128)(2,1)S(1)}, u32[]{:S(2)}, u32[]{:S(2)}) collective-permute-start(bf16[1,128,1024]{2,1,0:T(8,128)(2,1)S(1)} %get-tuple-element.136), channel_id=1, source_target_pairs={{0,24},{4,28},{8,16},{12,20},{16,8},{20,12},{24,0},{28,4},{1,25},{... | collective-permute-start | bytes 786440 | tf_op jit(solution)/shard_map/ppermute | solution.py:468
  117.5 11.8 %collective-permute-start.24 = (bf16[4,128,1024]{2,1,0:T(8,128)(2,1)S(1)}, bf16[4,128,1024]{2,1,0:T(8,128)(2,1)S(1)}, u32[]{:S(2)}, u32[]{:S(2)}) collective-permute-start(bf16[4,128,1024]{2,1,0:T(8,128)(2,1)S(1)} %get-tuple-element.131.refs_5_), channel_id=1, source_target_pairs={{0,4},{4,0},{8,12},{12,8},{16,20},{20,16},{24,28},{28,24},{1,5},{5... | collective-permute-start | bytes 3145736 | tf_op jit(solution)/shard_map/ppermute | solution.py:468
  122.2 19.7 %collective-permute-start.28 = (bf16[1,128,1024]{2,1,0:T(8,128)(2,1)S(1)}, bf16[1,128,1024]{2,1,0:T(8,128)(2,1)S(1)}, u32[]{:S(2)}, u32[]{:S(2)}) collective-permute-start(bf16[1,128,1024]{2,1,0:T(8,128)(2,1)S(1)} %bitcast.22), channel_id=1, source_target_pairs={{0,8},{4,12},{8,0},{12,4},{16,24},{20,28},{24,16},{28,20},{1,9},{5... | collective-permute-start | bytes 786440 | tf_op jit(solution)/shard_map/ppermute | solution.py:468
  122.8 19.2 %collective-permute-start.29 = (bf16[1,128,1024]{2,1,0:T(8,128)(2,1)S(1)}, bf16[1,128,1024]{2,1,0:T(8,128)(2,1)S(1)}, u32[]{:S(2)}, u32[]{:S(2)}) collective-permute-start(bf16[1,128,1024]{2,1,0:T(8,128)(2,1)S(1)} %bitcast.23), channel_id=1, source_target_pairs={{0,16},{4,20},{8,24},{12,28},{16,0},{20,4},{24,8},{28,12},{1,17},{... | collective-permute-start | bytes 786440 | tf_op jit(solution)/shard_map/ppermute | solution.py:468
  124.0 18.0 %collective-permute-start.30 = (bf16[1,128,1024]{2,1,0:T(8,128)(2,1)S(1)}, bf16[1,128,1024]{2,1,0:T(8,128)(2,1)S(1)}, u32[]{:S(2)}, u32[]{:S(2)}) collective-permute-start(bf16[1,128,1024]{2,1,0:T(8,128)(2,1)S(1)} %bitcast.24), channel_id=1, source_target_pairs={{0,24},{4,28},{8,16},{12,20},{16,8},{20,12},{24,0},{28,4},{1,25},{... | collective-permute-start | bytes 786440 | tf_op jit(solution)/shard_map/ppermute | solution.py:468
  (14 other events, 90.1 us)

commit v12 on v11

--- a/solution.py
+++ b/solution.py
@@ -31,7 +31,7 @@
 
 
 def silu(z):
-    return z * (1.0 / (1.0 + jnp.exp(-z)))
+    return 0.5 * z * (1.0 + jnp.tanh(0.5 * z))
 
 
 def softplus(v):
@@ -285,9 +285,9 @@
             d_state = own if d_state is None else own + d_state * fade_x[SPAN - 1 :, :]
 
 
-def pick_kernel(count, place_ref, *refs):
+def pick_kernel(count, unit, place_ref, *refs):
     terms, outs = refs[:count], refs[count:]
-    my = lax.rem(lax.div(place_ref[3], place_ref[4]), len(outs))
+    my = lax.rem(lax.div(place_ref[3], unit), len(outs))
     for mask, out_ref in enumerate(outs):
         at = lax.bitwise_xor(my, jnp.int32(mask))
         total = terms[0][:, at].astype(F32)
@@ -343,16 +343,22 @@
             one_core(own_core, 0)
             one_core(1 - own_core, 1)
 
-    @pl.when(pl.program_id(0) == 0)
-    def _():
-        lo = 0
-        for n, size in enumerate(sizes):
-            rows = slice(lo, lo + size)
-            lo += size
-            clipped = factor * deltas[n][...]
-            new_momentum = outer_beta * momentum_ref[rows, :] + clipped
-            new_momentum_ref[rows, :] = new_momentum
-            new_global_ref[rows, :] = global_ref[rows, :] - outer_rate * (clipped + outer_beta * new_momentum)
+    part = new_global_ref.shape[0]
+    lo = 0
+    for n, size in enumerate(sizes):
+        for row in range(0, size, min(size, part)):
+            rows = min(size, part)
+            at, here = slice(lo + row, lo + row + rows), (lo + row) % part
+
+            @pl.when(pl.program_id(0) == (lo + row) // part)
+            def _():
+                clipped = factor * deltas[n][row : row + rows, :]
+                new_momentum = outer_beta * momentum_ref[at, :] + clipped
+                new_momentum_ref[here : here + rows, :] = new_momentum
+                new_global = global_ref[at, :] - outer_rate * (clipped + outer_beta * new_momentum)
+                new_global_ref[here : here + rows, :] = new_global
+
+        lo += size
 
 
 def inward(axis_size):
@@ -370,10 +376,10 @@
     return body
 
 
-def stages(replicas):
+def stages(replicas, most=2):
     bit, left, found = 1, replicas // 2, []
     while left > 1:
-        bits = 2 if left >= 4 else 1
+        bits = most if left >= 1 << most else 1
         found.append((bit, bits))
         bit, left = bit + bits, left >> bits
     return found
@@ -403,14 +409,13 @@
     width = inner // groups
     owned = features // replicas
     chunks = max(2, min(4, owned // 16))
-    batches = [list(range(chunks // 2)), list(range(chunks // 2, chunks))]
+    batches = [[n] for n in range(chunks // 2)] + [list(range(chunks // 2, chunks))]
     piece = owned // chunks
     span_rows = replicas * piece
     place = lax.axis_index("tensor")
     me = lax.axis_index("replica")
     in_middle = (place == heads_over // 2 - 1) | (place == heads_over // 2)
-    one = jnp.int32(1)
-    places = jnp.stack([place, in_middle.astype(jnp.int32), lax.rem(me, 2), lax.div(me, 2), one]).astype(jnp.int32)
+    places = jnp.stack([place, in_middle.astype(jnp.int32), lax.rem(me, 2), lax.div(me, 2)]).astype(jnp.int32)
     stored = out_weight[0].reshape(replicas, owned, inner)
     gain = norm_gain.reshape(1, inner)
     dt_rows = dt_raw.T
@@ -469,19 +474,20 @@
 
     gathered = {}
 
-    def spread_rows(b, sent):
-        (bit, bits), *_ = stages(replicas)
-        gathered[b] = [sent[None]] + [exchange(sent[None], mask << bit) for mask in range(1, 1 << bits)]
-
-    def join(b, waits=()):
-        for at, (bit, bits) in enumerate(stages(replicas)):
-            if at > 0:
-                gathered[b] = [held] + [exchange(held, mask << bit) for mask in range(1, 1 << bits)]
-            one = gathered[b][0]
-            out = shape(len(gathered[b]) * one.shape[0], *one.shape[1:])
-            (held,) = step(join_kernel, gathered[b], [out], waits=waits if at == 0 else ())
-        gathered[b] = [held, exchange(held, 1)]
-
+    def landing(b, some):
+        (bit, bits), *_ = some
+        return [exchange(gathered[b], mask << bit) for mask in range(1, 1 << bits)]
+
+    def widen(b, some, landed=None):
+        for at, (bit, bits) in enumerate(some):
+            parts = [gathered[b]] + (landed if at == 0 and landed else landing(b, some[at:]))
+            out = shape(len(parts) * parts[0].shape[0], *parts[0].shape[1:])
+            (gathered[b],) = step(join_kernel, parts, [out])
+
+    def finish(b):
+        gathered[b] = [gathered[b], exchange(gathered[b], 1)]
+
+    by_two, by_one = stages(replicas), stages(replicas, 1)
     by_group, by_state, dt_spec, gain_spec = group_specs(0)
     shared = in_hbm(dt_rows, gate_z, b_proj, c_proj, gain, a_log, dt_bias, skip_d)
     later = [stored, target, global_weight, momentum]
@@ -506,7 +512,8 @@
     in_hops, across = inward(heads_over)
     parts = project([0])
     (kept,) = step(kept_kernel, [own_global, own_momentum], [shape(owned, inner)])
-    spread_rows("kept", kept)
+    gathered["kept"] = kept[None]
+    kept_landed = landing("kept", by_two)
     parts += project(list(range(1, chunks)))
     first_landed = [lax.ppermute(p, "tensor", in_hops[0]) if in_hops else None for p in parts]
     sums, cots = {}, {}
@@ -527,7 +534,7 @@
             out = back if pairs is in_hops[0] else jnp.where(in_middle, mid, back)
         cots[n] = (mid, out)
 
-    terms, deltas = {}, {}
+    held, deltas = {}, {}
     tile = shape(8, LANES, dtype=F32)
     squares = {-1: jnp.zeros((8, LANES), F32)}
 
@@ -543,31 +550,31 @@
         )
         return [keep, exchange(send, 1)]
 
-    def send_rows(b, held):
-        rows, left = len(batches[b]) * piece, replicas // 2
-        for bit, bits in stages(replicas):
+    def narrow(b, some, waits=()):
+        rows = len(batches[b]) * piece
+        for bit, bits in some:
             ways = 1 << bits
-            left //= ways
-            cut = [h.reshape(left, ways, rows, inner) for h in held]
+            left = held[b][0].shape[0] // ways
             picked = step(
-                functools.partial(pick_kernel, len(cut)),
-                cut,
+                functools.partial(pick_kernel, len(held[b]), 1 << (bit - 1)),
+                [h.reshape(left, ways, rows, inner) for h in held[b]],
                 [shape(left, rows, inner)] * ways,
-                scalars=[places.at[4].set(1 << (bit - 1))] if bit > 1 else [places],
+                scalars=[places],
+                waits=waits,
             )
-            held = [picked[0]] + [exchange(picked[mask], mask << bit) for mask in range(1, ways)]
-        terms[b] = held
-
-    def own_rows(b, cost=small_cost):
+            held[b] = [picked[0]] + [exchange(picked[mask], mask << bit) for mask in range(1, ways)]
+
+    def own_rows(b, cost=small_cost, waits=()):
         batch = batches[b]
         rows = len(batch) * piece
         deltas[b], sent, squares[b] = step(
-            functools.partial(delta_kernel, len(terms[b]), batch[0] * piece, replicas),
-            [own_global, squares[b - 1], *terms[b]],
+            functools.partial(delta_kernel, len(held[b]), batch[0] * piece, replicas),
+            [own_global, squares[b - 1], *held[b]],
             [shape(rows, inner, dtype=F32), shape(rows, inner), tile],
             cost=cost,
+            waits=waits,
         )
-        spread_rows(b, sent)
+        gathered[b] = sent[None]
 
     def backward(begin, count, so_far):
         wide, state, dt, gain_here = group_specs(begin)
@@ -592,40 +599,65 @@
         )
         return grad
 
-    first, second = range(2)
+    end = len(batches) - 1
+    early = end > 1
     for t in range(chunks):
-        sum_side(t, [cots[t - 3][1]] if t >= 3 else [])
+        if t == chunks - 1 and early:
+            held[0] = new_rows(0)
+        sum_side(t, [cots[t - 3][1]] if t >= 3 and not early else [])
         if t == 0:
-            join("kept")
-        else:
+            widen("kept", by_two, kept_landed)
+            finish("kept")
+        if t > 0:
             sum_all(t - 1)
-    held_first = new_rows(first)
+    if early:
+        narrow(0, by_one[:1])
+    held[end - 1] = new_rows(end - 1)
+    if early:
+        narrow(0, by_one[1:])
     sum_all(chunks - 1, cost=large_cost)
-    step(gate_kernel, [], [tile], waits=[cots[chunks - 2][1]])
-    send_rows(first, held_first)
-    held_second = new_rows(second, gathered["kept"][1:])
-    own_rows(first, large_cost)
-    send_rows(second, held_second)
+    narrow(end - 1, by_one[:1])
+    step(gate_kernel, [], [tile], waits=[cots[chunks - 2][1], gathered["kept"][1]])
+    landed = {}
+    if early:
+        own_rows(0)
+        landed[0] = landing(0, by_two)
+    narrow(end - 1, by_one[1:])
+    own_rows(end - 1, small_cost)
+    landed[end - 1] = landing(end - 1, by_two)
+    if early:
+        widen(0, by_two, landed[0])
+        finish(0)
+    held[end] = new_rows(end)
+    narrow(end, by_two)
     half = groups // 2
     grad_input = backward(0, half, None) if half else None
     grad_input = backward(half, groups - half, grad_input)
-    join(first)
-    own_rows(second, large_cost)
-    total = squares[second]
+    widen(end - 1, by_two, landed[end - 1])
+    finish(end - 1)
+    own_rows(end, large_cost, [gathered[0][1]] if early else [])
+    last_landed = landing(end, by_two)
+    total = squares[end]
     for bit in range(heads_over.bit_length() - 1):
         pairs = [(t, t ^ (1 << bit)) for t in range(heads_over)]
-        (total,) = step(add_squares_kernel, [total, lax.ppermute(total, "tensor", pairs)], [tile], waits=gathered[first][1:])
-    for bit, bits in stages(replicas):
+        waits = [gathered[b][1] for b in range(end)]
+        (total,) = step(add_squares_kernel, [total, lax.ppermute(total, "tensor", pairs)], [tile], waits=waits)
+    for bit, bits in by_two:
         landed = [exchange(total, mask << bit) for mask in range(1, 1 << bits)]
         (total,) = step(add_squares_kernel, [total, *landed], [tile])
-    join(second)
+    widen(end, by_two, last_landed)
+    finish(end)
     columns = [total, exchange(total, 1)]
 
     sizes = [len(batch) * piece for batch in batches]
     pair_spec = pl.BlockSpec((2 * owned, inner), lambda r: (r, 0))
-    held_spec = pl.BlockSpec((owned, inner), lambda r: (0, 0))
-    inputs = [own_global, own_momentum, *gathered["kept"], *gathered[first], *gathered[second]]
-    inputs += [deltas[first], deltas[second], *columns]
+    share = owned // (replicas // 2)
+    if share % 8 == 0:
+        held_spec = pl.BlockSpec((share, inner), lambda r: (r, 0))
+    else:
+        held_spec = pl.BlockSpec((owned, inner), lambda r: (0, 0))
+    inputs = [own_global, own_momentum, *gathered["kept"], *[v for b in range(end + 1) for v in gathered[b]]]
+    inputs += [*[deltas[b] for b in range(end + 1)], *columns]
     new_weight, new_global, new_momentum = run(
         functools.partial(weight_kernel, sizes, features * inner * heads_over),
         [places, *inputs],

time: 151 us -> 149 us (0.987)
  waiting for transfers between devices: 70.1 us -> 55.1 us
  starting transfers between devices: 44.6 us -> 56.5 us
  Pallas kernels: 34.4 us -> 36 us
    ppermute x4, waiting for transfers between devices: 14.3 us -> 7.13 us  [shards(): lax.ppermute(p, 'tensor', in_hops[0])]
    ppermute x24 -> x30, starting transfers between devices: 20.4 us -> 27.2 us  [exchange(): lax.ppermute(value, 'replica', [(r, r ^ mask) for r in range(replicas)])]
    ppermute x2, starting transfers between devices: 0.01 us -> 5 us  [shards(): lax.ppermute(total, 'tensor', pairs)]
    ppermute x2, waiting for transfers between devices: 8.1 us -> 3.17 us  [shards(): lax.ppermute(total, 'tensor', pairs)]
    ppermute x4, waiting for transfers between devices: 23.3 us -> 20.4 us  [sum_all(): back = lax.ppermute(out, 'tensor', [(b, a) for a, b in pairs])]
    pallas_call x28 -> x34, Pallas kernels: 34.4 us -> 36 us  [run(): pl.pallas_call(in_turn(kernel, len(inputs), len(waits), len(outs)), in_sp...]
    ppermute x24 -> x30, waiting for transfers between devices: 24.3 us -> 24.4 us  [exchange(): lax.ppermute(value, 'replica', [(r, r ^ mask) for r in range(replicas)])]
  transfers between devices with their start and end apart: 38 -> 44, of which waited for: 17 -> 19; matrix products, arithmetic and copies ran while one was open for 0% -> 0% of each run, Pallas kernels for 14% -> 14%
where the time goes in v12:
time: 149 us
  starting transfers between devices  56.5 us (38%)
  waiting for transfers between devices  55.1 us (37%)
  Pallas kernels  36 us (24%)
    pallas_call x34, Pallas kernels, run(): pl.pallas_call(in_turn(kernel, len(inputs), len(waits), len(outs)), in_sp...  36 us
    ppermute x30, starting transfers between devices, exchange(): lax.ppermute(value, 'replica', [(r, r ^ mask) for r in range(replicas)])  27.2 us
    ppermute x30, waiting for transfers between devices, exchange(): lax.ppermute(value, 'replica', [(r, r ^ mask) for r in range(replicas)])  24.4 us
    ppermute x4, waiting for transfers between devices, sum_all(): back = lax.ppermute(out, 'tensor', [(b, a) for a, b in pairs])  20.4 us
    ppermute x4, starting transfers between devices, shards(): lax.ppermute(p, 'tensor', in_hops[0])  16.2 us
    ppermute x4, waiting for transfers between devices, shards(): lax.ppermute(p, 'tensor', in_hops[0])  7.13 us
    ppermute x4, starting transfers between devices, sum_all(): back = lax.ppermute(out, 'tensor', [(b, a) for a, b in pairs])  5.34 us
    ppermute x2, starting transfers between devices, shards(): lax.ppermute(total, 'tensor', pairs)  5 us
  transfers between devices with their start and end apart: 44, of which 19 were waited for; matrix products, arithmetic and copies ran while one was open for 0% of the time, Pallas kernels for 14%

profile of v12, /device:TPU:0, one launch (start us, length us, event | category | flops | bytes accessed | tf_op | source)
XLA Modules:
  0.0 148.9 jit_solution(12466750728903671740)
XLA Ops:
  0.7 6.2 %shard_map.156 = (bf16[8,256,1024]{2,1,0:T(8,128)(2,1)S(1)}, bf16[128,2048]{1,0:T(8,128)(2,1)S(1)}, f32[256,1024]{1,0:T(8,128)S(1)}, f32[256,1024]{1,0:T(8,128)S...) custom-call(f32[16,512]{1,0:T(8,128)} %bitcast.48, bf16[512,1024]{1,0:T(8,128)(2,1)} %refs_1_.1, ...), custom_call_target="tpu_custom_call" | custom-call | flops 1 | bytes 1 | tf_op jit(solution)/shard_map/pallas_call | solution.py:438
  8.3 5.0 %collective-permute-start = (bf16[512,512]{1,0:T(8,128)(2,1)S(1)}, bf16[512,512]{1,0:T(8,128)(2,1)S(1)}, u32[]{:S(2)}, u32[]{:S(2)}) collective-permute-start(bf16[512,512]{1,0:T(8,128)(2,1)S(1)} %get-tuple-element.100.refs_0_), channel_id=1, source_target_pairs={{0,1},{3,2},{4,5},{7,6},{8,9},{11,10},{12,13},{15,14},{16,17},{19,... | collective-permute-start | bytes 1572872 | tf_op jit(solution)/shard_map/ppermute | solution.py:518
  17.0 2.5 %shard_map.159 = (bf16[512,512]{1,0:T(8,128)(2,1)S(1)}, bf16[512,512]{1,0:T(8,128)(2,1)S(1)}, bf16[512,512]{1,0:T(8,128)(2,1)S(1)}, f32[8,128]{1,0:T(8,128)S(1)}) custom-call(s32[4]{0:T(128)S(1)} %pad_add_fusion.refs_0_, bf16[8,256,1024]{2,1,0:T(8,128)(2,1)S(1)} %get-tuple-element.97.refs_1_.refs_4_.refs_6_.refs_11_, ...), custom_call_target="tpu_custom_call" | custom-call | flops 1 | bytes 1 | tf_op jit(solution)/shard_map/pallas_call | solution.py:438
  20.8 4.8 %collective-permute-done.refs_1_ = bf16[512,512]{1,0:T(8,128)(2,1)S(1)} collective-permute-done((bf16[512,512]{1,0:T(8,128)(2,1)S(1)}, bf16[512,512]{1,0:T(8,128)(2,1)S(1)}, u32[]{:S(2)}, u32[]{:S(2)}) %collective-permute-start) | collective-permute-done | bytes 524320 | tf_op jit(solution)/shard_map/ppermute | solution.py:518
  26.4 1.9 %collective-permute-done.3.refs_1_ = bf16[1,256,1024]{2,1,0:T(8,128)(2,1)S(1)} collective-permute-done((bf16[1,256,1024]{2,1,0:T(8,128)(2,1)S(1)}, bf16[1,256,1024]{2,1,0:T(8,128)(2,1)S(1)}, u32[]{:S(2)}, u32[]{:S(2)}) %collective-permute-start.3) | collective-permute-done | bytes 524320 | tf_op jit(solution)/shard_map/ppermute | solution.py:473
  28.3 5.3 %collective-permute-start.8 = (bf16[512,512]{1,0:T(8,128)(2,1)S(1)}, bf16[512,512]{1,0:T(8,128)(2,1)S(1)}, u32[]{:S(2)}, u32[]{:S(2)}) collective-permute-start(bf16[512,512]{1,0:T(8,128)(2,1)S(1)} %get-tuple-element.114.refs_0_), channel_id=1, source_target_pairs={{0,1},{3,2},{4,5},{7,6},{8,9},{11,10},{12,13},{15,14},{16,17},{19,... | collective-permute-start | bytes 1572872 | tf_op jit(solution)/shard_map/ppermute | solution.py:518
  33.6 5.7 %collective-permute-done.4.refs_2_ = bf16[1,256,1024]{2,1,0:T(8,128)(2,1)S(1)} collective-permute-done((bf16[1,256,1024]{2,1,0:T(8,128)(2,1)S(1)}, bf16[1,256,1024]{2,1,0:T(8,128)(2,1)S(1)}, u32[]{:S(2)}, u32[]{:S(2)}) %collective-permute-start.4) | collective-permute-done | bytes 524320 | tf_op jit(solution)/shard_map/ppermute | solution.py:473
  41.8 4.6 %collective-permute-start.11 = (bf16[512,512]{1,0:T(8,128)(2,1)S(1)}, bf16[512,512]{1,0:T(8,128)(2,1)S(1)}, u32[]{:S(2)}, u32[]{:S(2)}) collective-permute-start(bf16[512,512]{1,0:T(8,128)(2,1)S(1)} %get-tuple-element.119.refs_0_), channel_id=1, source_target_pairs={{0,1},{3,2},{4,5},{7,6},{8,9},{11,10},{12,13},{15,14},{16,17},{19,... | collective-permute-start | bytes 1572872 | tf_op jit(solution)/shard_map/ppermute | solution.py:518
  46.4 1.7 %collective-permute-done.8.refs_1_ = bf16[512,512]{1,0:T(8,128)(2,1)S(1)} collective-permute-done((bf16[512,512]{1,0:T(8,128)(2,1)S(1)}, bf16[512,512]{1,0:T(8,128)(2,1)S(1)}, u32[]{:S(2)}, u32[]{:S(2)}) %collective-permute-start.8) | collective-permute-done | bytes 524320 | tf_op jit(solution)/shard_map/ppermute | solution.py:518
  49.0 5.7 %collective-permute-done.6.refs_2_.refs_13_ = bf16[512,512]{1,0:T(8,128)(2,1)S(1)} collective-permute-done((bf16[512,512]{1,0:T(8,128)(2,1)S(1)}, bf16[512,512]{1,0:T(8,128)(2,1)S(1)}, u32[]{:S(2)}, u32[]{:S(2)}) %collective-permute-start.6) | collective-permute-done | bytes 524320 | tf_op jit(solution)/shard_map/ppermute | solution.py:533
  62.6 10.1 %collective-permute-done.9.refs_2_.refs_15_ = bf16[512,512]{1,0:T(8,128)(2,1)S(1)} collective-permute-done((bf16[512,512]{1,0:T(8,128)(2,1)S(1)}, bf16[512,512]{1,0:T(8,128)(2,1)S(1)}, u32[]{:S(2)}, u32[]{:S(2)}) %collective-permute-start.9) | collective-permute-done | bytes 524320 | tf_op jit(solution)/shard_map/ppermute | solution.py:533
  79.4 4.6 %collective-permute-done.12.refs_1_.refs_2_.refs_17_ = bf16[512,512]{1,0:T(8,128)(2,1)S(1)} collective-permute-done((bf16[512,512]{1,0:T(8,128)(2,1)S(1)}, bf16[512,512]{1,0:T(8,128)(2,1)S(1)}, u32[]{:S(2)}, u32[]{:S(2)}) %collective-permute-start.12) | collective-permute-done | bytes 524320 | tf_op jit(solution)/shard_map/ppermute | solution.py:533
  90.8 2.4 %collective-permute-done.24.refs_3_ = bf16[1,64,1024]{2,1,0:T(8,128)(2,1)S(1)} collective-permute-done((bf16[1,64,1024]{2,1,0:T(8,128)(2,1)S(1)}, bf16[1,64,1024]{2,1,0:T(8,128)(2,1)S(1)}, u32[]{:S(2)}, u32[]{:S(2)}) %collective-permute-start.24) | collective-permute-done | bytes 131104 | tf_op jit(solution)/shard_map/ppermute | solution.py:473
  93.4 3.9 %collective-permute-done.21.refs_2_ = bf16[1,64,1024]{2,1,0:T(8,128)(2,1)S(1)} collective-permute-done((bf16[1,64,1024]{2,1,0:T(8,128)(2,1)S(1)}, bf16[1,64,1024]{2,1,0:T(8,128)(2,1)S(1)}, u32[]{:S(2)}, u32[]{:S(2)}) %collective-permute-start.21) | collective-permute-done | bytes 131104 | tf_op jit(solution)/shard_map/ppermute | solution.py:473
  97.3 2.0 %shard_map.179 = (bf16[4,128,1024]{2,1,0:T(8,128)(2,1)S(1)}, bf16[4,128,1024]{2,1,0:T(8,128)(2,1)S(1)}, f32[8,128]{1,0:T(8,128)S(1)}) custom-call(s32[4]{0:T(128)S(1)} %pad_add_fusion.refs_0_, bf16[512,512]{1,0:T(8,128)(2,1)S(1)} %get-tuple-element.123.refs_1_.refs_16_, bf16[512,512]{1,0:T(8,128)(2,1)S(1)} %collective-permute-done.12.refs_1_.refs_2_.refs_17_, ...), custom_call_target="tpu_custom_call" | custom-call | flops 1 | bytes 1 | tf_op jit(solution)/shard_map/pallas_call | solution.py:438
  105.4 1.7 %collective-permute-start.33 = (bf16[1,128,1024]{2,1,0:T(8,128)(2,1)S(1)}, bf16[1,128,1024]{2,1,0:T(8,128)(2,1)S(1)}, u32[]{:S(2)}, u32[]{:S(2)}) collective-permute-start(bf16[1,128,1024]{2,1,0:T(8,128)(2,1)S(1)} %get-tuple-element.167), channel_id=1, source_target_pairs={{0,24},{4,28},{8,16},{12,20},{16,8},{20,12},{24,0},{28,4},{1,25},{... | collective-permute-start | bytes 786440 | tf_op jit(solution)/shard_map/ppermute | solution.py:473
  108.3 5.1 %shard_map.181 = (bf16[512,1024]{1,0:T(8,128)(2,1)}, f32[8,128]{1,0:T(8,128)S(1)}) custom-call(s32[4]{0:T(128)S(1)} %pad_add_fusion.refs_0_, f32[16,512]{1,0:T(8,128)} %bitcast.49, bf16[512,1024]{1,0:T(8,128)(2,1)} %refs_2_.5, bf16[512,256]{1,0:T(8,128)(2,1)} %refs_3_.5, bf16[512,256]{1,0:T(8,128)(2,1)} %refs_4_.5, f32[1,1024]{1,0:T(1,128)} %bitcast.52, ...), custom_call_target="tpu_custom_call" | custom-call | flops 1 | bytes 1 | tf_op jit(solution)/shard_map/pallas_call | solution.py:438
  113.5 5.1 %shard_map.182 = (bf16[512,1024]{1,0:T(8,128)(2,1)}, f32[8,128]{1,0:T(8,128)S(1)}) custom-call(s32[4]{0:T(128)S(1)} %pad_add_fusion.refs_0_, f32[16,512]{1,0:T(8,128)} %bitcast.50, bf16[512,1024]{1,0:T(8,128)(2,1)} %refs_2_.5, bf16[512,256]{1,0:T(8,128)(2,1)} %refs_3_.5, bf16[512,256]{1,0:T(8,128)(2,1)} %refs_4_.5, ...), custom_call_target="tpu_custom_call", output_to_operand_aliasing={{0}: (20, {})} | custom-call | flops 1 | bytes 1 | tf_op jit(solution)/shard_map/pallas_call | solution.py:438
  124.8 2.1 %collective-permute-start.37 = (f32[8,128]{1,0:T(8,128)S(1)}, f32[8,128]{1,0:T(8,128)S(1)}, u32[]{:S(2)}, u32[]{:S(2)}) collective-permute-start(f32[8,128]{1,0:T(8,128)S(1)} %get-tuple-element.170.refs_0_), channel_id=1, source_target_pairs={{0,1},{1,0},{2,3},{3,2},{4,5},{5,4},{6,7},{7,6},{8,9},{9,8},{10,11... | collective-permute-start | bytes 12296 | tf_op jit(solution)/shard_map/ppermute | solution.py:644
  128.5 2.9 %collective-permute-start.38 = (f32[8,128]{1,0:T(8,128)S(1)}, f32[8,128]{1,0:T(8,128)S(1)}, u32[]{:S(2)}, u32[]{:S(2)}) collective-permute-start(f32[8,128]{1,0:T(8,128)S(1)} %get-tuple-element.172.refs_0_), channel_id=1, source_target_pairs={{0,2},{1,3},{2,0},{3,1},{4,6},{5,7},{6,4},{7,5},{8,10},{9,11},{10,... | collective-permute-start | bytes 12296 | tf_op jit(solution)/shard_map/ppermute | solution.py:644
  134.9 1.7 %collective-permute-done.39.refs_1_ = f32[8,128]{1,0:T(8,128)S(1)} collective-permute-done((f32[8,128]{1,0:T(8,128)S(1)}, f32[8,128]{1,0:T(8,128)S(1)}, u32[]{:S(2)}, u32[]{:S(2)}) %collective-permute-start.39) | collective-permute-done | bytes 4128 | tf_op jit(solution)/shard_map/ppermute | solution.py:473
  137.9 3.2 %collective-permute-done.41.refs_3_ = f32[8,128]{1,0:T(8,128)S(1)} collective-permute-done((f32[8,128]{1,0:T(8,128)S(1)}, f32[8,128]{1,0:T(8,128)S(1)}, u32[]{:S(2)}, u32[]{:S(2)}) %collective-permute-start.41) | collective-permute-done | bytes 4128 | tf_op jit(solution)/shard_map/ppermute | solution.py:473
  141.8 2.2 %collective-permute-done.43.refs_15_ = f32[8,128]{1,0:T(8,128)S(1)} collective-permute-done((f32[8,128]{1,0:T(8,128)S(1)}, f32[8,128]{1,0:T(8,128)S(1)}, u32[]{:S(2)}, u32[]{:S(2)}) %collective-permute-start.43) | collective-permute-done | bytes 4128 | tf_op jit(solution)/shard_map/ppermute | solution.py:473
  143.9 4.8 %shard_map.189 = (bf16[2048,1024]{1,0:T(8,128)(2,1)}, f32[256,1024]{1,0:T(8,128)}, f32[256,1024]{1,0:T(8,128)}, f32[8,128]{1,0:T(8,128)}) custom-call(s32[4]{0:T(128)S(1)} %pad_add_fusion.refs_0_, f32[256,1024]{1,0:T(8,128)S(1)} %get-tuple-element.101.refs_0_.refs_1_, f32[256,1024]{1,0:T(8,128)S(1)} %get-tuple-element.102.refs_1_.refs_2_, ...), custom_call_target="tpu_custom_call" | custom-call | flops 1 | bytes 1 | tf_op jit(solution)/shard_map/pallas_call | solution.py:438
  (100 shorter events, 52.6 us)
Async XLA Ops:
  8.3 17.3 %collective-permute-start = (bf16[512,512]{1,0:T(8,128)(2,1)S(1)}, bf16[512,512]{1,0:T(8,128)(2,1)S(1)}, u32[]{:S(2)}, u32[]{:S(2)}) collective-permute-start(bf16[512,512]{1,0:T(8,128)(2,1)S(1)} %get-tuple-element.100.refs_0_), channel_id=1, source_target_pairs={{0,1},{3,2},{4,5},{7,6},{8,9},{11,10},{12,13},{15,14},{16,17},{19,... | collective-permute-start | bytes 1572872 | tf_op jit(solution)/shard_map/ppermute | solution.py:518
  13.4 14.9 %collective-permute-start.3 = (bf16[1,256,1024]{2,1,0:T(8,128)(2,1)S(1)}, bf16[1,256,1024]{2,1,0:T(8,128)(2,1)S(1)}, u32[]{:S(2)}, u32[]{:S(2)}) collective-permute-start(bf16[1,256,1024]{2,1,0:T(8,128)(2,1)S(1)} %bitcast.27), channel_id=1, source_target_pairs={{0,8},{4,12},{8,0},{12,4},{16,24},{20,28},{24,16},{28,20},{1,9},{5... | collective-permute-start | bytes 1572872 | tf_op jit(solution)/shard_map/ppermute | solution.py:473
  15.0 24.3 %collective-permute-start.4 = (bf16[1,256,1024]{2,1,0:T(8,128)(2,1)S(1)}, bf16[1,256,1024]{2,1,0:T(8,128)(2,1)S(1)}, u32[]{:S(2)}, u32[]{:S(2)}) collective-permute-start(bf16[1,256,1024]{2,1,0:T(8,128)(2,1)S(1)} %bitcast.28), channel_id=1, source_target_pairs={{0,16},{4,20},{8,24},{12,28},{16,0},{20,4},{24,8},{28,12},{1,17},{... | collective-permute-start | bytes 1572872 | tf_op jit(solution)/shard_map/ppermute | solution.py:473
  16.5 22.8 %collective-permute-start.5 = (bf16[1,256,1024]{2,1,0:T(8,128)(2,1)S(1)}, bf16[1,256,1024]{2,1,0:T(8,128)(2,1)S(1)}, u32[]{:S(2)}, u32[]{:S(2)}) collective-permute-start(bf16[1,256,1024]{2,1,0:T(8,128)(2,1)S(1)} %bitcast.29), channel_id=1, source_target_pairs={{0,24},{4,28},{8,16},{12,20},{16,8},{20,12},{24,0},{28,4},{1,25},{... | collective-permute-start | bytes 1572872 | tf_op jit(solution)/shard_map/ppermute | solution.py:473
  19.5 20.0 %collective-permute-start.2 = (bf16[512,512]{1,0:T(8,128)(2,1)S(1)}, bf16[512,512]{1,0:T(8,128)(2,1)S(1)}, u32[]{:S(2)}, u32[]{:S(2)}) collective-permute-start(bf16[512,512]{1,0:T(8,128)(2,1)S(1)} %get-tuple-element.107.refs_0_), channel_id=1, source_target_pairs={{0,1},{3,2},{4,5},{7,6},{8,9},{11,10},{12,13},{15,14},{16,17},{19,... | collective-permute-start | bytes 1572872 | tf_op jit(solution)/shard_map/ppermute | solution.py:518
  25.7 14.6 %collective-permute-start.1 = (bf16[512,512]{1,0:T(8,128)(2,1)S(1)}, bf16[512,512]{1,0:T(8,128)(2,1)S(1)}, u32[]{:S(2)}, u32[]{:S(2)}) collective-permute-start(bf16[512,512]{1,0:T(8,128)(2,1)S(1)} %get-tuple-element.106.refs_0_), channel_id=1, source_target_pairs={{1,2},{2,1},{5,6},{6,5},{9,10},{10,9},{13,14},{14,13},{17,18},{18,... | collective-permute-start | bytes 1572872 | tf_op jit(solution)/shard_map/ppermute | solution.py:529
  28.3 19.7 %collective-permute-start.8 = (bf16[512,512]{1,0:T(8,128)(2,1)S(1)}, bf16[512,512]{1,0:T(8,128)(2,1)S(1)}, u32[]{:S(2)}, u32[]{:S(2)}) collective-permute-start(bf16[512,512]{1,0:T(8,128)(2,1)S(1)} %get-tuple-element.114.refs_0_), channel_id=1, source_target_pairs={{0,1},{3,2},{4,5},{7,6},{8,9},{11,10},{12,13},{15,14},{16,17},{19,... | collective-permute-start | bytes 1572872 | tf_op jit(solution)/shard_map/ppermute | solution.py:518
  40.5 14.3 %collective-permute-start.6 = (bf16[512,512]{1,0:T(8,128)(2,1)S(1)}, bf16[512,512]{1,0:T(8,128)(2,1)S(1)}, u32[]{:S(2)}, u32[]{:S(2)}) collective-permute-start(bf16[512,512]{1,0:T(8,128)(2,1)S(1)} %get-tuple-element.112.refs_1_.refs_12_), channel_id=1, source_target_pairs={{1,0},{2,3},{5,4},{6,7},{9,8},{10,11},{13,12},{14,15},{17,16},{18,... | collective-permute-start | bytes 1572872 | tf_op jit(solution)/shard_map/ppermute | solution.py:533
  41.8 16.4 %collective-permute-start.11 = (bf16[512,512]{1,0:T(8,128)(2,1)S(1)}, bf16[512,512]{1,0:T(8,128)(2,1)S(1)}, u32[]{:S(2)}, u32[]{:S(2)}) collective-permute-start(bf16[512,512]{1,0:T(8,128)(2,1)S(1)} %get-tuple-element.119.refs_0_), channel_id=1, source_target_pairs={{0,1},{3,2},{4,5},{7,6},{8,9},{11,10},{12,13},{15,14},{16,17},{19,... | collective-permute-start | bytes 1572872 | tf_op jit(solution)/shard_map/ppermute | solution.py:518
  48.2 10.8 %collective-permute-start.10 = (bf16[512,512]{1,0:T(8,128)(2,1)S(1)}, bf16[512,512]{1,0:T(8,128)(2,1)S(1)}, u32[]{:S(2)}, u32[]{:S(2)}) collective-permute-start(bf16[512,512]{1,0:T(8,128)(2,1)S(1)} %get-tuple-element.118.refs_0_), channel_id=1, source_target_pairs={{1,2},{2,1},{5,6},{6,5},{9,10},{10,9},{13,14},{14,13},{17,18},{18,... | collective-permute-start | bytes 1572872 | tf_op jit(solution)/shard_map/ppermute | solution.py:529
  56.1 16.6 %collective-permute-start.9 = (bf16[512,512]{1,0:T(8,128)(2,1)S(1)}, bf16[512,512]{1,0:T(8,128)(2,1)S(1)}, u32[]{:S(2)}, u32[]{:S(2)}) collective-permute-start(bf16[512,512]{1,0:T(8,128)(2,1)S(1)} %get-tuple-element.117.refs_1_.refs_14_), channel_id=1, source_target_pairs={{1,0},{2,3},{5,4},{6,7},{9,8},{10,11},{13,12},{14,15},{17,16},{18,... | collective-permute-start | bytes 1572872 | tf_op jit(solution)/shard_map/ppermute | solution.py:533
  58.3 16.5 %collective-permute-start.13 = (bf16[512,512]{1,0:T(8,128)(2,1)S(1)}, bf16[512,512]{1,0:T(8,128)(2,1)S(1)}, u32[]{:S(2)}, u32[]{:S(2)}) collective-permute-start(bf16[512,512]{1,0:T(8,128)(2,1)S(1)} %get-tuple-element.124.refs_0_), channel_id=1, source_target_pairs={{1,2},{2,1},{5,6},{6,5},{9,10},{10,9},{13,14},{14,13},{17,18},{18,... | collective-permute-start | bytes 1572872 | tf_op jit(solution)/shard_map/ppermute | solution.py:529
  59.8 14.4 %collective-permute-start.15 = (bf16[2,64,1024]{2,1,0:T(8,128)(2,1)S(1)}, bf16[2,64,1024]{2,1,0:T(8,128)(2,1)S(1)}, u32[]{:S(2)}, u32[]{:S(2)}) collective-permute-start(bf16[2,64,1024]{2,1,0:T(8,128)(2,1)S(1)} %get-tuple-element.129), channel_id=1, source_target_pairs={{0,8},{4,12},{8,0},{12,4},{16,24},{20,28},{24,16},{28,20},{1,9},{5... | collective-permute-start | bytes 786440 | tf_op jit(solution)/shard_map/ppermute | solution.py:473
  61.3 22.6 %collective-permute-start.19 = (bf16[4,256,1024]{2,1,0:T(8,128)(2,1)S(1)}, bf16[4,256,1024]{2,1,0:T(8,128)(2,1)S(1)}, u32[]{:S(2)}, u32[]{:S(2)}) collective-permute-start(bf16[4,256,1024]{2,1,0:T(8,128)(2,1)S(1)} %get-tuple-element.140.refs_3_), channel_id=1, source_target_pairs={{0,4},{4,0},{8,12},{12,8},{16,20},{20,16},{24,28},{28,24},{1,5},{5... | collective-permute-start | bytes 6291464 | tf_op jit(solution)/shard_map/ppermute | solution.py:473
  61.4 22.6 %collective-permute-start.12 = (bf16[512,512]{1,0:T(8,128)(2,1)S(1)}, bf16[512,512]{1,0:T(8,128)(2,1)S(1)}, u32[]{:S(2)}, u32[]{:S(2)}) collective-permute-start(bf16[512,512]{1,0:T(8,128)(2,1)S(1)} %get-tuple-element.123.refs_1_.refs_16_), channel_id=1, source_target_pairs={{1,0},{2,3},{5,4},{6,7},{9,8},{10,11},{13,12},{14,15},{17,16},{18,... | collective-permute-start | bytes 1572872 | tf_op jit(solution)/shard_map/ppermute | solution.py:533
  74.9 22.4 %collective-permute-start.16 = (bf16[512,512]{1,0:T(8,128)(2,1)S(1)}, bf16[512,512]{1,0:T(8,128)(2,1)S(1)}, u32[]{:S(2)}, u32[]{:S(2)}) collective-permute-start(bf16[512,512]{1,0:T(8,128)(2,1)S(1)} %get-tuple-element.133.refs_3_.refs_18_), channel_id=1, source_target_pairs={{1,0},{2,3},{5,4},{6,7},{9,8},{10,11},{13,12},{14,15},{17,16},{18,... | collective-permute-start | bytes 1572872 | tf_op jit(solution)/shard_map/ppermute | solution.py:533
  99.4 20.7 %collective-permute-start.26 = (bf16[4,64,1024]{2,1,0:T(8,128)(2,1)S(1)}, bf16[4,64,1024]{2,1,0:T(8,128)(2,1)S(1)}, u32[]{:S(2)}, u32[]{:S(2)}) collective-permute-start(bf16[4,64,1024]{2,1,0:T(8,128)(2,1)S(1)} %get-tuple-element.159.refs_5_), channel_id=1, source_target_pairs={{0,4},{4,0},{8,12},{12,8},{16,20},{20,16},{24,28},{28,24},{1,5},{5... | collective-permute-start | bytes 1572872 | tf_op jit(solution)/shard_map/ppermute | solution.py:473
  103.0 17.2 %collective-permute-start.31 = (bf16[1,128,1024]{2,1,0:T(8,128)(2,1)S(1)}, bf16[1,128,1024]{2,1,0:T(8,128)(2,1)S(1)}, u32[]{:S(2)}, u32[]{:S(2)}) collective-permute-start(bf16[1,128,1024]{2,1,0:T(8,128)(2,1)S(1)} %get-tuple-element.165), channel_id=1, source_target_pairs={{0,8},{4,12},{8,0},{12,4},{16,24},{20,28},{24,16},{28,20},{1,9},{5... | collective-permute-start | bytes 786440 | tf_op jit(solution)/shard_map/ppermute | solution.py:473
  104.4 16.5 %collective-permute-start.32 = (bf16[1,128,1024]{2,1,0:T(8,128)(2,1)S(1)}, bf16[1,128,1024]{2,1,0:T(8,128)(2,1)S(1)}, u32[]{:S(2)}, u32[]{:S(2)}) collective-permute-start(bf16[1,128,1024]{2,1,0:T(8,128)(2,1)S(1)} %get-tuple-element.166), channel_id=1, source_target_pairs={{0,16},{4,20},{8,24},{12,28},{16,0},{20,4},{24,8},{28,12},{1,17},{... | collective-permute-start | bytes 786440 | tf_op jit(solution)/shard_map/ppermute | solution.py:473
  105.4 15.5 %collective-permute-start.33 = (bf16[1,128,1024]{2,1,0:T(8,128)(2,1)S(1)}, bf16[1,128,1024]{2,1,0:T(8,128)(2,1)S(1)}, u32[]{:S(2)}, u32[]{:S(2)}) collective-permute-start(bf16[1,128,1024]{2,1,0:T(8,128)(2,1)S(1)} %get-tuple-element.167), channel_id=1, source_target_pairs={{0,24},{4,28},{8,16},{12,20},{16,8},{20,12},{24,0},{28,4},{1,25},{... | collective-permute-start | bytes 786440 | tf_op jit(solution)/shard_map/ppermute | solution.py:473
  107.1 12.9 %collective-permute-start.29 = (bf16[1,64,1024]{2,1,0:T(8,128)(2,1)S(1)}, bf16[1,64,1024]{2,1,0:T(8,128)(2,1)S(1)}, u32[]{:S(2)}, u32[]{:S(2)}) collective-permute-start(bf16[1,64,1024]{2,1,0:T(8,128)(2,1)S(1)} %bitcast.41), channel_id=1, source_target_pairs={{0,24},{4,28},{8,16},{12,20},{16,8},{20,12},{24,0},{28,4},{1,25},{... | collective-permute-start | bytes 393224 | tf_op jit(solution)/shard_map/ppermute | solution.py:473
  121.3 19.8 %collective-permute-start.34 = (bf16[1,128,1024]{2,1,0:T(8,128)(2,1)S(1)}, bf16[1,128,1024]{2,1,0:T(8,128)(2,1)S(1)}, u32[]{:S(2)}, u32[]{:S(2)}) collective-permute-start(bf16[1,128,1024]{2,1,0:T(8,128)(2,1)S(1)} %bitcast.35), channel_id=1, source_target_pairs={{0,8},{4,12},{8,0},{12,4},{16,24},{20,28},{24,16},{28,20},{1,9},{5... | collective-permute-start | bytes 786440 | tf_op jit(solution)/shard_map/ppermute | solution.py:473
  122.1 19.1 %collective-permute-start.35 = (bf16[1,128,1024]{2,1,0:T(8,128)(2,1)S(1)}, bf16[1,128,1024]{2,1,0:T(8,128)(2,1)S(1)}, u32[]{:S(2)}, u32[]{:S(2)}) collective-permute-start(bf16[1,128,1024]{2,1,0:T(8,128)(2,1)S(1)} %bitcast.36), channel_id=1, source_target_pairs={{0,16},{4,20},{8,24},{12,28},{16,0},{20,4},{24,8},{28,12},{1,17},{... | collective-permute-start | bytes 786440 | tf_op jit(solution)/shard_map/ppermute | solution.py:473
  123.2 17.9 %collective-permute-start.36 = (bf16[1,128,1024]{2,1,0:T(8,128)(2,1)S(1)}, bf16[1,128,1024]{2,1,0:T(8,128)(2,1)S(1)}, u32[]{:S(2)}, u32[]{:S(2)}) collective-permute-start(bf16[1,128,1024]{2,1,0:T(8,128)(2,1)S(1)} %bitcast.37), channel_id=1, source_target_pairs={{0,24},{4,28},{8,16},{12,20},{16,8},{20,12},{24,0},{28,4},{1,25},{... | collective-permute-start | bytes 786440 | tf_op jit(solution)/shard_map/ppermute | solution.py:473
  (20 other events, 106.1 us)

commit v13 on v11

--- a/solution.py
+++ b/solution.py
@@ -31,7 +31,7 @@
 
 
 def silu(z):
-    return z * (1.0 / (1.0 + jnp.exp(-z)))
+    return 0.5 * z * (1.0 + jnp.tanh(0.5 * z))
 
 
 def softplus(v):
@@ -297,14 +297,16 @@
 
 
 def delta_kernel(count, lo, replicas, global_ref, before_ref, *refs):
-    terms, (delta_ref, sent_ref, squares_ref) = refs[:count], refs[count:]
+    terms, earlier, (delta_ref, sent_ref, squares_ref) = refs[:count], refs[count:-3], refs[-3:]
     rows, inner = delta_ref.shape
     total = terms[0][0].astype(F32)
     for term in terms[1:]:
         total = total + term[0].astype(F32)
     delta = global_ref[lo : lo + rows, :] - total / replicas
     delta_ref[...] = delta
-    sent_ref[...] = delta.astype(BF16)
+    if earlier:
+        sent_ref[:lo, :] = earlier[0][...]
+    sent_ref[lo:, :] = delta.astype(BF16)
     squares = jnp.sum(delta * delta, axis=0, keepdims=True)
     squares = before_ref[...] + jnp.broadcast_to(jnp.sum(squares, axis=1, keepdims=True), before_ref.shape)
     squares_ref[...] = squares
@@ -319,40 +321,38 @@
 
 
 def weight_kernel(sizes, entries, place_ref, global_ref, momentum_ref, *refs):
-    count = len(sizes)
-    pairs, deltas, squares = refs[: 2 * count + 2], refs[2 * count + 2 : 3 * count + 2], refs[3 * count + 2 : -3]
+    kepts, pairs, (*deltas, own_squares_ref, other_squares_ref) = refs[:2], refs[2:4], refs[4:-3]
     new_ref, new_global_ref, new_momentum_ref = refs[-3:]
-    mean = (squares[0][:1, :1] + squares[1][:1, :1]) / entries
+    mean = (own_squares_ref[:1, :1] + other_squares_ref[:1, :1]) / entries
     factor = jnp.minimum(1.0, clip_rms / jnp.sqrt(mean + 1e-06))
     at_chip = lax.bitwise_xor(pl.program_id(0), place_ref[3])
     owned = new_ref.shape[0] // 2
     scale = (outer_rate * (1.0 + outer_beta)) * factor
 
-    def one_core(core, side):
-        lo = 0
-        for n, size in enumerate(sizes):
-            kept = pairs[side][at_chip, lo : lo + size, :].astype(F32)
-            delta = pairs[2 * n + 2 + side][at_chip, :size, :].astype(F32)
-            new_ref[core * owned + lo : core * owned + lo + size, :] = (kept - scale * delta).astype(BF16)
-            lo += size
-
     for own_core in range(2):
 
         @pl.when(place_ref[2] == own_core)
         def _():
-            one_core(own_core, 0)
-            one_core(1 - own_core, 1)
-
-    @pl.when(pl.program_id(0) == 0)
-    def _():
-        lo = 0
-        for n, size in enumerate(sizes):
-            rows = slice(lo, lo + size)
-            lo += size
-            clipped = factor * deltas[n][...]
-            new_momentum = outer_beta * momentum_ref[rows, :] + clipped
-            new_momentum_ref[rows, :] = new_momentum
-            new_global_ref[rows, :] = global_ref[rows, :] - outer_rate * (clipped + outer_beta * new_momentum)
+            for core, kept_ref, delta_ref in zip((own_core, 1 - own_core), kepts, pairs):
+                new = kept_ref[at_chip].astype(F32) - scale * delta_ref[at_chip].astype(F32)
+                new_ref[core * owned : (core + 1) * owned, :] = new.astype(BF16)
+
+    part = new_global_ref.shape[0]
+    lo = 0
+    for n, size in enumerate(sizes):
+        rows = min(size, part)
+        for row in range(0, size, rows):
+            at, here = slice(lo + row, lo + row + rows), (lo + row) % part
+
+            @pl.when(pl.program_id(0) == (lo + row) // part)
+            def _():
+                clipped = factor * deltas[n][row : row + rows, :]
+                new_momentum = outer_beta * momentum_ref[at, :] + clipped
+                new_momentum_ref[here : here + rows, :] = new_momentum
+                new_global = global_ref[at, :] - outer_rate * (clipped + outer_beta * new_momentum)
+                new_global_ref[here : here + rows, :] = new_global
+
+        lo += size
 
 
 def inward(axis_size):
@@ -527,7 +527,7 @@
             out = back if pairs is in_hops[0] else jnp.where(in_middle, mid, back)
         cots[n] = (mid, out)
 
-    terms, deltas = {}, {}
+    terms, deltas, sent = {}, {}, {}
     tile = shape(8, LANES, dtype=F32)
     squares = {-1: jnp.zeros((8, LANES), F32)}
 
@@ -561,13 +561,12 @@
     def own_rows(b, cost=small_cost):
         batch = batches[b]
         rows = len(batch) * piece
-        deltas[b], sent, squares[b] = step(
+        deltas[b], sent[b], squares[b] = step(
             functools.partial(delta_kernel, len(terms[b]), batch[0] * piece, replicas),
-            [own_global, squares[b - 1], *terms[b]],
-            [shape(rows, inner, dtype=F32), shape(rows, inner), tile],
+            [own_global, squares[b - 1], *terms[b], *([sent[b - 1]] if b else [])],
+            [shape(rows, inner, dtype=F32), shape(batch[0] * piece + rows, inner), tile],
             cost=cost,
         )
-        spread_rows(b, sent)
 
     def backward(begin, count, so_far):
         wide, state, dt, gain_here = group_specs(begin)
@@ -606,25 +605,27 @@
     held_second = new_rows(second, gathered["kept"][1:])
     own_rows(first, large_cost)
     send_rows(second, held_second)
-    half = groups // 2
-    grad_input = backward(0, half, None) if half else None
-    grad_input = backward(half, groups - half, grad_input)
-    join(first)
+    grad_input = backward(0, groups, None)
     own_rows(second, large_cost)
+    spread_rows("all", sent[second])
     total = squares[second]
     for bit in range(heads_over.bit_length() - 1):
         pairs = [(t, t ^ (1 << bit)) for t in range(heads_over)]
-        (total,) = step(add_squares_kernel, [total, lax.ppermute(total, "tensor", pairs)], [tile], waits=gathered[first][1:])
+        (total,) = step(add_squares_kernel, [total, lax.ppermute(total, "tensor", pairs)], [tile])
     for bit, bits in stages(replicas):
         landed = [exchange(total, mask << bit) for mask in range(1, 1 << bits)]
         (total,) = step(add_squares_kernel, [total, *landed], [tile])
-    join(second)
+    join("all")
     columns = [total, exchange(total, 1)]
 
     sizes = [len(batch) * piece for batch in batches]
     pair_spec = pl.BlockSpec((2 * owned, inner), lambda r: (r, 0))
-    held_spec = pl.BlockSpec((owned, inner), lambda r: (0, 0))
-    inputs = [own_global, own_momentum, *gathered["kept"], *gathered[first], *gathered[second]]
+    share = owned // (replicas // 2)
+    if share % 8 == 0:
+        held_spec = pl.BlockSpec((share, inner), lambda r: (r, 0))
+    else:
+        held_spec = pl.BlockSpec((owned, inner), lambda r: (0, 0))
+    inputs = [own_global, own_momentum, *gathered["kept"], *gathered["all"]]
     inputs += [deltas[first], deltas[second], *columns]
     new_weight, new_global, new_momentum = run(
         functools.partial(weight_kernel, sizes, features * inner * heads_over),

time: 151 us -> 154 us (1.020)
  waiting for transfers between devices: 70.1 us -> 78.8 us
  starting transfers between devices: 44.6 us -> 41 us
  Pallas kernels: 34.4 us -> 32.2 us
    ppermute x24 -> x20, waiting for transfers between devices: 24.3 us -> 32.1 us  [exchange(): lax.ppermute(value, 'replica', [(r, r ^ mask) for r in range(replicas)])]
    ppermute x24 -> x20, starting transfers between devices: 20.4 us -> 17.5 us  [exchange(): lax.ppermute(value, 'replica', [(r, r ^ mask) for r in range(replicas)])]
    pallas_call x28 -> x26, Pallas kernels: 34.4 us -> 32.2 us  [run(): pl.pallas_call(in_turn(kernel, len(inputs), len(waits), len(outs)), in_sp...]
  transfers between devices with their start and end apart: 38 -> 34, of which waited for: 17 -> 18; matrix products, arithmetic and copies ran while one was open for 0% -> 0% of each run, Pallas kernels for 14% -> 12%
where the time goes in v13:
time: 154 us; the launch traced here: 153 us
  waiting for transfers between devices  78.8 us (51%)
  starting transfers between devices  41 us (27%)
  Pallas kernels  32.2 us (21%)
    pallas_call x26, Pallas kernels, run(): pl.pallas_call(in_turn(kernel, len(inputs), len(waits), len(outs)), in_sp...  32.2 us
    ppermute x20, waiting for transfers between devices, exchange(): lax.ppermute(value, 'replica', [(r, r ^ mask) for r in range(replicas)])  32.1 us
    ppermute x4, waiting for transfers between devices, sum_all(): back = lax.ppermute(out, 'tensor', [(b, a) for a, b in pairs])  24.2 us
    ppermute x20, starting transfers between devices, exchange(): lax.ppermute(value, 'replica', [(r, r ^ mask) for r in range(replicas)])  17.5 us
    ppermute x4, starting transfers between devices, shards(): lax.ppermute(p, 'tensor', in_hops[0])  15.4 us
    ppermute x4, waiting for transfers between devices, shards(): lax.ppermute(p, 'tensor', in_hops[0])  14.3 us
    ppermute x2, waiting for transfers between devices, shards(): lax.ppermute(total, 'tensor', pairs)  8.11 us
    ppermute x4, starting transfers between devices, sum_all(): back = lax.ppermute(out, 'tensor', [(b, a) for a, b in pairs])  5.35 us
  transfers between devices with their start and end apart: 34, of which 18 were waited for; matrix products, arithmetic and copies ran while one was open for 0% of the time, Pallas kernels for 12%

profile of v13, /device:TPU:0, one launch (start us, length us, event | category | flops | bytes accessed | tf_op | source)
XLA Modules:
  0.0 153.2 jit_solution(4311393285400284541)
XLA Ops:
  0.7 6.2 %shard_map.156 = (bf16[8,256,1024]{2,1,0:T(8,128)(2,1)S(1)}, bf16[128,2048]{1,0:T(8,128)(2,1)S(1)}, f32[256,1024]{1,0:T(8,128)S(1)}, f32[256,1024]{1,0:T(8,128)S...) custom-call(f32[16,512]{1,0:T(8,128)} %bitcast.26, bf16[512,1024]{1,0:T(8,128)(2,1)} %refs_1_.1, ...), custom_call_target="tpu_custom_call" | custom-call | flops 1 | bytes 1 | tf_op jit(solution)/shard_map/pallas_call | solution.py:433
  8.3 5.0 %collective-permute-start = (bf16[512,512]{1,0:T(8,128)(2,1)S(1)}, bf16[512,512]{1,0:T(8,128)(2,1)S(1)}, u32[]{:S(2)}, u32[]{:S(2)}) collective-permute-start(bf16[512,512]{1,0:T(8,128)(2,1)S(1)} %get-tuple-element.80.refs_0_), channel_id=1, source_target_pairs={{0,1},{3,2},{4,5},{7,6},{8,9},{11,10},{12,13},{15,14},{16,17},{19,... | collective-permute-start | bytes 1572872 | tf_op jit(solution)/shard_map/ppermute | solution.py:511
  13.4 2.5 %collective-permute-start.5 = (bf16[1,256,1024]{2,1,0:T(8,128)(2,1)S(1)}, bf16[1,256,1024]{2,1,0:T(8,128)(2,1)S(1)}, u32[]{:S(2)}, u32[]{:S(2)}) collective-permute-start(bf16[1,256,1024]{2,1,0:T(8,128)(2,1)S(1)} %bitcast.21), channel_id=1, source_target_pairs={{0,24},{4,28},{8,16},{12,20},{16,8},{20,12},{24,0},{28,4},{1,25},{... | collective-permute-start | bytes 1572872 | tf_op jit(solution)/shard_map/ppermute | solution.py:468
  17.0 2.5 %shard_map.159 = (bf16[512,512]{1,0:T(8,128)(2,1)S(1)}, bf16[512,512]{1,0:T(8,128)(2,1)S(1)}, bf16[512,512]{1,0:T(8,128)(2,1)S(1)}, f32[8,128]{1,0:T(8,128)S(1)}) custom-call(s32[5]{0:T(128)S(1)} %stack.23.refs_0_, bf16[8,256,1024]{2,1,0:T(8,128)(2,1)S(1)} %get-tuple-element.77.refs_1_.refs_6_.refs_11_, ...), custom_call_target="tpu_custom_call" | custom-call | flops 1 | bytes 1 | tf_op jit(solution)/shard_map/pallas_call | solution.py:433
  20.8 4.8 %collective-permute-done.refs_1_ = bf16[512,512]{1,0:T(8,128)(2,1)S(1)} collective-permute-done((bf16[512,512]{1,0:T(8,128)(2,1)S(1)}, bf16[512,512]{1,0:T(8,128)(2,1)S(1)}, u32[]{:S(2)}, u32[]{:S(2)}) %collective-permute-start) | collective-permute-done | bytes 524320 | tf_op jit(solution)/shard_map/ppermute | solution.py:511
  26.4 2.9 %collective-permute-done.5.refs_3_ = bf16[1,256,1024]{2,1,0:T(8,128)(2,1)S(1)} collective-permute-done((bf16[1,256,1024]{2,1,0:T(8,128)(2,1)S(1)}, bf16[1,256,1024]{2,1,0:T(8,128)(2,1)S(1)}, u32[]{:S(2)}, u32[]{:S(2)}) %collective-permute-start.5) | collective-permute-done | bytes 524320 | tf_op jit(solution)/shard_map/ppermute | solution.py:468
  29.3 4.3 %collective-permute-start.8 = (bf16[512,512]{1,0:T(8,128)(2,1)S(1)}, bf16[512,512]{1,0:T(8,128)(2,1)S(1)}, u32[]{:S(2)}, u32[]{:S(2)}) collective-permute-start(bf16[512,512]{1,0:T(8,128)(2,1)S(1)} %get-tuple-element.94.refs_0_), channel_id=1, source_target_pairs={{0,1},{3,2},{4,5},{7,6},{8,9},{11,10},{12,13},{15,14},{16,17},{19,... | collective-permute-start | bytes 1572872 | tf_op jit(solution)/shard_map/ppermute | solution.py:511
  33.6 5.4 %collective-permute-done.4.refs_2_ = bf16[1,256,1024]{2,1,0:T(8,128)(2,1)S(1)} collective-permute-done((bf16[1,256,1024]{2,1,0:T(8,128)(2,1)S(1)}, bf16[1,256,1024]{2,1,0:T(8,128)(2,1)S(1)}, u32[]{:S(2)}, u32[]{:S(2)}) %collective-permute-start.4) | collective-permute-done | bytes 524320 | tf_op jit(solution)/shard_map/ppermute | solution.py:468
  40.1 4.8 %collective-permute-start.11 = (bf16[512,512]{1,0:T(8,128)(2,1)S(1)}, bf16[512,512]{1,0:T(8,128)(2,1)S(1)}, u32[]{:S(2)}, u32[]{:S(2)}) collective-permute-start(bf16[512,512]{1,0:T(8,128)(2,1)S(1)} %get-tuple-element.99.refs_0_), channel_id=1, source_target_pairs={{0,1},{3,2},{4,5},{7,6},{8,9},{11,10},{12,13},{15,14},{16,17},{19,... | collective-permute-start | bytes 1572872 | tf_op jit(solution)/shard_map/ppermute | solution.py:511
  50.3 7.8 %collective-permute-done.11.refs_1_ = bf16[512,512]{1,0:T(8,128)(2,1)S(1)} collective-permute-done((bf16[512,512]{1,0:T(8,128)(2,1)S(1)}, bf16[512,512]{1,0:T(8,128)(2,1)S(1)}, u32[]{:S(2)}, u32[]{:S(2)}) %collective-permute-start.11) | collective-permute-done | bytes 524320 | tf_op jit(solution)/shard_map/ppermute | solution.py:511
  58.2 3.6 %collective-permute-done.6.refs_3_.refs_2_.refs_13_ = bf16[512,512]{1,0:T(8,128)(2,1)S(1)} collective-permute-done((bf16[512,512]{1,0:T(8,128)(2,1)S(1)}, bf16[512,512]{1,0:T(8,128)(2,1)S(1)}, u32[]{:S(2)}, u32[]{:S(2)}) %collective-permute-start.6) | collective-permute-done | bytes 524320 | tf_op jit(solution)/shard_map/ppermute | solution.py:526
  64.1 8.9 %collective-permute-done.9.refs_4_.refs_15_ = bf16[512,512]{1,0:T(8,128)(2,1)S(1)} collective-permute-done((bf16[512,512]{1,0:T(8,128)(2,1)S(1)}, bf16[512,512]{1,0:T(8,128)(2,1)S(1)}, u32[]{:S(2)}, u32[]{:S(2)}) %collective-permute-start.9) | collective-permute-done | bytes 524320 | tf_op jit(solution)/shard_map/ppermute | solution.py:526
  73.0 2.0 %shard_map.168 = (bf16[4,128,1024]{2,1,0:T(8,128)(2,1)S(1)}, bf16[4,128,1024]{2,1,0:T(8,128)(2,1)S(1)}, f32[8,128]{1,0:T(8,128)S(1)}) custom-call(s32[5]{0:T(128)S(1)} %stack.23.refs_0_, bf16[512,512]{1,0:T(8,128)(2,1)S(1)} %get-tuple-element.92.refs_1_.refs_12_, bf16[512,512]{1,0:T(8,128)(2,1)S(1)} %collective-permute-done.6.refs_3_.refs_2_.refs_13_, ...), custom_call_target="tpu_custom_call" | custom-call | flops 1 | bytes 1 | tf_op jit(solution)/shard_map/pallas_call | solution.py:433
  76.7 7.4 %collective-permute-done.12.refs_1_.refs_2_.refs_17_ = bf16[512,512]{1,0:T(8,128)(2,1)S(1)} collective-permute-done((bf16[512,512]{1,0:T(8,128)(2,1)S(1)}, bf16[512,512]{1,0:T(8,128)(2,1)S(1)}, u32[]{:S(2)}, u32[]{:S(2)}) %collective-permute-start.12) | collective-permute-done | bytes 524320 | tf_op jit(solution)/shard_map/ppermute | solution.py:526
  89.0 4.4 %collective-permute-done.14.refs_4_.refs_19_ = bf16[512,512]{1,0:T(8,128)(2,1)S(1)} collective-permute-done((bf16[512,512]{1,0:T(8,128)(2,1)S(1)}, bf16[512,512]{1,0:T(8,128)(2,1)S(1)}, u32[]{:S(2)}, u32[]{:S(2)}) %collective-permute-start.14) | collective-permute-done | bytes 524320 | tf_op jit(solution)/shard_map/ppermute | solution.py:526
  93.4 2.0 %shard_map.172 = (bf16[4,128,1024]{2,1,0:T(8,128)(2,1)S(1)}, bf16[4,128,1024]{2,1,0:T(8,128)(2,1)S(1)}, f32[8,128]{1,0:T(8,128)S(1)}) custom-call(s32[5]{0:T(128)S(1)} %stack.23.refs_0_, bf16[512,512]{1,0:T(8,128)(2,1)S(1)} %get-tuple-element.102.refs_1_.refs_16_, bf16[512,512]{1,0:T(8,128)(2,1)S(1)} %collective-permute-done.12.refs_1_.refs_2_.refs_17_, ...), custom_call_target="tpu_custom_call" | custom-call | flops 1 | bytes 1 | tf_op jit(solution)/shard_map/pallas_call | solution.py:433
  102.5 8.5 %shard_map.175 = (bf16[512,1024]{1,0:T(8,128)(2,1)}, f32[8,128]{1,0:T(8,128)S(1)}) custom-call(s32[5]{0:T(128)S(1)} %stack.23.refs_0_, f32[16,512]{1,0:T(8,128)} %bitcast.27, bf16[512,1024]{1,0:T(8,128)(2,1)} %refs_2_.3, bf16[512,256]{1,0:T(8,128)(2,1)} %refs_3_.3, bf16[512,256]{1,0:T(8,128)(2,1)} %refs_4_.3, f32[1,1024]{1,0:T(1,128)} %bitcast.29, ...), custom_call_target="tpu_custom_call" | custom-call | flops 1 | bytes 1 | tf_op jit(solution)/shard_map/pallas_call | solution.py:433
  111.0 3.2 %collective-permute-done.22.refs_4_ = bf16[1,128,1024]{2,1,0:T(8,128)(2,1)S(1)} collective-permute-done((bf16[1,128,1024]{2,1,0:T(8,128)(2,1)S(1)}, bf16[1,128,1024]{2,1,0:T(8,128)(2,1)S(1)}, u32[]{:S(2)}, u32[]{:S(2)}) %collective-permute-start.22) | collective-permute-done | bytes 262176 | tf_op jit(solution)/shard_map/ppermute | solution.py:468
  118.1 3.6 %collective-permute-done.27.refs_1_ = f32[8,128]{1,0:T(8,128)S(1)} collective-permute-done((f32[8,128]{1,0:T(8,128)S(1)}, f32[8,128]{1,0:T(8,128)S(1)}, u32[]{:S(2)}, u32[]{:S(2)}) %collective-permute-start.27) | collective-permute-done | bytes 4128 | tf_op jit(solution)/shard_map/ppermute | solution.py:614
  121.7 4.5 %collective-permute-done.28.refs_1_ = f32[8,128]{1,0:T(8,128)S(1)} collective-permute-done((f32[8,128]{1,0:T(8,128)S(1)}, f32[8,128]{1,0:T(8,128)S(1)}, u32[]{:S(2)}, u32[]{:S(2)}) %collective-permute-start.28) | collective-permute-done | bytes 4128 | tf_op jit(solution)/shard_map/ppermute | solution.py:614
  128.2 11.6 %collective-permute-done.31.refs_3_ = f32[8,128]{1,0:T(8,128)S(1)} collective-permute-done((f32[8,128]{1,0:T(8,128)S(1)}, f32[8,128]{1,0:T(8,128)S(1)}, u32[]{:S(2)}, u32[]{:S(2)}) %collective-permute-start.31) | collective-permute-done | bytes 4128 | tf_op jit(solution)/shard_map/ppermute | solution.py:468
  140.4 3.0 %collective-permute-done.29.refs_1_ = f32[8,128]{1,0:T(8,128)S(1)} collective-permute-done((f32[8,128]{1,0:T(8,128)S(1)}, f32[8,128]{1,0:T(8,128)S(1)}, u32[]{:S(2)}, u32[]{:S(2)}) %collective-permute-start.29) | collective-permute-done | bytes 4128 | tf_op jit(solution)/shard_map/ppermute | solution.py:468
  144.2 3.7 %collective-permute-done.33.refs_10_ = f32[8,128]{1,0:T(8,128)S(1)} collective-permute-done((f32[8,128]{1,0:T(8,128)S(1)}, f32[8,128]{1,0:T(8,128)S(1)}, u32[]{:S(2)}, u32[]{:S(2)}) %collective-permute-start.33) | collective-permute-done | bytes 4128 | tf_op jit(solution)/shard_map/ppermute | solution.py:468
  147.9 5.2 %shard_map.181 = (bf16[2048,1024]{1,0:T(8,128)(2,1)}, f32[256,1024]{1,0:T(8,128)}, f32[256,1024]{1,0:T(8,128)}, f32[8,128]{1,0:T(8,128)}) custom-call(s32[5]{0:T(128)S(1)} %stack.23.refs_0_, f32[256,1024]{1,0:T(8,128)S(1)} %get-tuple-element.81.refs_0_.refs_1_, f32[256,1024]{1,0:T(8,128)S(1)} %get-tuple-element.82.refs_1_.refs_2_, ...), custom_call_target="tpu_custom_call" | custom-call | flops 1 | bytes 1 | tf_op jit(solution)/shard_map/pallas_call | solution.py:433
  (72 shorter events, 34.5 us)
Async XLA Ops:
  8.3 17.2 %collective-permute-start = (bf16[512,512]{1,0:T(8,128)(2,1)S(1)}, bf16[512,512]{1,0:T(8,128)(2,1)S(1)}, u32[]{:S(2)}, u32[]{:S(2)}) collective-permute-start(bf16[512,512]{1,0:T(8,128)(2,1)S(1)} %get-tuple-element.80.refs_0_), channel_id=1, source_target_pairs={{0,1},{3,2},{4,5},{7,6},{8,9},{11,10},{12,13},{15,14},{16,17},{19,... | collective-permute-start | bytes 1572872 | tf_op jit(solution)/shard_map/ppermute | solution.py:511
  13.4 15.9 %collective-permute-start.5 = (bf16[1,256,1024]{2,1,0:T(8,128)(2,1)S(1)}, bf16[1,256,1024]{2,1,0:T(8,128)(2,1)S(1)}, u32[]{:S(2)}, u32[]{:S(2)}) collective-permute-start(bf16[1,256,1024]{2,1,0:T(8,128)(2,1)S(1)} %bitcast.21), channel_id=1, source_target_pairs={{0,24},{4,28},{8,16},{12,20},{16,8},{20,12},{24,0},{28,4},{1,25},{... | collective-permute-start | bytes 1572872 | tf_op jit(solution)/shard_map/ppermute | solution.py:468
  16.0 23.1 %collective-permute-start.4 = (bf16[1,256,1024]{2,1,0:T(8,128)(2,1)S(1)}, bf16[1,256,1024]{2,1,0:T(8,128)(2,1)S(1)}, u32[]{:S(2)}, u32[]{:S(2)}) collective-permute-start(bf16[1,256,1024]{2,1,0:T(8,128)(2,1)S(1)} %bitcast.22), channel_id=1, source_target_pairs={{0,16},{4,20},{8,24},{12,28},{16,0},{20,4},{24,8},{28,12},{1,17},{... | collective-permute-start | bytes 1572872 | tf_op jit(solution)/shard_map/ppermute | solution.py:468
  16.5 22.7 %collective-permute-start.3 = (bf16[1,256,1024]{2,1,0:T(8,128)(2,1)S(1)}, bf16[1,256,1024]{2,1,0:T(8,128)(2,1)S(1)}, u32[]{:S(2)}, u32[]{:S(2)}) collective-permute-start(bf16[1,256,1024]{2,1,0:T(8,128)(2,1)S(1)} %bitcast.23), channel_id=1, source_target_pairs={{0,8},{4,12},{8,0},{12,4},{16,24},{20,28},{24,16},{28,20},{1,9},{5... | collective-permute-start | bytes 1572872 | tf_op jit(solution)/shard_map/ppermute | solution.py:468
  19.5 19.8 %collective-permute-start.2 = (bf16[512,512]{1,0:T(8,128)(2,1)S(1)}, bf16[512,512]{1,0:T(8,128)(2,1)S(1)}, u32[]{:S(2)}, u32[]{:S(2)}) collective-permute-start(bf16[512,512]{1,0:T(8,128)(2,1)S(1)} %get-tuple-element.87.refs_0_), channel_id=1, source_target_pairs={{0,1},{3,2},{4,5},{7,6},{8,9},{11,10},{12,13},{15,14},{16,17},{19,... | collective-permute-start | bytes 1572872 | tf_op jit(solution)/shard_map/ppermute | solution.py:511
  25.7 19.2 %collective-permute-start.1 = (bf16[512,512]{1,0:T(8,128)(2,1)S(1)}, bf16[512,512]{1,0:T(8,128)(2,1)S(1)}, u32[]{:S(2)}, u32[]{:S(2)}) collective-permute-start(bf16[512,512]{1,0:T(8,128)(2,1)S(1)} %get-tuple-element.86.refs_0_), channel_id=1, source_target_pairs={{1,2},{2,1},{5,6},{6,5},{9,10},{10,9},{13,14},{14,13},{17,18},{18,... | collective-permute-start | bytes 1572872 | tf_op jit(solution)/shard_map/ppermute | solution.py:522
  29.3 18.8 %collective-permute-start.8 = (bf16[512,512]{1,0:T(8,128)(2,1)S(1)}, bf16[512,512]{1,0:T(8,128)(2,1)S(1)}, u32[]{:S(2)}, u32[]{:S(2)}) collective-permute-start(bf16[512,512]{1,0:T(8,128)(2,1)S(1)} %get-tuple-element.94.refs_0_), channel_id=1, source_target_pairs={{0,1},{3,2},{4,5},{7,6},{8,9},{11,10},{12,13},{15,14},{16,17},{19,... | collective-permute-start | bytes 1572872 | tf_op jit(solution)/shard_map/ppermute | solution.py:511
  40.1 18.0 %collective-permute-start.11 = (bf16[512,512]{1,0:T(8,128)(2,1)S(1)}, bf16[512,512]{1,0:T(8,128)(2,1)S(1)}, u32[]{:S(2)}, u32[]{:S(2)}) collective-permute-start(bf16[512,512]{1,0:T(8,128)(2,1)S(1)} %get-tuple-element.99.refs_0_), channel_id=1, source_target_pairs={{0,1},{3,2},{4,5},{7,6},{8,9},{11,10},{12,13},{15,14},{16,17},{19,... | collective-permute-start | bytes 1572872 | tf_op jit(solution)/shard_map/ppermute | solution.py:511
  45.0 16.8 %collective-permute-start.6 = (bf16[512,512]{1,0:T(8,128)(2,1)S(1)}, bf16[512,512]{1,0:T(8,128)(2,1)S(1)}, u32[]{:S(2)}, u32[]{:S(2)}) collective-permute-start(bf16[512,512]{1,0:T(8,128)(2,1)S(1)} %get-tuple-element.92.refs_1_.refs_12_), channel_id=1, source_target_pairs={{1,0},{2,3},{5,4},{6,7},{9,8},{10,11},{13,12},{14,15},{17,16},{18,... | collective-permute-start | bytes 1572872 | tf_op jit(solution)/shard_map/ppermute | solution.py:526
  48.2 14.5 %collective-permute-start.10 = (bf16[512,512]{1,0:T(8,128)(2,1)S(1)}, bf16[512,512]{1,0:T(8,128)(2,1)S(1)}, u32[]{:S(2)}, u32[]{:S(2)}) collective-permute-start(bf16[512,512]{1,0:T(8,128)(2,1)S(1)} %get-tuple-element.98.refs_0_), channel_id=1, source_target_pairs={{1,2},{2,1},{5,6},{6,5},{9,10},{10,9},{13,14},{14,13},{17,18},{18,... | collective-permute-start | bytes 1572872 | tf_op jit(solution)/shard_map/ppermute | solution.py:522
  49.0 24.0 %collective-permute-start.9 = (bf16[512,512]{1,0:T(8,128)(2,1)S(1)}, bf16[512,512]{1,0:T(8,128)(2,1)S(1)}, u32[]{:S(2)}, u32[]{:S(2)}) collective-permute-start(bf16[512,512]{1,0:T(8,128)(2,1)S(1)} %get-tuple-element.97.refs_3_.refs_14_), channel_id=1, source_target_pairs={{1,0},{2,3},{5,4},{6,7},{9,8},{10,11},{13,12},{14,15},{17,16},{18,... | collective-permute-start | bytes 1572872 | tf_op jit(solution)/shard_map/ppermute | solution.py:526
  61.9 13.2 %collective-permute-start.13 = (bf16[512,512]{1,0:T(8,128)(2,1)S(1)}, bf16[512,512]{1,0:T(8,128)(2,1)S(1)}, u32[]{:S(2)}, u32[]{:S(2)}) collective-permute-start(bf16[512,512]{1,0:T(8,128)(2,1)S(1)} %get-tuple-element.103.refs_0_), channel_id=1, source_target_pairs={{1,2},{2,1},{5,6},{6,5},{9,10},{10,9},{13,14},{14,13},{17,18},{18,... | collective-permute-start | bytes 1572872 | tf_op jit(solution)/shard_map/ppermute | solution.py:522
  62.6 30.8 %collective-permute-start.16 = (bf16[4,256,1024]{2,1,0:T(8,128)(2,1)S(1)}, bf16[4,256,1024]{2,1,0:T(8,128)(2,1)S(1)}, u32[]{:S(2)}, u32[]{:S(2)}) collective-permute-start(bf16[4,256,1024]{2,1,0:T(8,128)(2,1)S(1)} %get-tuple-element.112.refs_3_), channel_id=1, source_target_pairs={{0,4},{4,0},{8,12},{12,8},{16,20},{20,16},{24,28},{28,24},{1,5},{5... | collective-permute-start | bytes 6291464 | tf_op jit(solution)/shard_map/ppermute | solution.py:468
  62.8 21.3 %collective-permute-start.12 = (bf16[512,512]{1,0:T(8,128)(2,1)S(1)}, bf16[512,512]{1,0:T(8,128)(2,1)S(1)}, u32[]{:S(2)}, u32[]{:S(2)}) collective-permute-start(bf16[512,512]{1,0:T(8,128)(2,1)S(1)} %get-tuple-element.102.refs_1_.refs_16_), channel_id=1, source_target_pairs={{1,0},{2,3},{5,4},{6,7},{9,8},{10,11},{13,12},{14,15},{17,16},{18,... | collective-permute-start | bytes 1572872 | tf_op jit(solution)/shard_map/ppermute | solution.py:526
  75.2 18.2 %collective-permute-start.14 = (bf16[512,512]{1,0:T(8,128)(2,1)S(1)}, bf16[512,512]{1,0:T(8,128)(2,1)S(1)}, u32[]{:S(2)}, u32[]{:S(2)}) collective-permute-start(bf16[512,512]{1,0:T(8,128)(2,1)S(1)} %get-tuple-element.106.refs_3_.refs_18_), channel_id=1, source_target_pairs={{1,0},{2,3},{5,4},{6,7},{9,8},{10,11},{13,12},{14,15},{17,16},{18,... | collective-permute-start | bytes 1572872 | tf_op jit(solution)/shard_map/ppermute | solution.py:526
  85.5 10.0 %collective-permute-start.18 = (bf16[1,128,1024]{2,1,0:T(8,128)(2,1)S(1)}, bf16[1,128,1024]{2,1,0:T(8,128)(2,1)S(1)}, u32[]{:S(2)}, u32[]{:S(2)}) collective-permute-start(bf16[1,128,1024]{2,1,0:T(8,128)(2,1)S(1)} %get-tuple-element.116), channel_id=1, source_target_pairs={{0,8},{4,12},{8,0},{12,4},{16,24},{20,28},{24,16},{28,20},{1,9},{5... | collective-permute-start | bytes 786440 | tf_op jit(solution)/shard_map/ppermute | solution.py:468
  98.9 12.0 %collective-permute-start.21 = (bf16[1,128,1024]{2,1,0:T(8,128)(2,1)S(1)}, bf16[1,128,1024]{2,1,0:T(8,128)(2,1)S(1)}, u32[]{:S(2)}, u32[]{:S(2)}) collective-permute-start(bf16[1,128,1024]{2,1,0:T(8,128)(2,1)S(1)} %get-tuple-element.125), channel_id=1, source_target_pairs={{0,8},{4,12},{8,0},{12,4},{16,24},{20,28},{24,16},{28,20},{1,9},{5... | collective-permute-start | bytes 786440 | tf_op jit(solution)/shard_map/ppermute | solution.py:468
  100.5 13.7 %collective-permute-start.22 = (bf16[1,128,1024]{2,1,0:T(8,128)(2,1)S(1)}, bf16[1,128,1024]{2,1,0:T(8,128)(2,1)S(1)}, u32[]{:S(2)}, u32[]{:S(2)}) collective-permute-start(bf16[1,128,1024]{2,1,0:T(8,128)(2,1)S(1)} %get-tuple-element.126), channel_id=1, source_target_pairs={{0,16},{4,20},{8,24},{12,28},{16,0},{20,4},{24,8},{28,12},{1,17},{... | collective-permute-start | bytes 786440 | tf_op jit(solution)/shard_map/ppermute | solution.py:468
  100.6 13.6 %collective-permute-start.23 = (bf16[1,128,1024]{2,1,0:T(8,128)(2,1)S(1)}, bf16[1,128,1024]{2,1,0:T(8,128)(2,1)S(1)}, u32[]{:S(2)}, u32[]{:S(2)}) collective-permute-start(bf16[1,128,1024]{2,1,0:T(8,128)(2,1)S(1)} %get-tuple-element.127), channel_id=1, source_target_pairs={{0,24},{4,28},{8,16},{12,20},{16,8},{20,12},{24,0},{28,4},{1,25},{... | collective-permute-start | bytes 786440 | tf_op jit(solution)/shard_map/ppermute | solution.py:468
  114.6 28.9 %collective-permute-start.26 = (bf16[1,256,1024]{2,1,0:T(8,128)(2,1)S(1)}, bf16[1,256,1024]{2,1,0:T(8,128)(2,1)S(1)}, u32[]{:S(2)}, u32[]{:S(2)}) collective-permute-start(bf16[1,256,1024]{2,1,0:T(8,128)(2,1)S(1)} %bitcast.17), channel_id=1, source_target_pairs={{0,24},{4,28},{8,16},{12,20},{16,8},{20,12},{24,0},{28,4},{1,25},{... | collective-permute-start | bytes 1572872 | tf_op jit(solution)/shard_map/ppermute | solution.py:468
  116.1 27.4 %collective-permute-start.25 = (bf16[1,256,1024]{2,1,0:T(8,128)(2,1)S(1)}, bf16[1,256,1024]{2,1,0:T(8,128)(2,1)S(1)}, u32[]{:S(2)}, u32[]{:S(2)}) collective-permute-start(bf16[1,256,1024]{2,1,0:T(8,128)(2,1)S(1)} %bitcast.18), channel_id=1, source_target_pairs={{0,16},{4,20},{8,24},{12,28},{16,0},{20,4},{24,8},{28,12},{1,17},{... | collective-permute-start | bytes 1572872 | tf_op jit(solution)/shard_map/ppermute | solution.py:468
  116.6 26.9 %collective-permute-start.24 = (bf16[1,256,1024]{2,1,0:T(8,128)(2,1)S(1)}, bf16[1,256,1024]{2,1,0:T(8,128)(2,1)S(1)}, u32[]{:S(2)}, u32[]{:S(2)}) collective-permute-start(bf16[1,256,1024]{2,1,0:T(8,128)(2,1)S(1)} %bitcast.19), channel_id=1, source_target_pairs={{0,8},{4,12},{8,0},{12,4},{16,24},{20,28},{24,16},{28,20},{1,9},{5... | collective-permute-start | bytes 1572872 | tf_op jit(solution)/shard_map/ppermute | solution.py:468
  126.2 13.6 %collective-permute-start.31 = (f32[8,128]{1,0:T(8,128)S(1)}, f32[8,128]{1,0:T(8,128)S(1)}, u32[]{:S(2)}, u32[]{:S(2)}) collective-permute-start(f32[8,128]{1,0:T(8,128)S(1)} %get-tuple-element.135.refs_0_), channel_id=1, source_target_pairs={{0,24},{4,28},{8,16},{12,20},{16,8},{20,12},{24,0},{28,4},{1,25},{... | collective-permute-start | bytes 12296 | tf_op jit(solution)/shard_map/ppermute | solution.py:468
  127.7 12.7 %collective-permute-start.30 = (f32[8,128]{1,0:T(8,128)S(1)}, f32[8,128]{1,0:T(8,128)S(1)}, u32[]{:S(2)}, u32[]{:S(2)}) collective-permute-start(f32[8,128]{1,0:T(8,128)S(1)} %get-tuple-element.135.refs_0_), channel_id=1, source_target_pairs={{0,16},{4,20},{8,24},{12,28},{16,0},{20,4},{24,8},{28,12},{1,17},{... | collective-permute-start | bytes 12296 | tf_op jit(solution)/shard_map/ppermute | solution.py:468
  (10 other events, 61.3 us)

commit v14 on v12

--- a/solution.py
+++ b/solution.py
@@ -630,9 +630,7 @@
         finish(0)
     held[end] = new_rows(end)
     narrow(end, by_two)
-    half = groups // 2
-    grad_input = backward(0, half, None) if half else None
-    grad_input = backward(half, groups - half, grad_input)
+    grad_input = backward(0, groups, None)
     widen(end - 1, by_two, landed[end - 1])
     finish(end - 1)
     own_rows(end, large_cost, [gathered[0][1]] if early else [])
@@ -642,7 +640,7 @@
         pairs = [(t, t ^ (1 << bit)) for t in range(heads_over)]
         waits = [gathered[b][1] for b in range(end)]
         (total,) = step(add_squares_kernel, [total, lax.ppermute(total, "tensor", pairs)], [tile], waits=waits)
-    for bit, bits in by_two:
+    for bit, bits in by_one:
         landed = [exchange(total, mask << bit) for mask in range(1, 1 << bits)]
         (total,) = step(add_squares_kernel, [total, *landed], [tile])
     widen(end, by_two, last_landed)

time: 149 us -> 148 us (level)
  waiting for transfers between devices: 55.1 us -> 57.6 us
  Pallas kernels: 36 us -> 34.2 us
  starting transfers between devices: 56.5 us -> 54.8 us
    ppermute x30 -> x29, waiting for transfers between devices: 24.4 us -> 27 us  [exchange(): lax.ppermute(value, 'replica', [(r, r ^ mask) for r in range(replicas)])]
    pallas_call x34, Pallas kernels: 36 us -> 34.2 us  [run(): pl.pallas_call(in_turn(kernel, len(inputs), len(waits), len(outs)), in_sp...]
    ppermute x30 -> x29, starting transfers between devices: 27.2 us -> 25.6 us  [exchange(): lax.ppermute(value, 'replica', [(r, r ^ mask) for r in range(replicas)])]
  transfers between devices with their start and end apart: 44 -> 43, of which waited for: 19 -> 19; matrix products, arithmetic and copies ran while one was open for 0% -> 0% of each run, Pallas kernels for 14% -> 13%
where the time goes in v14:
time: 148 us
  waiting for transfers between devices  57.6 us (39%)
  starting transfers between devices  54.8 us (37%)
  Pallas kernels  34.2 us (23%)
    pallas_call x34, Pallas kernels, run(): pl.pallas_call(in_turn(kernel, len(inputs), len(waits), len(outs)), in_sp...  34.2 us
    ppermute x29, waiting for transfers between devices, exchange(): lax.ppermute(value, 'replica', [(r, r ^ mask) for r in range(replicas)])  27 us
    ppermute x29, starting transfers between devices, exchange(): lax.ppermute(value, 'replica', [(r, r ^ mask) for r in range(replicas)])  25.6 us
    ppermute x4, waiting for transfers between devices, sum_all(): back = lax.ppermute(out, 'tensor', [(b, a) for a, b in pairs])  20.3 us
    ppermute x4, starting transfers between devices, shards(): lax.ppermute(p, 'tensor', in_hops[0])  16.2 us
    ppermute x4, waiting for transfers between devices, shards(): lax.ppermute(p, 'tensor', in_hops[0])  7.16 us
    ppermute x4, starting transfers between devices, sum_all(): back = lax.ppermute(out, 'tensor', [(b, a) for a, b in pairs])  5.34 us
    ppermute x2, starting transfers between devices, shards(): lax.ppermute(total, 'tensor', pairs)  4.99 us
  transfers between devices with their start and end apart: 43, of which 19 were waited for; matrix products, arithmetic and copies ran while one was open for 0% of the time, Pallas kernels for 13%

profile of v14, /device:TPU:0, one launch (start us, length us, event | category | flops | bytes accessed | tf_op | source)
XLA Modules:
  0.0 147.9 jit_solution(5236181948571050143)
XLA Ops:
  0.7 6.2 %shard_map.156 = (bf16[8,256,1024]{2,1,0:T(8,128)(2,1)S(1)}, bf16[128,2048]{1,0:T(8,128)(2,1)S(1)}, f32[256,1024]{1,0:T(8,128)S(1)}, f32[256,1024]{1,0:T(8,128)S...) custom-call(f32[16,512]{1,0:T(8,128)} %bitcast.48, bf16[512,1024]{1,0:T(8,128)(2,1)} %refs_1_.1, ...), custom_call_target="tpu_custom_call" | custom-call | flops 1 | bytes 1 | tf_op jit(solution)/shard_map/pallas_call | solution.py:438
  8.3 5.0 %collective-permute-start = (bf16[512,512]{1,0:T(8,128)(2,1)S(1)}, bf16[512,512]{1,0:T(8,128)(2,1)S(1)}, u32[]{:S(2)}, u32[]{:S(2)}) collective-permute-start(bf16[512,512]{1,0:T(8,128)(2,1)S(1)} %get-tuple-element.100.refs_0_), channel_id=1, source_target_pairs={{0,1},{3,2},{4,5},{7,6},{8,9},{11,10},{12,13},{15,14},{16,17},{19,... | collective-permute-start | bytes 1572872 | tf_op jit(solution)/shard_map/ppermute | solution.py:518
  17.0 2.5 %shard_map.159 = (bf16[512,512]{1,0:T(8,128)(2,1)S(1)}, bf16[512,512]{1,0:T(8,128)(2,1)S(1)}, bf16[512,512]{1,0:T(8,128)(2,1)S(1)}, f32[8,128]{1,0:T(8,128)S(1)}) custom-call(s32[4]{0:T(128)S(1)} %pad_add_fusion.refs_0_, bf16[8,256,1024]{2,1,0:T(8,128)(2,1)S(1)} %get-tuple-element.97.refs_1_.refs_4_.refs_6_.refs_11_, ...), custom_call_target="tpu_custom_call" | custom-call | flops 1 | bytes 1 | tf_op jit(solution)/shard_map/pallas_call | solution.py:438
  20.8 4.8 %collective-permute-done.refs_1_ = bf16[512,512]{1,0:T(8,128)(2,1)S(1)} collective-permute-done((bf16[512,512]{1,0:T(8,128)(2,1)S(1)}, bf16[512,512]{1,0:T(8,128)(2,1)S(1)}, u32[]{:S(2)}, u32[]{:S(2)}) %collective-permute-start) | collective-permute-done | bytes 524320 | tf_op jit(solution)/shard_map/ppermute | solution.py:518
  26.4 1.9 %collective-permute-done.3.refs_1_ = bf16[1,256,1024]{2,1,0:T(8,128)(2,1)S(1)} collective-permute-done((bf16[1,256,1024]{2,1,0:T(8,128)(2,1)S(1)}, bf16[1,256,1024]{2,1,0:T(8,128)(2,1)S(1)}, u32[]{:S(2)}, u32[]{:S(2)}) %collective-permute-start.3) | collective-permute-done | bytes 524320 | tf_op jit(solution)/shard_map/ppermute | solution.py:473
  28.3 5.3 %collective-permute-start.8 = (bf16[512,512]{1,0:T(8,128)(2,1)S(1)}, bf16[512,512]{1,0:T(8,128)(2,1)S(1)}, u32[]{:S(2)}, u32[]{:S(2)}) collective-permute-start(bf16[512,512]{1,0:T(8,128)(2,1)S(1)} %get-tuple-element.114.refs_0_), channel_id=1, source_target_pairs={{0,1},{3,2},{4,5},{7,6},{8,9},{11,10},{12,13},{15,14},{16,17},{19,... | collective-permute-start | bytes 1572872 | tf_op jit(solution)/shard_map/ppermute | solution.py:518
  33.6 5.7 %collective-permute-done.4.refs_2_ = bf16[1,256,1024]{2,1,0:T(8,128)(2,1)S(1)} collective-permute-done((bf16[1,256,1024]{2,1,0:T(8,128)(2,1)S(1)}, bf16[1,256,1024]{2,1,0:T(8,128)(2,1)S(1)}, u32[]{:S(2)}, u32[]{:S(2)}) %collective-permute-start.4) | collective-permute-done | bytes 524320 | tf_op jit(solution)/shard_map/ppermute | solution.py:473
  41.8 4.6 %collective-permute-start.11 = (bf16[512,512]{1,0:T(8,128)(2,1)S(1)}, bf16[512,512]{1,0:T(8,128)(2,1)S(1)}, u32[]{:S(2)}, u32[]{:S(2)}) collective-permute-start(bf16[512,512]{1,0:T(8,128)(2,1)S(1)} %get-tuple-element.119.refs_0_), channel_id=1, source_target_pairs={{0,1},{3,2},{4,5},{7,6},{8,9},{11,10},{12,13},{15,14},{16,17},{19,... | collective-permute-start | bytes 1572872 | tf_op jit(solution)/shard_map/ppermute | solution.py:518
  46.4 1.7 %collective-permute-done.8.refs_1_ = bf16[512,512]{1,0:T(8,128)(2,1)S(1)} collective-permute-done((bf16[512,512]{1,0:T(8,128)(2,1)S(1)}, bf16[512,512]{1,0:T(8,128)(2,1)S(1)}, u32[]{:S(2)}, u32[]{:S(2)}) %collective-permute-start.8) | collective-permute-done | bytes 524320 | tf_op jit(solution)/shard_map/ppermute | solution.py:518
  49.0 5.7 %collective-permute-done.6.refs_2_.refs_13_ = bf16[512,512]{1,0:T(8,128)(2,1)S(1)} collective-permute-done((bf16[512,512]{1,0:T(8,128)(2,1)S(1)}, bf16[512,512]{1,0:T(8,128)(2,1)S(1)}, u32[]{:S(2)}, u32[]{:S(2)}) %collective-permute-start.6) | collective-permute-done | bytes 524320 | tf_op jit(solution)/shard_map/ppermute | solution.py:533
  62.6 10.1 %collective-permute-done.9.refs_2_.refs_15_ = bf16[512,512]{1,0:T(8,128)(2,1)S(1)} collective-permute-done((bf16[512,512]{1,0:T(8,128)(2,1)S(1)}, bf16[512,512]{1,0:T(8,128)(2,1)S(1)}, u32[]{:S(2)}, u32[]{:S(2)}) %collective-permute-start.9) | collective-permute-done | bytes 524320 | tf_op jit(solution)/shard_map/ppermute | solution.py:533
  79.4 4.6 %collective-permute-done.12.refs_1_.refs_2_.refs_17_ = bf16[512,512]{1,0:T(8,128)(2,1)S(1)} collective-permute-done((bf16[512,512]{1,0:T(8,128)(2,1)S(1)}, bf16[512,512]{1,0:T(8,128)(2,1)S(1)}, u32[]{:S(2)}, u32[]{:S(2)}) %collective-permute-start.12) | collective-permute-done | bytes 524320 | tf_op jit(solution)/shard_map/ppermute | solution.py:533
  90.8 2.4 %collective-permute-done.24.refs_3_ = bf16[1,64,1024]{2,1,0:T(8,128)(2,1)S(1)} collective-permute-done((bf16[1,64,1024]{2,1,0:T(8,128)(2,1)S(1)}, bf16[1,64,1024]{2,1,0:T(8,128)(2,1)S(1)}, u32[]{:S(2)}, u32[]{:S(2)}) %collective-permute-start.24) | collective-permute-done | bytes 131104 | tf_op jit(solution)/shard_map/ppermute | solution.py:473
  93.3 3.9 %collective-permute-done.21.refs_2_ = bf16[1,64,1024]{2,1,0:T(8,128)(2,1)S(1)} collective-permute-done((bf16[1,64,1024]{2,1,0:T(8,128)(2,1)S(1)}, bf16[1,64,1024]{2,1,0:T(8,128)(2,1)S(1)}, u32[]{:S(2)}, u32[]{:S(2)}) %collective-permute-start.21) | collective-permute-done | bytes 131104 | tf_op jit(solution)/shard_map/ppermute | solution.py:473
  97.3 2.0 %shard_map.179 = (bf16[4,128,1024]{2,1,0:T(8,128)(2,1)S(1)}, bf16[4,128,1024]{2,1,0:T(8,128)(2,1)S(1)}, f32[8,128]{1,0:T(8,128)S(1)}) custom-call(s32[4]{0:T(128)S(1)} %pad_add_fusion.refs_0_, bf16[512,512]{1,0:T(8,128)(2,1)S(1)} %get-tuple-element.123.refs_1_.refs_16_, bf16[512,512]{1,0:T(8,128)(2,1)S(1)} %collective-permute-done.12.refs_1_.refs_2_.refs_17_, ...), custom_call_target="tpu_custom_call" | custom-call | flops 1 | bytes 1 | tf_op jit(solution)/shard_map/pallas_call | solution.py:438
  105.4 1.7 %collective-permute-start.33 = (bf16[1,128,1024]{2,1,0:T(8,128)(2,1)S(1)}, bf16[1,128,1024]{2,1,0:T(8,128)(2,1)S(1)}, u32[]{:S(2)}, u32[]{:S(2)}) collective-permute-start(bf16[1,128,1024]{2,1,0:T(8,128)(2,1)S(1)} %get-tuple-element.165), channel_id=1, source_target_pairs={{0,24},{4,28},{8,16},{12,20},{16,8},{20,12},{24,0},{28,4},{1,25},{... | collective-permute-start | bytes 786440 | tf_op jit(solution)/shard_map/ppermute | solution.py:473
  108.3 8.5 %shard_map.181 = (bf16[512,1024]{1,0:T(8,128)(2,1)}, f32[8,128]{1,0:T(8,128)S(1)}) custom-call(s32[4]{0:T(128)S(1)} %pad_add_fusion.refs_0_, f32[16,512]{1,0:T(8,128)} %bitcast.49, bf16[512,1024]{1,0:T(8,128)(2,1)} %refs_2_.3, bf16[512,256]{1,0:T(8,128)(2,1)} %refs_3_.3, bf16[512,256]{1,0:T(8,128)(2,1)} %refs_4_.3, f32[1,1024]{1,0:T(1,128)} %bitcast.51, ...), custom_call_target="tpu_custom_call" | custom-call | flops 1 | bytes 1 | tf_op jit(solution)/shard_map/pallas_call | solution.py:438
  116.8 3.2 %collective-permute-done.29.refs_3_ = bf16[1,64,1024]{2,1,0:T(8,128)(2,1)S(1)} collective-permute-done((bf16[1,64,1024]{2,1,0:T(8,128)(2,1)S(1)}, bf16[1,64,1024]{2,1,0:T(8,128)(2,1)S(1)}, u32[]{:S(2)}, u32[]{:S(2)}) %collective-permute-start.29) | collective-permute-done | bytes 131104 | tf_op jit(solution)/shard_map/ppermute | solution.py:473
  124.8 2.1 %collective-permute-start.37 = (f32[8,128]{1,0:T(8,128)S(1)}, f32[8,128]{1,0:T(8,128)S(1)}, u32[]{:S(2)}, u32[]{:S(2)}) collective-permute-start(f32[8,128]{1,0:T(8,128)S(1)} %get-tuple-element.168.refs_0_), channel_id=1, source_target_pairs={{0,1},{1,0},{2,3},{3,2},{4,5},{5,4},{6,7},{7,6},{8,9},{9,8},{10,11... | collective-permute-start | bytes 12296 | tf_op jit(solution)/shard_map/ppermute | solution.py:642
  128.4 2.9 %collective-permute-start.38 = (f32[8,128]{1,0:T(8,128)S(1)}, f32[8,128]{1,0:T(8,128)S(1)}, u32[]{:S(2)}, u32[]{:S(2)}) collective-permute-start(f32[8,128]{1,0:T(8,128)S(1)} %get-tuple-element.170.refs_0_), channel_id=1, source_target_pairs={{0,2},{1,3},{2,0},{3,1},{4,6},{5,7},{6,4},{7,5},{8,10},{9,11},{10,... | collective-permute-start | bytes 12296 | tf_op jit(solution)/shard_map/ppermute | solution.py:642
  133.7 2.8 %collective-permute-done.39.refs_1_ = f32[8,128]{1,0:T(8,128)S(1)} collective-permute-done((f32[8,128]{1,0:T(8,128)S(1)}, f32[8,128]{1,0:T(8,128)S(1)}, u32[]{:S(2)}, u32[]{:S(2)}) %collective-permute-start.39) | collective-permute-done | bytes 4128 | tf_op jit(solution)/shard_map/ppermute | solution.py:473
  137.4 2.8 %collective-permute-done.40.refs_1_ = f32[8,128]{1,0:T(8,128)S(1)} collective-permute-done((f32[8,128]{1,0:T(8,128)S(1)}, f32[8,128]{1,0:T(8,128)S(1)}, u32[]{:S(2)}, u32[]{:S(2)}) %collective-permute-start.40) | collective-permute-done | bytes 4128 | tf_op jit(solution)/shard_map/ppermute | solution.py:473
  140.9 2.2 %collective-permute-done.42.refs_15_ = f32[8,128]{1,0:T(8,128)S(1)} collective-permute-done((f32[8,128]{1,0:T(8,128)S(1)}, f32[8,128]{1,0:T(8,128)S(1)}, u32[]{:S(2)}, u32[]{:S(2)}) %collective-permute-start.42) | collective-permute-done | bytes 4128 | tf_op jit(solution)/shard_map/ppermute | solution.py:473
  143.0 4.8 %shard_map.189 = (bf16[2048,1024]{1,0:T(8,128)(2,1)}, f32[256,1024]{1,0:T(8,128)}, f32[256,1024]{1,0:T(8,128)}, f32[8,128]{1,0:T(8,128)}) custom-call(s32[4]{0:T(128)S(1)} %pad_add_fusion.refs_0_, f32[256,1024]{1,0:T(8,128)S(1)} %get-tuple-element.101.refs_0_.refs_1_, f32[256,1024]{1,0:T(8,128)S(1)} %get-tuple-element.102.refs_1_.refs_2_, ...), custom_call_target="tpu_custom_call" | custom-call | flops 1 | bytes 1 | tf_op jit(solution)/shard_map/pallas_call | solution.py:438
  (98 shorter events, 49.6 us)
Async XLA Ops:
  8.3 17.3 %collective-permute-start = (bf16[512,512]{1,0:T(8,128)(2,1)S(1)}, bf16[512,512]{1,0:T(8,128)(2,1)S(1)}, u32[]{:S(2)}, u32[]{:S(2)}) collective-permute-start(bf16[512,512]{1,0:T(8,128)(2,1)S(1)} %get-tuple-element.100.refs_0_), channel_id=1, source_target_pairs={{0,1},{3,2},{4,5},{7,6},{8,9},{11,10},{12,13},{15,14},{16,17},{19,... | collective-permute-start | bytes 1572872 | tf_op jit(solution)/shard_map/ppermute | solution.py:518
  13.4 14.9 %collective-permute-start.3 = (bf16[1,256,1024]{2,1,0:T(8,128)(2,1)S(1)}, bf16[1,256,1024]{2,1,0:T(8,128)(2,1)S(1)}, u32[]{:S(2)}, u32[]{:S(2)}) collective-permute-start(bf16[1,256,1024]{2,1,0:T(8,128)(2,1)S(1)} %bitcast.27), channel_id=1, source_target_pairs={{0,8},{4,12},{8,0},{12,4},{16,24},{20,28},{24,16},{28,20},{1,9},{5... | collective-permute-start | bytes 1572872 | tf_op jit(solution)/shard_map/ppermute | solution.py:473
  15.0 24.3 %collective-permute-start.4 = (bf16[1,256,1024]{2,1,0:T(8,128)(2,1)S(1)}, bf16[1,256,1024]{2,1,0:T(8,128)(2,1)S(1)}, u32[]{:S(2)}, u32[]{:S(2)}) collective-permute-start(bf16[1,256,1024]{2,1,0:T(8,128)(2,1)S(1)} %bitcast.28), channel_id=1, source_target_pairs={{0,16},{4,20},{8,24},{12,28},{16,0},{20,4},{24,8},{28,12},{1,17},{... | collective-permute-start | bytes 1572872 | tf_op jit(solution)/shard_map/ppermute | solution.py:473
  16.5 22.8 %collective-permute-start.5 = (bf16[1,256,1024]{2,1,0:T(8,128)(2,1)S(1)}, bf16[1,256,1024]{2,1,0:T(8,128)(2,1)S(1)}, u32[]{:S(2)}, u32[]{:S(2)}) collective-permute-start(bf16[1,256,1024]{2,1,0:T(8,128)(2,1)S(1)} %bitcast.29), channel_id=1, source_target_pairs={{0,24},{4,28},{8,16},{12,20},{16,8},{20,12},{24,0},{28,4},{1,25},{... | collective-permute-start | bytes 1572872 | tf_op jit(solution)/shard_map/ppermute | solution.py:473
  19.5 20.0 %collective-permute-start.2 = (bf16[512,512]{1,0:T(8,128)(2,1)S(1)}, bf16[512,512]{1,0:T(8,128)(2,1)S(1)}, u32[]{:S(2)}, u32[]{:S(2)}) collective-permute-start(bf16[512,512]{1,0:T(8,128)(2,1)S(1)} %get-tuple-element.107.refs_0_), channel_id=1, source_target_pairs={{0,1},{3,2},{4,5},{7,6},{8,9},{11,10},{12,13},{15,14},{16,17},{19,... | collective-permute-start | bytes 1572872 | tf_op jit(solution)/shard_map/ppermute | solution.py:518
  25.7 14.6 %collective-permute-start.1 = (bf16[512,512]{1,0:T(8,128)(2,1)S(1)}, bf16[512,512]{1,0:T(8,128)(2,1)S(1)}, u32[]{:S(2)}, u32[]{:S(2)}) collective-permute-start(bf16[512,512]{1,0:T(8,128)(2,1)S(1)} %get-tuple-element.106.refs_0_), channel_id=1, source_target_pairs={{1,2},{2,1},{5,6},{6,5},{9,10},{10,9},{13,14},{14,13},{17,18},{18,... | collective-permute-start | bytes 1572872 | tf_op jit(solution)/shard_map/ppermute | solution.py:529
  28.3 19.7 %collective-permute-start.8 = (bf16[512,512]{1,0:T(8,128)(2,1)S(1)}, bf16[512,512]{1,0:T(8,128)(2,1)S(1)}, u32[]{:S(2)}, u32[]{:S(2)}) collective-permute-start(bf16[512,512]{1,0:T(8,128)(2,1)S(1)} %get-tuple-element.114.refs_0_), channel_id=1, source_target_pairs={{0,1},{3,2},{4,5},{7,6},{8,9},{11,10},{12,13},{15,14},{16,17},{19,... | collective-permute-start | bytes 1572872 | tf_op jit(solution)/shard_map/ppermute | solution.py:518
  40.5 14.3 %collective-permute-start.6 = (bf16[512,512]{1,0:T(8,128)(2,1)S(1)}, bf16[512,512]{1,0:T(8,128)(2,1)S(1)}, u32[]{:S(2)}, u32[]{:S(2)}) collective-permute-start(bf16[512,512]{1,0:T(8,128)(2,1)S(1)} %get-tuple-element.112.refs_1_.refs_12_), channel_id=1, source_target_pairs={{1,0},{2,3},{5,4},{6,7},{9,8},{10,11},{13,12},{14,15},{17,16},{18,... | collective-permute-start | bytes 1572872 | tf_op jit(solution)/shard_map/ppermute | solution.py:533
  41.8 16.4 %collective-permute-start.11 = (bf16[512,512]{1,0:T(8,128)(2,1)S(1)}, bf16[512,512]{1,0:T(8,128)(2,1)S(1)}, u32[]{:S(2)}, u32[]{:S(2)}) collective-permute-start(bf16[512,512]{1,0:T(8,128)(2,1)S(1)} %get-tuple-element.119.refs_0_), channel_id=1, source_target_pairs={{0,1},{3,2},{4,5},{7,6},{8,9},{11,10},{12,13},{15,14},{16,17},{19,... | collective-permute-start | bytes 1572872 | tf_op jit(solution)/shard_map/ppermute | solution.py:518
  48.2 10.8 %collective-permute-start.10 = (bf16[512,512]{1,0:T(8,128)(2,1)S(1)}, bf16[512,512]{1,0:T(8,128)(2,1)S(1)}, u32[]{:S(2)}, u32[]{:S(2)}) collective-permute-start(bf16[512,512]{1,0:T(8,128)(2,1)S(1)} %get-tuple-element.118.refs_0_), channel_id=1, source_target_pairs={{1,2},{2,1},{5,6},{6,5},{9,10},{10,9},{13,14},{14,13},{17,18},{18,... | collective-permute-start | bytes 1572872 | tf_op jit(solution)/shard_map/ppermute | solution.py:529
  56.1 16.6 %collective-permute-start.9 = (bf16[512,512]{1,0:T(8,128)(2,1)S(1)}, bf16[512,512]{1,0:T(8,128)(2,1)S(1)}, u32[]{:S(2)}, u32[]{:S(2)}) collective-permute-start(bf16[512,512]{1,0:T(8,128)(2,1)S(1)} %get-tuple-element.117.refs_1_.refs_14_), channel_id=1, source_target_pairs={{1,0},{2,3},{5,4},{6,7},{9,8},{10,11},{13,12},{14,15},{17,16},{18,... | collective-permute-start | bytes 1572872 | tf_op jit(solution)/shard_map/ppermute | solution.py:533
  58.3 16.5 %collective-permute-start.13 = (bf16[512,512]{1,0:T(8,128)(2,1)S(1)}, bf16[512,512]{1,0:T(8,128)(2,1)S(1)}, u32[]{:S(2)}, u32[]{:S(2)}) collective-permute-start(bf16[512,512]{1,0:T(8,128)(2,1)S(1)} %get-tuple-element.124.refs_0_), channel_id=1, source_target_pairs={{1,2},{2,1},{5,6},{6,5},{9,10},{10,9},{13,14},{14,13},{17,18},{18,... | collective-permute-start | bytes 1572872 | tf_op jit(solution)/shard_map/ppermute | solution.py:529
  59.8 14.4 %collective-permute-start.15 = (bf16[2,64,1024]{2,1,0:T(8,128)(2,1)S(1)}, bf16[2,64,1024]{2,1,0:T(8,128)(2,1)S(1)}, u32[]{:S(2)}, u32[]{:S(2)}) collective-permute-start(bf16[2,64,1024]{2,1,0:T(8,128)(2,1)S(1)} %get-tuple-element.129), channel_id=1, source_target_pairs={{0,8},{4,12},{8,0},{12,4},{16,24},{20,28},{24,16},{28,20},{1,9},{5... | collective-permute-start | bytes 786440 | tf_op jit(solution)/shard_map/ppermute | solution.py:473
  61.3 22.6 %collective-permute-start.19 = (bf16[4,256,1024]{2,1,0:T(8,128)(2,1)S(1)}, bf16[4,256,1024]{2,1,0:T(8,128)(2,1)S(1)}, u32[]{:S(2)}, u32[]{:S(2)}) collective-permute-start(bf16[4,256,1024]{2,1,0:T(8,128)(2,1)S(1)} %get-tuple-element.140.refs_3_), channel_id=1, source_target_pairs={{0,4},{4,0},{8,12},{12,8},{16,20},{20,16},{24,28},{28,24},{1,5},{5... | collective-permute-start | bytes 6291464 | tf_op jit(solution)/shard_map/ppermute | solution.py:473
  61.4 22.6 %collective-permute-start.12 = (bf16[512,512]{1,0:T(8,128)(2,1)S(1)}, bf16[512,512]{1,0:T(8,128)(2,1)S(1)}, u32[]{:S(2)}, u32[]{:S(2)}) collective-permute-start(bf16[512,512]{1,0:T(8,128)(2,1)S(1)} %get-tuple-element.123.refs_1_.refs_16_), channel_id=1, source_target_pairs={{1,0},{2,3},{5,4},{6,7},{9,8},{10,11},{13,12},{14,15},{17,16},{18,... | collective-permute-start | bytes 1572872 | tf_op jit(solution)/shard_map/ppermute | solution.py:533
  74.9 22.4 %collective-permute-start.16 = (bf16[512,512]{1,0:T(8,128)(2,1)S(1)}, bf16[512,512]{1,0:T(8,128)(2,1)S(1)}, u32[]{:S(2)}, u32[]{:S(2)}) collective-permute-start(bf16[512,512]{1,0:T(8,128)(2,1)S(1)} %get-tuple-element.133.refs_3_.refs_18_), channel_id=1, source_target_pairs={{1,0},{2,3},{5,4},{6,7},{9,8},{10,11},{13,12},{14,15},{17,16},{18,... | collective-permute-start | bytes 1572872 | tf_op jit(solution)/shard_map/ppermute | solution.py:533
  99.4 20.7 %collective-permute-start.26 = (bf16[4,64,1024]{2,1,0:T(8,128)(2,1)S(1)}, bf16[4,64,1024]{2,1,0:T(8,128)(2,1)S(1)}, u32[]{:S(2)}, u32[]{:S(2)}) collective-permute-start(bf16[4,64,1024]{2,1,0:T(8,128)(2,1)S(1)} %get-tuple-element.157.refs_5_), channel_id=1, source_target_pairs={{0,4},{4,0},{8,12},{12,8},{16,20},{20,16},{24,28},{28,24},{1,5},{5... | collective-permute-start | bytes 1572872 | tf_op jit(solution)/shard_map/ppermute | solution.py:473
  103.0 17.2 %collective-permute-start.31 = (bf16[1,128,1024]{2,1,0:T(8,128)(2,1)S(1)}, bf16[1,128,1024]{2,1,0:T(8,128)(2,1)S(1)}, u32[]{:S(2)}, u32[]{:S(2)}) collective-permute-start(bf16[1,128,1024]{2,1,0:T(8,128)(2,1)S(1)} %get-tuple-element.163), channel_id=1, source_target_pairs={{0,8},{4,12},{8,0},{12,4},{16,24},{20,28},{24,16},{28,20},{1,9},{5... | collective-permute-start | bytes 786440 | tf_op jit(solution)/shard_map/ppermute | solution.py:473
  104.4 16.5 %collective-permute-start.32 = (bf16[1,128,1024]{2,1,0:T(8,128)(2,1)S(1)}, bf16[1,128,1024]{2,1,0:T(8,128)(2,1)S(1)}, u32[]{:S(2)}, u32[]{:S(2)}) collective-permute-start(bf16[1,128,1024]{2,1,0:T(8,128)(2,1)S(1)} %get-tuple-element.164), channel_id=1, source_target_pairs={{0,16},{4,20},{8,24},{12,28},{16,0},{20,4},{24,8},{28,12},{1,17},{... | collective-permute-start | bytes 786440 | tf_op jit(solution)/shard_map/ppermute | solution.py:473
  105.4 15.5 %collective-permute-start.33 = (bf16[1,128,1024]{2,1,0:T(8,128)(2,1)S(1)}, bf16[1,128,1024]{2,1,0:T(8,128)(2,1)S(1)}, u32[]{:S(2)}, u32[]{:S(2)}) collective-permute-start(bf16[1,128,1024]{2,1,0:T(8,128)(2,1)S(1)} %get-tuple-element.165), channel_id=1, source_target_pairs={{0,24},{4,28},{8,16},{12,20},{16,8},{20,12},{24,0},{28,4},{1,25},{... | collective-permute-start | bytes 786440 | tf_op jit(solution)/shard_map/ppermute | solution.py:473
  107.1 12.9 %collective-permute-start.29 = (bf16[1,64,1024]{2,1,0:T(8,128)(2,1)S(1)}, bf16[1,64,1024]{2,1,0:T(8,128)(2,1)S(1)}, u32[]{:S(2)}, u32[]{:S(2)}) collective-permute-start(bf16[1,64,1024]{2,1,0:T(8,128)(2,1)S(1)} %bitcast.41), channel_id=1, source_target_pairs={{0,24},{4,28},{8,16},{12,20},{16,8},{20,12},{24,0},{28,4},{1,25},{... | collective-permute-start | bytes 393224 | tf_op jit(solution)/shard_map/ppermute | solution.py:473
  121.3 18.9 %collective-permute-start.34 = (bf16[1,128,1024]{2,1,0:T(8,128)(2,1)S(1)}, bf16[1,128,1024]{2,1,0:T(8,128)(2,1)S(1)}, u32[]{:S(2)}, u32[]{:S(2)}) collective-permute-start(bf16[1,128,1024]{2,1,0:T(8,128)(2,1)S(1)} %bitcast.35), channel_id=1, source_target_pairs={{0,8},{4,12},{8,0},{12,4},{16,24},{20,28},{24,16},{28,20},{1,9},{5... | collective-permute-start | bytes 786440 | tf_op jit(solution)/shard_map/ppermute | solution.py:473
  122.0 18.2 %collective-permute-start.35 = (bf16[1,128,1024]{2,1,0:T(8,128)(2,1)S(1)}, bf16[1,128,1024]{2,1,0:T(8,128)(2,1)S(1)}, u32[]{:S(2)}, u32[]{:S(2)}) collective-permute-start(bf16[1,128,1024]{2,1,0:T(8,128)(2,1)S(1)} %bitcast.36), channel_id=1, source_target_pairs={{0,16},{4,20},{8,24},{12,28},{16,0},{20,4},{24,8},{28,12},{1,17},{... | collective-permute-start | bytes 786440 | tf_op jit(solution)/shard_map/ppermute | solution.py:473
  123.2 17.0 %collective-permute-start.36 = (bf16[1,128,1024]{2,1,0:T(8,128)(2,1)S(1)}, bf16[1,128,1024]{2,1,0:T(8,128)(2,1)S(1)}, u32[]{:S(2)}, u32[]{:S(2)}) collective-permute-start(bf16[1,128,1024]{2,1,0:T(8,128)(2,1)S(1)} %bitcast.37), channel_id=1, source_target_pairs={{0,24},{4,28},{8,16},{12,20},{16,8},{20,12},{24,0},{28,4},{1,25},{... | collective-permute-start | bytes 786440 | tf_op jit(solution)/shard_map/ppermute | solution.py:473
  (19 other events, 101.1 us)

commit v15 on v14

--- a/solution.py
+++ b/solution.py
@@ -318,6 +318,10 @@
         lo += part.shape[0]
 
 
+def pass_kernel(rows_ref, out_ref):
+    out_ref[...] = rows_ref[...]
+
+
 def weight_kernel(sizes, entries, place_ref, global_ref, momentum_ref, *refs):
     count = len(sizes)
     pairs, deltas, squares = refs[: 2 * count + 2], refs[2 * count + 2 : 3 * count + 2], refs[3 * count + 2 : -3]
@@ -634,12 +638,15 @@
     widen(end - 1, by_two, landed[end - 1])
     finish(end - 1)
     own_rows(end, large_cost, [gathered[0][1]] if early else [])
+    (gathered[end],) = step(pass_kernel, [gathered[end]], [shape(*gathered[end].shape)])
     last_landed = landing(end, by_two)
     total = squares[end]
     for bit in range(heads_over.bit_length() - 1):
         pairs = [(t, t ^ (1 << bit)) for t in range(heads_over)]
         waits = [gathered[b][1] for b in range(end)]
-        (total,) = step(add_squares_kernel, [total, lax.ppermute(total, "tensor", pairs)], [tile], waits=waits)
+        cost = small_cost if bit else large_cost
+        landed = lax.ppermute(total, "tensor", pairs)
+        (total,) = step(add_squares_kernel, [total, landed], [tile], waits=waits, cost=cost)
     for bit, bits in by_one:
         landed = [exchange(total, mask << bit) for mask in range(1, 1 << bits)]
         (total,) = step(add_squares_kernel, [total, *landed], [tile])

time: 148 us -> 149 us (level)
  waiting for transfers between devices: 57.6 us -> 59.6 us
    ppermute x2, starting transfers between devices: 4.99 us -> 3.05 us  [shards(): landed = lax.ppermute(total, 'tensor', pairs)]
    ppermute x29, waiting for transfers between devices: 27 us -> 28.5 us  [exchange(): lax.ppermute(value, 'replica', [(r, r ^ mask) for r in range(replicas)])]
    pallas_call x34 -> x35, Pallas kernels: 34.2 us -> 34.2 us  [run(): pl.pallas_call(in_turn(kernel, len(inputs), len(waits), len(outs)), in_sp...]
  transfers between devices with their start and end apart: 43 -> 43, of which waited for: 19 -> 18; matrix products, arithmetic and copies ran while one was open for 0% -> 0% of each run, Pallas kernels for 13% -> 13%
where the time goes in v15:
time: 149 us; the launch traced here: 148 us
  waiting for transfers between devices  59.6 us (40%)
  starting transfers between devices  53.4 us (36%)
  Pallas kernels  34.2 us (23%)
    pallas_call x35, Pallas kernels, run(): pl.pallas_call(in_turn(kernel, len(inputs), len(waits), len(outs)), in_sp...  34.2 us
    ppermute x29, waiting for transfers between devices, exchange(): lax.ppermute(value, 'replica', [(r, r ^ mask) for r in range(replicas)])  28.5 us
    ppermute x29, starting transfers between devices, exchange(): lax.ppermute(value, 'replica', [(r, r ^ mask) for r in range(replicas)])  26.1 us
    ppermute x4, waiting for transfers between devices, sum_all(): back = lax.ppermute(out, 'tensor', [(b, a) for a, b in pairs])  20.3 us
    ppermute x4, starting transfers between devices, shards(): lax.ppermute(p, 'tensor', in_hops[0])  16.2 us
    ppermute x4, waiting for transfers between devices, shards(): lax.ppermute(p, 'tensor', in_hops[0])  7.16 us
    ppermute x4, starting transfers between devices, sum_all(): back = lax.ppermute(out, 'tensor', [(b, a) for a, b in pairs])  5.34 us
    ppermute x2, waiting for transfers between devices, shards(): landed = lax.ppermute(total, 'tensor', pairs)  3.59 us
  transfers between devices with their start and end apart: 43, of which 18 were waited for; matrix products, arithmetic and copies ran while one was open for 0% of the time, Pallas kernels for 13%

profile of v15, /device:TPU:0, one launch (start us, length us, event | category | flops | bytes accessed | tf_op | source)
XLA Modules:
  0.0 148.5 jit_solution(8328731958267443856)
XLA Ops:
  0.7 6.2 %shard_map.156 = (bf16[8,256,1024]{2,1,0:T(8,128)(2,1)S(1)}, bf16[128,2048]{1,0:T(8,128)(2,1)S(1)}, f32[256,1024]{1,0:T(8,128)S(1)}, f32[256,1024]{1,0:T(8,128)S...) custom-call(f32[16,512]{1,0:T(8,128)} %bitcast.45, bf16[512,1024]{1,0:T(8,128)(2,1)} %refs_1_.1, ...), custom_call_target="tpu_custom_call" | custom-call | flops 1 | bytes 1 | tf_op jit(solution)/shard_map/pallas_call | solution.py:442
  8.3 5.0 %collective-permute-start = (bf16[512,512]{1,0:T(8,128)(2,1)S(1)}, bf16[512,512]{1,0:T(8,128)(2,1)S(1)}, u32[]{:S(2)}, u32[]{:S(2)}) collective-permute-start(bf16[512,512]{1,0:T(8,128)(2,1)S(1)} %get-tuple-element.102.refs_0_), channel_id=1, source_target_pairs={{0,1},{3,2},{4,5},{7,6},{8,9},{11,10},{12,13},{15,14},{16,17},{19,... | collective-permute-start | bytes 1572872 | tf_op jit(solution)/shard_map/ppermute | solution.py:522
  17.0 2.5 %shard_map.159 = (bf16[512,512]{1,0:T(8,128)(2,1)S(1)}, bf16[512,512]{1,0:T(8,128)(2,1)S(1)}, bf16[512,512]{1,0:T(8,128)(2,1)S(1)}, f32[8,128]{1,0:T(8,128)S(1)}) custom-call(s32[4]{0:T(128)S(1)} %pad_add_fusion.refs_0_, bf16[8,256,1024]{2,1,0:T(8,128)(2,1)S(1)} %get-tuple-element.99.refs_1_.refs_4_.refs_6_.refs_11_, ...), custom_call_target="tpu_custom_call" | custom-call | flops 1 | bytes 1 | tf_op jit(solution)/shard_map/pallas_call | solution.py:442
  20.8 4.8 %collective-permute-done.refs_1_ = bf16[512,512]{1,0:T(8,128)(2,1)S(1)} collective-permute-done((bf16[512,512]{1,0:T(8,128)(2,1)S(1)}, bf16[512,512]{1,0:T(8,128)(2,1)S(1)}, u32[]{:S(2)}, u32[]{:S(2)}) %collective-permute-start) | collective-permute-done | bytes 524320 | tf_op jit(solution)/shard_map/ppermute | solution.py:522
  26.4 1.9 %collective-permute-done.3.refs_1_ = bf16[1,256,1024]{2,1,0:T(8,128)(2,1)S(1)} collective-permute-done((bf16[1,256,1024]{2,1,0:T(8,128)(2,1)S(1)}, bf16[1,256,1024]{2,1,0:T(8,128)(2,1)S(1)}, u32[]{:S(2)}, u32[]{:S(2)}) %collective-permute-start.3) | collective-permute-done | bytes 524320 | tf_op jit(solution)/shard_map/ppermute | solution.py:477
  28.3 5.3 %collective-permute-start.8 = (bf16[512,512]{1,0:T(8,128)(2,1)S(1)}, bf16[512,512]{1,0:T(8,128)(2,1)S(1)}, u32[]{:S(2)}, u32[]{:S(2)}) collective-permute-start(bf16[512,512]{1,0:T(8,128)(2,1)S(1)} %get-tuple-element.116.refs_0_), channel_id=1, source_target_pairs={{0,1},{3,2},{4,5},{7,6},{8,9},{11,10},{12,13},{15,14},{16,17},{19,... | collective-permute-start | bytes 1572872 | tf_op jit(solution)/shard_map/ppermute | solution.py:522
  33.6 5.7 %collective-permute-done.4.refs_2_ = bf16[1,256,1024]{2,1,0:T(8,128)(2,1)S(1)} collective-permute-done((bf16[1,256,1024]{2,1,0:T(8,128)(2,1)S(1)}, bf16[1,256,1024]{2,1,0:T(8,128)(2,1)S(1)}, u32[]{:S(2)}, u32[]{:S(2)}) %collective-permute-start.4) | collective-permute-done | bytes 524320 | tf_op jit(solution)/shard_map/ppermute | solution.py:477
  41.8 4.6 %collective-permute-start.11 = (bf16[512,512]{1,0:T(8,128)(2,1)S(1)}, bf16[512,512]{1,0:T(8,128)(2,1)S(1)}, u32[]{:S(2)}, u32[]{:S(2)}) collective-permute-start(bf16[512,512]{1,0:T(8,128)(2,1)S(1)} %get-tuple-element.121.refs_0_), channel_id=1, source_target_pairs={{0,1},{3,2},{4,5},{7,6},{8,9},{11,10},{12,13},{15,14},{16,17},{19,... | collective-permute-start | bytes 1572872 | tf_op jit(solution)/shard_map/ppermute | solution.py:522
  46.4 1.7 %collective-permute-done.8.refs_1_ = bf16[512,512]{1,0:T(8,128)(2,1)S(1)} collective-permute-done((bf16[512,512]{1,0:T(8,128)(2,1)S(1)}, bf16[512,512]{1,0:T(8,128)(2,1)S(1)}, u32[]{:S(2)}, u32[]{:S(2)}) %collective-permute-start.8) | collective-permute-done | bytes 524320 | tf_op jit(solution)/shard_map/ppermute | solution.py:522
  49.0 5.7 %collective-permute-done.6.refs_2_.refs_13_ = bf16[512,512]{1,0:T(8,128)(2,1)S(1)} collective-permute-done((bf16[512,512]{1,0:T(8,128)(2,1)S(1)}, bf16[512,512]{1,0:T(8,128)(2,1)S(1)}, u32[]{:S(2)}, u32[]{:S(2)}) %collective-permute-start.6) | collective-permute-done | bytes 524320 | tf_op jit(solution)/shard_map/ppermute | solution.py:537
  62.7 10.1 %collective-permute-done.9.refs_2_.refs_15_ = bf16[512,512]{1,0:T(8,128)(2,1)S(1)} collective-permute-done((bf16[512,512]{1,0:T(8,128)(2,1)S(1)}, bf16[512,512]{1,0:T(8,128)(2,1)S(1)}, u32[]{:S(2)}, u32[]{:S(2)}) %collective-permute-start.9) | collective-permute-done | bytes 524320 | tf_op jit(solution)/shard_map/ppermute | solution.py:537
  79.4 4.6 %collective-permute-done.12.refs_1_.refs_2_.refs_17_ = bf16[512,512]{1,0:T(8,128)(2,1)S(1)} collective-permute-done((bf16[512,512]{1,0:T(8,128)(2,1)S(1)}, bf16[512,512]{1,0:T(8,128)(2,1)S(1)}, u32[]{:S(2)}, u32[]{:S(2)}) %collective-permute-start.12) | collective-permute-done | bytes 524320 | tf_op jit(solution)/shard_map/ppermute | solution.py:537
  90.8 2.4 %collective-permute-done.24.refs_3_ = bf16[1,64,1024]{2,1,0:T(8,128)(2,1)S(1)} collective-permute-done((bf16[1,64,1024]{2,1,0:T(8,128)(2,1)S(1)}, bf16[1,64,1024]{2,1,0:T(8,128)(2,1)S(1)}, u32[]{:S(2)}, u32[]{:S(2)}) %collective-permute-start.24) | collective-permute-done | bytes 131104 | tf_op jit(solution)/shard_map/ppermute | solution.py:477
  93.3 3.9 %collective-permute-done.21.refs_2_ = bf16[1,64,1024]{2,1,0:T(8,128)(2,1)S(1)} collective-permute-done((bf16[1,64,1024]{2,1,0:T(8,128)(2,1)S(1)}, bf16[1,64,1024]{2,1,0:T(8,128)(2,1)S(1)}, u32[]{:S(2)}, u32[]{:S(2)}) %collective-permute-start.21) | collective-permute-done | bytes 131104 | tf_op jit(solution)/shard_map/ppermute | solution.py:477
  97.3 2.0 %shard_map.179 = (bf16[4,128,1024]{2,1,0:T(8,128)(2,1)S(1)}, bf16[4,128,1024]{2,1,0:T(8,128)(2,1)S(1)}, f32[8,128]{1,0:T(8,128)S(1)}) custom-call(s32[4]{0:T(128)S(1)} %pad_add_fusion.refs_0_, bf16[512,512]{1,0:T(8,128)(2,1)S(1)} %get-tuple-element.125.refs_1_.refs_16_, bf16[512,512]{1,0:T(8,128)(2,1)S(1)} %collective-permute-done.12.refs_1_.refs_2_.refs_17_, ...), custom_call_target="tpu_custom_call" | custom-call | flops 1 | bytes 1 | tf_op jit(solution)/shard_map/pallas_call | solution.py:442
  105.4 1.7 %collective-permute-start.33 = (bf16[1,128,1024]{2,1,0:T(8,128)(2,1)S(1)}, bf16[1,128,1024]{2,1,0:T(8,128)(2,1)S(1)}, u32[]{:S(2)}, u32[]{:S(2)}) collective-permute-start(bf16[1,128,1024]{2,1,0:T(8,128)(2,1)S(1)} %get-tuple-element.167), channel_id=1, source_target_pairs={{0,24},{4,28},{8,16},{12,20},{16,8},{20,12},{24,0},{28,4},{1,25},{... | collective-permute-start | bytes 786440 | tf_op jit(solution)/shard_map/ppermute | solution.py:477
  108.3 8.5 %shard_map.181 = (bf16[512,1024]{1,0:T(8,128)(2,1)}, f32[8,128]{1,0:T(8,128)S(1)}) custom-call(s32[4]{0:T(128)S(1)} %pad_add_fusion.refs_0_, f32[16,512]{1,0:T(8,128)} %bitcast.46, bf16[512,1024]{1,0:T(8,128)(2,1)} %refs_2_.3, bf16[512,256]{1,0:T(8,128)(2,1)} %refs_3_.3, bf16[512,256]{1,0:T(8,128)(2,1)} %refs_4_.3, f32[1,1024]{1,0:T(1,128)} %bitcast.48, ...), custom_call_target="tpu_custom_call" | custom-call | flops 1 | bytes 1 | tf_op jit(solution)/shard_map/pallas_call | solution.py:442
  116.8 3.2 %collective-permute-done.29.refs_3_ = bf16[1,64,1024]{2,1,0:T(8,128)(2,1)S(1)} collective-permute-done((bf16[1,64,1024]{2,1,0:T(8,128)(2,1)S(1)}, bf16[1,64,1024]{2,1,0:T(8,128)(2,1)S(1)}, u32[]{:S(2)}, u32[]{:S(2)}) %collective-permute-start.29) | collective-permute-done | bytes 131104 | tf_op jit(solution)/shard_map/ppermute | solution.py:477
  121.3 2.1 %collective-permute-start.37 = (f32[8,128]{1,0:T(8,128)S(1)}, f32[8,128]{1,0:T(8,128)S(1)}, u32[]{:S(2)}, u32[]{:S(2)}) collective-permute-start(f32[8,128]{1,0:T(8,128)S(1)} %get-tuple-element.172.refs_0_), channel_id=1, source_target_pairs={{0,1},{1,0},{2,3},{3,2},{4,5},{5,4},{6,7},{7,6},{8,9},{9,8},{10,11... | collective-permute-start | bytes 12296 | tf_op jit(solution)/shard_map/ppermute | solution.py:648
  127.9 3.6 %collective-permute-done.38.refs_1_ = f32[8,128]{1,0:T(8,128)S(1)} collective-permute-done((f32[8,128]{1,0:T(8,128)S(1)}, f32[8,128]{1,0:T(8,128)S(1)}, u32[]{:S(2)}, u32[]{:S(2)}) %collective-permute-start.38) | collective-permute-done | bytes 4128 | tf_op jit(solution)/shard_map/ppermute | solution.py:648
  132.3 4.8 %collective-permute-done.39.refs_1_ = f32[8,128]{1,0:T(8,128)S(1)} collective-permute-done((f32[8,128]{1,0:T(8,128)S(1)}, f32[8,128]{1,0:T(8,128)S(1)}, u32[]{:S(2)}, u32[]{:S(2)}) %collective-permute-start.39) | collective-permute-done | bytes 4128 | tf_op jit(solution)/shard_map/ppermute | solution.py:477
  138.4 2.3 %collective-permute-done.40.refs_1_ = f32[8,128]{1,0:T(8,128)S(1)} collective-permute-done((f32[8,128]{1,0:T(8,128)S(1)}, f32[8,128]{1,0:T(8,128)S(1)}, u32[]{:S(2)}, u32[]{:S(2)}) %collective-permute-start.40) | collective-permute-done | bytes 4128 | tf_op jit(solution)/shard_map/ppermute | solution.py:477
  141.4 2.2 %collective-permute-done.42.refs_15_ = f32[8,128]{1,0:T(8,128)S(1)} collective-permute-done((f32[8,128]{1,0:T(8,128)S(1)}, f32[8,128]{1,0:T(8,128)S(1)}, u32[]{:S(2)}, u32[]{:S(2)}) %collective-permute-start.42) | collective-permute-done | bytes 4128 | tf_op jit(solution)/shard_map/ppermute | solution.py:477
  143.5 4.8 %shard_map.190 = (bf16[2048,1024]{1,0:T(8,128)(2,1)}, f32[256,1024]{1,0:T(8,128)}, f32[256,1024]{1,0:T(8,128)}, f32[8,128]{1,0:T(8,128)}) custom-call(s32[4]{0:T(128)S(1)} %pad_add_fusion.refs_0_, f32[256,1024]{1,0:T(8,128)S(1)} %get-tuple-element.103.refs_0_.refs_1_, f32[256,1024]{1,0:T(8,128)S(1)} %get-tuple-element.104.refs_1_.refs_2_, ...), custom_call_target="tpu_custom_call" | custom-call | flops 1 | bytes 1 | tf_op jit(solution)/shard_map/pallas_call | solution.py:442
  (99 shorter events, 48.0 us)
Async XLA Ops:
  8.3 17.3 %collective-permute-start = (bf16[512,512]{1,0:T(8,128)(2,1)S(1)}, bf16[512,512]{1,0:T(8,128)(2,1)S(1)}, u32[]{:S(2)}, u32[]{:S(2)}) collective-permute-start(bf16[512,512]{1,0:T(8,128)(2,1)S(1)} %get-tuple-element.102.refs_0_), channel_id=1, source_target_pairs={{0,1},{3,2},{4,5},{7,6},{8,9},{11,10},{12,13},{15,14},{16,17},{19,... | collective-permute-start | bytes 1572872 | tf_op jit(solution)/shard_map/ppermute | solution.py:522
  13.4 14.9 %collective-permute-start.3 = (bf16[1,256,1024]{2,1,0:T(8,128)(2,1)S(1)}, bf16[1,256,1024]{2,1,0:T(8,128)(2,1)S(1)}, u32[]{:S(2)}, u32[]{:S(2)}) collective-permute-start(bf16[1,256,1024]{2,1,0:T(8,128)(2,1)S(1)} %bitcast.27), channel_id=1, source_target_pairs={{0,8},{4,12},{8,0},{12,4},{16,24},{20,28},{24,16},{28,20},{1,9},{5... | collective-permute-start | bytes 1572872 | tf_op jit(solution)/shard_map/ppermute | solution.py:477
  15.0 24.3 %collective-permute-start.4 = (bf16[1,256,1024]{2,1,0:T(8,128)(2,1)S(1)}, bf16[1,256,1024]{2,1,0:T(8,128)(2,1)S(1)}, u32[]{:S(2)}, u32[]{:S(2)}) collective-permute-start(bf16[1,256,1024]{2,1,0:T(8,128)(2,1)S(1)} %bitcast.28), channel_id=1, source_target_pairs={{0,16},{4,20},{8,24},{12,28},{16,0},{20,4},{24,8},{28,12},{1,17},{... | collective-permute-start | bytes 1572872 | tf_op jit(solution)/shard_map/ppermute | solution.py:477
  16.5 22.8 %collective-permute-start.5 = (bf16[1,256,1024]{2,1,0:T(8,128)(2,1)S(1)}, bf16[1,256,1024]{2,1,0:T(8,128)(2,1)S(1)}, u32[]{:S(2)}, u32[]{:S(2)}) collective-permute-start(bf16[1,256,1024]{2,1,0:T(8,128)(2,1)S(1)} %bitcast.29), channel_id=1, source_target_pairs={{0,24},{4,28},{8,16},{12,20},{16,8},{20,12},{24,0},{28,4},{1,25},{... | collective-permute-start | bytes 1572872 | tf_op jit(solution)/shard_map/ppermute | solution.py:477
  19.5 20.0 %collective-permute-start.2 = (bf16[512,512]{1,0:T(8,128)(2,1)S(1)}, bf16[512,512]{1,0:T(8,128)(2,1)S(1)}, u32[]{:S(2)}, u32[]{:S(2)}) collective-permute-start(bf16[512,512]{1,0:T(8,128)(2,1)S(1)} %get-tuple-element.109.refs_0_), channel_id=1, source_target_pairs={{0,1},{3,2},{4,5},{7,6},{8,9},{11,10},{12,13},{15,14},{16,17},{19,... | collective-permute-start | bytes 1572872 | tf_op jit(solution)/shard_map/ppermute | solution.py:522
  25.7 14.6 %collective-permute-start.1 = (bf16[512,512]{1,0:T(8,128)(2,1)S(1)}, bf16[512,512]{1,0:T(8,128)(2,1)S(1)}, u32[]{:S(2)}, u32[]{:S(2)}) collective-permute-start(bf16[512,512]{1,0:T(8,128)(2,1)S(1)} %get-tuple-element.108.refs_0_), channel_id=1, source_target_pairs={{1,2},{2,1},{5,6},{6,5},{9,10},{10,9},{13,14},{14,13},{17,18},{18,... | collective-permute-start | bytes 1572872 | tf_op jit(solution)/shard_map/ppermute | solution.py:533
  28.3 19.7 %collective-permute-start.8 = (bf16[512,512]{1,0:T(8,128)(2,1)S(1)}, bf16[512,512]{1,0:T(8,128)(2,1)S(1)}, u32[]{:S(2)}, u32[]{:S(2)}) collective-permute-start(bf16[512,512]{1,0:T(8,128)(2,1)S(1)} %get-tuple-element.116.refs_0_), channel_id=1, source_target_pairs={{0,1},{3,2},{4,5},{7,6},{8,9},{11,10},{12,13},{15,14},{16,17},{19,... | collective-permute-start | bytes 1572872 | tf_op jit(solution)/shard_map/ppermute | solution.py:522
  40.5 14.3 %collective-permute-start.6 = (bf16[512,512]{1,0:T(8,128)(2,1)S(1)}, bf16[512,512]{1,0:T(8,128)(2,1)S(1)}, u32[]{:S(2)}, u32[]{:S(2)}) collective-permute-start(bf16[512,512]{1,0:T(8,128)(2,1)S(1)} %get-tuple-element.114.refs_1_.refs_12_), channel_id=1, source_target_pairs={{1,0},{2,3},{5,4},{6,7},{9,8},{10,11},{13,12},{14,15},{17,16},{18,... | collective-permute-start | bytes 1572872 | tf_op jit(solution)/shard_map/ppermute | solution.py:537
  41.8 16.4 %collective-permute-start.11 = (bf16[512,512]{1,0:T(8,128)(2,1)S(1)}, bf16[512,512]{1,0:T(8,128)(2,1)S(1)}, u32[]{:S(2)}, u32[]{:S(2)}) collective-permute-start(bf16[512,512]{1,0:T(8,128)(2,1)S(1)} %get-tuple-element.121.refs_0_), channel_id=1, source_target_pairs={{0,1},{3,2},{4,5},{7,6},{8,9},{11,10},{12,13},{15,14},{16,17},{19,... | collective-permute-start | bytes 1572872 | tf_op jit(solution)/shard_map/ppermute | solution.py:522
  48.2 10.8 %collective-permute-start.10 = (bf16[512,512]{1,0:T(8,128)(2,1)S(1)}, bf16[512,512]{1,0:T(8,128)(2,1)S(1)}, u32[]{:S(2)}, u32[]{:S(2)}) collective-permute-start(bf16[512,512]{1,0:T(8,128)(2,1)S(1)} %get-tuple-element.120.refs_0_), channel_id=1, source_target_pairs={{1,2},{2,1},{5,6},{6,5},{9,10},{10,9},{13,14},{14,13},{17,18},{18,... | collective-permute-start | bytes 1572872 | tf_op jit(solution)/shard_map/ppermute | solution.py:533
  56.1 16.6 %collective-permute-start.9 = (bf16[512,512]{1,0:T(8,128)(2,1)S(1)}, bf16[512,512]{1,0:T(8,128)(2,1)S(1)}, u32[]{:S(2)}, u32[]{:S(2)}) collective-permute-start(bf16[512,512]{1,0:T(8,128)(2,1)S(1)} %get-tuple-element.119.refs_1_.refs_14_), channel_id=1, source_target_pairs={{1,0},{2,3},{5,4},{6,7},{9,8},{10,11},{13,12},{14,15},{17,16},{18,... | collective-permute-start | bytes 1572872 | tf_op jit(solution)/shard_map/ppermute | solution.py:537
  58.3 16.5 %collective-permute-start.13 = (bf16[512,512]{1,0:T(8,128)(2,1)S(1)}, bf16[512,512]{1,0:T(8,128)(2,1)S(1)}, u32[]{:S(2)}, u32[]{:S(2)}) collective-permute-start(bf16[512,512]{1,0:T(8,128)(2,1)S(1)} %get-tuple-element.126.refs_0_), channel_id=1, source_target_pairs={{1,2},{2,1},{5,6},{6,5},{9,10},{10,9},{13,14},{14,13},{17,18},{18,... | collective-permute-start | bytes 1572872 | tf_op jit(solution)/shard_map/ppermute | solution.py:533
  59.8 14.4 %collective-permute-start.15 = (bf16[2,64,1024]{2,1,0:T(8,128)(2,1)S(1)}, bf16[2,64,1024]{2,1,0:T(8,128)(2,1)S(1)}, u32[]{:S(2)}, u32[]{:S(2)}) collective-permute-start(bf16[2,64,1024]{2,1,0:T(8,128)(2,1)S(1)} %get-tuple-element.131), channel_id=1, source_target_pairs={{0,8},{4,12},{8,0},{12,4},{16,24},{20,28},{24,16},{28,20},{1,9},{5... | collective-permute-start | bytes 786440 | tf_op jit(solution)/shard_map/ppermute | solution.py:477
  61.4 22.6 %collective-permute-start.19 = (bf16[4,256,1024]{2,1,0:T(8,128)(2,1)S(1)}, bf16[4,256,1024]{2,1,0:T(8,128)(2,1)S(1)}, u32[]{:S(2)}, u32[]{:S(2)}) collective-permute-start(bf16[4,256,1024]{2,1,0:T(8,128)(2,1)S(1)} %get-tuple-element.142.refs_3_), channel_id=1, source_target_pairs={{0,4},{4,0},{8,12},{12,8},{16,20},{20,16},{24,28},{28,24},{1,5},{5... | collective-permute-start | bytes 6291464 | tf_op jit(solution)/shard_map/ppermute | solution.py:477
  61.4 22.6 %collective-permute-start.12 = (bf16[512,512]{1,0:T(8,128)(2,1)S(1)}, bf16[512,512]{1,0:T(8,128)(2,1)S(1)}, u32[]{:S(2)}, u32[]{:S(2)}) collective-permute-start(bf16[512,512]{1,0:T(8,128)(2,1)S(1)} %get-tuple-element.125.refs_1_.refs_16_), channel_id=1, source_target_pairs={{1,0},{2,3},{5,4},{6,7},{9,8},{10,11},{13,12},{14,15},{17,16},{18,... | collective-permute-start | bytes 1572872 | tf_op jit(solution)/shard_map/ppermute | solution.py:537
  74.9 22.4 %collective-permute-start.16 = (bf16[512,512]{1,0:T(8,128)(2,1)S(1)}, bf16[512,512]{1,0:T(8,128)(2,1)S(1)}, u32[]{:S(2)}, u32[]{:S(2)}) collective-permute-start(bf16[512,512]{1,0:T(8,128)(2,1)S(1)} %get-tuple-element.135.refs_3_.refs_18_), channel_id=1, source_target_pairs={{1,0},{2,3},{5,4},{6,7},{9,8},{10,11},{13,12},{14,15},{17,16},{18,... | collective-permute-start | bytes 1572872 | tf_op jit(solution)/shard_map/ppermute | solution.py:537
  99.4 20.7 %collective-permute-start.26 = (bf16[4,64,1024]{2,1,0:T(8,128)(2,1)S(1)}, bf16[4,64,1024]{2,1,0:T(8,128)(2,1)S(1)}, u32[]{:S(2)}, u32[]{:S(2)}) collective-permute-start(bf16[4,64,1024]{2,1,0:T(8,128)(2,1)S(1)} %get-tuple-element.159.refs_5_), channel_id=1, source_target_pairs={{0,4},{4,0},{8,12},{12,8},{16,20},{20,16},{24,28},{28,24},{1,5},{5... | collective-permute-start | bytes 1572872 | tf_op jit(solution)/shard_map/ppermute | solution.py:477
  103.0 17.2 %collective-permute-start.31 = (bf16[1,128,1024]{2,1,0:T(8,128)(2,1)S(1)}, bf16[1,128,1024]{2,1,0:T(8,128)(2,1)S(1)}, u32[]{:S(2)}, u32[]{:S(2)}) collective-permute-start(bf16[1,128,1024]{2,1,0:T(8,128)(2,1)S(1)} %get-tuple-element.165), channel_id=1, source_target_pairs={{0,8},{4,12},{8,0},{12,4},{16,24},{20,28},{24,16},{28,20},{1,9},{5... | collective-permute-start | bytes 786440 | tf_op jit(solution)/shard_map/ppermute | solution.py:477
  104.4 16.5 %collective-permute-start.32 = (bf16[1,128,1024]{2,1,0:T(8,128)(2,1)S(1)}, bf16[1,128,1024]{2,1,0:T(8,128)(2,1)S(1)}, u32[]{:S(2)}, u32[]{:S(2)}) collective-permute-start(bf16[1,128,1024]{2,1,0:T(8,128)(2,1)S(1)} %get-tuple-element.166), channel_id=1, source_target_pairs={{0,16},{4,20},{8,24},{12,28},{16,0},{20,4},{24,8},{28,12},{1,17},{... | collective-permute-start | bytes 786440 | tf_op jit(solution)/shard_map/ppermute | solution.py:477
  105.4 15.5 %collective-permute-start.33 = (bf16[1,128,1024]{2,1,0:T(8,128)(2,1)S(1)}, bf16[1,128,1024]{2,1,0:T(8,128)(2,1)S(1)}, u32[]{:S(2)}, u32[]{:S(2)}) collective-permute-start(bf16[1,128,1024]{2,1,0:T(8,128)(2,1)S(1)} %get-tuple-element.167), channel_id=1, source_target_pairs={{0,24},{4,28},{8,16},{12,20},{16,8},{20,12},{24,0},{28,4},{1,25},{... | collective-permute-start | bytes 786440 | tf_op jit(solution)/shard_map/ppermute | solution.py:477
  107.1 12.9 %collective-permute-start.29 = (bf16[1,64,1024]{2,1,0:T(8,128)(2,1)S(1)}, bf16[1,64,1024]{2,1,0:T(8,128)(2,1)S(1)}, u32[]{:S(2)}, u32[]{:S(2)}) collective-permute-start(bf16[1,64,1024]{2,1,0:T(8,128)(2,1)S(1)} %bitcast.38), channel_id=1, source_target_pairs={{0,24},{4,28},{8,16},{12,20},{16,8},{20,12},{24,0},{28,4},{1,25},{... | collective-permute-start | bytes 393224 | tf_op jit(solution)/shard_map/ppermute | solution.py:477
  123.4 17.3 %collective-permute-start.34 = (bf16[1,128,1024]{2,1,0:T(8,128)(2,1)S(1)}, bf16[1,128,1024]{2,1,0:T(8,128)(2,1)S(1)}, u32[]{:S(2)}, u32[]{:S(2)}) collective-permute-start(bf16[1,128,1024]{2,1,0:T(8,128)(2,1)S(1)} %get-tuple-element.171.refs_0_), channel_id=1, source_target_pairs={{0,8},{4,12},{8,0},{12,4},{16,24},{20,28},{24,16},{28,20},{1,9},{5... | collective-permute-start | bytes 786440 | tf_op jit(solution)/shard_map/ppermute | solution.py:477
  124.2 16.5 %collective-permute-start.35 = (bf16[1,128,1024]{2,1,0:T(8,128)(2,1)S(1)}, bf16[1,128,1024]{2,1,0:T(8,128)(2,1)S(1)}, u32[]{:S(2)}, u32[]{:S(2)}) collective-permute-start(bf16[1,128,1024]{2,1,0:T(8,128)(2,1)S(1)} %get-tuple-element.171.refs_0_), channel_id=1, source_target_pairs={{0,16},{4,20},{8,24},{12,28},{16,0},{20,4},{24,8},{28,12},{1,17},{... | collective-permute-start | bytes 786440 | tf_op jit(solution)/shard_map/ppermute | solution.py:477
  125.4 15.4 %collective-permute-start.36 = (bf16[1,128,1024]{2,1,0:T(8,128)(2,1)S(1)}, bf16[1,128,1024]{2,1,0:T(8,128)(2,1)S(1)}, u32[]{:S(2)}, u32[]{:S(2)}) collective-permute-start(bf16[1,128,1024]{2,1,0:T(8,128)(2,1)S(1)} %get-tuple-element.171.refs_0_), channel_id=1, source_target_pairs={{0,24},{4,28},{8,16},{12,20},{16,8},{20,12},{24,0},{28,4},{1,25},{... | collective-permute-start | bytes 786440 | tf_op jit(solution)/shard_map/ppermute | solution.py:477
  (19 other events, 103.6 us)

commit v16 on v14

--- a/solution.py
+++ b/solution.py
@@ -631,10 +631,10 @@
     held[end] = new_rows(end)
     narrow(end, by_two)
     grad_input = backward(0, groups, None)
+    own_rows(end, large_cost, [gathered[0][1]] if early else [])
+    last_landed = landing(end, by_two)
     widen(end - 1, by_two, landed[end - 1])
     finish(end - 1)
-    own_rows(end, large_cost, [gathered[0][1]] if early else [])
-    last_landed = landing(end, by_two)
     total = squares[end]
     for bit in range(heads_over.bit_length() - 1):
         pairs = [(t, t ^ (1 << bit)) for t in range(heads_over)]

time: 148 us -> 151 us (1.020)
  waiting for transfers between devices: 57.6 us -> 60.4 us
    ppermute x29, waiting for transfers between devices: 27 us -> 29.7 us  [exchange(): lax.ppermute(value, 'replica', [(r, r ^ mask) for r in range(replicas)])]
where the time goes in v16:
time: 151 us
  waiting for transfers between devices  60.4 us (40%)
  starting transfers between devices  54.9 us (36%)
  Pallas kernels  34.2 us (23%)
    pallas_call x34, Pallas kernels, run(): pl.pallas_call(in_turn(kernel, len(inputs), len(waits), len(outs)), in_sp...  34.2 us
    ppermute x29, waiting for transfers between devices, exchange(): lax.ppermute(value, 'replica', [(r, r ^ mask) for r in range(replicas)])  29.7 us
    ppermute x29, starting transfers between devices, exchange(): lax.ppermute(value, 'replica', [(r, r ^ mask) for r in range(replicas)])  25.7 us
    ppermute x4, waiting for transfers between devices, sum_all(): back = lax.ppermute(out, 'tensor', [(b, a) for a, b in pairs])  20.3 us
    ppermute x4, starting transfers between devices, shards(): lax.ppermute(p, 'tensor', in_hops[0])  16.2 us
    ppermute x4, waiting for transfers between devices, shards(): lax.ppermute(p, 'tensor', in_hops[0])  7.16 us
    ppermute x4, starting transfers between devices, sum_all(): back = lax.ppermute(out, 'tensor', [(b, a) for a, b in pairs])  5.34 us
    ppermute x2, starting transfers between devices, shards(): lax.ppermute(total, 'tensor', pairs)  4.91 us
  transfers between devices with their start and end apart: 43, of which 19 were waited for; matrix products, arithmetic and copies ran while one was open for 0% of the time, Pallas kernels for 13%

profile of v16, /device:TPU:0, one launch (start us, length us, event | category | flops | bytes accessed | tf_op | source)
XLA Modules:
  0.0 150.8 jit_solution(5558271001968833845)
XLA Ops:
  0.7 6.2 %shard_map.156 = (bf16[8,256,1024]{2,1,0:T(8,128)(2,1)S(1)}, bf16[128,2048]{1,0:T(8,128)(2,1)S(1)}, f32[256,1024]{1,0:T(8,128)S(1)}, f32[256,1024]{1,0:T(8,128)S...) custom-call(f32[16,512]{1,0:T(8,128)} %bitcast.48, bf16[512,1024]{1,0:T(8,128)(2,1)} %refs_1_.1, ...), custom_call_target="tpu_custom_call" | custom-call | flops 1 | bytes 1 | tf_op jit(solution)/shard_map/pallas_call | solution.py:438
  8.3 5.0 %collective-permute-start = (bf16[512,512]{1,0:T(8,128)(2,1)S(1)}, bf16[512,512]{1,0:T(8,128)(2,1)S(1)}, u32[]{:S(2)}, u32[]{:S(2)}) collective-permute-start(bf16[512,512]{1,0:T(8,128)(2,1)S(1)} %get-tuple-element.100.refs_0_), channel_id=1, source_target_pairs={{0,1},{3,2},{4,5},{7,6},{8,9},{11,10},{12,13},{15,14},{16,17},{19,... | collective-permute-start | bytes 1572872 | tf_op jit(solution)/shard_map/ppermute | solution.py:518
  17.0 2.5 %shard_map.159 = (bf16[512,512]{1,0:T(8,128)(2,1)S(1)}, bf16[512,512]{1,0:T(8,128)(2,1)S(1)}, bf16[512,512]{1,0:T(8,128)(2,1)S(1)}, f32[8,128]{1,0:T(8,128)S(1)}) custom-call(s32[4]{0:T(128)S(1)} %pad_add_fusion.refs_0_, bf16[8,256,1024]{2,1,0:T(8,128)(2,1)S(1)} %get-tuple-element.97.refs_1_.refs_4_.refs_6_.refs_11_, ...), custom_call_target="tpu_custom_call" | custom-call | flops 1 | bytes 1 | tf_op jit(solution)/shard_map/pallas_call | solution.py:438
  20.8 4.8 %collective-permute-done.refs_1_ = bf16[512,512]{1,0:T(8,128)(2,1)S(1)} collective-permute-done((bf16[512,512]{1,0:T(8,128)(2,1)S(1)}, bf16[512,512]{1,0:T(8,128)(2,1)S(1)}, u32[]{:S(2)}, u32[]{:S(2)}) %collective-permute-start) | collective-permute-done | bytes 524320 | tf_op jit(solution)/shard_map/ppermute | solution.py:518
  26.4 1.9 %collective-permute-done.3.refs_1_ = bf16[1,256,1024]{2,1,0:T(8,128)(2,1)S(1)} collective-permute-done((bf16[1,256,1024]{2,1,0:T(8,128)(2,1)S(1)}, bf16[1,256,1024]{2,1,0:T(8,128)(2,1)S(1)}, u32[]{:S(2)}, u32[]{:S(2)}) %collective-permute-start.3) | collective-permute-done | bytes 524320 | tf_op jit(solution)/shard_map/ppermute | solution.py:473
  28.3 5.3 %collective-permute-start.8 = (bf16[512,512]{1,0:T(8,128)(2,1)S(1)}, bf16[512,512]{1,0:T(8,128)(2,1)S(1)}, u32[]{:S(2)}, u32[]{:S(2)}) collective-permute-start(bf16[512,512]{1,0:T(8,128)(2,1)S(1)} %get-tuple-element.114.refs_0_), channel_id=1, source_target_pairs={{0,1},{3,2},{4,5},{7,6},{8,9},{11,10},{12,13},{15,14},{16,17},{19,... | collective-permute-start | bytes 1572872 | tf_op jit(solution)/shard_map/ppermute | solution.py:518
  33.6 5.7 %collective-permute-done.4.refs_2_ = bf16[1,256,1024]{2,1,0:T(8,128)(2,1)S(1)} collective-permute-done((bf16[1,256,1024]{2,1,0:T(8,128)(2,1)S(1)}, bf16[1,256,1024]{2,1,0:T(8,128)(2,1)S(1)}, u32[]{:S(2)}, u32[]{:S(2)}) %collective-permute-start.4) | collective-permute-done | bytes 524320 | tf_op jit(solution)/shard_map/ppermute | solution.py:473
  41.8 4.6 %collective-permute-start.11 = (bf16[512,512]{1,0:T(8,128)(2,1)S(1)}, bf16[512,512]{1,0:T(8,128)(2,1)S(1)}, u32[]{:S(2)}, u32[]{:S(2)}) collective-permute-start(bf16[512,512]{1,0:T(8,128)(2,1)S(1)} %get-tuple-element.119.refs_0_), channel_id=1, source_target_pairs={{0,1},{3,2},{4,5},{7,6},{8,9},{11,10},{12,13},{15,14},{16,17},{19,... | collective-permute-start | bytes 1572872 | tf_op jit(solution)/shard_map/ppermute | solution.py:518
  49.0 5.7 %collective-permute-done.6.refs_2_.refs_13_ = bf16[512,512]{1,0:T(8,128)(2,1)S(1)} collective-permute-done((bf16[512,512]{1,0:T(8,128)(2,1)S(1)}, bf16[512,512]{1,0:T(8,128)(2,1)S(1)}, u32[]{:S(2)}, u32[]{:S(2)}) %collective-permute-start.6) | collective-permute-done | bytes 524320 | tf_op jit(solution)/shard_map/ppermute | solution.py:533
  62.6 10.1 %collective-permute-done.9.refs_2_.refs_15_ = bf16[512,512]{1,0:T(8,128)(2,1)S(1)} collective-permute-done((bf16[512,512]{1,0:T(8,128)(2,1)S(1)}, bf16[512,512]{1,0:T(8,128)(2,1)S(1)}, u32[]{:S(2)}, u32[]{:S(2)}) %collective-permute-start.9) | collective-permute-done | bytes 524320 | tf_op jit(solution)/shard_map/ppermute | solution.py:533
  79.4 4.6 %collective-permute-done.12.refs_1_.refs_2_.refs_17_ = bf16[512,512]{1,0:T(8,128)(2,1)S(1)} collective-permute-done((bf16[512,512]{1,0:T(8,128)(2,1)S(1)}, bf16[512,512]{1,0:T(8,128)(2,1)S(1)}, u32[]{:S(2)}, u32[]{:S(2)}) %collective-permute-start.12) | collective-permute-done | bytes 524320 | tf_op jit(solution)/shard_map/ppermute | solution.py:533
  90.8 2.4 %collective-permute-done.24.refs_3_ = bf16[1,64,1024]{2,1,0:T(8,128)(2,1)S(1)} collective-permute-done((bf16[1,64,1024]{2,1,0:T(8,128)(2,1)S(1)}, bf16[1,64,1024]{2,1,0:T(8,128)(2,1)S(1)}, u32[]{:S(2)}, u32[]{:S(2)}) %collective-permute-start.24) | collective-permute-done | bytes 131104 | tf_op jit(solution)/shard_map/ppermute | solution.py:473
  93.3 3.9 %collective-permute-done.21.refs_2_ = bf16[1,64,1024]{2,1,0:T(8,128)(2,1)S(1)} collective-permute-done((bf16[1,64,1024]{2,1,0:T(8,128)(2,1)S(1)}, bf16[1,64,1024]{2,1,0:T(8,128)(2,1)S(1)}, u32[]{:S(2)}, u32[]{:S(2)}) %collective-permute-start.21) | collective-permute-done | bytes 131104 | tf_op jit(solution)/shard_map/ppermute | solution.py:473
  97.3 2.0 %shard_map.179 = (bf16[4,128,1024]{2,1,0:T(8,128)(2,1)S(1)}, bf16[4,128,1024]{2,1,0:T(8,128)(2,1)S(1)}, f32[8,128]{1,0:T(8,128)S(1)}) custom-call(s32[4]{0:T(128)S(1)} %pad_add_fusion.refs_0_, bf16[512,512]{1,0:T(8,128)(2,1)S(1)} %get-tuple-element.123.refs_1_.refs_16_, bf16[512,512]{1,0:T(8,128)(2,1)S(1)} %collective-permute-done.12.refs_1_.refs_2_.refs_17_, ...), custom_call_target="tpu_custom_call" | custom-call | flops 1 | bytes 1 | tf_op jit(solution)/shard_map/pallas_call | solution.py:438
  99.9 2.1 %collective-permute-done.25 = bf16[4,128,1024]{2,1,0:T(8,128)(2,1)S(1)} collective-permute-done((bf16[4,128,1024]{2,1,0:T(8,128)(2,1)S(1)}, bf16[4,128,1024]{2,1,0:T(8,128)(2,1)S(1)}, u32[]{:S(2)}, u32[]{:S(2)}) %collective-permute-start.25) | collective-permute-done | bytes 1048608 | tf_op jit(solution)/shard_map/ppermute | solution.py:473
  107.9 8.5 %shard_map.181 = (bf16[512,1024]{1,0:T(8,128)(2,1)}, f32[8,128]{1,0:T(8,128)S(1)}) custom-call(s32[4]{0:T(128)S(1)} %pad_add_fusion.refs_0_, f32[16,512]{1,0:T(8,128)} %bitcast.49, bf16[512,1024]{1,0:T(8,128)(2,1)} %refs_2_.3, bf16[512,256]{1,0:T(8,128)(2,1)} %refs_3_.3, bf16[512,256]{1,0:T(8,128)(2,1)} %refs_4_.3, f32[1,1024]{1,0:T(1,128)} %bitcast.51, ...), custom_call_target="tpu_custom_call" | custom-call | flops 1 | bytes 1 | tf_op jit(solution)/shard_map/pallas_call | solution.py:438
  120.2 3.8 %collective-permute-done.28.refs_2_ = bf16[1,64,1024]{2,1,0:T(8,128)(2,1)S(1)} collective-permute-done((bf16[1,64,1024]{2,1,0:T(8,128)(2,1)S(1)}, bf16[1,64,1024]{2,1,0:T(8,128)(2,1)S(1)}, u32[]{:S(2)}, u32[]{:S(2)}) %collective-permute-start.28) | collective-permute-done | bytes 131104 | tf_op jit(solution)/shard_map/ppermute | solution.py:473
  125.8 1.9 %collective-permute-start.36 = (bf16[1,128,1024]{2,1,0:T(8,128)(2,1)S(1)}, bf16[1,128,1024]{2,1,0:T(8,128)(2,1)S(1)}, u32[]{:S(2)}, u32[]{:S(2)}) collective-permute-start(bf16[1,128,1024]{2,1,0:T(8,128)(2,1)S(1)} %bitcast.37), channel_id=1, source_target_pairs={{0,24},{4,28},{8,16},{12,20},{16,8},{20,12},{24,0},{28,4},{1,25},{... | collective-permute-start | bytes 786440 | tf_op jit(solution)/shard_map/ppermute | solution.py:473
  127.7 2.1 %collective-permute-start.37 = (f32[8,128]{1,0:T(8,128)S(1)}, f32[8,128]{1,0:T(8,128)S(1)}, u32[]{:S(2)}, u32[]{:S(2)}) collective-permute-start(f32[8,128]{1,0:T(8,128)S(1)} %get-tuple-element.168.refs_0_), channel_id=1, source_target_pairs={{0,1},{1,0},{2,3},{3,2},{4,5},{5,4},{6,7},{7,6},{8,9},{9,8},{10,11... | collective-permute-start | bytes 12296 | tf_op jit(solution)/shard_map/ppermute | solution.py:642
  131.3 2.9 %collective-permute-start.38 = (f32[8,128]{1,0:T(8,128)S(1)}, f32[8,128]{1,0:T(8,128)S(1)}, u32[]{:S(2)}, u32[]{:S(2)}) collective-permute-start(f32[8,128]{1,0:T(8,128)S(1)} %get-tuple-element.170.refs_0_), channel_id=1, source_target_pairs={{0,2},{1,3},{2,0},{3,1},{4,6},{5,7},{6,4},{7,5},{8,10},{9,11},{10,... | collective-permute-start | bytes 12296 | tf_op jit(solution)/shard_map/ppermute | solution.py:642
  136.7 2.7 %collective-permute-done.39.refs_1_ = f32[8,128]{1,0:T(8,128)S(1)} collective-permute-done((f32[8,128]{1,0:T(8,128)S(1)}, f32[8,128]{1,0:T(8,128)S(1)}, u32[]{:S(2)}, u32[]{:S(2)}) %collective-permute-start.39) | collective-permute-done | bytes 4128 | tf_op jit(solution)/shard_map/ppermute | solution.py:473
  140.4 2.6 %collective-permute-done.40.refs_1_ = f32[8,128]{1,0:T(8,128)S(1)} collective-permute-done((f32[8,128]{1,0:T(8,128)S(1)}, f32[8,128]{1,0:T(8,128)S(1)}, u32[]{:S(2)}, u32[]{:S(2)}) %collective-permute-start.40) | collective-permute-done | bytes 4128 | tf_op jit(solution)/shard_map/ppermute | solution.py:473
  143.7 2.2 %collective-permute-done.42.refs_15_ = f32[8,128]{1,0:T(8,128)S(1)} collective-permute-done((f32[8,128]{1,0:T(8,128)S(1)}, f32[8,128]{1,0:T(8,128)S(1)}, u32[]{:S(2)}, u32[]{:S(2)}) %collective-permute-start.42) | collective-permute-done | bytes 4128 | tf_op jit(solution)/shard_map/ppermute | solution.py:473
  145.9 4.8 %shard_map.189 = (bf16[2048,1024]{1,0:T(8,128)(2,1)}, f32[256,1024]{1,0:T(8,128)}, f32[256,1024]{1,0:T(8,128)}, f32[8,128]{1,0:T(8,128)}) custom-call(s32[4]{0:T(128)S(1)} %pad_add_fusion.refs_0_, f32[256,1024]{1,0:T(8,128)S(1)} %get-tuple-element.101.refs_0_.refs_1_, f32[256,1024]{1,0:T(8,128)S(1)} %get-tuple-element.102.refs_1_.refs_2_, ...), custom_call_target="tpu_custom_call" | custom-call | flops 1 | bytes 1 | tf_op jit(solution)/shard_map/pallas_call | solution.py:438
  (98 shorter events, 51.7 us)
Async XLA Ops:
  8.3 17.3 %collective-permute-start = (bf16[512,512]{1,0:T(8,128)(2,1)S(1)}, bf16[512,512]{1,0:T(8,128)(2,1)S(1)}, u32[]{:S(2)}, u32[]{:S(2)}) collective-permute-start(bf16[512,512]{1,0:T(8,128)(2,1)S(1)} %get-tuple-element.100.refs_0_), channel_id=1, source_target_pairs={{0,1},{3,2},{4,5},{7,6},{8,9},{11,10},{12,13},{15,14},{16,17},{19,... | collective-permute-start | bytes 1572872 | tf_op jit(solution)/shard_map/ppermute | solution.py:518
  13.4 14.9 %collective-permute-start.3 = (bf16[1,256,1024]{2,1,0:T(8,128)(2,1)S(1)}, bf16[1,256,1024]{2,1,0:T(8,128)(2,1)S(1)}, u32[]{:S(2)}, u32[]{:S(2)}) collective-permute-start(bf16[1,256,1024]{2,1,0:T(8,128)(2,1)S(1)} %bitcast.27), channel_id=1, source_target_pairs={{0,8},{4,12},{8,0},{12,4},{16,24},{20,28},{24,16},{28,20},{1,9},{5... | collective-permute-start | bytes 1572872 | tf_op jit(solution)/shard_map/ppermute | solution.py:473
  15.0 24.3 %collective-permute-start.4 = (bf16[1,256,1024]{2,1,0:T(8,128)(2,1)S(1)}, bf16[1,256,1024]{2,1,0:T(8,128)(2,1)S(1)}, u32[]{:S(2)}, u32[]{:S(2)}) collective-permute-start(bf16[1,256,1024]{2,1,0:T(8,128)(2,1)S(1)} %bitcast.28), channel_id=1, source_target_pairs={{0,16},{4,20},{8,24},{12,28},{16,0},{20,4},{24,8},{28,12},{1,17},{... | collective-permute-start | bytes 1572872 | tf_op jit(solution)/shard_map/ppermute | solution.py:473
  16.5 22.8 %collective-permute-start.5 = (bf16[1,256,1024]{2,1,0:T(8,128)(2,1)S(1)}, bf16[1,256,1024]{2,1,0:T(8,128)(2,1)S(1)}, u32[]{:S(2)}, u32[]{:S(2)}) collective-permute-start(bf16[1,256,1024]{2,1,0:T(8,128)(2,1)S(1)} %bitcast.29), channel_id=1, source_target_pairs={{0,24},{4,28},{8,16},{12,20},{16,8},{20,12},{24,0},{28,4},{1,25},{... | collective-permute-start | bytes 1572872 | tf_op jit(solution)/shard_map/ppermute | solution.py:473
  19.5 20.0 %collective-permute-start.2 = (bf16[512,512]{1,0:T(8,128)(2,1)S(1)}, bf16[512,512]{1,0:T(8,128)(2,1)S(1)}, u32[]{:S(2)}, u32[]{:S(2)}) collective-permute-start(bf16[512,512]{1,0:T(8,128)(2,1)S(1)} %get-tuple-element.107.refs_0_), channel_id=1, source_target_pairs={{0,1},{3,2},{4,5},{7,6},{8,9},{11,10},{12,13},{15,14},{16,17},{19,... | collective-permute-start | bytes 1572872 | tf_op jit(solution)/shard_map/ppermute | solution.py:518
  25.7 14.6 %collective-permute-start.1 = (bf16[512,512]{1,0:T(8,128)(2,1)S(1)}, bf16[512,512]{1,0:T(8,128)(2,1)S(1)}, u32[]{:S(2)}, u32[]{:S(2)}) collective-permute-start(bf16[512,512]{1,0:T(8,128)(2,1)S(1)} %get-tuple-element.106.refs_0_), channel_id=1, source_target_pairs={{1,2},{2,1},{5,6},{6,5},{9,10},{10,9},{13,14},{14,13},{17,18},{18,... | collective-permute-start | bytes 1572872 | tf_op jit(solution)/shard_map/ppermute | solution.py:529
  28.3 19.7 %collective-permute-start.8 = (bf16[512,512]{1,0:T(8,128)(2,1)S(1)}, bf16[512,512]{1,0:T(8,128)(2,1)S(1)}, u32[]{:S(2)}, u32[]{:S(2)}) collective-permute-start(bf16[512,512]{1,0:T(8,128)(2,1)S(1)} %get-tuple-element.114.refs_0_), channel_id=1, source_target_pairs={{0,1},{3,2},{4,5},{7,6},{8,9},{11,10},{12,13},{15,14},{16,17},{19,... | collective-permute-start | bytes 1572872 | tf_op jit(solution)/shard_map/ppermute | solution.py:518
  40.5 14.3 %collective-permute-start.6 = (bf16[512,512]{1,0:T(8,128)(2,1)S(1)}, bf16[512,512]{1,0:T(8,128)(2,1)S(1)}, u32[]{:S(2)}, u32[]{:S(2)}) collective-permute-start(bf16[512,512]{1,0:T(8,128)(2,1)S(1)} %get-tuple-element.112.refs_1_.refs_12_), channel_id=1, source_target_pairs={{1,0},{2,3},{5,4},{6,7},{9,8},{10,11},{13,12},{14,15},{17,16},{18,... | collective-permute-start | bytes 1572872 | tf_op jit(solution)/shard_map/ppermute | solution.py:533
  41.8 16.4 %collective-permute-start.11 = (bf16[512,512]{1,0:T(8,128)(2,1)S(1)}, bf16[512,512]{1,0:T(8,128)(2,1)S(1)}, u32[]{:S(2)}, u32[]{:S(2)}) collective-permute-start(bf16[512,512]{1,0:T(8,128)(2,1)S(1)} %get-tuple-element.119.refs_0_), channel_id=1, source_target_pairs={{0,1},{3,2},{4,5},{7,6},{8,9},{11,10},{12,13},{15,14},{16,17},{19,... | collective-permute-start | bytes 1572872 | tf_op jit(solution)/shard_map/ppermute | solution.py:518
  48.2 10.8 %collective-permute-start.10 = (bf16[512,512]{1,0:T(8,128)(2,1)S(1)}, bf16[512,512]{1,0:T(8,128)(2,1)S(1)}, u32[]{:S(2)}, u32[]{:S(2)}) collective-permute-start(bf16[512,512]{1,0:T(8,128)(2,1)S(1)} %get-tuple-element.118.refs_0_), channel_id=1, source_target_pairs={{1,2},{2,1},{5,6},{6,5},{9,10},{10,9},{13,14},{14,13},{17,18},{18,... | collective-permute-start | bytes 1572872 | tf_op jit(solution)/shard_map/ppermute | solution.py:529
  56.1 16.6 %collective-permute-start.9 = (bf16[512,512]{1,0:T(8,128)(2,1)S(1)}, bf16[512,512]{1,0:T(8,128)(2,1)S(1)}, u32[]{:S(2)}, u32[]{:S(2)}) collective-permute-start(bf16[512,512]{1,0:T(8,128)(2,1)S(1)} %get-tuple-element.117.refs_1_.refs_14_), channel_id=1, source_target_pairs={{1,0},{2,3},{5,4},{6,7},{9,8},{10,11},{13,12},{14,15},{17,16},{18,... | collective-permute-start | bytes 1572872 | tf_op jit(solution)/shard_map/ppermute | solution.py:533
  58.3 16.5 %collective-permute-start.13 = (bf16[512,512]{1,0:T(8,128)(2,1)S(1)}, bf16[512,512]{1,0:T(8,128)(2,1)S(1)}, u32[]{:S(2)}, u32[]{:S(2)}) collective-permute-start(bf16[512,512]{1,0:T(8,128)(2,1)S(1)} %get-tuple-element.124.refs_0_), channel_id=1, source_target_pairs={{1,2},{2,1},{5,6},{6,5},{9,10},{10,9},{13,14},{14,13},{17,18},{18,... | collective-permute-start | bytes 1572872 | tf_op jit(solution)/shard_map/ppermute | solution.py:529
  59.8 14.4 %collective-permute-start.15 = (bf16[2,64,1024]{2,1,0:T(8,128)(2,1)S(1)}, bf16[2,64,1024]{2,1,0:T(8,128)(2,1)S(1)}, u32[]{:S(2)}, u32[]{:S(2)}) collective-permute-start(bf16[2,64,1024]{2,1,0:T(8,128)(2,1)S(1)} %get-tuple-element.129), channel_id=1, source_target_pairs={{0,8},{4,12},{8,0},{12,4},{16,24},{20,28},{24,16},{28,20},{1,9},{5... | collective-permute-start | bytes 786440 | tf_op jit(solution)/shard_map/ppermute | solution.py:473
  61.3 22.6 %collective-permute-start.19 = (bf16[4,256,1024]{2,1,0:T(8,128)(2,1)S(1)}, bf16[4,256,1024]{2,1,0:T(8,128)(2,1)S(1)}, u32[]{:S(2)}, u32[]{:S(2)}) collective-permute-start(bf16[4,256,1024]{2,1,0:T(8,128)(2,1)S(1)} %get-tuple-element.140.refs_3_), channel_id=1, source_target_pairs={{0,4},{4,0},{8,12},{12,8},{16,20},{20,16},{24,28},{28,24},{1,5},{5... | collective-permute-start | bytes 6291464 | tf_op jit(solution)/shard_map/ppermute | solution.py:473
  61.4 22.6 %collective-permute-start.12 = (bf16[512,512]{1,0:T(8,128)(2,1)S(1)}, bf16[512,512]{1,0:T(8,128)(2,1)S(1)}, u32[]{:S(2)}, u32[]{:S(2)}) collective-permute-start(bf16[512,512]{1,0:T(8,128)(2,1)S(1)} %get-tuple-element.123.refs_1_.refs_16_), channel_id=1, source_target_pairs={{1,0},{2,3},{5,4},{6,7},{9,8},{10,11},{13,12},{14,15},{17,16},{18,... | collective-permute-start | bytes 1572872 | tf_op jit(solution)/shard_map/ppermute | solution.py:533
  74.9 22.4 %collective-permute-start.16 = (bf16[512,512]{1,0:T(8,128)(2,1)S(1)}, bf16[512,512]{1,0:T(8,128)(2,1)S(1)}, u32[]{:S(2)}, u32[]{:S(2)}) collective-permute-start(bf16[512,512]{1,0:T(8,128)(2,1)S(1)} %get-tuple-element.133.refs_3_.refs_18_), channel_id=1, source_target_pairs={{1,0},{2,3},{5,4},{6,7},{9,8},{10,11},{13,12},{14,15},{17,16},{18,... | collective-permute-start | bytes 1572872 | tf_op jit(solution)/shard_map/ppermute | solution.py:533
  99.4 17.0 %collective-permute-start.26 = (bf16[4,64,1024]{2,1,0:T(8,128)(2,1)S(1)}, bf16[4,64,1024]{2,1,0:T(8,128)(2,1)S(1)}, u32[]{:S(2)}, u32[]{:S(2)}) collective-permute-start(bf16[4,64,1024]{2,1,0:T(8,128)(2,1)S(1)} %get-tuple-element.157.refs_5_), channel_id=1, source_target_pairs={{0,4},{4,0},{8,12},{12,8},{16,20},{20,16},{24,28},{28,24},{1,5},{5... | collective-permute-start | bytes 1572872 | tf_op jit(solution)/shard_map/ppermute | solution.py:473
  102.8 14.4 %collective-permute-start.30 = (bf16[1,128,1024]{2,1,0:T(8,128)(2,1)S(1)}, bf16[1,128,1024]{2,1,0:T(8,128)(2,1)S(1)}, u32[]{:S(2)}, u32[]{:S(2)}) collective-permute-start(bf16[1,128,1024]{2,1,0:T(8,128)(2,1)S(1)} %get-tuple-element.161), channel_id=1, source_target_pairs={{0,8},{4,12},{8,0},{12,4},{16,24},{20,28},{24,16},{28,20},{1,9},{5... | collective-permute-start | bytes 786440 | tf_op jit(solution)/shard_map/ppermute | solution.py:473
  104.4 14.1 %collective-permute-start.31 = (bf16[1,128,1024]{2,1,0:T(8,128)(2,1)S(1)}, bf16[1,128,1024]{2,1,0:T(8,128)(2,1)S(1)}, u32[]{:S(2)}, u32[]{:S(2)}) collective-permute-start(bf16[1,128,1024]{2,1,0:T(8,128)(2,1)S(1)} %get-tuple-element.162), channel_id=1, source_target_pairs={{0,16},{4,20},{8,24},{12,28},{16,0},{20,4},{24,8},{28,12},{1,17},{... | collective-permute-start | bytes 786440 | tf_op jit(solution)/shard_map/ppermute | solution.py:473
  105.2 13.3 %collective-permute-start.32 = (bf16[1,128,1024]{2,1,0:T(8,128)(2,1)S(1)}, bf16[1,128,1024]{2,1,0:T(8,128)(2,1)S(1)}, u32[]{:S(2)}, u32[]{:S(2)}) collective-permute-start(bf16[1,128,1024]{2,1,0:T(8,128)(2,1)S(1)} %get-tuple-element.163), channel_id=1, source_target_pairs={{0,24},{4,28},{8,16},{12,20},{16,8},{20,12},{24,0},{28,4},{1,25},{... | collective-permute-start | bytes 786440 | tf_op jit(solution)/shard_map/ppermute | solution.py:473
  106.4 13.8 %collective-permute-start.27 = (bf16[1,64,1024]{2,1,0:T(8,128)(2,1)S(1)}, bf16[1,64,1024]{2,1,0:T(8,128)(2,1)S(1)}, u32[]{:S(2)}, u32[]{:S(2)}) collective-permute-start(bf16[1,64,1024]{2,1,0:T(8,128)(2,1)S(1)} %bitcast.39), channel_id=1, source_target_pairs={{0,8},{4,12},{8,0},{12,4},{16,24},{20,28},{24,16},{28,20},{1,9},{5... | collective-permute-start | bytes 393224 | tf_op jit(solution)/shard_map/ppermute | solution.py:473
  124.1 18.9 %collective-permute-start.34 = (bf16[1,128,1024]{2,1,0:T(8,128)(2,1)S(1)}, bf16[1,128,1024]{2,1,0:T(8,128)(2,1)S(1)}, u32[]{:S(2)}, u32[]{:S(2)}) collective-permute-start(bf16[1,128,1024]{2,1,0:T(8,128)(2,1)S(1)} %bitcast.35), channel_id=1, source_target_pairs={{0,8},{4,12},{8,0},{12,4},{16,24},{20,28},{24,16},{28,20},{1,9},{5... | collective-permute-start | bytes 786440 | tf_op jit(solution)/shard_map/ppermute | solution.py:473
  125.0 18.1 %collective-permute-start.35 = (bf16[1,128,1024]{2,1,0:T(8,128)(2,1)S(1)}, bf16[1,128,1024]{2,1,0:T(8,128)(2,1)S(1)}, u32[]{:S(2)}, u32[]{:S(2)}) collective-permute-start(bf16[1,128,1024]{2,1,0:T(8,128)(2,1)S(1)} %bitcast.36), channel_id=1, source_target_pairs={{0,16},{4,20},{8,24},{12,28},{16,0},{20,4},{24,8},{28,12},{1,17},{... | collective-permute-start | bytes 786440 | tf_op jit(solution)/shard_map/ppermute | solution.py:473
  125.8 17.3 %collective-permute-start.36 = (bf16[1,128,1024]{2,1,0:T(8,128)(2,1)S(1)}, bf16[1,128,1024]{2,1,0:T(8,128)(2,1)S(1)}, u32[]{:S(2)}, u32[]{:S(2)}) collective-permute-start(bf16[1,128,1024]{2,1,0:T(8,128)(2,1)S(1)} %bitcast.37), channel_id=1, source_target_pairs={{0,24},{4,28},{8,16},{12,20},{16,8},{20,12},{24,0},{28,4},{1,25},{... | collective-permute-start | bytes 786440 | tf_op jit(solution)/shard_map/ppermute | solution.py:473
  (19 other events, 103.0 us)
